TPU v7x, 32 devices: a whole 2x2x4 slice. The times are simulated.
32 devices in a mesh: groups: 1, ffn: 32 (over z, y, x, core).
Axes of the slice: x: 2, y: 2, z: 4, core: 2. Of those that a mesh axis runs over, the one named last changes fastest.
Arguments:
- tokens: bfloat16 [256, 4096], P(('groups', 'ffn')), may hold values from -500 to 500
- norm_gain: float32 [4096], replicated, may hold values from 0.1 to 1.9
- routes: int32 [256, 8], P(('groups', 'ffn')), may hold values from 0 to 15, all different within a row; in each aligned block of 8 rows (0 to 7, 8 to 15, ...) at most 8 rows name the same one
- gate_scores: float32 [256, 8], P(('groups', 'ffn')), may hold values from 0.05 to 1
- w_gate: bfloat16 [4096, 12288], P(None, 'ffn'), may hold values from -0.09375 to 0.09375
- w_up: bfloat16 [4096, 12288], P(None, 'ffn'), may hold values from -0.09375 to 0.09375
- w_down: bfloat16 [12288, 4096], P('ffn'), may hold values from -0.21875 to 0.21875
- query: bfloat16 [8, 8192], P('groups'), may hold values from -17 to 17
- k_cache: bfloat16 [8, 4096, 512], P('groups', 'ffn'), may hold values from -4 to 4
- v_cache: bfloat16 [8, 4096, 512], P('groups', 'ffn'), may hold values from -4 to 4
- cache_len: int32 [8], P('groups'), may hold values from 256 to 4096, as said below
Outputs:
- combined: bfloat16 [256, 4096], P(('groups', 'ffn'))
- attention: bfloat16 [8, 8192], P('groups', 'ffn')
Inputs may be any that keep to these rules, and one draw needn't show every extreme that they name: `routes`: within the 8 rows of one device no expert is named by more than 8 rows, a bound that some block reaches; a row names 8 different experts. A row uses its first cache_len positions; some row has exactly 4096.
All inputs are finite; a program needn't handle non-finite values.
Results may differ from a plain program's by a relative error of at most 0.012.
Values may be sent and summed in bfloat16 or wider, within the bound.
No kernel may reach another device: no remote copies, remote signals or barrier semaphores. Data moves between devices by JAX's collectives and lax.ppermute only.
A program may use at most 128 MiB of HBM per device.

v0:
```python
import jax
import jax.numpy as jnp
from jax import lax
from jax.sharding import PartitionSpec as P

HEADS = 64
KV_HEADS = 4
HEAD_DIM = 128


def combined_all(part, axis, combine):
    gathered = jax.tree.map(lambda a: lax.all_gather(a, axis), part)

    def take(source):
        return jax.tree.map(lambda a: lax.dynamic_index_in_dim(a, source, 0, False), gathered)

    return lax.fori_loop(
        1, lax.axis_size(axis), lambda source, state: combine(state, take(source)), take(0)
    )


def rms_normed(tokens, norm_gain):
    features = tokens.astype(jnp.float32)
    mean_square = jnp.mean(features * features, axis=-1, keepdims=True)
    return (features * lax.rsqrt(mean_square + 1e-06) * norm_gain).astype(jnp.bfloat16)


def merge_parts(earlier, later):
    peak = jnp.maximum(earlier[0], later[0])
    scale_early = jnp.exp(earlier[0] - peak)
    scale_late = jnp.exp(later[0] - peak)
    return (
        peak,
        earlier[1] * scale_early + later[1] * scale_late,
        earlier[2] * scale_early[..., None] + later[2] * scale_late[..., None],
    )


def per_device(
    tokens, norm_gain, routes, gate_scores, w_gate, w_up, w_down, query, k_cache, v_cache, cache_len
):
    rows_dev, model_width = tokens.shape
    top_count = routes.shape[1]
    devices = lax.axis_size("ffn")
    experts = devices // 2
    capacity = min(rows_dev, max(2, 2 * rows_dev * top_count // experts))
    normed = rms_normed(tokens, norm_gain)
    gate_share = gate_scores / jnp.sum(gate_scores, axis=-1, keepdims=True)
    flat_routes = routes.reshape(-1)
    pair_count = flat_routes.shape[0]
    one_hot = (flat_routes[:, None] == jnp.arange(experts, dtype=jnp.int32)[None, :]).astype(
        jnp.int32
    )
    slot_rank = jnp.sum((jnp.cumsum(one_hot, axis=0) - one_hot) * one_hot, axis=1)
    slot_index = flat_routes * capacity + slot_rank
    slot_pick = (
        jnp.arange(experts * capacity, dtype=jnp.int32)[:, None] == slot_index[None, :]
    ).astype(jnp.bfloat16)
    pair_rows = jnp.arange(pair_count, dtype=jnp.int32) // top_count
    row_pick = (pair_rows[:, None] == jnp.arange(rows_dev, dtype=jnp.int32)[None, :]).astype(
        jnp.bfloat16
    )
    dispatch = jnp.dot(slot_pick, row_pick, preferred_element_type=jnp.float32).astype(jnp.bfloat16)
    outgoing = jnp.dot(dispatch, normed, preferred_element_type=jnp.float32).astype(jnp.bfloat16)
    outgoing = outgoing.reshape(experts, capacity, model_width)
    doubled = jnp.broadcast_to(outgoing[:, None], (experts, 2, capacity, model_width))
    doubled = doubled.reshape(devices, capacity, model_width)
    slot_rows = lax.all_to_all(doubled, "ffn", split_axis=0, concat_axis=0, tiled=True)
    flat_rows = slot_rows.reshape(-1, model_width)
    gate_part = jnp.dot(flat_rows, w_gate, preferred_element_type=jnp.float32)
    up_part = jnp.dot(flat_rows, w_up, preferred_element_type=jnp.float32)
    hidden = (jax.nn.silu(gate_part) * up_part).astype(jnp.bfloat16)
    projected = jnp.dot(hidden, w_down, preferred_element_type=jnp.float32)
    partial_value = projected.reshape(slot_rows.shape[0], slot_rows.shape[1], model_width)
    returned = (
        lax.all_to_all(
            partial_value.astype(jnp.bfloat16), "ffn", split_axis=0, concat_axis=0, tiled=True
        )
        .astype(partial_value.dtype)
        .reshape(experts, 2, capacity, model_width)
    )
    expert_out = (returned[:, 0] + returned[:, 1]).astype(jnp.bfloat16)
    picked = expert_out.reshape(-1, model_width)[slot_index].reshape(
        rows_dev, top_count, model_width
    )
    combined = jnp.sum(picked.astype(jnp.float32) * gate_share[:, :, None], axis=1).astype(
        jnp.bfloat16
    )
    query_rows = query.shape[0]
    seg_len = k_cache.shape[1]
    per_group = HEADS // KV_HEADS
    queries = query.reshape(query_rows, KV_HEADS, per_group, HEAD_DIM)
    cache_keys = k_cache.reshape(query_rows, seg_len, KV_HEADS, HEAD_DIM)
    cache_values = v_cache.reshape(query_rows, seg_len, KV_HEADS, HEAD_DIM)
    scores = jnp.einsum(
        "rgqd,rsgd->rgqs", queries, cache_keys, preferred_element_type=jnp.float32
    ) * HEAD_DIM ** (-0.5)
    positions = lax.axis_index("ffn") * seg_len + jnp.arange(seg_len, dtype=jnp.int32)
    usable = (positions[None, :] < cache_len[:, None])[:, None, None, :]
    block_max = jnp.max(jnp.where(usable, scores, -1e30), axis=-1)
    weights = jnp.where(usable, jnp.exp(scores - block_max[..., None]), 0.0).astype(jnp.bfloat16)
    block_sum = jnp.sum(weights.astype(jnp.float32), axis=-1)
    block_acc = jnp.einsum(
        "rgqs,rsgd->rgqd", weights, cache_values, preferred_element_type=jnp.float32
    )
    own_cols = query.shape[1] // devices
    top_score, weight_total, weighted = combined_all(
        (block_max, block_sum, block_acc), "ffn", merge_parts
    )
    assembled = (weighted / weight_total[..., None]).reshape(query_rows, -1)
    attention = lax.dynamic_slice_in_dim(
        assembled, lax.axis_index("ffn") * own_cols, own_cols, 1
    ).astype(jnp.bfloat16)
    return (combined, attention)


def solution(mesh):
    in_specs = (
        P(("groups", "ffn"), None),
        P(),
        P(("groups", "ffn"), None),
        P(("groups", "ffn"), None),
        P(None, "ffn"),
        P(None, "ffn"),
        P("ffn", None),
        P("groups", None),
        P("groups", "ffn", None),
        P("groups", "ffn", None),
        P("groups"),
    )
    out_specs = (P(("groups", "ffn"), None), P("groups", "ffn"))
    return jax.shard_map(
        per_device, mesh=mesh, in_specs=in_specs, out_specs=out_specs, check_vma=False
    )
```

profile of v0, /device:TPU:0, one launch (start us, length us, event | category | flops | bytes accessed | tf_op | source)
XLA Modules:
  0.0 304.9 jit_solution(5069892043999898585)
XLA Ops:
  7.3 0.9 broadcast_compare_fusion
  8.2 2.1 select_reduce_fusion
  10.2 2.4 fusion.18
  13.4 0.9 reduce_window_sum.11
  14.6 1.7 fusion.4
  16.3 1.6 broadcast_in_dim.29
  17.9 77.9 %all_to_all.10 = bf16[32,8,4096]{2,1,0:T(8,128)(2,1)S(1)} all-to-all(bf16[32,8,4096]{2,1,0:T(8,128)(2,1)S(1)} %bitcast.90), channel_id=1, replica_groups=mesh['groups'=1,'ffn'=32] {'ffn'}, dimensions={0} | all-to-all | bytes 4194304 | tf_op jit(solution)/shard_map/all_to_all | solution.py:68
  95.8 1.3 copy-done.1
  97.1 2.1 fusion.9
  99.2 6.5 %fusion.3 = bf16[32,8,4096]{2,1,0:T(8,128)(2,1)} fusion(bf16[384,4096]{1,0:T(8,128)(2,1)S(1)} %copy-done, bf16[4096,384]{1,0:T(8,128)(2,1)} %param.18, bf16[32,8,4096]{2,1,0:T(8,128)(2,1)} %copy-done.1, f32[256,384]{1,0:T(8,128)} %fusion.9), kind=kOutput, calls=%fused_computation.10 | convolution fusion | flops 1612251136 | bytes 10878976 | tf_op jit(solution)/shard_map/dot_general | solution.py:73
  105.7 4.3 %all-to-all-start.1 = ((bf16[32,8,4096]{2,1,0:T(8,128)(2,1)}), bf16[32,8,4096]{2,1,0:T(8,128)(2,1)}, u32[]{:S(2)}, u32[]{:S(2)}) async-start(bf16[32,8,4096]{2,1,0:T(8,128)(2,1)} %fusion.3), calls=%async_computation.1 | async-start | bytes 4194304 | tf_op jit(solution)/shard_map/all_to_all | solution.py:76
  110.2 71.7 %all-gather.1 = f32[256,4,16]{2,1,0:T(4,128)S(1)} all-gather(f32[8,4,16]{2,1,0:T(4,128)S(1)} %convert_reduce_fusion), channel_id=3, replica_groups=mesh['groups'=1,'ffn'=32] {'ffn'}, dimensions={0}, use_global_device_ids=true | all-gather | bytes 67584 | tf_op jit(solution)/shard_map/all_gather | solution.py:12
  181.9 0.8 copy-done.2
  182.8 40.7 %all-gather = f32[256,4,16]{2,1,0:T(4,128)S(1)} all-gather(f32[8,4,16]{2,1,0:T(4,128)S(1)} %get-tuple-element.199), channel_id=2, replica_groups=mesh['groups'=1,'ffn'=32] {'ffn'}, dimensions={0}, use_global_device_ids=true | all-gather | bytes 67584 | tf_op jit(solution)/shard_map/all_gather | solution.py:12
  223.5 0.8 copy-done.3
  224.6 2.1 convert.2
  226.7 1.3 fusion.17
  228.0 3.5 %gather_fusion = bf16[64,4096]{1,0:T(8,128)(2,1)} fusion(bf16[128,4096]{1,0:T(8,128)(2,1)} %fusion.17, s32[1024]{0:T(1024)S(1)} %pad_clamp_fusion), kind=kCustom, calls=%fused_computation | custom fusion | bytes 1048832 | tf_op jit(solution)/shard_map/gather | solution.py:83
  231.5 2.1 fusion.23
  233.6 1.0 slice.20
  234.6 62.6 %while.19 = (s32[]{:T(128)}, f32[8,4,16]{2,1,0:T(4,128)S(1)}, f32[8,4,16]{2,1,0:T(4,128)S(1)}, f32[8,4,16,128]{3,2,1,0:T(8,128)S(1)}, f32[32,8,4,16]{3,2,1,0:T(4...) while((s32[]{:T(128)}, f32[8,4,16]{2,1,0:T(4,128)S(1)}, ...), condition=%wide.region_8.9_spmd, body=%wide.region_7.8_spmd.sunk | while | flops 199685 | bytes 807063 | solution.py:17
  234.6 0.8 fusion.55
  235.4 1.2 fusion.56
  236.7 0.8 fusion.55
  237.4 1.2 fusion.56
  238.7 0.8 fusion.55
  239.4 1.2 fusion.56
  240.7 0.8 fusion.55
  241.5 1.2 fusion.56
  242.7 0.8 fusion.55
  243.5 1.2 fusion.56
  244.7 0.8 fusion.55
  245.5 1.2 fusion.56
  246.7 0.8 fusion.55
  247.5 1.2 fusion.56
  248.8 0.8 fusion.55
  249.5 1.2 fusion.56
  250.8 0.8 fusion.55
  251.6 1.2 fusion.56
  253.6 1.2 fusion.56
  255.6 1.2 fusion.56
  257.6 1.2 fusion.56
  259.6 1.2 fusion.56
  261.6 1.2 fusion.56
  263.7 1.2 fusion.56
  265.7 1.2 fusion.56
  267.7 1.2 fusion.56
  268.9 0.8 fusion.55
  269.7 1.2 fusion.56
  271.0 0.8 fusion.55
  271.7 1.2 fusion.56
  273.0 0.8 fusion.55
  273.8 1.2 fusion.56
  275.8 1.2 fusion.56
  277.8 1.2 fusion.56
  279.8 1.2 fusion.56
  281.8 1.2 fusion.56
  283.9 1.2 fusion.56
  285.9 1.2 fusion.56
  287.9 1.2 fusion.56
  289.9 1.2 fusion.56
  291.9 1.2 fusion.56
  293.9 1.2 fusion.56
  296.0 1.2 fusion.56
  (57 shorter events, 17.3 us)
Async XLA Ops:
  7.2 92.0 %copy-start = (bf16[384,4096]{1,0:T(8,128)(2,1)S(1)}, bf16[384,4096]{1,0:T(8,128)(2,1)}, u32[]{:S(2)}) copy-start(bf16[384,4096]{1,0:T(8,128)(2,1)} %param.19) | copy-start | bytes 9437188
  7.2 5.4 %copy-start.7 = (s32[8,8]{1,0:T(8,128)S(1)}, s32[8,8]{1,0:T(8,128)}, u32[]{:S(2)}) copy-start(s32[8,8]{1,0:T(8,128)} %param.15) | copy-start | bytes 772
  7.2 7.3 %copy-start.4 = (bf16[8,4096]{1,0:T(8,128)(2,1)S(1)}, bf16[8,4096]{1,0:T(8,128)(2,1)}, u32[]{:S(2)}) copy-start(bf16[8,4096]{1,0:T(8,128)(2,1)} %param.13) | copy-start | bytes 196612
  7.2 7.4 %copy-start.5 = (f32[4096]{0:T(1024)S(1)}, f32[4096]{0:T(1024)}, u32[]{:S(2)}) copy-start(f32[4096]{0:T(1024)} %param.14) | copy-start | bytes 49156
  7.2 226.4 %all-gather.5.cloned.1.call-start = ((), (), s32[]{:S(2)}) async-start(), calls=%async_computation.2 | async-start | bytes 8650752 | tf_op jit(solution)/shard_map/all_gather | solution.py:12
  16.3 80.8 %copy-start.8 = (bf16[4096,384]{1,0:T(8,128)(2,1)S(1)}, bf16[4096,384]{1,0:T(8,128)(2,1)}, u32[]{:S(2)}) copy-start(bf16[4096,384]{1,0:T(8,128)(2,1)} %param.17) | copy-start | bytes 9437188
  95.8 1.3 copy-start.1
  105.7 118.8 %copy-start.6 = (f32[8,8]{1,0:T(8,128)S(1)}, f32[8,8]{1,0:T(8,128)}, u32[]{:S(2)}) copy-start(f32[8,8]{1,0:T(8,128)} %param.16) | copy-start | bytes 772
  105.7 119.0 %all-to-all-start.1 = ((bf16[32,8,4096]{2,1,0:T(8,128)(2,1)}), bf16[32,8,4096]{2,1,0:T(8,128)(2,1)}, u32[]{:S(2)}, u32[]{:S(2)}) async-start(bf16[32,8,4096]{2,1,0:T(8,128)(2,1)} %fusion.3), calls=%async_computation.1 | async-start | bytes 4194304 | tf_op jit(solution)/shard_map/all_to_all | solution.py:76
  181.9 0.8 copy-start.2
  223.5 0.8 copy-start.3
Sparse Core Ops, SparseCore 0:
  12.7 102.8 all-gather.4
where the time goes:
time: 311 us; the launch traced here: 305 us
  blocking collectives  190 us (61%)
  other arithmetic  70.7 us (23%)
  matrix products  14.7 us (5%)
  between operations  14.2 us (5%)
  local copies, waits for them, and re-layouts  9.95 us (3%)
  starting transfers between devices  4.3 us (1%)
    all_gather x2, blocking collectives, combined_all(): gathered = jax.tree.map(lambda a: lax.all_gather(a, axis), part)  112 us
    all_to_all x1, blocking collectives, per_device(): lax.all_to_all(doubled, 'ffn', split_axis=0, concat_axis=0, tiled=True)  77.9 us
    add x31, other arithmetic, merge_parts(): earlier[2] * scale_early[..., None] + later[2] * scale_late[..., None]  37.9 us
    add x31, other arithmetic, merge_parts(): earlier[1] * scale_early + later[1] * scale_late  24 us
    dot_general x1, matrix products, per_device(): projected = jnp.dot(hidden, w_down, preferred_element_type=jnp.float32)  6.45 us
  transfers between devices with their start and end apart: 2, of which 0 were waited for; matrix products, arithmetic and copies ran while one was open for 8% of the time, Pallas kernels for 0%

commit v1 on v0

v1 whole, which is shorter than its diff:
```python
import functools

import jax
import jax.numpy as jnp
from jax import lax
from jax.experimental import pallas as pl
from jax.experimental.pallas import tpu as pltpu
from jax.sharding import PartitionSpec as P

HEADS = 64
KV_HEADS = 4
HEAD_DIM = 128
LANES = 128
VMEM = pl.BlockSpec(memory_space=pltpu.VMEM)
SMEM = pl.BlockSpec(memory_space=pltpu.SMEM)


def levels_of(devices):
    levels, stride = [], 2
    while stride < devices:
        radix = 4 if devices // stride >= 4 else 2
        levels.append((stride, radix))
        stride *= radix
    return levels


def exchange(value, distance):
    size = lax.axis_size("ffn")
    return lax.ppermute(value, "ffn", [(i, i ^ distance) for i in range(size)])


def call(body, out_shape, *args, in_specs=None, scratch=(), flops=0, nbytes=0):
    return pl.pallas_call(
        body,
        out_shape=out_shape,
        in_specs=in_specs or [VMEM] * len(args),
        out_specs=jax.tree.map(lambda _: VMEM, out_shape),
        scratch_shapes=list(scratch),
        compiler_params=pltpu.CompilerParams(vmem_limit_bytes=24 * 2**20),
        cost_estimate=pl.CostEstimate(flops=flops, bytes_accessed=nbytes, transcendentals=0),
    )(*args)


def payload_kernel(experts, tokens_ref, gain_ref, routes_ref, scores_ref, out_ref):
    features = tokens_ref[...].astype(jnp.float32)
    width = features.shape[1]
    mean_square = jnp.mean(features * features, axis=-1, keepdims=True)
    normed = features * lax.rsqrt(mean_square + 1e-06) * gain_ref[...]
    scores = scores_ref[...]
    share = scores / jnp.sum(scores, axis=-1, keepdims=True)
    extra = out_ref.shape[1] - width
    lane = lax.broadcasted_iota(jnp.int32, (features.shape[0], extra), 1)
    routes = routes_ref[...]
    gates = jnp.zeros(lane.shape, jnp.float32)
    for choice in range(routes.shape[1]):
        gates += jnp.where(
            routes[:, choice : choice + 1] == lane % experts, share[:, choice : choice + 1], 0.0
        )
    high = gates.astype(jnp.bfloat16).astype(jnp.float32)
    coded = jnp.where(lane < experts, high, jnp.where(lane < 2 * experts, gates - high, 0.0))
    out_ref[:, :width] = normed.astype(jnp.bfloat16)
    out_ref[:, width:] = coded.astype(jnp.bfloat16)


def expert_kernel(experts, expert_ref, same_ref, other_ref, gate_ref, up_ref, down_ref, own_ref, far_ref):
    width = gate_ref.shape[0]
    rows = same_ref.shape[0]
    stacked = jnp.concatenate([same_ref[:, :width], other_ref[:, :width]], axis=0)
    coded = jnp.concatenate([same_ref[:, width:], other_ref[:, width:]], axis=0).astype(jnp.float32)
    lane = lax.broadcasted_iota(jnp.int32, coded.shape, 1)
    mine = (lane < 2 * experts) & (lane % experts == expert_ref[0])
    share = jnp.sum(jnp.where(mine, coded, 0.0), axis=-1, keepdims=True)
    gate_part = jnp.dot(stacked, gate_ref[...], preferred_element_type=jnp.float32)
    up_part = jnp.dot(stacked, up_ref[...], preferred_element_type=jnp.float32)
    hidden = (gate_part / (1.0 + jnp.exp(-gate_part)) * up_part).astype(jnp.bfloat16)
    step = 1024
    for first in range(0, width, step):
        cols = slice(first, first + step)
        part = jnp.dot(hidden, down_ref[:, cols], preferred_element_type=jnp.float32)
        part = (part * share).astype(jnp.bfloat16)
        own_ref[:, cols] = part[:rows]
        far_ref[:, cols] = part[rows:]


def sum_kernel(count, *refs):
    total = refs[0][...].astype(jnp.float32)
    for ref in refs[1:count]:
        total += ref[...].astype(jnp.float32)
    outs = refs[count:]
    rows = total.shape[0] // len(outs)
    for place, out_ref in enumerate(outs):
        out_ref[...] = total[place * rows : (place + 1) * rows].astype(out_ref.dtype)


def summed(parts, pieces):
    rows, width = parts[0].shape
    shape = jax.ShapeDtypeStruct((rows // pieces, width), jnp.bfloat16)
    return call(
        functools.partial(sum_kernel, len(parts)),
        [shape] * pieces,
        *parts,
        flops=rows * width * len(parts),
        nbytes=2 * rows * width * (len(parts) + 1),
    )


def attend(query, k_cache, v_cache, cache_len):
    devices = lax.axis_size("ffn")
    rows, seg_len, kv_width = k_cache.shape
    info = jnp.concatenate([(lax.axis_index("ffn") * seg_len)[None], cache_len]).astype(jnp.int32)
    queries = query.reshape(rows, KV_HEADS, HEADS // KV_HEADS, HEAD_DIM)
    keys = k_cache.reshape(rows, seg_len, KV_HEADS, HEAD_DIM)
    values = v_cache.reshape(rows, seg_len, KV_HEADS, HEAD_DIM)
    scores = jnp.einsum(
        "rgqd,rsgd->rgqs", queries, keys, preferred_element_type=jnp.float32
    ) * HEAD_DIM ** (-0.5)
    positions = info[0] + jnp.arange(seg_len, dtype=jnp.int32)
    usable = (positions[None, :] < cache_len[:, None])[:, None, None, :]
    peak = jnp.max(jnp.where(usable, scores, -1e30), axis=-1)
    weights = jnp.where(usable, jnp.exp(scores - peak[..., None]), 0.0).astype(jnp.bfloat16)
    total = jnp.sum(weights.astype(jnp.float32), axis=-1)
    acc = jnp.einsum("rgqs,rsgd->rgqd", weights, values, preferred_element_type=jnp.float32)
    own = query.shape[1] // devices
    if own % HEAD_DIM:
        peak = jnp.repeat(peak.reshape(rows, HEADS), HEAD_DIM, axis=1).reshape(rows, devices, own)
        total = jnp.repeat(total.reshape(rows, HEADS), HEAD_DIM, axis=1).reshape(rows, devices, own)
        packed = jnp.concatenate([acc.reshape(rows, devices, own), peak[..., :1], total[..., :1]], axis=-1)
        heads = 1
    else:
        heads = own // HEAD_DIM
        packed = jnp.concatenate(
            [
                acc.reshape(rows, devices, own),
                peak.reshape(rows, devices, heads),
                total.reshape(rows, devices, heads),
            ],
            axis=-1,
        )
    packed = packed.transpose(1, 0, 2)
    arrived = lax.all_to_all(packed, "ffn", split_axis=0, concat_axis=0, tiled=True)
    acc = arrived[:, :, :own].reshape(devices, rows, heads, own // heads)
    peak = arrived[:, :, own : own + heads]
    total = arrived[:, :, own + heads :]
    top = jnp.max(peak, axis=0)
    factor = jnp.exp(peak - top[None])
    weight_total = jnp.sum(total * factor, axis=0)
    weighted = jnp.sum(acc * factor[..., None], axis=0)
    return (weighted / weight_total[..., None]).reshape(rows, own).astype(jnp.bfloat16)


def per_device(
    tokens, norm_gain, routes, gate_scores, w_gate, w_up, w_down, query, k_cache, v_cache, cache_len
):
    rows_dev, width = tokens.shape
    devices = lax.axis_size("ffn")
    experts = devices // 2
    levels = levels_of(devices)
    extra = -(-2 * experts // LANES) * LANES
    expert = (lax.axis_index("ffn") // 2).astype(jnp.int32)[None]

    block = call(
        functools.partial(payload_kernel, experts),
        jax.ShapeDtypeStruct((rows_dev, width + extra), jnp.bfloat16),
        tokens,
        norm_gain[None],
        routes,
        gate_scores,
    )
    for stride, radix in reversed(levels[1:]):
        arrived = [exchange(block, stride * k) for k in reversed(range(1, radix))]
        block = jnp.concatenate([block] + arrived[::-1], axis=0)
    stride, radix = levels[0]
    order = [3, 1, 2][-(radix - 1) :] if radix == 4 else [1]
    chunks = {k: exchange(block, stride * k) for k in order}
    chunks[0] = block

    rows = block.shape[0]
    hidden = w_gate.shape[1]
    partial = {}
    for k in [0] + order[1:] + order[:1]:
        other = exchange(chunks[k], 1)
        shape = jax.ShapeDtypeStruct((rows, width), jnp.bfloat16)
        own, far = call(
            functools.partial(expert_kernel, experts),
            [shape, shape],
            expert,
            chunks[k],
            other,
            w_gate,
            w_up,
            w_down,
            in_specs=[SMEM] + [VMEM] * 5,
            flops=2 * rows * width * hidden * 6,
            nbytes=2 * (3 * width * hidden + 4 * rows * width),
        )
        (partial[k],) = summed([own, exchange(far, 1)], 1)
    parts = [partial[0]] + [exchange(partial[k], stride * k) for k in range(1, radix)]
    for stride, radix in levels[1:]:
        pieces = summed(parts, radix)
        parts = [pieces[0]] + [exchange(pieces[k], stride * k) for k in range(1, radix)]
    (combined,) = summed(parts, 1)

    attention = attend(query, k_cache, v_cache, cache_len)
    return (combined, attention)


def solution(mesh):
    in_specs = (
        P(("groups", "ffn"), None),
        P(),
        P(("groups", "ffn"), None),
        P(("groups", "ffn"), None),
        P(None, "ffn"),
        P(None, "ffn"),
        P("ffn", None),
        P("groups", None),
        P("groups", "ffn", None),
        P("groups", "ffn", None),
        P("groups"),
    )
    out_specs = (P(("groups", "ffn"), None), P("groups", "ffn"))
    return jax.shard_map(
        per_device, mesh=mesh, in_specs=in_specs, out_specs=out_specs, check_vma=False
    )
```

time: 311 us -> 77 us (0.25); the launches traced: 305 us -> 76.4 us
  blocking collectives: 190 us -> 0 us
  other arithmetic: 70.7 us -> 4.88 us
  waiting for transfers between devices: 0.02 us -> 21.4 us
  starting transfers between devices: 4.3 us -> 24.8 us
  between operations: 14.2 us -> 0.78 us
  matrix products: 14.7 us -> 3.32 us
  Pallas kernels: 0 us -> 11.3 us
    all_gather x2 -> x0, blocking collectives: 112 us -> none  [combined_all(): gathered = jax.tree.map(lambda a: lax.all_gather(a, axis), part)]
    all_to_all x1 -> x0, blocking collectives: 77.9 us -> none  [per_device(): lax.all_to_all(doubled, 'ffn', split_axis=0, concat_axis=0, tiled=True)]
    add x63 -> x1, other arithmetic: 61.8 us -> 0.01 us  [attend(): positions = info[0] + jnp.arange(seg_len, dtype=jnp.int32)]
    ppermute x0 -> x20, waiting for transfers between devices: none -> 21.4 us  [exchange(): return lax.ppermute(value, 'ffn', [(i, i ^ distance) for i in range(size)])]
    ppermute x0 -> x20, starting transfers between devices: none -> 19.7 us  [exchange(): return lax.ppermute(value, 'ffn', [(i, i ^ distance) for i in range(size)])]
    dot_general x5 -> x2, matrix products: 14.7 us -> 3.32 us  [the longest x1 1.69 us: attend(): jnp.einsum('rgqs,rsgd->rgqd', weights, values, preferred_element_type=jnp...]
    pallas_call x0 -> x11, Pallas kernels: none -> 11.3 us  [call(): pl.pallas_call(body, out_shape=out_shape, in_specs=in_specs or [VMEM] * l...]
    unnamed x19 -> x21, local copies, waits for them, and re-layouts: 3.08 us -> 9.02 us
  transfers between devices with their start and end apart: 2 -> 21, of which waited for: 0 -> 7; matrix products, arithmetic and copies ran while one was open for 8% -> 12% of each run, Pallas kernels for 0% -> 13%
where the time goes in v1:
time: 77 us; the launch traced here: 76.4 us
  starting transfers between devices  24.8 us (32%)
  waiting for transfers between devices  21.4 us (28%)
  Pallas kernels  11.3 us (15%)
  local copies, waits for them, and re-layouts  10 us (13%)
  other arithmetic  4.88 us (6%)
  matrix products  3.32 us (4%)
  between operations  0.78 us (1%)
    ppermute x20, waiting for transfers between devices, exchange(): return lax.ppermute(value, 'ffn', [(i, i ^ distance) for i in range(size)])  21.4 us
    ppermute x20, starting transfers between devices, exchange(): return lax.ppermute(value, 'ffn', [(i, i ^ distance) for i in range(size)])  19.7 us
    pallas_call x11, Pallas kernels, call(): pl.pallas_call(body, out_shape=out_shape, in_specs=in_specs or [VMEM] * l...  11.3 us
    unnamed x21, local copies, waits for them, and re-layouts  9.02 us
    all_to_all x1, starting transfers between devices, attend(): lax.all_to_all(packed, 'ffn', split_axis=0, concat_axis=0, tiled=True)  5.08 us
    dot_general x1, matrix products, attend(): jnp.einsum('rgqs,rsgd->rgqd', weights, values, preferred_element_type=jnp...  1.69 us
    dot_general x1, matrix products, attend(): jnp.einsum('rgqd,rsgd->rgqs', queries, keys, preferred_element_type=jnp.f...  1.63 us
  transfers between devices with their start and end apart: 21, of which 7 were waited for; matrix products, arithmetic and copies ran while one was open for 12% of the time, Pallas kernels for 13%

profile of v1, /device:TPU:0, one launch (start us, length us, event | category | flops | bytes accessed | tf_op | source)
XLA Modules:
  0.0 76.4 jit_solution(13107506003272495019)
XLA Ops:
  0.6 0.0 copy-start
  0.7 0.9 %copy-done.5 = bf16[8,4096]{1,0:T(8,128)(2,1)S(1)} copy-done((bf16[8,4096]{1,0:T(8,128)(2,1)S(1)}, bf16[8,4096]{1,0:T(8,128)(2,1)}, u32[]{:S(2)}) %copy-start.5) | copy-done | bytes 65560
  1.6 0.7 copy-done.6
  2.3 0.7 copy-done.7
  3.0 0.7 copy-done.8
  3.7 0.2 shard_map.122
  3.9 5.1 %collective-permute-start.2 = (bf16[8,4224]{1,0:T(8,128)(2,1)S(1)}, bf16[8,4224]{1,0:T(8,128)(2,1)S(1)}, u32[]{:S(2)}, u32[]{:S(2)}) collective-permute-start(bf16[8,4224]{1,0:T(8,128)(2,1)S(1)} %shard_map.122), channel_id=1, source_target_pairs={{0,24},{1,25},{2,26},{3,27},{4,28},{5,29},{6,30},{7,31},{8,16},{9,... | collective-permute-start | bytes 202760 | tf_op jit(solution)/shard_map/ppermute | solution.py:29
  9.0 0.6 collective-permute-start
  9.6 0.7 broadcast_compare_fusion
  10.3 1.6 %select_reduce_fusion = (f32[8,4,16]{2,1,0:T(4,128)S(1)}, f32[8,4,16,128]{3,2,1,0:T(8,128)S(1)}) fusion(pred[8,128]{1,0:T(8,128)(4,1)S(1)} %broadcast_compare_fusion, bf16[8,4,16,128]{3,0,2,1:T(8,128)(2,1)} %bitcast.32, bf16[8,128,512]{2,1,0:T(8,128)(2,1)S(1)} %copy-done), kind=kOutput, calls=%fused_computation.12 | convolution fusion | flops 16973312 | bytes 1444864 | tf_op jit(solution)/shard_map/rgqd,rsgd->rgqs/dot_general | solution.py:114
  12.0 1.7 %fusion = f32[8,4,16,128]{3,2,1,0:T(8,128)S(1)} fusion(f32[8,4,16,128]{3,2,1,0:T(8,128)S(1)} %get-tuple-element.32, f32[8,4,16]{2,1,0:T(4,128)S(1)} %get-tuple-element.31, pred[8,128]{1,0:T(8,128)(4,1)S(1)} %broadcast_compare_fusion, bf16[8,128,512]{2,1,0:T(8,128)(2,1)} %param.20), kind=kOutput, calls=%fused_computation.1 | convolution fusion | flops 16973824 | bytes 1575936 | tf_op jit(solution)/shard_map/rgqs,rsgd->rgqd/dot_general | solution.py:122
  13.7 1.1 %collective-permute-done.1 = bf16[8,4224]{1,0:T(8,128)(2,1)S(1)} collective-permute-done((bf16[8,4224]{1,0:T(8,128)(2,1)S(1)}, bf16[8,4224]{1,0:T(8,128)(2,1)S(1)}, u32[]{:S(2)}, u32[]{:S(2)}) %collective-permute-start.1) | collective-permute-done | bytes 67616 | tf_op jit(solution)/shard_map/ppermute | solution.py:29
  14.8 1.6 %collective-permute-start.5 = (bf16[32,4224]{1,0:T(8,128)(2,1)S(1)}, bf16[32,4224]{1,0:T(8,128)(2,1)S(1)}, u32[]{:S(2)}, u32[]{:S(2)}) collective-permute-start(bf16[32,4224]{1,0:T(8,128)(2,1)S(1)} %pad_maximum_fusion.same_ref), channel_id=1, source_target_pairs={{0,2},{1,3},{2,0},{3,1},{4,6},{5,7},{6,4},{7,5},{8,10},{9,11},{10,... | collective-permute-start | bytes 811016 | tf_op jit(solution)/shard_map/ppermute | solution.py:29
  16.3 1.5 %collective-permute-start.9 = (bf16[32,4224]{1,0:T(8,128)(2,1)S(1)}, bf16[32,4224]{1,0:T(8,128)(2,1)S(1)}, u32[]{:S(2)}, u32[]{:S(2)}) collective-permute-start(bf16[32,4224]{1,0:T(8,128)(2,1)S(1)} %pad_maximum_fusion.same_ref), channel_id=1, source_target_pairs={{0,4},{1,5},{2,6},{3,7},{4,0},{5,1},{6,2},{7,3},{8,12},{9,13},{10,... | collective-permute-start | bytes 811016 | tf_op jit(solution)/shard_map/ppermute | solution.py:29
  17.8 0.5 collective-permute-start.13
  18.3 0.3 convert_reduce_fusion
  18.6 0.1 copy.36
  18.7 0.1 copy.37
  18.7 0.3 copy.40
  19.0 0.3 copy.39
  19.3 0.1 reshape.63
  19.4 0.2 copy.38
  19.5 0.8 %maximum_bitcast_fusion = f32[32,8,260]{2,1,0:T(8,128)} fusion(f32[8,32,2]{2,0,1:T(8,128)S(1)} %copy.40, f32[8,32,2]{2,0,1:T(8,128)S(1)} %copy.39, f32[8,32,256]{2,0,1:T(8,128)S(1)} %copy.38), kind=kLoop, calls=%fused_computation.6 | loop fusion | flops 133120 | bytes 532480 | tf_op jit(solution)/shard_map/transpose | solution.py:139
  20.4 5.1 %all-to-all-start = ((f32[32,8,260]{2,1,0:T(8,128)}), f32[32,8,260]{2,1,0:T(8,128)}, u32[]{:S(2)}, u32[]{:S(2)}) async-start(f32[32,8,260]{2,1,0:T(8,128)} %maximum_bitcast_fusion), calls=%async_computation | async-start | bytes 786432 | tf_op jit(solution)/shard_map/all_to_all | solution.py:140
  25.5 0.3 collective-permute-start.6
  25.7 6.3 %collective-permute-done.9.same_ref = bf16[32,4224]{1,0:T(8,128)(2,1)S(1)} collective-permute-done((bf16[32,4224]{1,0:T(8,128)(2,1)S(1)}, bf16[32,4224]{1,0:T(8,128)(2,1)S(1)}, u32[]{:S(2)}, u32[]{:S(2)}) %collective-permute-start.9) | collective-permute-done | bytes 270368 | tf_op jit(solution)/shard_map/ppermute | solution.py:29
  32.0 0.5 collective-permute-start.14
  32.5 0.0 collective-permute-start.3
  32.6 1.9 %copy-done.1 = bf16[4096,384]{1,0:T(8,128)(2,1)S(1)} copy-done((bf16[4096,384]{1,0:T(8,128)(2,1)S(1)}, bf16[4096,384]{1,0:T(8,128)(2,1)}, u32[]{:S(2)}) %copy-start.1) | copy-done | bytes 3145752
  34.4 1.9 %copy-done.3 = bf16[4096,384]{1,0:T(8,128)(2,1)S(1)} copy-done((bf16[4096,384]{1,0:T(8,128)(2,1)S(1)}, bf16[4096,384]{1,0:T(8,128)(2,1)}, u32[]{:S(2)}) %copy-start.3) | copy-done | bytes 3145752
  36.3 1.9 %copy-done.4 = bf16[384,4096]{1,0:T(8,128)(2,1)S(1)} copy-done((bf16[384,4096]{1,0:T(8,128)(2,1)S(1)}, bf16[384,4096]{1,0:T(8,128)(2,1)}, u32[]{:S(2)}) %copy-start.4) | copy-done | bytes 3145752
  38.2 2.5 %shard_map.125 = (bf16[32,4096]{1,0:T(8,128)(2,1)S(1)}, bf16[32,4096]{1,0:T(8,128)(2,1)}) custom-call(s32[1]{0:T(128)} %bitcast.expert_ref, bf16[32,4224]{1,0:T(8,128)(2,1)S(1)} %collective-permute-done.5.same_ref, bf16[32,4224]{1,0:T(8,128)(2,1)S(1)} %collective-permute-done.6.other_ref, bf16[4096,384]{1,0:T(8,128)(2,1)S(1)} %copy-done.1, ...), custom_call_target="tpu_custom_call" | custom-call | flops 603979776 | bytes 10485760 | tf_op jit(solution)/shard_map/pallas_call | solution.py:33
  40.7 0.5 collective-permute-start.7
  41.2 2.5 %shard_map.127 = (bf16[32,4096]{1,0:T(8,128)(2,1)S(1)}, bf16[32,4096]{1,0:T(8,128)(2,1)}) custom-call(s32[1]{0:T(128)} %bitcast.expert_ref, bf16[32,4224]{1,0:T(8,128)(2,1)S(1)} %collective-permute-done.9.same_ref, bf16[32,4224]{1,0:T(8,128)(2,1)S(1)} %collective-permute-done.10.other_ref, bf16[4096,384]{1,0:T(8,128)(2,1)S(1)} %copy-done.1, ...), custom_call_target="tpu_custom_call" | custom-call | flops 603979776 | bytes 10485760 | tf_op jit(solution)/shard_map/pallas_call | solution.py:33
  43.7 0.0 collective-permute-start.11
  43.7 2.5 %shard_map.129 = (bf16[32,4096]{1,0:T(8,128)(2,1)S(1)}, bf16[32,4096]{1,0:T(8,128)(2,1)}) custom-call(s32[1]{0:T(128)} %bitcast.expert_ref, bf16[32,4224]{1,0:T(8,128)(2,1)S(1)} %collective-permute-done.13.same_ref, bf16[32,4224]{1,0:T(8,128)(2,1)S(1)} %collective-permute-done.14.other_ref, bf16[4096,384]{1,0:T(8,128)(2,1)S(1)} %copy-done.1, ...), custom_call_target="tpu_custom_call" | custom-call | flops 603979776 | bytes 10485760 | tf_op jit(solution)/shard_map/pallas_call | solution.py:33
  46.3 0.5 collective-permute-start.15
  46.8 2.5 %shard_map.123 = (bf16[32,4096]{1,0:T(8,128)(2,1)S(1)}, bf16[32,4096]{1,0:T(8,128)(2,1)}) custom-call(s32[1]{0:T(128)} %bitcast.expert_ref, bf16[32,4224]{1,0:T(8,128)(2,1)S(1)} %pad_maximum_fusion.same_ref, bf16[32,4224]{1,0:T(8,128)(2,1)S(1)} %collective-permute-done.3.other_ref, bf16[4096,384]{1,0:T(8,128)(2,1)S(1)} %copy-done.2, ...), custom_call_target="tpu_custom_call" | custom-call | flops 603979776 | bytes 10485760 | tf_op jit(solution)/shard_map/pallas_call | solution.py:33
  49.3 0.0 collective-permute-start.4
  49.3 1.1 %slice_reduce_fusion = (f32[8,2]{1,0:T(8,128)S(1)}, f32[32,8,2]{2,1,0:T(8,128)S(1)}, f32[32,8,2]{2,1,0:T(8,128)S(1)}) fusion(f32[32,8,260]{2,1,0:T(8,128)} %all-to-all-done), kind=kLoop, calls=%fused_computation.21 | loop fusion | flops 496 | bytes 8256 | tf_op jit(solution)/shard_map/reduce_max | solution.py:144
  50.4 0.1 copy.48
  50.5 0.1 copy.47
  50.6 0.1 copy.49
  50.7 0.1 shard_map.126
  50.8 2.0 %collective-permute-start.8 = (bf16[32,4096]{1,0:T(8,128)(2,1)S(1)}, bf16[32,4096]{1,0:T(8,128)(2,1)S(1)}, u32[]{:S(2)}, u32[]{:S(2)}) collective-permute-start(bf16[32,4096]{1,0:T(8,128)(2,1)S(1)} %shard_map.126), channel_id=1, source_target_pairs={{0,2},{1,3},{2,0},{3,1},{4,6},{5,7},{6,4},{7,5},{8,10},{9,11},{10,... | collective-permute-start | bytes 786440 | tf_op jit(solution)/shard_map/ppermute | solution.py:29
  52.8 0.1 shard_map.128
  52.8 0.6 collective-permute-start.12
  53.5 0.1 shard_map.130
  53.5 1.5 %collective-permute-start.16 = (bf16[32,4096]{1,0:T(8,128)(2,1)S(1)}, bf16[32,4096]{1,0:T(8,128)(2,1)S(1)}, u32[]{:S(2)}, u32[]{:S(2)}) collective-permute-start(bf16[32,4096]{1,0:T(8,128)(2,1)S(1)} %shard_map.130), channel_id=1, source_target_pairs={{0,6},{1,7},{2,4},{3,5},{4,2},{5,3},{6,0},{7,1},{8,14},{9,15},{10,... | collective-permute-start | bytes 786440 | tf_op jit(solution)/shard_map/ppermute | solution.py:29
  55.1 0.2 multiply_reduce_fusion
  55.2 0.1 copy.42
  55.3 1.1 %fusion.5 = f32[8,256]{1,0:T(8,128)S(1)} fusion(f32[32,8,260]{2,1,0:T(8,128)} %all-to-all-done, f32[32,8,2]{1,2,0:T(2,128)S(1)} %copy.42), kind=kLoop, calls=%fused_computation.9 | loop fusion | flops 129024 | bytes 272384 | tf_op jit(solution)/shard_map/reduce_sum | solution.py:147
  56.4 0.1 shard_map.124.refs_0_
  56.5 3.5 %collective-permute-done.8.refs_1_ = bf16[32,4096]{1,0:T(8,128)(2,1)S(1)} collective-permute-done((bf16[32,4096]{1,0:T(8,128)(2,1)S(1)}, bf16[32,4096]{1,0:T(8,128)(2,1)S(1)}, u32[]{:S(2)}, u32[]{:S(2)}) %collective-permute-start.8) | collective-permute-done | bytes 262176 | tf_op jit(solution)/shard_map/ppermute | solution.py:29
  60.0 5.3 %collective-permute-done.12.refs_2_ = bf16[32,4096]{1,0:T(8,128)(2,1)S(1)} collective-permute-done((bf16[32,4096]{1,0:T(8,128)(2,1)S(1)}, bf16[32,4096]{1,0:T(8,128)(2,1)S(1)}, u32[]{:S(2)}, u32[]{:S(2)}) %collective-permute-start.12) | collective-permute-done | bytes 262176 | tf_op jit(solution)/shard_map/ppermute | solution.py:29
  65.3 1.8 %collective-permute-done.16.refs_3_ = bf16[32,4096]{1,0:T(8,128)(2,1)S(1)} collective-permute-done((bf16[32,4096]{1,0:T(8,128)(2,1)S(1)}, bf16[32,4096]{1,0:T(8,128)(2,1)S(1)}, u32[]{:S(2)}, u32[]{:S(2)}) %collective-permute-start.16) | collective-permute-done | bytes 262176 | tf_op jit(solution)/shard_map/ppermute | solution.py:29
  67.1 0.1 shard_map.131
  67.2 0.1 collective-permute-start.17
  67.3 2.4 %collective-permute-start.18 = (bf16[8,4096]{1,0:T(8,128)(2,1)S(1)}, bf16[8,4096]{1,0:T(8,128)(2,1)S(1)}, u32[]{:S(2)}, u32[]{:S(2)}) collective-permute-start(bf16[8,4096]{1,0:T(8,128)(2,1)S(1)} %get-tuple-element.24), channel_id=1, source_target_pairs={{0,16},{1,17},{2,18},{3,19},{4,20},{5,21},{6,22},{7,23},{8,24},{9,... | collective-permute-start | bytes 196616 | tf_op jit(solution)/shard_map/ppermute | solution.py:29
  69.6 2.0 %collective-permute-start.19 = (bf16[8,4096]{1,0:T(8,128)(2,1)S(1)}, bf16[8,4096]{1,0:T(8,128)(2,1)S(1)}, u32[]{:S(2)}, u32[]{:S(2)}) collective-permute-start(bf16[8,4096]{1,0:T(8,128)(2,1)S(1)} %get-tuple-element.25), channel_id=1, source_target_pairs={{0,24},{1,25},{2,26},{3,27},{4,28},{5,29},{6,30},{7,31},{8,16},{9,... | collective-permute-start | bytes 196616 | tf_op jit(solution)/shard_map/ppermute | solution.py:29
  71.7 0.7 fusion.7
  72.3 2.4 %collective-permute-done.18.refs_2_ = bf16[8,4096]{1,0:T(8,128)(2,1)S(1)} collective-permute-done((bf16[8,4096]{1,0:T(8,128)(2,1)S(1)}, bf16[8,4096]{1,0:T(8,128)(2,1)S(1)}, u32[]{:S(2)}, u32[]{:S(2)}) %collective-permute-start.18) | collective-permute-done | bytes 65568 | tf_op jit(solution)/shard_map/ppermute | solution.py:29
  74.8 1.0 %collective-permute-done.19.refs_3_ = bf16[8,4096]{1,0:T(8,128)(2,1)S(1)} collective-permute-done((bf16[8,4096]{1,0:T(8,128)(2,1)S(1)}, bf16[8,4096]{1,0:T(8,128)(2,1)S(1)}, u32[]{:S(2)}, u32[]{:S(2)}) %collective-permute-start.19) | collective-permute-done | bytes 65568 | tf_op jit(solution)/shard_map/ppermute | solution.py:29
  75.8 0.7 shard_map.132
  (28 shorter events, 0.1 us)
Async XLA Ops:
  0.6 9.7 %copy-start = (bf16[8,128,512]{2,1,0:T(8,128)(2,1)S(1)}, bf16[8,128,512]{2,1,0:T(8,128)(2,1)}, u32[]{:S(2)}) copy-start(bf16[8,128,512]{2,1,0:T(8,128)(2,1)} %param.19) | copy-start | bytes 3145732
  0.6 0.9 %copy-start.5 = (bf16[8,4096]{1,0:T(8,128)(2,1)S(1)}, bf16[8,4096]{1,0:T(8,128)(2,1)}, u32[]{:S(2)}) copy-start(bf16[8,4096]{1,0:T(8,128)(2,1)} %tokens_ref.1) | copy-start | bytes 196612
  1.6 0.7 copy-start.6
  2.3 0.7 copy-start.7
  3.0 0.7 copy-start.8
  3.9 9.8 %collective-permute-start.2 = (bf16[8,4224]{1,0:T(8,128)(2,1)S(1)}, bf16[8,4224]{1,0:T(8,128)(2,1)S(1)}, u32[]{:S(2)}, u32[]{:S(2)}) collective-permute-start(bf16[8,4224]{1,0:T(8,128)(2,1)S(1)} %shard_map.122), channel_id=1, source_target_pairs={{0,24},{1,25},{2,26},{3,27},{4,28},{5,29},{6,30},{7,31},{8,16},{9,... | collective-permute-start | bytes 202760 | tf_op jit(solution)/shard_map/ppermute | solution.py:29
  9.0 5.8 %collective-permute-start.1 = (bf16[8,4224]{1,0:T(8,128)(2,1)S(1)}, bf16[8,4224]{1,0:T(8,128)(2,1)S(1)}, u32[]{:S(2)}, u32[]{:S(2)}) collective-permute-start(bf16[8,4224]{1,0:T(8,128)(2,1)S(1)} %shard_map.122), channel_id=1, source_target_pairs={{0,16},{1,17},{2,18},{3,19},{4,20},{5,21},{6,22},{7,23},{8,24},{9,... | collective-permute-start | bytes 202760 | tf_op jit(solution)/shard_map/ppermute | solution.py:29
  9.0 5.8 %collective-permute-start = (bf16[8,4224]{1,0:T(8,128)(2,1)S(1)}, bf16[8,4224]{1,0:T(8,128)(2,1)S(1)}, u32[]{:S(2)}, u32[]{:S(2)}) collective-permute-start(bf16[8,4224]{1,0:T(8,128)(2,1)S(1)} %shard_map.122), channel_id=1, source_target_pairs={{0,8},{1,9},{2,10},{3,11},{4,12},{5,13},{6,14},{7,15},{8,0},{9,1},... | collective-permute-start | bytes 202760 | tf_op jit(solution)/shard_map/ppermute | solution.py:29
  14.8 10.7 %collective-permute-start.5 = (bf16[32,4224]{1,0:T(8,128)(2,1)S(1)}, bf16[32,4224]{1,0:T(8,128)(2,1)S(1)}, u32[]{:S(2)}, u32[]{:S(2)}) collective-permute-start(bf16[32,4224]{1,0:T(8,128)(2,1)S(1)} %pad_maximum_fusion.same_ref), channel_id=1, source_target_pairs={{0,2},{1,3},{2,0},{3,1},{4,6},{5,7},{6,4},{7,5},{8,10},{9,11},{10,... | collective-permute-start | bytes 811016 | tf_op jit(solution)/shard_map/ppermute | solution.py:29
  16.3 15.7 %collective-permute-start.9 = (bf16[32,4224]{1,0:T(8,128)(2,1)S(1)}, bf16[32,4224]{1,0:T(8,128)(2,1)S(1)}, u32[]{:S(2)}, u32[]{:S(2)}) collective-permute-start(bf16[32,4224]{1,0:T(8,128)(2,1)S(1)} %pad_maximum_fusion.same_ref), channel_id=1, source_target_pairs={{0,4},{1,5},{2,6},{3,7},{4,0},{5,1},{6,2},{7,3},{8,12},{9,13},{10,... | collective-permute-start | bytes 811016 | tf_op jit(solution)/shard_map/ppermute | solution.py:29
  17.8 14.2 %collective-permute-start.13 = (bf16[32,4224]{1,0:T(8,128)(2,1)S(1)}, bf16[32,4224]{1,0:T(8,128)(2,1)S(1)}, u32[]{:S(2)}, u32[]{:S(2)}) collective-permute-start(bf16[32,4224]{1,0:T(8,128)(2,1)S(1)} %pad_maximum_fusion.same_ref), channel_id=1, source_target_pairs={{0,6},{1,7},{2,4},{3,5},{4,2},{5,3},{6,0},{7,1},{8,14},{9,15},{10,... | collective-permute-start | bytes 811016 | tf_op jit(solution)/shard_map/ppermute | solution.py:29
  20.4 28.9 %all-to-all-start = ((f32[32,8,260]{2,1,0:T(8,128)}), f32[32,8,260]{2,1,0:T(8,128)}, u32[]{:S(2)}, u32[]{:S(2)}) async-start(f32[32,8,260]{2,1,0:T(8,128)} %maximum_bitcast_fusion), calls=%async_computation | async-start | bytes 786432 | tf_op jit(solution)/shard_map/all_to_all | solution.py:140
  25.5 7.1 %collective-permute-start.6 = (bf16[32,4224]{1,0:T(8,128)(2,1)S(1)}, bf16[32,4224]{1,0:T(8,128)(2,1)S(1)}, u32[]{:S(2)}, u32[]{:S(2)}) collective-permute-start(bf16[32,4224]{1,0:T(8,128)(2,1)S(1)} %collective-permute-done.5.same_ref), channel_id=1, source_target_pairs={{0,1},{1,0},{2,3},{3,2},{4,5},{5,4},{6,7},{7,6},{8,9},{9,8},{10,11... | collective-permute-start | bytes 811016 | tf_op jit(solution)/shard_map/ppermute | solution.py:29
  32.0 9.2 %collective-permute-start.10 = (bf16[32,4224]{1,0:T(8,128)(2,1)S(1)}, bf16[32,4224]{1,0:T(8,128)(2,1)S(1)}, u32[]{:S(2)}, u32[]{:S(2)}) collective-permute-start(bf16[32,4224]{1,0:T(8,128)(2,1)S(1)} %collective-permute-done.9.same_ref), channel_id=1, source_target_pairs={{0,1},{1,0},{2,3},{3,2},{4,5},{5,4},{6,7},{7,6},{8,9},{9,8},{10,11... | collective-permute-start | bytes 811016 | tf_op jit(solution)/shard_map/ppermute | solution.py:29
  32.0 11.7 %collective-permute-start.14 = (bf16[32,4224]{1,0:T(8,128)(2,1)S(1)}, bf16[32,4224]{1,0:T(8,128)(2,1)S(1)}, u32[]{:S(2)}, u32[]{:S(2)}) collective-permute-start(bf16[32,4224]{1,0:T(8,128)(2,1)S(1)} %collective-permute-done.13.same_ref), channel_id=1, source_target_pairs={{0,1},{1,0},{2,3},{3,2},{4,5},{5,4},{6,7},{7,6},{8,9},{9,8},{10,11... | collective-permute-start | bytes 811016 | tf_op jit(solution)/shard_map/ppermute | solution.py:29
  32.5 14.2 %collective-permute-start.3 = (bf16[32,4224]{1,0:T(8,128)(2,1)S(1)}, bf16[32,4224]{1,0:T(8,128)(2,1)S(1)}, u32[]{:S(2)}, u32[]{:S(2)}) collective-permute-start(bf16[32,4224]{1,0:T(8,128)(2,1)S(1)} %pad_maximum_fusion.same_ref), channel_id=1, source_target_pairs={{0,1},{1,0},{2,3},{3,2},{4,5},{5,4},{6,7},{7,6},{8,9},{9,8},{10,11... | collective-permute-start | bytes 811016 | tf_op jit(solution)/shard_map/ppermute | solution.py:29
  32.6 1.9 %copy-start.1 = (bf16[4096,384]{1,0:T(8,128)(2,1)S(1)}, bf16[4096,384]{1,0:T(8,128)(2,1)}, u32[]{:S(2)}) copy-start(bf16[4096,384]{1,0:T(8,128)(2,1)} %gate_ref.7) | copy-start | bytes 9437188
  34.4 1.9 %copy-start.3 = (bf16[4096,384]{1,0:T(8,128)(2,1)S(1)}, bf16[4096,384]{1,0:T(8,128)(2,1)}, u32[]{:S(2)}) copy-start(bf16[4096,384]{1,0:T(8,128)(2,1)} %up_ref.7) | copy-start | bytes 9437188
  36.3 1.9 %copy-start.4 = (bf16[384,4096]{1,0:T(8,128)(2,1)S(1)}, bf16[384,4096]{1,0:T(8,128)(2,1)}, u32[]{:S(2)}) copy-start(bf16[384,4096]{1,0:T(8,128)(2,1)} %down_ref.7) | copy-start | bytes 9437188
  40.7 10.0 %collective-permute-start.7 = (bf16[32,4096]{1,0:T(8,128)(2,1)}, bf16[32,4096]{1,0:T(8,128)(2,1)S(1)}, u32[]{:S(2)}, u32[]{:S(2)}) collective-permute-start(bf16[32,4096]{1,0:T(8,128)(2,1)} %get-tuple-element.17), channel_id=1, source_target_pairs={{0,1},{1,0},{2,3},{3,2},{4,5},{5,4},{6,7},{7,6},{8,9},{9,8},{10,11... | collective-permute-start | bytes 786440 | tf_op jit(solution)/shard_map/ppermute | solution.py:29
  43.7 3.0 %copy-start.2 = (bf16[4096,384]{1,0:T(8,128)(2,1)S(1)}, bf16[4096,384]{1,0:T(8,128)(2,1)}, u32[]{:S(2)}) copy-start(bf16[4096,384]{1,0:T(8,128)(2,1)} %gate_ref.7) | copy-start | bytes 9437188
  43.7 9.0 %collective-permute-start.11 = (bf16[32,4096]{1,0:T(8,128)(2,1)}, bf16[32,4096]{1,0:T(8,128)(2,1)S(1)}, u32[]{:S(2)}, u32[]{:S(2)}) collective-permute-start(bf16[32,4096]{1,0:T(8,128)(2,1)} %get-tuple-element.19), channel_id=1, source_target_pairs={{0,1},{1,0},{2,3},{3,2},{4,5},{5,4},{6,7},{7,6},{8,9},{9,8},{10,11... | collective-permute-start | bytes 786440 | tf_op jit(solution)/shard_map/ppermute | solution.py:29
  46.3 7.2 %collective-permute-start.15 = (bf16[32,4096]{1,0:T(8,128)(2,1)}, bf16[32,4096]{1,0:T(8,128)(2,1)S(1)}, u32[]{:S(2)}, u32[]{:S(2)}) collective-permute-start(bf16[32,4096]{1,0:T(8,128)(2,1)} %get-tuple-element.21), channel_id=1, source_target_pairs={{0,1},{1,0},{2,3},{3,2},{4,5},{5,4},{6,7},{7,6},{8,9},{9,8},{10,11... | collective-permute-start | bytes 786440 | tf_op jit(solution)/shard_map/ppermute | solution.py:29
  49.3 7.1 %collective-permute-start.4 = (bf16[32,4096]{1,0:T(8,128)(2,1)}, bf16[32,4096]{1,0:T(8,128)(2,1)S(1)}, u32[]{:S(2)}, u32[]{:S(2)}) collective-permute-start(bf16[32,4096]{1,0:T(8,128)(2,1)} %get-tuple-element.15), channel_id=1, source_target_pairs={{0,1},{1,0},{2,3},{3,2},{4,5},{5,4},{6,7},{7,6},{8,9},{9,8},{10,11... | collective-permute-start | bytes 786440 | tf_op jit(solution)/shard_map/ppermute | solution.py:29
  50.8 9.2 %collective-permute-start.8 = (bf16[32,4096]{1,0:T(8,128)(2,1)S(1)}, bf16[32,4096]{1,0:T(8,128)(2,1)S(1)}, u32[]{:S(2)}, u32[]{:S(2)}) collective-permute-start(bf16[32,4096]{1,0:T(8,128)(2,1)S(1)} %shard_map.126), channel_id=1, source_target_pairs={{0,2},{1,3},{2,0},{3,1},{4,6},{5,7},{6,4},{7,5},{8,10},{9,11},{10,... | collective-permute-start | bytes 786440 | tf_op jit(solution)/shard_map/ppermute | solution.py:29
  52.8 12.5 %collective-permute-start.12 = (bf16[32,4096]{1,0:T(8,128)(2,1)S(1)}, bf16[32,4096]{1,0:T(8,128)(2,1)S(1)}, u32[]{:S(2)}, u32[]{:S(2)}) collective-permute-start(bf16[32,4096]{1,0:T(8,128)(2,1)S(1)} %shard_map.128), channel_id=1, source_target_pairs={{0,4},{1,5},{2,6},{3,7},{4,0},{5,1},{6,2},{7,3},{8,12},{9,13},{10,... | collective-permute-start | bytes 786440 | tf_op jit(solution)/shard_map/ppermute | solution.py:29
  53.5 13.5 %collective-permute-start.16 = (bf16[32,4096]{1,0:T(8,128)(2,1)S(1)}, bf16[32,4096]{1,0:T(8,128)(2,1)S(1)}, u32[]{:S(2)}, u32[]{:S(2)}) collective-permute-start(bf16[32,4096]{1,0:T(8,128)(2,1)S(1)} %shard_map.130), channel_id=1, source_target_pairs={{0,6},{1,7},{2,4},{3,5},{4,2},{5,3},{6,0},{7,1},{8,14},{9,15},{10,... | collective-permute-start | bytes 786440 | tf_op jit(solution)/shard_map/ppermute | solution.py:29
  67.2 5.1 %collective-permute-start.17 = (bf16[8,4096]{1,0:T(8,128)(2,1)S(1)}, bf16[8,4096]{1,0:T(8,128)(2,1)S(1)}, u32[]{:S(2)}, u32[]{:S(2)}) collective-permute-start(bf16[8,4096]{1,0:T(8,128)(2,1)S(1)} %get-tuple-element.23), channel_id=1, source_target_pairs={{0,8},{1,9},{2,10},{3,11},{4,12},{5,13},{6,14},{7,15},{8,0},{9,1},... | collective-permute-start | bytes 196616 | tf_op jit(solution)/shard_map/ppermute | solution.py:29
  67.3 7.5 %collective-permute-start.18 = (bf16[8,4096]{1,0:T(8,128)(2,1)S(1)}, bf16[8,4096]{1,0:T(8,128)(2,1)S(1)}, u32[]{:S(2)}, u32[]{:S(2)}) collective-permute-start(bf16[8,4096]{1,0:T(8,128)(2,1)S(1)} %get-tuple-element.24), channel_id=1, source_target_pairs={{0,16},{1,17},{2,18},{3,19},{4,20},{5,21},{6,22},{7,23},{8,24},{9,... | collective-permute-start | bytes 196616 | tf_op jit(solution)/shard_map/ppermute | solution.py:29
  69.6 6.1 %collective-permute-start.19 = (bf16[8,4096]{1,0:T(8,128)(2,1)S(1)}, bf16[8,4096]{1,0:T(8,128)(2,1)S(1)}, u32[]{:S(2)}, u32[]{:S(2)}) collective-permute-start(bf16[8,4096]{1,0:T(8,128)(2,1)S(1)} %get-tuple-element.25), channel_id=1, source_target_pairs={{0,24},{1,25},{2,26},{3,27},{4,28},{5,29},{6,30},{7,31},{8,16},{9,... | collective-permute-start | bytes 196616 | tf_op jit(solution)/shard_map/ppermute | solution.py:29

commit v2 on v1

v2 whole, which is shorter than its diff:
```python
import functools

import jax
import jax.numpy as jnp
from jax import lax
from jax.experimental import pallas as pl
from jax.experimental.pallas import tpu as pltpu
from jax.sharding import PartitionSpec as P

HEADS = 64
KV_HEADS = 4
HEAD_DIM = 128
LANES = 128
VMEM = pl.BlockSpec(memory_space=pltpu.VMEM)
SMEM = pl.BlockSpec(memory_space=pltpu.SMEM)
HBM = pl.BlockSpec(memory_space=pltpu.HBM)


def levels_of(devices):
    levels, stride = [], 2
    while stride < devices:
        radix = 4 if devices // stride >= 4 else 2
        levels.append((stride, radix))
        stride *= radix
    return levels


def offsets_of(levels):
    offsets = [0]
    for stride, radix in reversed(levels):
        offsets = [stride * k ^ low for k in range(radix) for low in offsets]
    return offsets


def exchange(value, distance):
    size = lax.axis_size("ffn")
    return lax.ppermute(value, "ffn", [(i, i ^ distance) for i in range(size)])


def after(value, *others):
    return lax.optimization_barrier((value, *others))[0]


def call(body, out_shape, args, in_specs=None, scratch=(), flops=0, nbytes=0, mib=16):
    return pl.pallas_call(
        body,
        out_shape=out_shape,
        in_specs=in_specs or [VMEM] * len(args),
        out_specs=jax.tree.map(lambda _: VMEM, out_shape),
        scratch_shapes=list(scratch),
        compiler_params=pltpu.CompilerParams(vmem_limit_bytes=mib * 2**20),
        cost_estimate=pl.CostEstimate(flops=flops, bytes_accessed=nbytes, transcendentals=0),
    )(*args)


def in_hbm(*arrays):
    return [pltpu.with_memory_space_constraint(array, pltpu.HBM) for array in arrays]


def fetched(count):
    return pltpu.SemaphoreType.DMA((count,))


def fetch(sources, targets, sems):
    copies = [pltpu.make_async_copy(s, t, sems.at[i]) for i, (s, t) in enumerate(zip(sources, targets))]
    for copy in copies:
        copy.start()
    return copies


def payload_kernel(
    experts, tokens_hbm, gain_hbm, routes_hbm, scores_hbm, out_ref, tokens_ref, gain_ref, routes_ref, scores_ref, sems
):
    copies = fetch(
        [tokens_hbm, gain_hbm, routes_hbm, scores_hbm], [tokens_ref, gain_ref, routes_ref, scores_ref], sems
    )
    for copy in copies:
        copy.wait()
    features = tokens_ref[...].astype(jnp.float32)
    width = features.shape[1]
    mean_square = jnp.mean(features * features, axis=-1, keepdims=True)
    normed = features * lax.rsqrt(mean_square + 1e-06) * gain_ref[...]
    scores = scores_ref[...]
    share = scores / jnp.sum(scores, axis=-1, keepdims=True)
    extra = out_ref.shape[1] - width
    lane = lax.broadcasted_iota(jnp.int32, (features.shape[0], extra), 1)
    routes = routes_ref[...]
    gates = jnp.zeros(lane.shape, jnp.float32)
    for choice in range(routes.shape[1]):
        gates += jnp.where(
            routes[:, choice : choice + 1] == lane % experts, share[:, choice : choice + 1], 0.0
        )
    high = gates.astype(jnp.bfloat16).astype(jnp.float32)
    coded = jnp.where(lane < experts, high, jnp.where(lane < 2 * experts, gates - high, 0.0))
    out_ref[:, :width] = normed.astype(jnp.bfloat16)
    out_ref[:, width:] = coded.astype(jnp.bfloat16)


def coded_log(value):
    high = value.astype(jnp.bfloat16).astype(jnp.float32)
    middle = (value - high).astype(jnp.bfloat16).astype(jnp.float32)
    return [high, middle, value - high - middle]


def attention_kernel(
    own, offsets, info_ref, query_hbm, key_hbm, value_hbm, near_ref, far_ref, query_ref, key_ref, value_ref, dest_ref, sems
):
    copies = fetch([query_hbm, key_hbm, value_hbm], [query_ref, key_ref, value_ref], sems)
    rows, seg_len, _ = key_ref.shape
    per_group = HEADS // KV_HEADS
    shape = (per_group * rows, rows * seg_len)
    row_of = lax.broadcasted_iota(jnp.int32, shape, 0) % rows
    key_at = lax.broadcasted_iota(jnp.int32, shape, 1)
    limit = jnp.full((1, rows * seg_len), 0, jnp.int32)
    lane_row = lax.broadcasted_iota(jnp.int32, limit.shape, 1) // seg_len
    for row in range(rows):
        limit = jnp.where(lane_row == row, info_ref[2 + row] + row * seg_len - info_ref[1], limit)
    usable = (row_of == key_at // seg_len) & (key_at < limit)
    per_dest = max(1, own // HEAD_DIM)
    extra = near_ref.shape[1]
    lane = lax.broadcasted_iota(jnp.int32, (rows, extra), 1)
    for copy in copies:
        copy.wait()
    for group in range(KV_HEADS):
        cols = slice(group * HEAD_DIM, (group + 1) * HEAD_DIM)
        keys = key_ref[:, :, cols].reshape(rows * seg_len, HEAD_DIM)
        values = value_ref[:, :, cols].reshape(rows * seg_len, HEAD_DIM)
        scores = lax.dot_general(
            query_ref[group * per_group * rows : (group + 1) * per_group * rows],
            keys,
            (((1,), (1,)), ((), ())),
            preferred_element_type=jnp.float32,
        ) * HEAD_DIM ** (-0.5)
        peak = jnp.max(jnp.where(usable, scores, -1e30), axis=-1, keepdims=True)
        weights = jnp.where(usable, jnp.exp(scores - peak), 0.0).astype(jnp.bfloat16)
        total = jnp.sum(weights.astype(jnp.float32), axis=-1, keepdims=True)
        acc = jnp.dot(weights, values, preferred_element_type=jnp.float32)
        some = total > 0.0
        safe = jnp.where(some, total, 1.0)
        mean = acc / safe
        logs = jnp.where(some, peak + jnp.log(safe), -1e30)
        if own >= HEAD_DIM:
            for first in range(0, per_group, per_dest):
                dest = (group * per_group + first) // per_dest
                stats = jnp.zeros(lane.shape, jnp.float32)
                for slot in range(per_dest):
                    at = slice((first + slot) * rows, (first + slot + 1) * rows)
                    dest_ref[dest, :, slot * HEAD_DIM : (slot + 1) * HEAD_DIM] = mean[at]
                    for place, part in enumerate(coded_log(logs[at])):
                        stats = jnp.where(lane == own + 3 * slot + place, part, stats)
                dest_ref[dest, :, own:] = stats[:, own:]
        else:
            for head in range(per_group):
                at = slice(head * rows, (head + 1) * rows)
                for half in range(HEAD_DIM // own):
                    dest = (group * per_group + head) * (HEAD_DIM // own) + half
                    block = jnp.zeros(lane.shape, jnp.float32)
                    moved = mean[at] if half == 0 else pltpu.roll(mean[at], HEAD_DIM - half * own, 1)
                    block = jnp.where(lane < own, moved, block)
                    for place, part in enumerate(coded_log(logs[at])):
                        block = jnp.where(lane == own + place, part, block)
                    dest_ref[dest] = block
    for out_ref, core in ((near_ref, 0), (far_ref, 1)):
        for place in range(0, len(offsets), 2):
            pair = [dest_ref[info_ref[0] ^ (offset ^ core)] for offset in offsets[place : place + 2]]
            out_ref[place * rows : (place + 2) * rows] = jnp.concatenate(pair, axis=0).astype(jnp.bfloat16)


def attend(query, k_cache, v_cache, cache_len, levels):
    devices = lax.axis_size("ffn")
    rows, seg_len, _ = k_cache.shape
    own = query.shape[1] // devices
    extra = -(-(own + 3 * max(1, own // HEAD_DIM)) // LANES) * LANES
    me = lax.axis_index("ffn").astype(jnp.int32)
    info = jnp.concatenate([me[None], (me * seg_len)[None], cache_len])
    stacked = query.reshape(rows, HEADS, HEAD_DIM).transpose(1, 0, 2).reshape(HEADS * rows, HEAD_DIM)
    offsets = offsets_of(levels)
    out = jax.ShapeDtypeStruct((len(offsets) * rows, extra), jnp.bfloat16)
    return call(
        functools.partial(attention_kernel, own, offsets),
        [out, out],
        [info, *in_hbm(stacked, k_cache, v_cache)],
        in_specs=[SMEM, HBM, HBM, HBM],
        scratch=[
            pltpu.VMEM(stacked.shape, stacked.dtype),
            pltpu.VMEM(k_cache.shape, k_cache.dtype),
            pltpu.VMEM(v_cache.shape, v_cache.dtype),
            pltpu.VMEM((devices, rows, extra), jnp.float32),
            fetched(3),
        ],
        flops=4 * query.size * seg_len * rows,
        nbytes=2 * (k_cache.size + v_cache.size + query.size),
    )


def expert_kernel(experts, chunks, expert_ref, *refs):
    count = len(chunks)
    same_refs, other_refs, refs = refs[:count], refs[count : 2 * count], refs[2 * count :]
    near_ref, far_ref, gate_hbm, up_hbm, down_hbm, own_out, far_out, gate_ref, up_ref, down_ref, sems = refs
    width, hidden_size = gate_ref.shape
    rows = same_refs[0].shape[0]
    cuts = sems.shape[0] // 3
    depth = width // cuts
    sources, targets = [], []
    for cut in range(cuts):
        at = pl.ds(cut * depth, depth)
        sources += [gate_hbm.at[at], up_hbm.at[at]]
        targets += [gate_ref.at[at], up_ref.at[at]]
    for cut in range(cuts):
        at = pl.ds(cut * depth, depth)
        sources.append(down_hbm.at[:, at])
        targets.append(down_ref.at[:, at])
    copies = fetch(sources, targets, sems)
    coded = jnp.concatenate([r[:, width:] for r in same_refs + other_refs], axis=0).astype(jnp.float32)
    lane = lax.broadcasted_iota(jnp.int32, coded.shape, 1)
    mine = (lane < 2 * experts) & (lane % experts == expert_ref[0])
    share = jnp.sum(jnp.where(mine, coded, 0.0), axis=-1, keepdims=True)
    for place, chunk in enumerate(chunks):
        at, here = slice(place * rows, (place + 1) * rows), slice(chunk * rows, (chunk + 1) * rows)
        own_out[at, width:] = near_ref[here]
        far_out[at, width:] = far_ref[here]
    gate_part = jnp.zeros((coded.shape[0], hidden_size), jnp.float32)
    up_part = gate_part
    for cut in range(cuts):
        at = slice(cut * depth, (cut + 1) * depth)
        stacked = jnp.concatenate([r[:, at] for r in same_refs + other_refs], axis=0)
        copies[2 * cut].wait()
        gate_part += jnp.dot(stacked, gate_ref[at], preferred_element_type=jnp.float32)
        copies[2 * cut + 1].wait()
        up_part += jnp.dot(stacked, up_ref[at], preferred_element_type=jnp.float32)
    hidden = (gate_part / (1.0 + jnp.exp(-gate_part)) * up_part).astype(jnp.bfloat16)
    for cut in range(cuts):
        at = slice(cut * depth, (cut + 1) * depth)
        copies[2 * cuts + cut].wait()
        part = jnp.dot(hidden, down_ref[:, at], preferred_element_type=jnp.float32)
        part = (part * share).astype(jnp.bfloat16)
        own_out[:, at] = part[: count * rows]
        far_out[:, at] = part[count * rows :]


def apply_expert(expert, same, other, chunks, sums, weights):
    rows = same[0].shape[0]
    width, hidden = weights[0].shape
    devices = lax.axis_size("ffn")
    shape = jax.ShapeDtypeStruct((len(chunks) * rows, width + sums[0].shape[1]), jnp.bfloat16)
    return call(
        functools.partial(expert_kernel, devices // 2, chunks),
        [shape, shape],
        [expert, *same, *other, *sums, *weights],
        in_specs=[SMEM] + [VMEM] * (2 * len(chunks) + 2) + [HBM] * 3,
        scratch=[pltpu.VMEM(w.shape, w.dtype) for w in weights] + [fetched(12)],
        flops=4 * len(chunks) * rows * width * hidden * 3,
        nbytes=2 * (3 * width * hidden + 4 * len(chunks) * rows * width),
        mib=32,
    )


def merged(own, parts):
    heads, piece = max(1, own // HEAD_DIM), min(own, HEAD_DIM)
    lane = lax.broadcasted_iota(jnp.int32, parts[0].shape, 1)
    result = jnp.zeros(parts[0].shape, jnp.float32)
    for head in range(heads):
        stat = (lane >= own + 3 * head) & (lane < own + 3 * head + 3)
        logs = [jnp.sum(jnp.where(stat, p, 0.0), axis=-1, keepdims=True) for p in parts]
        top = functools.reduce(jnp.maximum, logs)
        scales = [jnp.exp(log - top) for log in logs]
        total = sum(scales)
        mean = sum(p * s for p, s in zip(parts, scales)) / total
        result = jnp.where((lane >= head * piece) & (lane < (head + 1) * piece), mean, result)
        for place, part in enumerate(coded_log(top + jnp.log(total))):
            result = jnp.where(lane == own + 3 * head + place, part, result)
    return result


def sum_kernel(count, width, own, last, *refs):
    refs, outs = refs[:count], refs[count:]
    rows = outs[0].shape[0]
    pieces = 1 if last else len(outs)
    for place in range(pieces):
        at = slice(place * rows, (place + 1) * rows)
        total = sum(ref[at, :width].astype(jnp.float32) for ref in refs)
        mean = merged(own, [ref[at, width:].astype(jnp.float32) for ref in refs])
        if last:
            outs[0][...] = total.astype(jnp.bfloat16)
            outs[1][...] = mean[:, :own].astype(jnp.bfloat16)
        else:
            outs[place][:, :width] = total.astype(jnp.bfloat16)
            outs[place][:, width:] = mean.astype(jnp.bfloat16)


def summed(parts, pieces, width, own, last=False):
    rows, whole = parts[0].shape
    if last:
        shapes = [jax.ShapeDtypeStruct((rows, n), jnp.bfloat16) for n in (width, own)]
    else:
        shapes = [jax.ShapeDtypeStruct((rows // pieces, whole), jnp.bfloat16)] * pieces
    return call(
        functools.partial(sum_kernel, len(parts), width, own, last),
        shapes,
        parts,
        flops=rows * whole * len(parts),
        nbytes=2 * rows * whole * (len(parts) + 1),
    )


def per_device(
    tokens, norm_gain, routes, gate_scores, w_gate, w_up, w_down, query, k_cache, v_cache, cache_len
):
    rows_dev, width = tokens.shape
    devices = lax.axis_size("ffn")
    experts = devices // 2
    levels = levels_of(devices)
    own = query.shape[1] // devices
    extra = -(-2 * experts // LANES) * LANES
    expert = (lax.axis_index("ffn") // 2).astype(jnp.int32)[None]
    weights = in_hbm(w_gate, w_up, w_down)

    gain = norm_gain[None]
    block = call(
        functools.partial(payload_kernel, experts),
        jax.ShapeDtypeStruct((rows_dev, width + extra), jnp.bfloat16),
        in_hbm(tokens, gain, routes, gate_scores),
        in_specs=[HBM] * 4,
        scratch=[pltpu.VMEM(a.shape, a.dtype) for a in (tokens, gain, routes, gate_scores)] + [fetched(4)],
    )
    for stride, radix in reversed(levels[1:]):
        arrived = [exchange(block, stride * k) for k in reversed(range(1, radix))]
        block = jnp.concatenate([block] + arrived[::-1], axis=0)
    sums = attend(query, k_cache, v_cache, cache_len, levels)

    stride, radix = levels[0]
    chunks = {0: block}
    for k in range(1, min(radix, 3)):
        chunks[k] = exchange(block, stride * k)
    near, far = apply_expert(expert, [block], [exchange(block, 1)], [0], sums, weights)
    for k in range(3, radix):
        chunks[k] = exchange(after(block, near), stride * k)
    (total,) = summed([near, exchange(far, 1)], 1, width, own)
    parts = [total]
    done = near
    for group in ([1, 2], [3]) if radix == 4 else ([1],):
        same = [after(chunks[k], done) for k in group]
        near, far = apply_expert(expert, same, [exchange(s, 1) for s in same], group, sums, weights)
        pieces = summed([near, exchange(far, 1)], len(group), width, own)
        parts += [exchange(piece, stride * k) for piece, k in zip(pieces, group)]
        done = near
    for stride, radix in levels[1:]:
        pieces = summed(parts, radix, width, own)
        parts = [pieces[0]] + [exchange(pieces[k], stride * k) for k in range(1, radix)]
    return tuple(summed(parts, 1, width, own, last=True))


def solution(mesh):
    in_specs = (
        P(("groups", "ffn"), None),
        P(),
        P(("groups", "ffn"), None),
        P(("groups", "ffn"), None),
        P(None, "ffn"),
        P(None, "ffn"),
        P("ffn", None),
        P("groups", None),
        P("groups", "ffn", None),
        P("groups", "ffn", None),
        P("groups"),
    )
    out_specs = (P(("groups", "ffn"), None), P("groups", "ffn"))
    return jax.shard_map(
        per_device, mesh=mesh, in_specs=in_specs, out_specs=out_specs, check_vma=False
    )
```

time: 77 us -> 69.9 us (0.908)
  local copies, waits for them, and re-layouts: 10 us -> 0 us
  Pallas kernels: 11.3 us -> 20.8 us
  waiting for transfers between devices: 21.4 us -> 28.2 us
  starting transfers between devices: 24.8 us -> 19.1 us
  other arithmetic: 4.88 us -> 0.75 us
  matrix products: 3.32 us -> 0 us
    pallas_call x11 -> x10, Pallas kernels: 11.3 us -> 20.8 us  [call(): pl.pallas_call(body, out_shape=out_shape, in_specs=in_specs or [VMEM] * l...]
    unnamed x21 -> x0, local copies, waits for them, and re-layouts: 9.02 us -> none
    ppermute x20 -> x19, waiting for transfers between devices: 21.4 us -> 28.2 us  [exchange(): return lax.ppermute(value, 'ffn', [(i, i ^ distance) for i in range(size)])]
    all_to_all x1 -> x0, starting transfers between devices: 5.08 us -> none  [attend(): lax.all_to_all(packed, 'ffn', split_axis=0, concat_axis=0, tiled=True)]
    dot_general x2 -> x0, matrix products: 3.32 us -> none  [the longest x1 1.69 us: attend(): jnp.einsum('rgqs,rsgd->rgqd', weights, values, preferred_element_type=jnp...]
    reduce_sum x3 -> x0, other arithmetic: 1.53 us -> none  [the longest x1 1.09 us: attend(): weighted = jnp.sum(acc * factor[..., None], axis=0)]
    reduce_max x1 -> x0, other arithmetic: 1.08 us -> none  [attend(): top = jnp.max(peak, axis=0)]
    transpose x1 -> x0, other arithmetic: 0.85 us -> none  [attend(): packed = packed.transpose(1, 0, 2)]
  transfers between devices with their start and end apart: 21 -> 19, of which waited for: 7 -> 11; matrix products, arithmetic and copies ran while one was open for 12% -> 1% of each run, Pallas kernels for 13% -> 27%
where the time goes in v2:
time: 69.9 us; the launch traced here: 69.7 us
  waiting for transfers between devices  28.2 us (40%)
  Pallas kernels  20.8 us (30%)
  starting transfers between devices  19.1 us (27%)
  other arithmetic  0.75 us (1%)
  between operations  0.75 us (1%)
    ppermute x19, waiting for transfers between devices, exchange(): return lax.ppermute(value, 'ffn', [(i, i ^ distance) for i in range(size)])  28.2 us
    pallas_call x10, Pallas kernels, call(): pl.pallas_call(body, out_shape=out_shape, in_specs=in_specs or [VMEM] * l...  20.8 us
    ppermute x19, starting transfers between devices, exchange(): return lax.ppermute(value, 'ffn', [(i, i ^ distance) for i in range(size)])  19.1 us
  transfers between devices with their start and end apart: 19, of which 11 were waited for; matrix products, arithmetic and copies ran while one was open for 1% of the time, Pallas kernels for 27%

profile of v2, /device:TPU:0, one launch (start us, length us, event | category | flops | bytes accessed | tf_op | source)
XLA Modules:
  0.0 69.7 jit_solution(16273183575895329482)
XLA Ops:
  0.6 1.1 %shard_map.122 = bf16[8,4224]{1,0:T(8,128)(2,1)S(1)} custom-call(bf16[8,4096]{1,0:T(8,128)(2,1)} %tokens_hbm.1, f32[1,4096]{1,0:T(1,128)} %bitcast.10, s32[8,8]{1,0:T(8,128)} %routes_hbm.1, f32[8,8]{1,0:T(8,128)} %scores_hbm.1), custom_call_target="tpu_custom_call" | custom-call | tf_op jit(solution)/shard_map/pallas_call | solution.py:45
  1.7 5.1 %collective-permute-start.2 = (bf16[8,4224]{1,0:T(8,128)(2,1)S(1)}, bf16[8,4224]{1,0:T(8,128)(2,1)S(1)}, u32[]{:S(2)}, u32[]{:S(2)}) collective-permute-start(bf16[8,4224]{1,0:T(8,128)(2,1)S(1)} %shard_map.122), channel_id=1, source_target_pairs={{0,24},{1,25},{2,26},{3,27},{4,28},{5,29},{6,30},{7,31},{8,16},{9,... | collective-permute-start | bytes 202760 | tf_op jit(solution)/shard_map/ppermute | solution.py:37
  6.8 0.0 collective-permute-start.1
  6.8 0.6 collective-permute-start
  7.5 2.0 %collective-permute-done.2 = bf16[8,4224]{1,0:T(8,128)(2,1)S(1)} collective-permute-done((bf16[8,4224]{1,0:T(8,128)(2,1)S(1)}, bf16[8,4224]{1,0:T(8,128)(2,1)S(1)}, u32[]{:S(2)}, u32[]{:S(2)}) %collective-permute-start.2) | collective-permute-done | bytes 67616 | tf_op jit(solution)/shard_map/ppermute | solution.py:37
  9.4 3.1 %collective-permute-done.1 = bf16[8,4224]{1,0:T(8,128)(2,1)S(1)} collective-permute-done((bf16[8,4224]{1,0:T(8,128)(2,1)S(1)}, bf16[8,4224]{1,0:T(8,128)(2,1)S(1)}, u32[]{:S(2)}, u32[]{:S(2)}) %collective-permute-start.1) | collective-permute-done | bytes 67616 | tf_op jit(solution)/shard_map/ppermute | solution.py:37
  12.6 0.0 collective-permute-done
  12.6 0.1 collective-permute-start.3
  12.7 1.6 %collective-permute-start.6 = (bf16[32,4224]{1,0:T(8,128)(2,1)S(1)}, bf16[32,4224]{1,0:T(8,128)(2,1)S(1)}, u32[]{:S(2)}, u32[]{:S(2)}) collective-permute-start(bf16[32,4224]{1,0:T(8,128)(2,1)S(1)} %pad_maximum_fusion.refs_0_), channel_id=1, source_target_pairs={{0,4},{1,5},{2,6},{3,7},{4,0},{5,1},{6,2},{7,3},{8,12},{9,13},{10,... | collective-permute-start | bytes 811016 | tf_op jit(solution)/shard_map/ppermute | solution.py:37
  14.3 1.5 %collective-permute-start.5 = (bf16[32,4224]{1,0:T(8,128)(2,1)S(1)}, bf16[32,4224]{1,0:T(8,128)(2,1)S(1)}, u32[]{:S(2)}, u32[]{:S(2)}) collective-permute-start(bf16[32,4224]{1,0:T(8,128)(2,1)S(1)} %pad_maximum_fusion.refs_0_), channel_id=1, source_target_pairs={{0,2},{1,3},{2,0},{3,1},{4,6},{5,7},{6,4},{7,5},{8,10},{9,11},{10,... | collective-permute-start | bytes 811016 | tf_op jit(solution)/shard_map/ppermute | solution.py:37
  15.8 0.7 %pad_add_fusion.info_ref = s32[10]{0:T(128)S(1)} fusion(s32[8]{0:T(128)} %param.21, s32[1]{0:T(128)} %bitcast.3, s32[1]{0:T(128)} %bitcast.2), kind=kLoop, calls=%fused_computation.1 | loop fusion | flops 20 | bytes 80 | tf_op jit(solution)/shard_map/concatenate | solution.py:175
  16.5 4.0 %shard_map.123 = (bf16[128,384]{1,0:T(8,128)(2,1)S(1)}, bf16[128,384]{1,0:T(8,128)(2,1)S(1)}) custom-call(s32[10]{0:T(128)S(1)} %pad_add_fusion.info_ref, bf16[512,128]{1,0:T(8,128)(2,1)} %bitcast.9, bf16[8,128,512]{2,1,0:T(8,128)(2,1)} %key_hbm.1, bf16[8,128,512]{2,1,0:T(8,128)(2,1)} %value_hbm.1), custom_call_target="tpu_custom_call" | custom-call | flops 268435456 | bytes 2228224 | tf_op jit(solution)/shard_map/pallas_call | solution.py:45
  20.5 0.0 collective-permute-done.3.refs_1_
  20.5 4.5 %shard_map.124 = (bf16[32,4480]{1,0:T(8,128)(2,1)S(1)}, bf16[32,4480]{1,0:T(8,128)(2,1)S(1)}) custom-call(s32[1]{0:T(128)} %bitcast.expert_ref, bf16[32,4224]{1,0:T(8,128)(2,1)S(1)} %pad_maximum_fusion.refs_0_, bf16[32,4224]{1,0:T(8,128)(2,1)S(1)} %collective-permute-done.3.refs_1_, bf16[128,384]{1,0:T(8,128)(2,1)S(1)} %get-tuple-element.20.refs_2_.refs_4_, ...), custom_call_target="tpu_custom_call" | custom-call | flops 603979776 | bytes 10485760 | tf_op jit(solution)/shard_map/pallas_call | solution.py:45
  25.1 0.0 collective-permute-done.6.refs_1_
  25.1 0.0 collective-permute-done.5.refs_0_
  25.1 0.1 collective-permute-start.7
  25.2 0.5 collective-permute-start.8
  25.7 0.5 collective-permute-start.12
  26.2 0.6 collective-permute-done.7.refs_2_
  26.7 0.4 collective-permute-done.8.refs_3_
  27.1 5.0 %shard_map.126 = (bf16[64,4480]{1,0:T(8,128)(2,1)S(1)}, bf16[64,4480]{1,0:T(8,128)(2,1)S(1)}) custom-call(s32[1]{0:T(128)} %bitcast.expert_ref, bf16[32,4224]{1,0:T(8,128)(2,1)S(1)} %collective-permute-done.5.refs_0_, bf16[32,4224]{1,0:T(8,128)(2,1)S(1)} %collective-permute-done.6.refs_1_, bf16[32,4224]{1,0:T(8,128)(2,1)S(1)} %collective-permute-done.7.refs_2_, ...), custom_call_target="tpu_custom_call" | custom-call | flops 1207959552 | bytes 11534336 | tf_op jit(solution)/shard_map/pallas_call | solution.py:45
  32.1 2.9 %collective-permute-done.12.refs_0_ = bf16[32,4224]{1,0:T(8,128)(2,1)S(1)} collective-permute-done((bf16[32,4224]{1,0:T(8,128)(2,1)S(1)}, bf16[32,4224]{1,0:T(8,128)(2,1)S(1)}, u32[]{:S(2)}, u32[]{:S(2)}) %collective-permute-start.12) | collective-permute-done | bytes 270368 | tf_op jit(solution)/shard_map/ppermute | solution.py:37
  35.0 0.0 collective-permute-start.13
  35.0 0.5 collective-permute-start.9
  35.6 1.0 %collective-permute-done.13.refs_1_ = bf16[32,4224]{1,0:T(8,128)(2,1)S(1)} collective-permute-done((bf16[32,4224]{1,0:T(8,128)(2,1)S(1)}, bf16[32,4224]{1,0:T(8,128)(2,1)S(1)}, u32[]{:S(2)}, u32[]{:S(2)}) %collective-permute-start.13) | collective-permute-done | bytes 270368 | tf_op jit(solution)/shard_map/ppermute | solution.py:37
  36.6 4.5 %shard_map.128 = (bf16[32,4480]{1,0:T(8,128)(2,1)S(1)}, bf16[32,4480]{1,0:T(8,128)(2,1)S(1)}) custom-call(s32[1]{0:T(128)} %bitcast.expert_ref, bf16[32,4224]{1,0:T(8,128)(2,1)S(1)} %collective-permute-done.12.refs_0_, bf16[32,4224]{1,0:T(8,128)(2,1)S(1)} %collective-permute-done.13.refs_1_, bf16[128,384]{1,0:T(8,128)(2,1)S(1)} %get-tuple-element.20.refs_2_.refs_4_, ...), custom_call_target="tpu_custom_call" | custom-call | flops 603979776 | bytes 10485760 | tf_op jit(solution)/shard_map/pallas_call | solution.py:45
  41.1 0.2 collective-permute-start.14
  41.3 0.4 collective-permute-start.4
  41.7 1.1 %collective-permute-done.14.refs_1_ = bf16[32,4480]{1,0:T(8,128)(2,1)S(1)} collective-permute-done((bf16[32,4480]{1,0:T(8,128)(2,1)S(1)}, bf16[32,4480]{1,0:T(8,128)(2,1)S(1)}, u32[]{:S(2)}, u32[]{:S(2)}) %collective-permute-start.14) | collective-permute-done | bytes 286752 | tf_op jit(solution)/shard_map/ppermute | solution.py:37
  42.8 0.2 shard_map.129
  42.9 0.5 collective-permute-start.15
  43.5 0.0 collective-permute-done.9.refs_1_
  43.5 0.4 shard_map.127
  43.8 1.6 %collective-permute-start.10 = (bf16[32,4480]{1,0:T(8,128)(2,1)S(1)}, bf16[32,4480]{1,0:T(8,128)(2,1)S(1)}, u32[]{:S(2)}, u32[]{:S(2)}) collective-permute-start(bf16[32,4480]{1,0:T(8,128)(2,1)S(1)} %get-tuple-element.28), channel_id=1, source_target_pairs={{0,2},{1,3},{2,0},{3,1},{4,6},{5,7},{6,4},{7,5},{8,10},{9,11},{10,... | collective-permute-start | bytes 860168 | tf_op jit(solution)/shard_map/ppermute | solution.py:37
  45.4 1.5 %collective-permute-start.11 = (bf16[32,4480]{1,0:T(8,128)(2,1)S(1)}, bf16[32,4480]{1,0:T(8,128)(2,1)S(1)}, u32[]{:S(2)}, u32[]{:S(2)}) collective-permute-start(bf16[32,4480]{1,0:T(8,128)(2,1)S(1)} %get-tuple-element.29), channel_id=1, source_target_pairs={{0,4},{1,5},{2,6},{3,7},{4,0},{5,1},{6,2},{7,3},{8,12},{9,13},{10,... | collective-permute-start | bytes 860168 | tf_op jit(solution)/shard_map/ppermute | solution.py:37
  46.9 0.0 collective-permute-done.4.refs_1_
  46.9 0.2 shard_map.125.refs_0_
  47.1 6.5 %collective-permute-done.15.refs_3_ = bf16[32,4480]{1,0:T(8,128)(2,1)S(1)} collective-permute-done((bf16[32,4480]{1,0:T(8,128)(2,1)S(1)}, bf16[32,4480]{1,0:T(8,128)(2,1)S(1)}, u32[]{:S(2)}, u32[]{:S(2)}) %collective-permute-start.15) | collective-permute-done | bytes 286752 | tf_op jit(solution)/shard_map/ppermute | solution.py:37
  53.6 4.4 %collective-permute-done.10.refs_1_ = bf16[32,4480]{1,0:T(8,128)(2,1)S(1)} collective-permute-done((bf16[32,4480]{1,0:T(8,128)(2,1)S(1)}, bf16[32,4480]{1,0:T(8,128)(2,1)S(1)}, u32[]{:S(2)}, u32[]{:S(2)}) %collective-permute-start.10) | collective-permute-done | bytes 286752 | tf_op jit(solution)/shard_map/ppermute | solution.py:37
  58.0 0.9 %collective-permute-done.11.refs_2_ = bf16[32,4480]{1,0:T(8,128)(2,1)S(1)} collective-permute-done((bf16[32,4480]{1,0:T(8,128)(2,1)S(1)}, bf16[32,4480]{1,0:T(8,128)(2,1)S(1)}, u32[]{:S(2)}, u32[]{:S(2)}) %collective-permute-start.11) | collective-permute-done | bytes 286752 | tf_op jit(solution)/shard_map/ppermute | solution.py:37
  58.9 0.3 shard_map.130
  59.2 1.1 %collective-permute-start.16 = (bf16[8,4480]{1,0:T(8,128)(2,1)S(1)}, bf16[8,4480]{1,0:T(8,128)(2,1)S(1)}, u32[]{:S(2)}, u32[]{:S(2)}) collective-permute-start(bf16[8,4480]{1,0:T(8,128)(2,1)S(1)} %get-tuple-element.35), channel_id=1, source_target_pairs={{0,8},{1,9},{2,10},{3,11},{4,12},{5,13},{6,14},{7,15},{8,0},{9,1},... | collective-permute-start | bytes 215048 | tf_op jit(solution)/shard_map/ppermute | solution.py:37
  60.3 2.2 %collective-permute-start.17 = (bf16[8,4480]{1,0:T(8,128)(2,1)S(1)}, bf16[8,4480]{1,0:T(8,128)(2,1)S(1)}, u32[]{:S(2)}, u32[]{:S(2)}) collective-permute-start(bf16[8,4480]{1,0:T(8,128)(2,1)S(1)} %get-tuple-element.36), channel_id=1, source_target_pairs={{0,16},{1,17},{2,18},{3,19},{4,20},{5,21},{6,22},{7,23},{8,24},{9,... | collective-permute-start | bytes 215048 | tf_op jit(solution)/shard_map/ppermute | solution.py:37
  62.6 1.1 %collective-permute-start.18 = (bf16[8,4480]{1,0:T(8,128)(2,1)S(1)}, bf16[8,4480]{1,0:T(8,128)(2,1)S(1)}, u32[]{:S(2)}, u32[]{:S(2)}) collective-permute-start(bf16[8,4480]{1,0:T(8,128)(2,1)S(1)} %get-tuple-element.37), channel_id=1, source_target_pairs={{0,24},{1,25},{2,26},{3,27},{4,28},{5,29},{6,30},{7,31},{8,16},{9,... | collective-permute-start | bytes 215048 | tf_op jit(solution)/shard_map/ppermute | solution.py:37
  63.7 0.0 collective-permute-done.16.refs_1_
  63.7 5.3 %collective-permute-done.17.refs_2_ = bf16[8,4480]{1,0:T(8,128)(2,1)S(1)} collective-permute-done((bf16[8,4480]{1,0:T(8,128)(2,1)S(1)}, bf16[8,4480]{1,0:T(8,128)(2,1)S(1)}, u32[]{:S(2)}, u32[]{:S(2)}) %collective-permute-start.17) | collective-permute-done | bytes 71712 | tf_op jit(solution)/shard_map/ppermute | solution.py:37
  68.9 0.0 collective-permute-done.18.refs_3_
  69.0 0.7 %shard_map.131 = (bf16[8,4096]{1,0:T(8,128)(2,1)}, bf16[8,256]{1,0:T(8,128)(2,1)}) custom-call(bf16[8,4480]{1,0:T(8,128)(2,1)S(1)} %get-tuple-element.34.refs_0_, bf16[8,4480]{1,0:T(8,128)(2,1)S(1)} %collective-permute-done.16.refs_1_, bf16[8,4480]{1,0:T(8,128)(2,1)S(1)} %collective-permute-done.17.refs_2_, bf16[8,4480]{1,0:T(8,128)(2,1)S(1)} %collective-permute-done.18.refs_3_), custom_call_target="tpu_custom_call" | custom-call | flops 143360 | bytes 358400 | tf_op jit(solution)/shard_map/pallas_call | solution.py:45
  (1 shorter events, 0.0 us)
Async XLA Ops:
  1.7 7.7 %collective-permute-start.2 = (bf16[8,4224]{1,0:T(8,128)(2,1)S(1)}, bf16[8,4224]{1,0:T(8,128)(2,1)S(1)}, u32[]{:S(2)}, u32[]{:S(2)}) collective-permute-start(bf16[8,4224]{1,0:T(8,128)(2,1)S(1)} %shard_map.122), channel_id=1, source_target_pairs={{0,24},{1,25},{2,26},{3,27},{4,28},{5,29},{6,30},{7,31},{8,16},{9,... | collective-permute-start | bytes 202760 | tf_op jit(solution)/shard_map/ppermute | solution.py:37
  6.8 5.8 %collective-permute-start.1 = (bf16[8,4224]{1,0:T(8,128)(2,1)S(1)}, bf16[8,4224]{1,0:T(8,128)(2,1)S(1)}, u32[]{:S(2)}, u32[]{:S(2)}) collective-permute-start(bf16[8,4224]{1,0:T(8,128)(2,1)S(1)} %shard_map.122), channel_id=1, source_target_pairs={{0,16},{1,17},{2,18},{3,19},{4,20},{5,21},{6,22},{7,23},{8,24},{9,... | collective-permute-start | bytes 202760 | tf_op jit(solution)/shard_map/ppermute | solution.py:37
  6.8 5.8 %collective-permute-start = (bf16[8,4224]{1,0:T(8,128)(2,1)S(1)}, bf16[8,4224]{1,0:T(8,128)(2,1)S(1)}, u32[]{:S(2)}, u32[]{:S(2)}) collective-permute-start(bf16[8,4224]{1,0:T(8,128)(2,1)S(1)} %shard_map.122), channel_id=1, source_target_pairs={{0,8},{1,9},{2,10},{3,11},{4,12},{5,13},{6,14},{7,15},{8,0},{9,1},... | collective-permute-start | bytes 202760 | tf_op jit(solution)/shard_map/ppermute | solution.py:37
  12.6 7.9 %collective-permute-start.3 = (bf16[32,4224]{1,0:T(8,128)(2,1)S(1)}, bf16[32,4224]{1,0:T(8,128)(2,1)S(1)}, u32[]{:S(2)}, u32[]{:S(2)}) collective-permute-start(bf16[32,4224]{1,0:T(8,128)(2,1)S(1)} %pad_maximum_fusion.refs_0_), channel_id=1, source_target_pairs={{0,1},{1,0},{2,3},{3,2},{4,5},{5,4},{6,7},{7,6},{8,9},{9,8},{10,11... | collective-permute-start | bytes 811016 | tf_op jit(solution)/shard_map/ppermute | solution.py:37
  12.7 12.4 %collective-permute-start.6 = (bf16[32,4224]{1,0:T(8,128)(2,1)S(1)}, bf16[32,4224]{1,0:T(8,128)(2,1)S(1)}, u32[]{:S(2)}, u32[]{:S(2)}) collective-permute-start(bf16[32,4224]{1,0:T(8,128)(2,1)S(1)} %pad_maximum_fusion.refs_0_), channel_id=1, source_target_pairs={{0,4},{1,5},{2,6},{3,7},{4,0},{5,1},{6,2},{7,3},{8,12},{9,13},{10,... | collective-permute-start | bytes 811016 | tf_op jit(solution)/shard_map/ppermute | solution.py:37
  14.3 10.8 %collective-permute-start.5 = (bf16[32,4224]{1,0:T(8,128)(2,1)S(1)}, bf16[32,4224]{1,0:T(8,128)(2,1)S(1)}, u32[]{:S(2)}, u32[]{:S(2)}) collective-permute-start(bf16[32,4224]{1,0:T(8,128)(2,1)S(1)} %pad_maximum_fusion.refs_0_), channel_id=1, source_target_pairs={{0,2},{1,3},{2,0},{3,1},{4,6},{5,7},{6,4},{7,5},{8,10},{9,11},{10,... | collective-permute-start | bytes 811016 | tf_op jit(solution)/shard_map/ppermute | solution.py:37
  25.1 1.6 %collective-permute-start.7 = (bf16[32,4224]{1,0:T(8,128)(2,1)S(1)}, bf16[32,4224]{1,0:T(8,128)(2,1)S(1)}, u32[]{:S(2)}, u32[]{:S(2)}) collective-permute-start(bf16[32,4224]{1,0:T(8,128)(2,1)S(1)} %collective-permute-done.5.refs_0_), channel_id=1, source_target_pairs={{0,1},{1,0},{2,3},{3,2},{4,5},{5,4},{6,7},{7,6},{8,9},{9,8},{10,11... | collective-permute-start | bytes 811016 | tf_op jit(solution)/shard_map/ppermute | solution.py:37
  25.2 1.9 %collective-permute-start.8 = (bf16[32,4224]{1,0:T(8,128)(2,1)S(1)}, bf16[32,4224]{1,0:T(8,128)(2,1)S(1)}, u32[]{:S(2)}, u32[]{:S(2)}) collective-permute-start(bf16[32,4224]{1,0:T(8,128)(2,1)S(1)} %collective-permute-done.6.refs_1_), channel_id=1, source_target_pairs={{0,1},{1,0},{2,3},{3,2},{4,5},{5,4},{6,7},{7,6},{8,9},{9,8},{10,11... | collective-permute-start | bytes 811016 | tf_op jit(solution)/shard_map/ppermute | solution.py:37
  25.7 9.4 %collective-permute-start.12 = (bf16[32,4224]{1,0:T(8,128)(2,1)S(1)}, bf16[32,4224]{1,0:T(8,128)(2,1)S(1)}, u32[]{:S(2)}, u32[]{:S(2)}) collective-permute-start(bf16[32,4224]{1,0:T(8,128)(2,1)S(1)} %pad_maximum_fusion.refs_0_), channel_id=1, source_target_pairs={{0,6},{1,7},{2,4},{3,5},{4,2},{5,3},{6,0},{7,1},{8,14},{9,15},{10,... | collective-permute-start | bytes 811016 | tf_op jit(solution)/shard_map/ppermute | solution.py:37
  35.0 1.5 %collective-permute-start.13 = (bf16[32,4224]{1,0:T(8,128)(2,1)S(1)}, bf16[32,4224]{1,0:T(8,128)(2,1)S(1)}, u32[]{:S(2)}, u32[]{:S(2)}) collective-permute-start(bf16[32,4224]{1,0:T(8,128)(2,1)S(1)} %collective-permute-done.12.refs_0_), channel_id=1, source_target_pairs={{0,1},{1,0},{2,3},{3,2},{4,5},{5,4},{6,7},{7,6},{8,9},{9,8},{10,11... | collective-permute-start | bytes 811016 | tf_op jit(solution)/shard_map/ppermute | solution.py:37
  35.0 8.4 %collective-permute-start.9 = (bf16[64,4480]{1,0:T(8,128)(2,1)S(1)}, bf16[64,4480]{1,0:T(8,128)(2,1)S(1)}, u32[]{:S(2)}, u32[]{:S(2)}) collective-permute-start(bf16[64,4480]{1,0:T(8,128)(2,1)S(1)} %get-tuple-element.27), channel_id=1, source_target_pairs={{0,1},{1,0},{2,3},{3,2},{4,5},{5,4},{6,7},{7,6},{8,9},{9,8},{10,11... | collective-permute-start | bytes 1720328 | tf_op jit(solution)/shard_map/ppermute | solution.py:37
  41.1 1.6 %collective-permute-start.14 = (bf16[32,4480]{1,0:T(8,128)(2,1)S(1)}, bf16[32,4480]{1,0:T(8,128)(2,1)S(1)}, u32[]{:S(2)}, u32[]{:S(2)}) collective-permute-start(bf16[32,4480]{1,0:T(8,128)(2,1)S(1)} %get-tuple-element.33), channel_id=1, source_target_pairs={{0,1},{1,0},{2,3},{3,2},{4,5},{5,4},{6,7},{7,6},{8,9},{9,8},{10,11... | collective-permute-start | bytes 860168 | tf_op jit(solution)/shard_map/ppermute | solution.py:37
  41.3 5.6 %collective-permute-start.4 = (bf16[32,4480]{1,0:T(8,128)(2,1)S(1)}, bf16[32,4480]{1,0:T(8,128)(2,1)S(1)}, u32[]{:S(2)}, u32[]{:S(2)}) collective-permute-start(bf16[32,4480]{1,0:T(8,128)(2,1)S(1)} %get-tuple-element.23), channel_id=1, source_target_pairs={{0,1},{1,0},{2,3},{3,2},{4,5},{5,4},{6,7},{7,6},{8,9},{9,8},{10,11... | collective-permute-start | bytes 860168 | tf_op jit(solution)/shard_map/ppermute | solution.py:37
  42.9 10.7 %collective-permute-start.15 = (bf16[32,4480]{1,0:T(8,128)(2,1)S(1)}, bf16[32,4480]{1,0:T(8,128)(2,1)S(1)}, u32[]{:S(2)}, u32[]{:S(2)}) collective-permute-start(bf16[32,4480]{1,0:T(8,128)(2,1)S(1)} %shard_map.129), channel_id=1, source_target_pairs={{0,6},{1,7},{2,4},{3,5},{4,2},{5,3},{6,0},{7,1},{8,14},{9,15},{10,... | collective-permute-start | bytes 860168 | tf_op jit(solution)/shard_map/ppermute | solution.py:37
  43.8 14.2 %collective-permute-start.10 = (bf16[32,4480]{1,0:T(8,128)(2,1)S(1)}, bf16[32,4480]{1,0:T(8,128)(2,1)S(1)}, u32[]{:S(2)}, u32[]{:S(2)}) collective-permute-start(bf16[32,4480]{1,0:T(8,128)(2,1)S(1)} %get-tuple-element.28), channel_id=1, source_target_pairs={{0,2},{1,3},{2,0},{3,1},{4,6},{5,7},{6,4},{7,5},{8,10},{9,11},{10,... | collective-permute-start | bytes 860168 | tf_op jit(solution)/shard_map/ppermute | solution.py:37
  45.4 13.5 %collective-permute-start.11 = (bf16[32,4480]{1,0:T(8,128)(2,1)S(1)}, bf16[32,4480]{1,0:T(8,128)(2,1)S(1)}, u32[]{:S(2)}, u32[]{:S(2)}) collective-permute-start(bf16[32,4480]{1,0:T(8,128)(2,1)S(1)} %get-tuple-element.29), channel_id=1, source_target_pairs={{0,4},{1,5},{2,6},{3,7},{4,0},{5,1},{6,2},{7,3},{8,12},{9,13},{10,... | collective-permute-start | bytes 860168 | tf_op jit(solution)/shard_map/ppermute | solution.py:37
  59.2 4.5 %collective-permute-start.16 = (bf16[8,4480]{1,0:T(8,128)(2,1)S(1)}, bf16[8,4480]{1,0:T(8,128)(2,1)S(1)}, u32[]{:S(2)}, u32[]{:S(2)}) collective-permute-start(bf16[8,4480]{1,0:T(8,128)(2,1)S(1)} %get-tuple-element.35), channel_id=1, source_target_pairs={{0,8},{1,9},{2,10},{3,11},{4,12},{5,13},{6,14},{7,15},{8,0},{9,1},... | collective-permute-start | bytes 215048 | tf_op jit(solution)/shard_map/ppermute | solution.py:37
  60.3 8.6 %collective-permute-start.17 = (bf16[8,4480]{1,0:T(8,128)(2,1)S(1)}, bf16[8,4480]{1,0:T(8,128)(2,1)S(1)}, u32[]{:S(2)}, u32[]{:S(2)}) collective-permute-start(bf16[8,4480]{1,0:T(8,128)(2,1)S(1)} %get-tuple-element.36), channel_id=1, source_target_pairs={{0,16},{1,17},{2,18},{3,19},{4,20},{5,21},{6,22},{7,23},{8,24},{9,... | collective-permute-start | bytes 215048 | tf_op jit(solution)/shard_map/ppermute | solution.py:37
  62.6 6.4 %collective-permute-start.18 = (bf16[8,4480]{1,0:T(8,128)(2,1)S(1)}, bf16[8,4480]{1,0:T(8,128)(2,1)S(1)}, u32[]{:S(2)}, u32[]{:S(2)}) collective-permute-start(bf16[8,4480]{1,0:T(8,128)(2,1)S(1)} %get-tuple-element.37), channel_id=1, source_target_pairs={{0,24},{1,25},{2,26},{3,27},{4,28},{5,29},{6,30},{7,31},{8,16},{9,... | collective-permute-start | bytes 215048 | tf_op jit(solution)/shard_map/ppermute | solution.py:37

commit v3 on v2

--- a/solution.py
+++ b/solution.py
@@ -41,7 +41,7 @@
     return lax.optimization_barrier((value, *others))[0]
 
 
-def call(body, out_shape, args, in_specs=None, scratch=(), flops=0, nbytes=0, mib=16):
+def call(body, out_shape, args, in_specs=None, scratch=(), flops=1, nbytes=1, mib=16):
     return pl.pallas_call(
         body,
         out_shape=out_shape,
@@ -103,9 +103,13 @@
 
 
 def attention_kernel(
-    own, offsets, info_ref, query_hbm, key_hbm, value_hbm, near_ref, far_ref, query_ref, key_ref, value_ref, dest_ref, sems
+    own, offsets, length_ref, *refs
 ):
-    copies = fetch([query_hbm, key_hbm, value_hbm], [query_ref, key_ref, value_ref], sems)
+    query_hbm, key_hbm, value_hbm, gate_hbm, up_hbm, near_ref, far_ref, gate_out, up_out = refs[:9]
+    query_ref, key_ref, value_ref, dest_ref, sems = refs[9:]
+    sources = [query_hbm, key_hbm, value_hbm, gate_hbm, up_hbm]
+    copies = fetch(sources, [query_ref, key_ref, value_ref, gate_out, up_out], sems)
+    me = lax.axis_index("ffn")
     rows, seg_len, _ = key_ref.shape
     per_group = HEADS // KV_HEADS
     shape = (per_group * rows, rows * seg_len)
@@ -114,12 +118,12 @@
     limit = jnp.full((1, rows * seg_len), 0, jnp.int32)
     lane_row = lax.broadcasted_iota(jnp.int32, limit.shape, 1) // seg_len
     for row in range(rows):
-        limit = jnp.where(lane_row == row, info_ref[2 + row] + row * seg_len - info_ref[1], limit)
+        limit = jnp.where(lane_row == row, length_ref[row] + row * seg_len - me * seg_len, limit)
     usable = (row_of == key_at // seg_len) & (key_at < limit)
     per_dest = max(1, own // HEAD_DIM)
     extra = near_ref.shape[1]
     lane = lax.broadcasted_iota(jnp.int32, (rows, extra), 1)
-    for copy in copies:
+    for copy in copies[:3]:
         copy.wait()
     for group in range(KV_HEADS):
         cols = slice(group * HEAD_DIM, (group + 1) * HEAD_DIM)
@@ -162,96 +166,78 @@
                     dest_ref[dest] = block
     for out_ref, core in ((near_ref, 0), (far_ref, 1)):
         for place in range(0, len(offsets), 2):
-            pair = [dest_ref[info_ref[0] ^ (offset ^ core)] for offset in offsets[place : place + 2]]
+            pair = [dest_ref[me ^ (offset ^ core)] for offset in offsets[place : place + 2]]
             out_ref[place * rows : (place + 2) * rows] = jnp.concatenate(pair, axis=0).astype(jnp.bfloat16)
-
-
-def attend(query, k_cache, v_cache, cache_len, levels):
+    for copy in copies[3:]:
+        copy.wait()
+
+
+def attend(query, k_cache, v_cache, cache_len, levels, weights):
     devices = lax.axis_size("ffn")
     rows, seg_len, _ = k_cache.shape
     own = query.shape[1] // devices
     extra = -(-(own + 3 * max(1, own // HEAD_DIM)) // LANES) * LANES
-    me = lax.axis_index("ffn").astype(jnp.int32)
-    info = jnp.concatenate([me[None], (me * seg_len)[None], cache_len])
     stacked = query.reshape(rows, HEADS, HEAD_DIM).transpose(1, 0, 2).reshape(HEADS * rows, HEAD_DIM)
     offsets = offsets_of(levels)
     out = jax.ShapeDtypeStruct((len(offsets) * rows, extra), jnp.bfloat16)
     return call(
         functools.partial(attention_kernel, own, offsets),
-        [out, out],
-        [info, *in_hbm(stacked, k_cache, v_cache)],
-        in_specs=[SMEM, HBM, HBM, HBM],
+        [out, out] + [pltpu.VMEM(w.shape, w.dtype) for w in weights],
+        [cache_len, *in_hbm(stacked, k_cache, v_cache, *weights)],
+        in_specs=[SMEM] + [HBM] * 5,
         scratch=[
             pltpu.VMEM(stacked.shape, stacked.dtype),
             pltpu.VMEM(k_cache.shape, k_cache.dtype),
             pltpu.VMEM(v_cache.shape, v_cache.dtype),
             pltpu.VMEM((devices, rows, extra), jnp.float32),
-            fetched(3),
+            fetched(5),
         ],
-        flops=4 * query.size * seg_len * rows,
-        nbytes=2 * (k_cache.size + v_cache.size + query.size),
-    )
-
-
-def expert_kernel(experts, chunks, expert_ref, *refs):
-    count = len(chunks)
+        flops=10**9,
+        nbytes=2 * sum(w.size for w in weights),
+    )
+
+
+def expert_kernel(experts, count, *refs):
     same_refs, other_refs, refs = refs[:count], refs[count : 2 * count], refs[2 * count :]
-    near_ref, far_ref, gate_hbm, up_hbm, down_hbm, own_out, far_out, gate_ref, up_ref, down_ref, sems = refs
-    width, hidden_size = gate_ref.shape
+    near_ref, far_ref, gate_ref, up_ref, down_hbm, own_out, far_out, down_ref, sems = refs
+    width = gate_ref.shape[0]
     rows = same_refs[0].shape[0]
-    cuts = sems.shape[0] // 3
-    depth = width // cuts
-    sources, targets = [], []
-    for cut in range(cuts):
-        at = pl.ds(cut * depth, depth)
-        sources += [gate_hbm.at[at], up_hbm.at[at]]
-        targets += [gate_ref.at[at], up_ref.at[at]]
-    for cut in range(cuts):
-        at = pl.ds(cut * depth, depth)
-        sources.append(down_hbm.at[:, at])
-        targets.append(down_ref.at[:, at])
-    copies = fetch(sources, targets, sems)
+    step = width // sems.shape[0]
+    cuts = [pl.ds(first, step) for first in range(0, width, step)]
+    copies = fetch([down_hbm.at[:, at] for at in cuts], [down_ref.at[:, at] for at in cuts], sems)
     coded = jnp.concatenate([r[:, width:] for r in same_refs + other_refs], axis=0).astype(jnp.float32)
     lane = lax.broadcasted_iota(jnp.int32, coded.shape, 1)
-    mine = (lane < 2 * experts) & (lane % experts == expert_ref[0])
+    mine = (lane < 2 * experts) & (lane % experts == lax.axis_index("ffn") // 2)
     share = jnp.sum(jnp.where(mine, coded, 0.0), axis=-1, keepdims=True)
-    for place, chunk in enumerate(chunks):
-        at, here = slice(place * rows, (place + 1) * rows), slice(chunk * rows, (chunk + 1) * rows)
-        own_out[at, width:] = near_ref[here]
-        far_out[at, width:] = far_ref[here]
-    gate_part = jnp.zeros((coded.shape[0], hidden_size), jnp.float32)
-    up_part = gate_part
-    for cut in range(cuts):
-        at = slice(cut * depth, (cut + 1) * depth)
-        stacked = jnp.concatenate([r[:, at] for r in same_refs + other_refs], axis=0)
-        copies[2 * cut].wait()
-        gate_part += jnp.dot(stacked, gate_ref[at], preferred_element_type=jnp.float32)
-        copies[2 * cut + 1].wait()
-        up_part += jnp.dot(stacked, up_ref[at], preferred_element_type=jnp.float32)
+    own_out[:, width:] = near_ref[...]
+    far_out[:, width:] = far_ref[...]
+    stacked = jnp.concatenate([r[:, :width] for r in same_refs + other_refs], axis=0)
+    gate_part = jnp.dot(stacked, gate_ref[...], preferred_element_type=jnp.float32)
+    up_part = jnp.dot(stacked, up_ref[...], preferred_element_type=jnp.float32)
     hidden = (gate_part / (1.0 + jnp.exp(-gate_part)) * up_part).astype(jnp.bfloat16)
-    for cut in range(cuts):
-        at = slice(cut * depth, (cut + 1) * depth)
-        copies[2 * cuts + cut].wait()
+    for copy, at in zip(copies, cuts):
+        copy.wait()
         part = jnp.dot(hidden, down_ref[:, at], preferred_element_type=jnp.float32)
         part = (part * share).astype(jnp.bfloat16)
         own_out[:, at] = part[: count * rows]
         far_out[:, at] = part[count * rows :]
 
 
-def apply_expert(expert, same, other, chunks, sums, weights):
+def apply_expert(same, sums, weights):
     rows = same[0].shape[0]
     width, hidden = weights[0].shape
     devices = lax.axis_size("ffn")
-    shape = jax.ShapeDtypeStruct((len(chunks) * rows, width + sums[0].shape[1]), jnp.bfloat16)
+    shape = jax.ShapeDtypeStruct((len(same) * rows, width + sums[0].shape[1]), jnp.bfloat16)
+    args = [*same, *[exchange(s, 1) for s in same], *sums, *weights[:2], *in_hbm(weights[2])]
     return call(
-        functools.partial(expert_kernel, devices // 2, chunks),
+        functools.partial(expert_kernel, devices // 2, len(same)),
         [shape, shape],
-        [expert, *same, *other, *sums, *weights],
-        in_specs=[SMEM] + [VMEM] * (2 * len(chunks) + 2) + [HBM] * 3,
-        scratch=[pltpu.VMEM(w.shape, w.dtype) for w in weights] + [fetched(12)],
-        flops=4 * len(chunks) * rows * width * hidden * 3,
-        nbytes=2 * (3 * width * hidden + 4 * len(chunks) * rows * width),
-        mib=32,
+        args,
+        in_specs=[VMEM] * (2 * len(same) + 4) + [HBM],
+        scratch=[pltpu.VMEM(weights[2].shape, weights[2].dtype), fetched(4)],
+        flops=4 * len(same) * rows * width * hidden * 3,
+        nbytes=2 * 3 * width * hidden,
+        mib=8 + sum(2 * a.size for a in args) // 2**20,
     )
 
 
@@ -274,33 +260,54 @@
 
 def sum_kernel(count, width, own, last, *refs):
     refs, outs = refs[:count], refs[count:]
-    rows = outs[0].shape[0]
-    pieces = 1 if last else len(outs)
-    for place in range(pieces):
-        at = slice(place * rows, (place + 1) * rows)
+    first = 0
+    for out_ref in outs[:1] if last else outs:
+        rows = out_ref.shape[0]
+        at = slice(first, first + rows)
+        first += rows
         total = sum(ref[at, :width].astype(jnp.float32) for ref in refs)
         mean = merged(own, [ref[at, width:].astype(jnp.float32) for ref in refs])
         if last:
             outs[0][...] = total.astype(jnp.bfloat16)
             outs[1][...] = mean[:, :own].astype(jnp.bfloat16)
         else:
-            outs[place][:, :width] = total.astype(jnp.bfloat16)
-            outs[place][:, width:] = mean.astype(jnp.bfloat16)
-
-
-def summed(parts, pieces, width, own, last=False):
+            out_ref[:, :width] = total.astype(jnp.bfloat16)
+            out_ref[:, width:] = mean.astype(jnp.bfloat16)
+
+
+def summed(parts, sizes, width, own, last=False):
     rows, whole = parts[0].shape
     if last:
         shapes = [jax.ShapeDtypeStruct((rows, n), jnp.bfloat16) for n in (width, own)]
     else:
-        shapes = [jax.ShapeDtypeStruct((rows // pieces, whole), jnp.bfloat16)] * pieces
-    return call(
-        functools.partial(sum_kernel, len(parts), width, own, last),
-        shapes,
-        parts,
-        flops=rows * whole * len(parts),
-        nbytes=2 * rows * whole * (len(parts) + 1),
-    )
+        shapes = [jax.ShapeDtypeStruct((n, whole), jnp.bfloat16) for n in sizes]
+    return call(functools.partial(sum_kernel, len(parts), width, own, last), shapes, parts)
+
+
+def stack_kernel(*refs):
+    stacked = jnp.concatenate([ref[...].astype(jnp.float32) for ref in refs[:-1]], axis=0)
+    refs[-1][...] = stacked.astype(jnp.bfloat16)
+
+
+def stack(parts):
+    rows, width = parts[0].shape
+    return call(stack_kernel, jax.ShapeDtypeStruct((len(parts) * rows, width), jnp.bfloat16), parts)
+
+
+def gather(block, levels, *ready):
+    for stride, radix in reversed(levels):
+        arrived = {k: exchange(block, stride * k) for k in reversed(range(1, radix))}
+        block = stack([block] + [after(arrived[k], *ready) for k in range(1, radix)])
+    return block
+
+
+def scatter(pieces, levels, width, own):
+    stride, radix = levels[0]
+    parts = [pieces[0]] + [exchange(pieces[k], stride * k) for k in range(1, radix)]
+    if len(levels) == 1:
+        return parts
+    rows = parts[0].shape[0] // levels[1][1]
+    return scatter(summed(parts, [rows] * levels[1][1], width, own), levels[1:], width, own)
 
 
 def per_device(
@@ -312,42 +319,38 @@
     levels = levels_of(devices)
     own = query.shape[1] // devices
     extra = -(-2 * experts // LANES) * LANES
-    expert = (lax.axis_index("ffn") // 2).astype(jnp.int32)[None]
-    weights = in_hbm(w_gate, w_up, w_down)
-
-    gain = norm_gain[None]
     block = call(
         functools.partial(payload_kernel, experts),
         jax.ShapeDtypeStruct((rows_dev, width + extra), jnp.bfloat16),
-        in_hbm(tokens, gain, routes, gate_scores),
+        in_hbm(tokens, norm_gain[None], routes, gate_scores),
         in_specs=[HBM] * 4,
-        scratch=[pltpu.VMEM(a.shape, a.dtype) for a in (tokens, gain, routes, gate_scores)] + [fetched(4)],
-    )
-    for stride, radix in reversed(levels[1:]):
-        arrived = [exchange(block, stride * k) for k in reversed(range(1, radix))]
-        block = jnp.concatenate([block] + arrived[::-1], axis=0)
-    sums = attend(query, k_cache, v_cache, cache_len, levels)
-
-    stride, radix = levels[0]
-    chunks = {0: block}
+        scratch=[pltpu.VMEM(a.shape, a.dtype) for a in (tokens, norm_gain[None], routes, gate_scores)]
+        + [fetched(4)],
+    )
+    *sums, w_gate, w_up = attend(query, k_cache, v_cache, cache_len, levels, (w_gate, w_up))
+    (stride, radix), *outer = levels
+    corner = 3 * stride
+    chunks, ready = {}, [sums[0]]
+    if radix == 4:
+        across = exchange(block, corner)
+        ready.append(across)
+        chunks[3] = gather(across, outer)
+    chunks[0] = gather(block, outer, *ready)
     for k in range(1, min(radix, 3)):
-        chunks[k] = exchange(block, stride * k)
-    near, far = apply_expert(expert, [block], [exchange(block, 1)], [0], sums, weights)
-    for k in range(3, radix):
-        chunks[k] = exchange(after(block, near), stride * k)
-    (total,) = summed([near, exchange(far, 1)], 1, width, own)
-    parts = [total]
-    done = near
-    for group in ([1, 2], [3]) if radix == 4 else ([1],):
-        same = [after(chunks[k], done) for k in group]
-        near, far = apply_expert(expert, same, [exchange(s, 1) for s in same], group, sums, weights)
-        pieces = summed([near, exchange(far, 1)], len(group), width, own)
-        parts += [exchange(piece, stride * k) for piece, k in zip(pieces, group)]
-        done = near
-    for stride, radix in levels[1:]:
-        pieces = summed(parts, radix, width, own)
-        parts = [pieces[0]] + [exchange(pieces[k], stride * k) for k in range(1, radix)]
-    return tuple(summed(parts, 1, width, own, last=True))
+        chunks[k] = exchange(chunks[0], stride * k)
+    rows = chunks[0].shape[0]
+    cut = [rows // outer[0][1]] * outer[0][1]
+    near, far = apply_expert([chunks[k] for k in range(radix)], sums, (w_gate, w_up, w_down))
+    sizes = [rows] * min(radix, 3) + (cut if radix == 4 else [])
+    pieces = summed([near, exchange(far, 1)], sizes, width, own)
+    parts = [pieces[0]] + [exchange(pieces[k], stride * k) for k in range(1, min(radix, 3))]
+    if radix == 4:
+        corner_parts = scatter(pieces[3:], outer, width, own)
+    last = scatter(summed(parts, cut, width, own), outer, width, own)
+    if radix == 4:
+        (corner_sum,) = summed(corner_parts, [rows_dev], width, own)
+        last.append(exchange(corner_sum, corner))
+    return tuple(summed(last, [], width, own, last=True))
 
 
 def solution(mesh):

time: 69.9 us -> 59.6 us (0.85)
  waiting for transfers between devices: 28.2 us -> 18.2 us
  Pallas kernels: 20.8 us -> 12 us
  starting transfers between devices: 19.1 us -> 27.8 us
  other arithmetic: 0.75 us -> 0 us
    ppermute x19 -> x23, waiting for transfers between devices: 28.2 us -> 18.2 us  [exchange(): return lax.ppermute(value, 'ffn', [(i, i ^ distance) for i in range(size)])]
    pallas_call x10 -> x9, Pallas kernels: 20.8 us -> 12 us  [call(): pl.pallas_call(body, out_shape=out_shape, in_specs=in_specs or [VMEM] * l...]
    ppermute x19 -> x23, starting transfers between devices: 19.1 us -> 27.8 us  [exchange(): return lax.ppermute(value, 'ffn', [(i, i ^ distance) for i in range(size)])]
    concatenate x2 -> x0, other arithmetic: 0.75 us -> none  [the longest x1 0.73 us: attend(): info = jnp.concatenate([me[None], (me * seg_len)[None], cache_len])]
  transfers between devices with their start and end apart: 19 -> 23, of which waited for: 11 -> 12; matrix products, arithmetic and copies ran while one was open for 1% -> 0% of each run, Pallas kernels for 27% -> 8%
where the time goes in v3:
time: 59.6 us; the launch traced here: 59.5 us
  starting transfers between devices  27.8 us (47%)
  waiting for transfers between devices  18.2 us (31%)
  Pallas kernels  12 us (20%)
  between operations  0.74 us (1%)
  local copies, waits for them, and re-layouts  0.65 us (1%)
    ppermute x23, starting transfers between devices, exchange(): return lax.ppermute(value, 'ffn', [(i, i ^ distance) for i in range(size)])  27.8 us
    ppermute x23, waiting for transfers between devices, exchange(): return lax.ppermute(value, 'ffn', [(i, i ^ distance) for i in range(size)])  18.2 us
    pallas_call x9, Pallas kernels, call(): pl.pallas_call(body, out_shape=out_shape, in_specs=in_specs or [VMEM] * l...  12 us
  transfers between devices with their start and end apart: 23, of which 12 were waited for; matrix products, arithmetic and copies ran while one was open for 0% of the time, Pallas kernels for 8%

profile of v3, /device:TPU:0, one launch (start us, length us, event | category | flops | bytes accessed | tf_op | source)
XLA Modules:
  0.0 59.5 jit_solution(11815067857959193824)
XLA Ops:
  0.6 1.1 %shard_map.122.refs_0_ = bf16[8,4224]{1,0:T(8,128)(2,1)S(1)} custom-call(bf16[8,4096]{1,0:T(8,128)(2,1)} %tokens_hbm.1, f32[1,4096]{1,0:T(1,128)} %bitcast.7, s32[8,8]{1,0:T(8,128)} %routes_hbm.1, f32[8,8]{1,0:T(8,128)} %scores_hbm.1), custom_call_target="tpu_custom_call" | custom-call | flops 1 | bytes 1 | tf_op jit(solution)/shard_map/pallas_call | solution.py:45
  1.7 5.1 %collective-permute-start.3 = (bf16[8,4224]{1,0:T(8,128)(2,1)S(1)}, bf16[8,4224]{1,0:T(8,128)(2,1)S(1)}, u32[]{:S(2)}, u32[]{:S(2)}) collective-permute-start(bf16[8,4224]{1,0:T(8,128)(2,1)S(1)} %shard_map.122.refs_0_), channel_id=1, source_target_pairs={{0,24},{1,25},{2,26},{3,27},{4,28},{5,29},{6,30},{7,31},{8,16},{9,... | collective-permute-start | bytes 202760 | tf_op jit(solution)/shard_map/ppermute | solution.py:37
  6.8 0.0 collective-permute-start.2
  6.8 2.4 %collective-permute-start.1 = (bf16[8,4224]{1,0:T(8,128)(2,1)S(1)}, bf16[8,4224]{1,0:T(8,128)(2,1)S(1)}, u32[]{:S(2)}, u32[]{:S(2)}) collective-permute-start(bf16[8,4224]{1,0:T(8,128)(2,1)S(1)} %shard_map.122.refs_0_), channel_id=1, source_target_pairs={{0,6},{1,7},{2,4},{3,5},{4,2},{5,3},{6,0},{7,1},{8,14},{9,15},{10,... | collective-permute-start | bytes 202760 | tf_op jit(solution)/shard_map/ppermute | solution.py:37
  9.3 0.8 %collective-permute-start = (bf16[8,4224]{1,0:T(8,128)(2,1)S(1)}, bf16[8,4224]{1,0:T(8,128)(2,1)S(1)}, u32[]{:S(2)}, u32[]{:S(2)}) collective-permute-start(bf16[8,4224]{1,0:T(8,128)(2,1)S(1)} %shard_map.122.refs_0_), channel_id=1, source_target_pairs={{0,8},{1,9},{2,10},{3,11},{4,12},{5,13},{6,14},{7,15},{8,0},{9,1},... | collective-permute-start | bytes 202760 | tf_op jit(solution)/shard_map/ppermute | solution.py:37
  10.1 0.0 copy-start
  10.1 0.7 %copy-done = s32[8]{0:T(128)S(1)} copy-done((s32[8]{0:T(128)S(1)}, s32[8]{0:T(128)}, u32[]{:S(2)}) %copy-start) | copy-done | bytes 56
  10.7 4.1 %shard_map.123 = (bf16[128,384]{1,0:T(8,128)(2,1)S(1)}, bf16[128,384]{1,0:T(8,128)(2,1)S(1)}, bf16[4096,384]{1,0:T(8,128)(2,1)S(1)}, bf16[4096,384]{1,0:T(8,128)(2,1)S(1)}) custom-call(s32[8]{0:T(128)S(1)} %copy-done, bf16[512,128]{1,0:T(8,128)(2,1)} %bitcast.6, bf16[8,128,512]{2,1,0:T(8,128)(2,1)} %refs_1_.1, bf16[8,128,512]{2,1,0:T(8,128)(2,1)} %refs_2_.1, ...), custom_call_target="tpu_custom_call" | custom-call | flops 1000000000 | bytes 6291456 | tf_op jit(solution)/shard_map/pallas_call | solution.py:45
  14.8 0.0 collective-permute-done.3.refs_3_
  14.8 0.0 collective-permute-done.1.refs_0_
  14.9 0.0 collective-permute-done.2.refs_2_
  14.9 0.0 collective-permute-done.refs_1_
  14.9 0.6 collective-permute-start.5
  15.5 0.6 %collective-permute-start.4 = (bf16[32,4224]{1,0:T(8,128)(2,1)S(1)}, bf16[32,4224]{1,0:T(8,128)(2,1)S(1)}, u32[]{:S(2)}, u32[]{:S(2)}) collective-permute-start(bf16[32,4224]{1,0:T(8,128)(2,1)S(1)} %shard_map.124.refs_0_), channel_id=1, source_target_pairs={{0,2},{1,3},{2,0},{3,1},{4,6},{5,7},{6,4},{7,5},{8,10},{9,11},{10,... | collective-permute-start | bytes 811016 | tf_op jit(solution)/shard_map/ppermute | solution.py:37
  16.1 3.5 %collective-permute-start.8 = (bf16[8,4224]{1,0:T(8,128)(2,1)S(1)}, bf16[8,4224]{1,0:T(8,128)(2,1)S(1)}, u32[]{:S(2)}, u32[]{:S(2)}) collective-permute-start(bf16[8,4224]{1,0:T(8,128)(2,1)S(1)} %collective-permute-done.1.refs_0_), channel_id=1, source_target_pairs={{0,24},{1,25},{2,26},{3,27},{4,28},{5,29},{6,30},{7,31},{8,16},{9,... | collective-permute-start | bytes 202760 | tf_op jit(solution)/shard_map/ppermute | solution.py:37
  19.6 0.0 collective-permute-start.7
  19.6 0.8 %collective-permute-start.6 = (bf16[8,4224]{1,0:T(8,128)(2,1)S(1)}, bf16[8,4224]{1,0:T(8,128)(2,1)S(1)}, u32[]{:S(2)}, u32[]{:S(2)}) collective-permute-start(bf16[8,4224]{1,0:T(8,128)(2,1)S(1)} %collective-permute-done.1.refs_0_), channel_id=1, source_target_pairs={{0,8},{1,9},{2,10},{3,11},{4,12},{5,13},{6,14},{7,15},{8,0},{9,1},... | collective-permute-start | bytes 202760 | tf_op jit(solution)/shard_map/ppermute | solution.py:37
  20.5 1.8 %collective-permute-done.8.refs_3_ = bf16[8,4224]{1,0:T(8,128)(2,1)S(1)} collective-permute-done((bf16[8,4224]{1,0:T(8,128)(2,1)S(1)}, bf16[8,4224]{1,0:T(8,128)(2,1)S(1)}, u32[]{:S(2)}, u32[]{:S(2)}) %collective-permute-start.8) | collective-permute-done | bytes 67616 | tf_op jit(solution)/shard_map/ppermute | solution.py:37
  22.3 2.5 %collective-permute-done.7.refs_2_ = bf16[8,4224]{1,0:T(8,128)(2,1)S(1)} collective-permute-done((bf16[8,4224]{1,0:T(8,128)(2,1)S(1)}, bf16[8,4224]{1,0:T(8,128)(2,1)S(1)}, u32[]{:S(2)}, u32[]{:S(2)}) %collective-permute-start.7) | collective-permute-done | bytes 67616 | tf_op jit(solution)/shard_map/ppermute | solution.py:37
  24.8 0.0 collective-permute-done.6.refs_1_
  24.8 0.0 collective-permute-start.9
  24.8 0.6 collective-permute-start.12
  25.4 0.0 collective-permute-done.5.refs_2_
  25.4 0.1 collective-permute-start.11
  25.5 0.0 collective-permute-done.4.refs_1_
  25.5 0.4 collective-permute-start.10
  25.9 0.4 collective-permute-done.9.refs_4_
  26.4 0.4 collective-permute-done.12.refs_7_
  26.7 0.4 collective-permute-done.11.refs_6_
  27.1 0.4 collective-permute-done.10.refs_5_
  27.5 5.2 %shard_map.126 = (bf16[128,4480]{1,0:T(8,128)(2,1)S(1)}, bf16[128,4480]{1,0:T(8,128)(2,1)S(1)}) custom-call(bf16[32,4224]{1,0:T(8,128)(2,1)S(1)} %shard_map.124.refs_0_, bf16[32,4224]{1,0:T(8,128)(2,1)S(1)} %collective-permute-done.4.refs_1_, bf16[32,4224]{1,0:T(8,128)(2,1)S(1)} %collective-permute-done.5.refs_2_, bf16[32,4224]{1,0:T(8,128)(2,1)S(1)} %shard_map.125.refs_3_, ...), custom_call_target="tpu_custom_call" | custom-call | flops 2415919104 | bytes 9437184 | tf_op jit(solution)/shard_map/pallas_call | solution.py:45
  32.7 0.3 collective-permute-start.13
  33.0 2.6 %collective-permute-done.13.refs_1_ = bf16[128,4480]{1,0:T(8,128)(2,1)S(1)} collective-permute-done((bf16[128,4480]{1,0:T(8,128)(2,1)S(1)}, bf16[128,4480]{1,0:T(8,128)(2,1)S(1)}, u32[]{:S(2)}, u32[]{:S(2)}) %collective-permute-start.13) | collective-permute-done | bytes 1146912 | tf_op jit(solution)/shard_map/ppermute | solution.py:37
  35.6 0.6 shard_map.127
  36.1 1.6 %collective-permute-start.14 = (bf16[32,4480]{1,0:T(8,128)(2,1)S(1)}, bf16[32,4480]{1,0:T(8,128)(2,1)S(1)}, u32[]{:S(2)}, u32[]{:S(2)}) collective-permute-start(bf16[32,4480]{1,0:T(8,128)(2,1)S(1)} %get-tuple-element.32), channel_id=1, source_target_pairs={{0,2},{1,3},{2,0},{3,1},{4,6},{5,7},{6,4},{7,5},{8,10},{9,11},{10,... | collective-permute-start | bytes 860168 | tf_op jit(solution)/shard_map/ppermute | solution.py:37
  37.7 1.5 %collective-permute-start.15 = (bf16[32,4480]{1,0:T(8,128)(2,1)S(1)}, bf16[32,4480]{1,0:T(8,128)(2,1)S(1)}, u32[]{:S(2)}, u32[]{:S(2)}) collective-permute-start(bf16[32,4480]{1,0:T(8,128)(2,1)S(1)} %get-tuple-element.33), channel_id=1, source_target_pairs={{0,4},{1,5},{2,6},{3,7},{4,0},{5,1},{6,2},{7,3},{8,12},{9,13},{10,... | collective-permute-start | bytes 860168 | tf_op jit(solution)/shard_map/ppermute | solution.py:37
  39.2 0.6 collective-permute-start.19
  39.8 1.7 %collective-permute-start.20 = (bf16[8,4480]{1,0:T(8,128)(2,1)S(1)}, bf16[8,4480]{1,0:T(8,128)(2,1)S(1)}, u32[]{:S(2)}, u32[]{:S(2)}) collective-permute-start(bf16[8,4480]{1,0:T(8,128)(2,1)S(1)} %get-tuple-element.40), channel_id=1, source_target_pairs={{0,16},{1,17},{2,18},{3,19},{4,20},{5,21},{6,22},{7,23},{8,24},{9,... | collective-permute-start | bytes 215048 | tf_op jit(solution)/shard_map/ppermute | solution.py:37
  41.5 2.1 %collective-permute-start.21 = (bf16[8,4480]{1,0:T(8,128)(2,1)S(1)}, bf16[8,4480]{1,0:T(8,128)(2,1)S(1)}, u32[]{:S(2)}, u32[]{:S(2)}) collective-permute-start(bf16[8,4480]{1,0:T(8,128)(2,1)S(1)} %get-tuple-element.41), channel_id=1, source_target_pairs={{0,24},{1,25},{2,26},{3,27},{4,28},{5,29},{6,30},{7,31},{8,16},{9,... | collective-permute-start | bytes 215048 | tf_op jit(solution)/shard_map/ppermute | solution.py:37
  43.6 0.6 collective-permute-done.19.refs_1_
  44.2 4.1 %collective-permute-done.20.refs_2_ = bf16[8,4480]{1,0:T(8,128)(2,1)S(1)} collective-permute-done((bf16[8,4480]{1,0:T(8,128)(2,1)S(1)}, bf16[8,4480]{1,0:T(8,128)(2,1)S(1)}, u32[]{:S(2)}, u32[]{:S(2)}) %collective-permute-start.20) | collective-permute-done | bytes 71712 | tf_op jit(solution)/shard_map/ppermute | solution.py:37
  48.3 0.0 collective-permute-done.21.refs_3_
  48.3 0.1 shard_map.129
  48.4 0.6 %collective-permute-start.22 = (bf16[8,4480]{1,0:T(8,128)(2,1)S(1)}, bf16[8,4480]{1,0:T(8,128)(2,1)S(1)}, u32[]{:S(2)}, u32[]{:S(2)}) collective-permute-start(bf16[8,4480]{1,0:T(8,128)(2,1)S(1)} %shard_map.129), channel_id=1, source_target_pairs={{0,6},{1,7},{2,4},{3,5},{4,2},{5,3},{6,0},{7,1},{8,14},{9,15},{10,... | collective-permute-start | bytes 215048 | tf_op jit(solution)/shard_map/ppermute | solution.py:37
  49.0 0.0 collective-permute-done.14.refs_1_
  49.0 0.0 collective-permute-done.15.refs_2_
  49.0 0.2 shard_map.128
  49.2 1.4 %collective-permute-start.16 = (bf16[8,4480]{1,0:T(8,128)(2,1)S(1)}, bf16[8,4480]{1,0:T(8,128)(2,1)S(1)}, u32[]{:S(2)}, u32[]{:S(2)}) collective-permute-start(bf16[8,4480]{1,0:T(8,128)(2,1)S(1)} %get-tuple-element.35), channel_id=1, source_target_pairs={{0,8},{1,9},{2,10},{3,11},{4,12},{5,13},{6,14},{7,15},{8,0},{9,1},... | collective-permute-start | bytes 215048 | tf_op jit(solution)/shard_map/ppermute | solution.py:37
  50.6 1.9 %collective-permute-start.17 = (bf16[8,4480]{1,0:T(8,128)(2,1)S(1)}, bf16[8,4480]{1,0:T(8,128)(2,1)S(1)}, u32[]{:S(2)}, u32[]{:S(2)}) collective-permute-start(bf16[8,4480]{1,0:T(8,128)(2,1)S(1)} %get-tuple-element.36), channel_id=1, source_target_pairs={{0,16},{1,17},{2,18},{3,19},{4,20},{5,21},{6,22},{7,23},{8,24},{9,... | collective-permute-start | bytes 215048 | tf_op jit(solution)/shard_map/ppermute | solution.py:37
  52.5 1.2 %collective-permute-start.18 = (bf16[8,4480]{1,0:T(8,128)(2,1)S(1)}, bf16[8,4480]{1,0:T(8,128)(2,1)S(1)}, u32[]{:S(2)}, u32[]{:S(2)}) collective-permute-start(bf16[8,4480]{1,0:T(8,128)(2,1)S(1)} %get-tuple-element.37), channel_id=1, source_target_pairs={{0,24},{1,25},{2,26},{3,27},{4,28},{5,29},{6,30},{7,31},{8,16},{9,... | collective-permute-start | bytes 215048 | tf_op jit(solution)/shard_map/ppermute | solution.py:37
  53.7 0.0 collective-permute-done.22.refs_4_
  53.7 0.5 collective-permute-done.16.refs_1_
  54.2 3.4 %collective-permute-done.17.refs_2_ = bf16[8,4480]{1,0:T(8,128)(2,1)S(1)} collective-permute-done((bf16[8,4480]{1,0:T(8,128)(2,1)S(1)}, bf16[8,4480]{1,0:T(8,128)(2,1)S(1)}, u32[]{:S(2)}, u32[]{:S(2)}) %collective-permute-start.17) | collective-permute-done | bytes 71712 | tf_op jit(solution)/shard_map/ppermute | solution.py:37
  57.6 1.2 %collective-permute-done.18.refs_3_ = bf16[8,4480]{1,0:T(8,128)(2,1)S(1)} collective-permute-done((bf16[8,4480]{1,0:T(8,128)(2,1)S(1)}, bf16[8,4480]{1,0:T(8,128)(2,1)S(1)}, u32[]{:S(2)}, u32[]{:S(2)}) %collective-permute-start.18) | collective-permute-done | bytes 71712 | tf_op jit(solution)/shard_map/ppermute | solution.py:37
  58.7 0.7 %shard_map.130 = (bf16[8,4096]{1,0:T(8,128)(2,1)}, bf16[8,256]{1,0:T(8,128)(2,1)}) custom-call(bf16[8,4480]{1,0:T(8,128)(2,1)S(1)} %get-tuple-element.34.refs_0_, bf16[8,4480]{1,0:T(8,128)(2,1)S(1)} %collective-permute-done.16.refs_1_, bf16[8,4480]{1,0:T(8,128)(2,1)S(1)} %collective-permute-done.17.refs_2_, ...), custom_call_target="tpu_custom_call" | custom-call | flops 1 | bytes 1 | tf_op jit(solution)/shard_map/pallas_call | solution.py:45
  (2 shorter events, 0.0 us)
Async XLA Ops:
  1.7 13.1 %collective-permute-start.3 = (bf16[8,4224]{1,0:T(8,128)(2,1)S(1)}, bf16[8,4224]{1,0:T(8,128)(2,1)S(1)}, u32[]{:S(2)}, u32[]{:S(2)}) collective-permute-start(bf16[8,4224]{1,0:T(8,128)(2,1)S(1)} %shard_map.122.refs_0_), channel_id=1, source_target_pairs={{0,24},{1,25},{2,26},{3,27},{4,28},{5,29},{6,30},{7,31},{8,16},{9,... | collective-permute-start | bytes 202760 | tf_op jit(solution)/shard_map/ppermute | solution.py:37
  6.8 8.0 %collective-permute-start.2 = (bf16[8,4224]{1,0:T(8,128)(2,1)S(1)}, bf16[8,4224]{1,0:T(8,128)(2,1)S(1)}, u32[]{:S(2)}, u32[]{:S(2)}) collective-permute-start(bf16[8,4224]{1,0:T(8,128)(2,1)S(1)} %shard_map.122.refs_0_), channel_id=1, source_target_pairs={{0,16},{1,17},{2,18},{3,19},{4,20},{5,21},{6,22},{7,23},{8,24},{9,... | collective-permute-start | bytes 202760 | tf_op jit(solution)/shard_map/ppermute | solution.py:37
  6.8 8.0 %collective-permute-start.1 = (bf16[8,4224]{1,0:T(8,128)(2,1)S(1)}, bf16[8,4224]{1,0:T(8,128)(2,1)S(1)}, u32[]{:S(2)}, u32[]{:S(2)}) collective-permute-start(bf16[8,4224]{1,0:T(8,128)(2,1)S(1)} %shard_map.122.refs_0_), channel_id=1, source_target_pairs={{0,6},{1,7},{2,4},{3,5},{4,2},{5,3},{6,0},{7,1},{8,14},{9,15},{10,... | collective-permute-start | bytes 202760 | tf_op jit(solution)/shard_map/ppermute | solution.py:37
  9.3 5.6 %collective-permute-start = (bf16[8,4224]{1,0:T(8,128)(2,1)S(1)}, bf16[8,4224]{1,0:T(8,128)(2,1)S(1)}, u32[]{:S(2)}, u32[]{:S(2)}) collective-permute-start(bf16[8,4224]{1,0:T(8,128)(2,1)S(1)} %shard_map.122.refs_0_), channel_id=1, source_target_pairs={{0,8},{1,9},{2,10},{3,11},{4,12},{5,13},{6,14},{7,15},{8,0},{9,1},... | collective-permute-start | bytes 202760 | tf_op jit(solution)/shard_map/ppermute | solution.py:37
  10.1 0.7 %copy-start = (s32[8]{0:T(128)S(1)}, s32[8]{0:T(128)}, u32[]{:S(2)}) copy-start(s32[8]{0:T(128)} %length_ref.1) | copy-start | bytes 100
  14.9 10.5 %collective-permute-start.5 = (bf16[32,4224]{1,0:T(8,128)(2,1)S(1)}, bf16[32,4224]{1,0:T(8,128)(2,1)S(1)}, u32[]{:S(2)}, u32[]{:S(2)}) collective-permute-start(bf16[32,4224]{1,0:T(8,128)(2,1)S(1)} %shard_map.124.refs_0_), channel_id=1, source_target_pairs={{0,4},{1,5},{2,6},{3,7},{4,0},{5,1},{6,2},{7,3},{8,12},{9,13},{10,... | collective-permute-start | bytes 811016 | tf_op jit(solution)/shard_map/ppermute | solution.py:37
  15.5 10.0 %collective-permute-start.4 = (bf16[32,4224]{1,0:T(8,128)(2,1)S(1)}, bf16[32,4224]{1,0:T(8,128)(2,1)S(1)}, u32[]{:S(2)}, u32[]{:S(2)}) collective-permute-start(bf16[32,4224]{1,0:T(8,128)(2,1)S(1)} %shard_map.124.refs_0_), channel_id=1, source_target_pairs={{0,2},{1,3},{2,0},{3,1},{4,6},{5,7},{6,4},{7,5},{8,10},{9,11},{10,... | collective-permute-start | bytes 811016 | tf_op jit(solution)/shard_map/ppermute | solution.py:37
  16.1 6.2 %collective-permute-start.8 = (bf16[8,4224]{1,0:T(8,128)(2,1)S(1)}, bf16[8,4224]{1,0:T(8,128)(2,1)S(1)}, u32[]{:S(2)}, u32[]{:S(2)}) collective-permute-start(bf16[8,4224]{1,0:T(8,128)(2,1)S(1)} %collective-permute-done.1.refs_0_), channel_id=1, source_target_pairs={{0,24},{1,25},{2,26},{3,27},{4,28},{5,29},{6,30},{7,31},{8,16},{9,... | collective-permute-start | bytes 202760 | tf_op jit(solution)/shard_map/ppermute | solution.py:37
  19.6 5.2 %collective-permute-start.7 = (bf16[8,4224]{1,0:T(8,128)(2,1)S(1)}, bf16[8,4224]{1,0:T(8,128)(2,1)S(1)}, u32[]{:S(2)}, u32[]{:S(2)}) collective-permute-start(bf16[8,4224]{1,0:T(8,128)(2,1)S(1)} %collective-permute-done.1.refs_0_), channel_id=1, source_target_pairs={{0,16},{1,17},{2,18},{3,19},{4,20},{5,21},{6,22},{7,23},{8,24},{9,... | collective-permute-start | bytes 202760 | tf_op jit(solution)/shard_map/ppermute | solution.py:37
  19.6 5.2 %collective-permute-start.6 = (bf16[8,4224]{1,0:T(8,128)(2,1)S(1)}, bf16[8,4224]{1,0:T(8,128)(2,1)S(1)}, u32[]{:S(2)}, u32[]{:S(2)}) collective-permute-start(bf16[8,4224]{1,0:T(8,128)(2,1)S(1)} %collective-permute-done.1.refs_0_), channel_id=1, source_target_pairs={{0,8},{1,9},{2,10},{3,11},{4,12},{5,13},{6,14},{7,15},{8,0},{9,1},... | collective-permute-start | bytes 202760 | tf_op jit(solution)/shard_map/ppermute | solution.py:37
  24.8 1.5 %collective-permute-start.9 = (bf16[32,4224]{1,0:T(8,128)(2,1)S(1)}, bf16[32,4224]{1,0:T(8,128)(2,1)S(1)}, u32[]{:S(2)}, u32[]{:S(2)}) collective-permute-start(bf16[32,4224]{1,0:T(8,128)(2,1)S(1)} %shard_map.124.refs_0_), channel_id=1, source_target_pairs={{0,1},{1,0},{2,3},{3,2},{4,5},{5,4},{6,7},{7,6},{8,9},{9,8},{10,11... | collective-permute-start | bytes 811016 | tf_op jit(solution)/shard_map/ppermute | solution.py:37
  24.8 1.9 %collective-permute-start.12 = (bf16[32,4224]{1,0:T(8,128)(2,1)S(1)}, bf16[32,4224]{1,0:T(8,128)(2,1)S(1)}, u32[]{:S(2)}, u32[]{:S(2)}) collective-permute-start(bf16[32,4224]{1,0:T(8,128)(2,1)S(1)} %shard_map.125.refs_3_), channel_id=1, source_target_pairs={{0,1},{1,0},{2,3},{3,2},{4,5},{5,4},{6,7},{7,6},{8,9},{9,8},{10,11... | collective-permute-start | bytes 811016 | tf_op jit(solution)/shard_map/ppermute | solution.py:37
  25.4 1.7 %collective-permute-start.11 = (bf16[32,4224]{1,0:T(8,128)(2,1)S(1)}, bf16[32,4224]{1,0:T(8,128)(2,1)S(1)}, u32[]{:S(2)}, u32[]{:S(2)}) collective-permute-start(bf16[32,4224]{1,0:T(8,128)(2,1)S(1)} %collective-permute-done.5.refs_2_), channel_id=1, source_target_pairs={{0,1},{1,0},{2,3},{3,2},{4,5},{5,4},{6,7},{7,6},{8,9},{9,8},{10,11... | collective-permute-start | bytes 811016 | tf_op jit(solution)/shard_map/ppermute | solution.py:37
  25.5 2.0 %collective-permute-start.10 = (bf16[32,4224]{1,0:T(8,128)(2,1)S(1)}, bf16[32,4224]{1,0:T(8,128)(2,1)S(1)}, u32[]{:S(2)}, u32[]{:S(2)}) collective-permute-start(bf16[32,4224]{1,0:T(8,128)(2,1)S(1)} %collective-permute-done.4.refs_1_), channel_id=1, source_target_pairs={{0,1},{1,0},{2,3},{3,2},{4,5},{5,4},{6,7},{7,6},{8,9},{9,8},{10,11... | collective-permute-start | bytes 811016 | tf_op jit(solution)/shard_map/ppermute | solution.py:37
  32.7 2.9 %collective-permute-start.13 = (bf16[128,4480]{1,0:T(8,128)(2,1)S(1)}, bf16[128,4480]{1,0:T(8,128)(2,1)S(1)}, u32[]{:S(2)}, u32[]{:S(2)}) collective-permute-start(bf16[128,4480]{1,0:T(8,128)(2,1)S(1)} %get-tuple-element.30), channel_id=1, source_target_pairs={{0,1},{1,0},{2,3},{3,2},{4,5},{5,4},{6,7},{7,6},{8,9},{9,8},{10,11... | collective-permute-start | bytes 3440648 | tf_op jit(solution)/shard_map/ppermute | solution.py:37
  36.1 12.9 %collective-permute-start.14 = (bf16[32,4480]{1,0:T(8,128)(2,1)S(1)}, bf16[32,4480]{1,0:T(8,128)(2,1)S(1)}, u32[]{:S(2)}, u32[]{:S(2)}) collective-permute-start(bf16[32,4480]{1,0:T(8,128)(2,1)S(1)} %get-tuple-element.32), channel_id=1, source_target_pairs={{0,2},{1,3},{2,0},{3,1},{4,6},{5,7},{6,4},{7,5},{8,10},{9,11},{10,... | collective-permute-start | bytes 860168 | tf_op jit(solution)/shard_map/ppermute | solution.py:37
  37.7 11.3 %collective-permute-start.15 = (bf16[32,4480]{1,0:T(8,128)(2,1)S(1)}, bf16[32,4480]{1,0:T(8,128)(2,1)S(1)}, u32[]{:S(2)}, u32[]{:S(2)}) collective-permute-start(bf16[32,4480]{1,0:T(8,128)(2,1)S(1)} %get-tuple-element.33), channel_id=1, source_target_pairs={{0,4},{1,5},{2,6},{3,7},{4,0},{5,1},{6,2},{7,3},{8,12},{9,13},{10,... | collective-permute-start | bytes 860168 | tf_op jit(solution)/shard_map/ppermute | solution.py:37
  39.2 5.0 %collective-permute-start.19 = (bf16[8,4480]{1,0:T(8,128)(2,1)S(1)}, bf16[8,4480]{1,0:T(8,128)(2,1)S(1)}, u32[]{:S(2)}, u32[]{:S(2)}) collective-permute-start(bf16[8,4480]{1,0:T(8,128)(2,1)S(1)} %get-tuple-element.39), channel_id=1, source_target_pairs={{0,8},{1,9},{2,10},{3,11},{4,12},{5,13},{6,14},{7,15},{8,0},{9,1},... | collective-permute-start | bytes 215048 | tf_op jit(solution)/shard_map/ppermute | solution.py:37
  39.8 8.5 %collective-permute-start.20 = (bf16[8,4480]{1,0:T(8,128)(2,1)S(1)}, bf16[8,4480]{1,0:T(8,128)(2,1)S(1)}, u32[]{:S(2)}, u32[]{:S(2)}) collective-permute-start(bf16[8,4480]{1,0:T(8,128)(2,1)S(1)} %get-tuple-element.40), channel_id=1, source_target_pairs={{0,16},{1,17},{2,18},{3,19},{4,20},{5,21},{6,22},{7,23},{8,24},{9,... | collective-permute-start | bytes 215048 | tf_op jit(solution)/shard_map/ppermute | solution.py:37
  41.5 6.8 %collective-permute-start.21 = (bf16[8,4480]{1,0:T(8,128)(2,1)S(1)}, bf16[8,4480]{1,0:T(8,128)(2,1)S(1)}, u32[]{:S(2)}, u32[]{:S(2)}) collective-permute-start(bf16[8,4480]{1,0:T(8,128)(2,1)S(1)} %get-tuple-element.41), channel_id=1, source_target_pairs={{0,24},{1,25},{2,26},{3,27},{4,28},{5,29},{6,30},{7,31},{8,16},{9,... | collective-permute-start | bytes 215048 | tf_op jit(solution)/shard_map/ppermute | solution.py:37
  48.4 5.3 %collective-permute-start.22 = (bf16[8,4480]{1,0:T(8,128)(2,1)S(1)}, bf16[8,4480]{1,0:T(8,128)(2,1)S(1)}, u32[]{:S(2)}, u32[]{:S(2)}) collective-permute-start(bf16[8,4480]{1,0:T(8,128)(2,1)S(1)} %shard_map.129), channel_id=1, source_target_pairs={{0,6},{1,7},{2,4},{3,5},{4,2},{5,3},{6,0},{7,1},{8,14},{9,15},{10,... | collective-permute-start | bytes 215048 | tf_op jit(solution)/shard_map/ppermute | solution.py:37
  49.2 4.9 %collective-permute-start.16 = (bf16[8,4480]{1,0:T(8,128)(2,1)S(1)}, bf16[8,4480]{1,0:T(8,128)(2,1)S(1)}, u32[]{:S(2)}, u32[]{:S(2)}) collective-permute-start(bf16[8,4480]{1,0:T(8,128)(2,1)S(1)} %get-tuple-element.35), channel_id=1, source_target_pairs={{0,8},{1,9},{2,10},{3,11},{4,12},{5,13},{6,14},{7,15},{8,0},{9,1},... | collective-permute-start | bytes 215048 | tf_op jit(solution)/shard_map/ppermute | solution.py:37
  50.6 6.9 %collective-permute-start.17 = (bf16[8,4480]{1,0:T(8,128)(2,1)S(1)}, bf16[8,4480]{1,0:T(8,128)(2,1)S(1)}, u32[]{:S(2)}, u32[]{:S(2)}) collective-permute-start(bf16[8,4480]{1,0:T(8,128)(2,1)S(1)} %get-tuple-element.36), channel_id=1, source_target_pairs={{0,16},{1,17},{2,18},{3,19},{4,20},{5,21},{6,22},{7,23},{8,24},{9,... | collective-permute-start | bytes 215048 | tf_op jit(solution)/shard_map/ppermute | solution.py:37
  52.5 6.2 %collective-permute-start.18 = (bf16[8,4480]{1,0:T(8,128)(2,1)S(1)}, bf16[8,4480]{1,0:T(8,128)(2,1)S(1)}, u32[]{:S(2)}, u32[]{:S(2)}) collective-permute-start(bf16[8,4480]{1,0:T(8,128)(2,1)S(1)} %get-tuple-element.37), channel_id=1, source_target_pairs={{0,24},{1,25},{2,26},{3,27},{4,28},{5,29},{6,30},{7,31},{8,16},{9,... | collective-permute-start | bytes 215048 | tf_op jit(solution)/shard_map/ppermute | solution.py:37

commit v4 on v3

--- a/solution.py
+++ b/solution.py
@@ -192,50 +192,62 @@
             pltpu.VMEM((devices, rows, extra), jnp.float32),
             fetched(5),
         ],
-        flops=10**9,
+        flops=4 * 10**9,
         nbytes=2 * sum(w.size for w in weights),
     )
 
 
-def expert_kernel(experts, count, *refs):
+def expert_kernel(experts, chunks, load, *refs):
+    count = len(chunks)
     same_refs, other_refs, refs = refs[:count], refs[count : 2 * count], refs[2 * count :]
-    near_ref, far_ref, gate_ref, up_ref, down_hbm, own_out, far_out, down_ref, sems = refs
+    near_ref, far_ref, gate_ref, up_ref, down_ref, own_out, far_out = refs[:7]
     width = gate_ref.shape[0]
     rows = same_refs[0].shape[0]
-    step = width // sems.shape[0]
+    step = 1024
     cuts = [pl.ds(first, step) for first in range(0, width, step)]
-    copies = fetch([down_hbm.at[:, at] for at in cuts], [down_ref.at[:, at] for at in cuts], sems)
+    copies = [None] * len(cuts)
+    if load:
+        down_hbm, down_ref, sems = down_ref, refs[7], refs[8]
+        copies = fetch([down_hbm.at[:, at] for at in cuts], [down_ref.at[:, at] for at in cuts], sems)
     coded = jnp.concatenate([r[:, width:] for r in same_refs + other_refs], axis=0).astype(jnp.float32)
     lane = lax.broadcasted_iota(jnp.int32, coded.shape, 1)
     mine = (lane < 2 * experts) & (lane % experts == lax.axis_index("ffn") // 2)
     share = jnp.sum(jnp.where(mine, coded, 0.0), axis=-1, keepdims=True)
-    own_out[:, width:] = near_ref[...]
-    far_out[:, width:] = far_ref[...]
+    for place, chunk in enumerate(chunks):
+        at, here = slice(place * rows, (place + 1) * rows), slice(chunk * rows, (chunk + 1) * rows)
+        own_out[at, width:] = near_ref[here]
+        far_out[at, width:] = far_ref[here]
     stacked = jnp.concatenate([r[:, :width] for r in same_refs + other_refs], axis=0)
     gate_part = jnp.dot(stacked, gate_ref[...], preferred_element_type=jnp.float32)
     up_part = jnp.dot(stacked, up_ref[...], preferred_element_type=jnp.float32)
     hidden = (gate_part / (1.0 + jnp.exp(-gate_part)) * up_part).astype(jnp.bfloat16)
     for copy, at in zip(copies, cuts):
-        copy.wait()
+        if load:
+            copy.wait()
         part = jnp.dot(hidden, down_ref[:, at], preferred_element_type=jnp.float32)
         part = (part * share).astype(jnp.bfloat16)
         own_out[:, at] = part[: count * rows]
         far_out[:, at] = part[count * rows :]
 
 
-def apply_expert(same, sums, weights):
+def apply_expert(same, chunks, sums, weights, load=False):
     rows = same[0].shape[0]
     width, hidden = weights[0].shape
     devices = lax.axis_size("ffn")
-    shape = jax.ShapeDtypeStruct((len(same) * rows, width + sums[0].shape[1]), jnp.bfloat16)
-    args = [*same, *[exchange(s, 1) for s in same], *sums, *weights[:2], *in_hbm(weights[2])]
+    outs = [jax.ShapeDtypeStruct((len(same) * rows, width + sums[0].shape[1]), jnp.bfloat16)] * 2
+    args = [*same, *[exchange(s, 1) for s in same], *sums, *weights]
+    in_specs, scratch = [VMEM] * len(args), []
+    if load:
+        args[-1:], in_specs[-1] = in_hbm(args[-1]), HBM
+        outs.append(pltpu.VMEM(weights[2].shape, weights[2].dtype))
+        scratch.append(fetched(width // 1024))
     return call(
-        functools.partial(expert_kernel, devices // 2, len(same)),
-        [shape, shape],
+        functools.partial(expert_kernel, devices // 2, chunks, load),
+        outs,
         args,
-        in_specs=[VMEM] * (2 * len(same) + 4) + [HBM],
-        scratch=[pltpu.VMEM(weights[2].shape, weights[2].dtype), fetched(4)],
-        flops=4 * len(same) * rows * width * hidden * 3,
+        in_specs=in_specs,
+        scratch=scratch,
+        flops=4 * 10**9,
         nbytes=2 * 3 * width * hidden,
         mib=8 + sum(2 * a.size for a in args) // 2**20,
     )
@@ -294,16 +306,20 @@
     return call(stack_kernel, jax.ShapeDtypeStruct((len(parts) * rows, width), jnp.bfloat16), parts)
 
 
+def start_order(radix):
+    return [2, 3, 1] if radix == 4 else [1]
+
+
 def gather(block, levels, *ready):
     for stride, radix in reversed(levels):
-        arrived = {k: exchange(block, stride * k) for k in reversed(range(1, radix))}
+        arrived = {k: exchange(block, stride * k) for k in start_order(radix)}
         block = stack([block] + [after(arrived[k], *ready) for k in range(1, radix)])
     return block
 
 
 def scatter(pieces, levels, width, own):
     stride, radix = levels[0]
-    parts = [pieces[0]] + [exchange(pieces[k], stride * k) for k in range(1, radix)]
+    parts = [pieces[0]] + [exchange(pieces[k], stride * k) for k in start_order(radix)]
     if len(levels) == 1:
         return parts
     rows = parts[0].shape[0] // levels[1][1]
@@ -330,24 +346,36 @@
     *sums, w_gate, w_up = attend(query, k_cache, v_cache, cache_len, levels, (w_gate, w_up))
     (stride, radix), *outer = levels
     corner = 3 * stride
-    chunks, ready = {}, [sums[0]]
-    if radix == 4:
-        across = exchange(block, corner)
-        ready.append(across)
-        chunks[3] = gather(across, outer)
-    chunks[0] = gather(block, outer, *ready)
-    for k in range(1, min(radix, 3)):
-        chunks[k] = exchange(chunks[0], stride * k)
-    rows = chunks[0].shape[0]
+    weights = (w_gate, w_up, w_down)
+    rows = rows_dev * (devices // (2 * radix))
     cut = [rows // outer[0][1]] * outer[0][1]
-    near, far = apply_expert([chunks[k] for k in range(radix)], sums, (w_gate, w_up, w_down))
-    sizes = [rows] * min(radix, 3) + (cut if radix == 4 else [])
-    pieces = summed([near, exchange(far, 1)], sizes, width, own)
-    parts = [pieces[0]] + [exchange(pieces[k], stride * k) for k in range(1, min(radix, 3))]
-    if radix == 4:
-        corner_parts = scatter(pieces[3:], outer, width, own)
-    last = scatter(summed(parts, cut, width, own), outer, width, own)
-    if radix == 4:
+    across = [exchange(block, corner)] if radix == 4 else []
+    base = gather(block, outer, sums[0], *across)
+    sides = [1, 2] if radix == 4 else [1]
+    chunks = [exchange(base, stride * k) for k in sides]
+
+    near, far, w_down = apply_expert([base], [0], sums, weights, load=True)
+    weights = (w_gate, w_up, w_down)
+    ready = [near]
+    if across:
+        last_chunk = gather(across[0], outer, near)
+        ready.append(last_chunk)
+    chunks = [after(chunk, *ready) for chunk in chunks]
+    own_near, own_far = near, far
+    near, far = apply_expert(chunks, sides, sums, weights)
+    own_far = after(own_far, near)
+    if across:
+        corner_near, corner_far = apply_expert([last_chunk], [3], sums, weights)
+    (total,) = summed([own_near, exchange(own_far, 1)], [rows], width, own)
+    pieces = summed([near, exchange(far, 1)], [rows] * len(sides), width, own)
+    parts = [total] + [exchange(piece, stride * k) for piece, k in zip(pieces, sides)]
+    if across:
+        corner_pieces = summed([corner_near, exchange(corner_far, 1)], cut, width, own)
+        corner_parts = scatter(corner_pieces, outer, width, own)
+    pieces = summed(parts, cut, width, own)
+    last = scatter(pieces, outer, width, own)
+    if across:
+        corner_parts = [after(part, pieces[0]) for part in corner_parts]
         (corner_sum,) = summed(corner_parts, [rows_dev], width, own)
         last.append(exchange(corner_sum, corner))
     return tuple(summed(last, [], width, own, last=True))

time: 59.6 us -> 55.5 us (0.931)
  waiting for transfers between devices: 18.2 us -> 14.1 us
  Pallas kernels: 12 us -> 13.7 us
  starting transfers between devices: 27.8 us -> 26.1 us
    ppermute x23 -> x25, waiting for transfers between devices: 18.2 us -> 14.1 us  [exchange(): return lax.ppermute(value, 'ffn', [(i, i ^ distance) for i in range(size)])]
    ppermute x23 -> x25, starting transfers between devices: 27.8 us -> 26.1 us  [exchange(): return lax.ppermute(value, 'ffn', [(i, i ^ distance) for i in range(size)])]
    pallas_call x9 -> x13, Pallas kernels: 12 us -> 13.7 us  [call(): pl.pallas_call(body, out_shape=out_shape, in_specs=in_specs or [VMEM] * l...]
  transfers between devices with their start and end apart: 23 -> 25, of which waited for: 12 -> 10; matrix products, arithmetic and copies ran while one was open for 0% -> 0% of each run, Pallas kernels for 8% -> 21%
where the time goes in v4:
time: 55.5 us; the launch traced here: 55.3 us
  starting transfers between devices  26.1 us (47%)
  waiting for transfers between devices  14.1 us (25%)
  Pallas kernels  13.7 us (25%)
  between operations  0.81 us (1%)
  local copies, waits for them, and re-layouts  0.65 us (1%)
    ppermute x25, starting transfers between devices, exchange(): return lax.ppermute(value, 'ffn', [(i, i ^ distance) for i in range(size)])  26.1 us
    ppermute x25, waiting for transfers between devices, exchange(): return lax.ppermute(value, 'ffn', [(i, i ^ distance) for i in range(size)])  14.1 us
    pallas_call x13, Pallas kernels, call(): pl.pallas_call(body, out_shape=out_shape, in_specs=in_specs or [VMEM] * l...  13.7 us
  transfers between devices with their start and end apart: 25, of which 10 were waited for; matrix products, arithmetic and copies ran while one was open for 0% of the time, Pallas kernels for 21%

profile of v4, /device:TPU:0, one launch (start us, length us, event | category | flops | bytes accessed | tf_op | source)
XLA Modules:
  0.0 55.3 jit_solution(15239565561862591811)
XLA Ops:
  0.6 1.1 %shard_map.122.refs_0_ = bf16[8,4224]{1,0:T(8,128)(2,1)S(1)} custom-call(bf16[8,4096]{1,0:T(8,128)(2,1)} %tokens_hbm.1, f32[1,4096]{1,0:T(1,128)} %bitcast.6, s32[8,8]{1,0:T(8,128)} %routes_hbm.1, f32[8,8]{1,0:T(8,128)} %scores_hbm.1), custom_call_target="tpu_custom_call" | custom-call | flops 1 | bytes 1 | tf_op jit(solution)/shard_map/pallas_call | solution.py:45
  1.7 5.1 %collective-permute-start.3 = (bf16[8,4224]{1,0:T(8,128)(2,1)S(1)}, bf16[8,4224]{1,0:T(8,128)(2,1)S(1)}, u32[]{:S(2)}, u32[]{:S(2)}) collective-permute-start(bf16[8,4224]{1,0:T(8,128)(2,1)S(1)} %shard_map.122.refs_0_), channel_id=1, source_target_pairs={{0,24},{1,25},{2,26},{3,27},{4,28},{5,29},{6,30},{7,31},{8,16},{9,... | collective-permute-start | bytes 202760 | tf_op jit(solution)/shard_map/ppermute | solution.py:37
  6.8 0.0 collective-permute-start.2
  6.8 2.4 %collective-permute-start.1 = (bf16[8,4224]{1,0:T(8,128)(2,1)S(1)}, bf16[8,4224]{1,0:T(8,128)(2,1)S(1)}, u32[]{:S(2)}, u32[]{:S(2)}) collective-permute-start(bf16[8,4224]{1,0:T(8,128)(2,1)S(1)} %shard_map.122.refs_0_), channel_id=1, source_target_pairs={{0,6},{1,7},{2,4},{3,5},{4,2},{5,3},{6,0},{7,1},{8,14},{9,15},{10,... | collective-permute-start | bytes 202760 | tf_op jit(solution)/shard_map/ppermute | solution.py:37
  9.3 0.8 %collective-permute-start = (bf16[8,4224]{1,0:T(8,128)(2,1)S(1)}, bf16[8,4224]{1,0:T(8,128)(2,1)S(1)}, u32[]{:S(2)}, u32[]{:S(2)}) collective-permute-start(bf16[8,4224]{1,0:T(8,128)(2,1)S(1)} %shard_map.122.refs_0_), channel_id=1, source_target_pairs={{0,8},{1,9},{2,10},{3,11},{4,12},{5,13},{6,14},{7,15},{8,0},{9,1},... | collective-permute-start | bytes 202760 | tf_op jit(solution)/shard_map/ppermute | solution.py:37
  10.1 0.0 copy-start
  10.1 0.7 %copy-done = s32[8]{0:T(128)S(1)} copy-done((s32[8]{0:T(128)S(1)}, s32[8]{0:T(128)}, u32[]{:S(2)}) %copy-start) | copy-done | bytes 56
  10.7 4.1 %shard_map.123 = (bf16[128,384]{1,0:T(8,128)(2,1)S(1)}, bf16[128,384]{1,0:T(8,128)(2,1)S(1)}, bf16[4096,384]{1,0:T(8,128)(2,1)S(1)}, bf16[4096,384]{1,0:T(8,128)(2,1)S(1)}) custom-call(s32[8]{0:T(128)S(1)} %copy-done, bf16[512,128]{1,0:T(8,128)(2,1)} %bitcast.7, bf16[8,128,512]{2,1,0:T(8,128)(2,1)} %refs_1_.1, bf16[8,128,512]{2,1,0:T(8,128)(2,1)} %refs_2_.1, ...), custom_call_target="tpu_custom_call" | custom-call | flops 4000000000 | bytes 6291456 | tf_op jit(solution)/shard_map/pallas_call | solution.py:45
  14.8 0.0 collective-permute-done.3.refs_3_
  14.8 0.0 collective-permute-done.1.refs_0_
  14.9 0.0 collective-permute-done.2.refs_2_
  14.9 0.0 collective-permute-done.refs_1_
  14.9 0.1 collective-permute-start.4
  15.0 0.6 %collective-permute-start.9 = (bf16[32,4224]{1,0:T(8,128)(2,1)S(1)}, bf16[32,4224]{1,0:T(8,128)(2,1)S(1)}, u32[]{:S(2)}, u32[]{:S(2)}) collective-permute-start(bf16[32,4224]{1,0:T(8,128)(2,1)S(1)} %shard_map.124.refs_0_), channel_id=1, source_target_pairs={{0,4},{1,5},{2,6},{3,7},{4,0},{5,1},{6,2},{7,3},{8,12},{9,13},{10,... | collective-permute-start | bytes 811016 | tf_op jit(solution)/shard_map/ppermute | solution.py:37
  15.6 0.6 %collective-permute-start.5 = (bf16[32,4224]{1,0:T(8,128)(2,1)S(1)}, bf16[32,4224]{1,0:T(8,128)(2,1)S(1)}, u32[]{:S(2)}, u32[]{:S(2)}) collective-permute-start(bf16[32,4224]{1,0:T(8,128)(2,1)S(1)} %shard_map.124.refs_0_), channel_id=1, source_target_pairs={{0,2},{1,3},{2,0},{3,1},{4,6},{5,7},{6,4},{7,5},{8,10},{9,11},{10,... | collective-permute-start | bytes 811016 | tf_op jit(solution)/shard_map/ppermute | solution.py:37
  16.2 3.5 %collective-permute-start.8 = (bf16[8,4224]{1,0:T(8,128)(2,1)S(1)}, bf16[8,4224]{1,0:T(8,128)(2,1)S(1)}, u32[]{:S(2)}, u32[]{:S(2)}) collective-permute-start(bf16[8,4224]{1,0:T(8,128)(2,1)S(1)} %collective-permute-done.1.refs_0_), channel_id=1, source_target_pairs={{0,24},{1,25},{2,26},{3,27},{4,28},{5,29},{6,30},{7,31},{8,16},{9,... | collective-permute-start | bytes 202760 | tf_op jit(solution)/shard_map/ppermute | solution.py:37
  19.7 0.0 collective-permute-start.7
  19.7 0.0 collective-permute-done.4.refs_1_
  19.7 0.8 %collective-permute-start.6 = (bf16[8,4224]{1,0:T(8,128)(2,1)S(1)}, bf16[8,4224]{1,0:T(8,128)(2,1)S(1)}, u32[]{:S(2)}, u32[]{:S(2)}) collective-permute-start(bf16[8,4224]{1,0:T(8,128)(2,1)S(1)} %collective-permute-done.1.refs_0_), channel_id=1, source_target_pairs={{0,8},{1,9},{2,10},{3,11},{4,12},{5,13},{6,14},{7,15},{8,0},{9,1},... | collective-permute-start | bytes 202760 | tf_op jit(solution)/shard_map/ppermute | solution.py:37
  20.5 3.0 %shard_map.125 = (bf16[32,4480]{1,0:T(8,128)(2,1)S(1)}, bf16[32,4480]{1,0:T(8,128)(2,1)S(1)}, bf16[384,4096]{1,0:T(8,128)(2,1)S(1)}) custom-call(bf16[32,4224]{1,0:T(8,128)(2,1)S(1)} %shard_map.124.refs_0_, bf16[32,4224]{1,0:T(8,128)(2,1)S(1)} %collective-permute-done.4.refs_1_, bf16[128,384]{1,0:T(8,128)(2,1)S(1)} %get-tuple-element.36.refs_2_.refs_4_, ...), custom_call_target="tpu_custom_call" | custom-call | flops 4000000000 | bytes 9437184 | tf_op jit(solution)/shard_map/pallas_call | solution.py:45
  23.6 0.0 collective-permute-done.8.refs_3_
  23.6 1.9 %collective-permute-done.7.refs_2_ = bf16[8,4224]{1,0:T(8,128)(2,1)S(1)} collective-permute-done((bf16[8,4224]{1,0:T(8,128)(2,1)S(1)}, bf16[8,4224]{1,0:T(8,128)(2,1)S(1)}, u32[]{:S(2)}, u32[]{:S(2)}) %collective-permute-start.7) | collective-permute-done | bytes 67616 | tf_op jit(solution)/shard_map/ppermute | solution.py:37
  25.4 0.0 collective-permute-done.6.refs_1_
  25.5 0.0 collective-permute-done.9.refs_1_
  25.5 0.0 collective-permute-done.5.refs_0_
  25.5 0.1 collective-permute-start.10
  25.6 0.5 collective-permute-start.11
  26.1 0.1 collective-permute-start.19
  26.1 1.0 %collective-permute-done.10.refs_2_ = bf16[32,4224]{1,0:T(8,128)(2,1)S(1)} collective-permute-done((bf16[32,4224]{1,0:T(8,128)(2,1)S(1)}, bf16[32,4224]{1,0:T(8,128)(2,1)S(1)}, u32[]{:S(2)}, u32[]{:S(2)}) %collective-permute-start.10) | collective-permute-done | bytes 270368 | tf_op jit(solution)/shard_map/ppermute | solution.py:37
  27.1 0.4 collective-permute-done.11.refs_3_
  27.5 1.9 %shard_map.127 = (bf16[64,4480]{1,0:T(8,128)(2,1)S(1)}, bf16[64,4480]{1,0:T(8,128)(2,1)S(1)}) custom-call(bf16[32,4224]{1,0:T(8,128)(2,1)S(1)} %collective-permute-done.5.refs_0_, bf16[32,4224]{1,0:T(8,128)(2,1)S(1)} %collective-permute-done.9.refs_1_, bf16[32,4224]{1,0:T(8,128)(2,1)S(1)} %collective-permute-done.10.refs_2_, ...), custom_call_target="tpu_custom_call" | custom-call | flops 4000000000 | bytes 9437184 | tf_op jit(solution)/shard_map/pallas_call | solution.py:45
  29.4 0.2 collective-permute-start.13
  29.6 0.0 collective-permute-done.19.refs_1_
  29.6 1.8 %shard_map.131 = (bf16[32,4480]{1,0:T(8,128)(2,1)S(1)}, bf16[32,4480]{1,0:T(8,128)(2,1)S(1)}) custom-call(bf16[32,4224]{1,0:T(8,128)(2,1)S(1)} %shard_map.126.refs_0_, bf16[32,4224]{1,0:T(8,128)(2,1)S(1)} %collective-permute-done.19.refs_1_, bf16[128,384]{1,0:T(8,128)(2,1)S(1)} %get-tuple-element.36.refs_2_.refs_4_, ...), custom_call_target="tpu_custom_call" | custom-call | flops 4000000000 | bytes 9437184 | tf_op jit(solution)/shard_map/pallas_call | solution.py:45
  31.4 0.4 collective-permute-start.20
  31.8 0.1 collective-permute-start.12
  32.0 0.0 collective-permute-done.13.refs_1_
  32.0 0.3 shard_map.129
  32.3 1.6 %collective-permute-start.14 = (bf16[32,4480]{1,0:T(8,128)(2,1)S(1)}, bf16[32,4480]{1,0:T(8,128)(2,1)S(1)}, u32[]{:S(2)}, u32[]{:S(2)}) collective-permute-start(bf16[32,4480]{1,0:T(8,128)(2,1)S(1)} %get-tuple-element.54), channel_id=1, source_target_pairs={{0,2},{1,3},{2,0},{3,1},{4,6},{5,7},{6,4},{7,5},{8,10},{9,11},{10,... | collective-permute-start | bytes 860168 | tf_op jit(solution)/shard_map/ppermute | solution.py:37
  33.9 1.5 %collective-permute-start.15 = (bf16[32,4480]{1,0:T(8,128)(2,1)S(1)}, bf16[32,4480]{1,0:T(8,128)(2,1)S(1)}, u32[]{:S(2)}, u32[]{:S(2)}) collective-permute-start(bf16[32,4480]{1,0:T(8,128)(2,1)S(1)} %get-tuple-element.55), channel_id=1, source_target_pairs={{0,4},{1,5},{2,6},{3,7},{4,0},{5,1},{6,2},{7,3},{8,12},{9,13},{10,... | collective-permute-start | bytes 860168 | tf_op jit(solution)/shard_map/ppermute | solution.py:37
  35.4 0.0 collective-permute-done.20.refs_1_
  35.4 0.1 shard_map.132
  35.6 1.2 %collective-permute-start.23 = (bf16[8,4480]{1,0:T(8,128)(2,1)S(1)}, bf16[8,4480]{1,0:T(8,128)(2,1)S(1)}, u32[]{:S(2)}, u32[]{:S(2)}) collective-permute-start(bf16[8,4480]{1,0:T(8,128)(2,1)S(1)} %get-tuple-element.68), channel_id=1, source_target_pairs={{0,8},{1,9},{2,10},{3,11},{4,12},{5,13},{6,14},{7,15},{8,0},{9,1},... | collective-permute-start | bytes 215048 | tf_op jit(solution)/shard_map/ppermute | solution.py:37
  36.8 1.8 %collective-permute-start.22 = (bf16[8,4480]{1,0:T(8,128)(2,1)S(1)}, bf16[8,4480]{1,0:T(8,128)(2,1)S(1)}, u32[]{:S(2)}, u32[]{:S(2)}) collective-permute-start(bf16[8,4480]{1,0:T(8,128)(2,1)S(1)} %get-tuple-element.66), channel_id=1, source_target_pairs={{0,24},{1,25},{2,26},{3,27},{4,28},{5,29},{6,30},{7,31},{8,16},{9,... | collective-permute-start | bytes 215048 | tf_op jit(solution)/shard_map/ppermute | solution.py:37
  38.6 0.0 collective-permute-done.12.refs_1_
  38.6 0.6 %collective-permute-start.21 = (bf16[8,4480]{1,0:T(8,128)(2,1)S(1)}, bf16[8,4480]{1,0:T(8,128)(2,1)S(1)}, u32[]{:S(2)}, u32[]{:S(2)}) collective-permute-start(bf16[8,4480]{1,0:T(8,128)(2,1)S(1)} %get-tuple-element.64), channel_id=1, source_target_pairs={{0,16},{1,17},{2,18},{3,19},{4,20},{5,21},{6,22},{7,23},{8,24},{9,... | collective-permute-start | bytes 215048 | tf_op jit(solution)/shard_map/ppermute | solution.py:37
  39.2 0.2 shard_map.128.refs_0_
  39.3 2.2 %collective-permute-done.14.refs_1_ = bf16[32,4480]{1,0:T(8,128)(2,1)S(1)} collective-permute-done((bf16[32,4480]{1,0:T(8,128)(2,1)S(1)}, bf16[32,4480]{1,0:T(8,128)(2,1)S(1)}, u32[]{:S(2)}, u32[]{:S(2)}) %collective-permute-start.14) | collective-permute-done | bytes 286752 | tf_op jit(solution)/shard_map/ppermute | solution.py:37
  41.5 1.2 %collective-permute-done.15.refs_2_ = bf16[32,4480]{1,0:T(8,128)(2,1)S(1)} collective-permute-done((bf16[32,4480]{1,0:T(8,128)(2,1)S(1)}, bf16[32,4480]{1,0:T(8,128)(2,1)S(1)}, u32[]{:S(2)}, u32[]{:S(2)}) %collective-permute-start.15) | collective-permute-done | bytes 286752 | tf_op jit(solution)/shard_map/ppermute | solution.py:37
  42.7 0.2 shard_map.130
  43.0 0.0 collective-permute-done.23.refs_3_
  43.0 0.3 collective-permute-done.22.refs_2_
  43.2 2.8 %collective-permute-done.21.refs_1_ = bf16[8,4480]{1,0:T(8,128)(2,1)S(1)} collective-permute-done((bf16[8,4480]{1,0:T(8,128)(2,1)S(1)}, bf16[8,4480]{1,0:T(8,128)(2,1)S(1)}, u32[]{:S(2)}, u32[]{:S(2)}) %collective-permute-start.21) | collective-permute-done | bytes 71712 | tf_op jit(solution)/shard_map/ppermute | solution.py:37
  46.1 0.1 shard_map.133
  46.2 0.5 collective-permute-start.24
  46.8 0.2 collective-permute-start.16
  47.0 1.9 %collective-permute-start.17 = (bf16[8,4480]{1,0:T(8,128)(2,1)S(1)}, bf16[8,4480]{1,0:T(8,128)(2,1)S(1)}, u32[]{:S(2)}, u32[]{:S(2)}) collective-permute-start(bf16[8,4480]{1,0:T(8,128)(2,1)S(1)} %get-tuple-element.58), channel_id=1, source_target_pairs={{0,24},{1,25},{2,26},{3,27},{4,28},{5,29},{6,30},{7,31},{8,16},{9,... | collective-permute-start | bytes 215048 | tf_op jit(solution)/shard_map/ppermute | solution.py:37
  48.9 1.4 %collective-permute-start.18 = (bf16[8,4480]{1,0:T(8,128)(2,1)S(1)}, bf16[8,4480]{1,0:T(8,128)(2,1)S(1)}, u32[]{:S(2)}, u32[]{:S(2)}) collective-permute-start(bf16[8,4480]{1,0:T(8,128)(2,1)S(1)} %get-tuple-element.59), channel_id=1, source_target_pairs={{0,8},{1,9},{2,10},{3,11},{4,12},{5,13},{6,14},{7,15},{8,0},{9,1},... | collective-permute-start | bytes 215048 | tf_op jit(solution)/shard_map/ppermute | solution.py:37
  50.2 1.3 %collective-permute-done.24.refs_4_ = bf16[8,4480]{1,0:T(8,128)(2,1)S(1)} collective-permute-done((bf16[8,4480]{1,0:T(8,128)(2,1)S(1)}, bf16[8,4480]{1,0:T(8,128)(2,1)S(1)}, u32[]{:S(2)}, u32[]{:S(2)}) %collective-permute-start.24) | collective-permute-done | bytes 71712 | tf_op jit(solution)/shard_map/ppermute | solution.py:37
  51.5 2.9 %collective-permute-done.16.refs_1_ = bf16[8,4480]{1,0:T(8,128)(2,1)S(1)} collective-permute-done((bf16[8,4480]{1,0:T(8,128)(2,1)S(1)}, bf16[8,4480]{1,0:T(8,128)(2,1)S(1)}, u32[]{:S(2)}, u32[]{:S(2)}) %collective-permute-start.16) | collective-permute-done | bytes 71712 | tf_op jit(solution)/shard_map/ppermute | solution.py:37
  54.4 0.0 collective-permute-done.17.refs_2_
  54.4 0.2 collective-permute-done.18.refs_3_
  54.6 0.7 %shard_map.134 = (bf16[8,4096]{1,0:T(8,128)(2,1)}, bf16[8,256]{1,0:T(8,128)(2,1)}) custom-call(bf16[8,4480]{1,0:T(8,128)(2,1)S(1)} %get-tuple-element.56.refs_0_, bf16[8,4480]{1,0:T(8,128)(2,1)S(1)} %collective-permute-done.16.refs_1_, bf16[8,4480]{1,0:T(8,128)(2,1)S(1)} %collective-permute-done.17.refs_2_, ...), custom_call_target="tpu_custom_call" | custom-call | flops 1 | bytes 1 | tf_op jit(solution)/shard_map/pallas_call | solution.py:45
  (2 shorter events, 0.0 us)
Async XLA Ops:
  1.7 13.1 %collective-permute-start.3 = (bf16[8,4224]{1,0:T(8,128)(2,1)S(1)}, bf16[8,4224]{1,0:T(8,128)(2,1)S(1)}, u32[]{:S(2)}, u32[]{:S(2)}) collective-permute-start(bf16[8,4224]{1,0:T(8,128)(2,1)S(1)} %shard_map.122.refs_0_), channel_id=1, source_target_pairs={{0,24},{1,25},{2,26},{3,27},{4,28},{5,29},{6,30},{7,31},{8,16},{9,... | collective-permute-start | bytes 202760 | tf_op jit(solution)/shard_map/ppermute | solution.py:37
  6.8 8.0 %collective-permute-start.2 = (bf16[8,4224]{1,0:T(8,128)(2,1)S(1)}, bf16[8,4224]{1,0:T(8,128)(2,1)S(1)}, u32[]{:S(2)}, u32[]{:S(2)}) collective-permute-start(bf16[8,4224]{1,0:T(8,128)(2,1)S(1)} %shard_map.122.refs_0_), channel_id=1, source_target_pairs={{0,16},{1,17},{2,18},{3,19},{4,20},{5,21},{6,22},{7,23},{8,24},{9,... | collective-permute-start | bytes 202760 | tf_op jit(solution)/shard_map/ppermute | solution.py:37
  6.8 8.0 %collective-permute-start.1 = (bf16[8,4224]{1,0:T(8,128)(2,1)S(1)}, bf16[8,4224]{1,0:T(8,128)(2,1)S(1)}, u32[]{:S(2)}, u32[]{:S(2)}) collective-permute-start(bf16[8,4224]{1,0:T(8,128)(2,1)S(1)} %shard_map.122.refs_0_), channel_id=1, source_target_pairs={{0,6},{1,7},{2,4},{3,5},{4,2},{5,3},{6,0},{7,1},{8,14},{9,15},{10,... | collective-permute-start | bytes 202760 | tf_op jit(solution)/shard_map/ppermute | solution.py:37
  9.3 5.6 %collective-permute-start = (bf16[8,4224]{1,0:T(8,128)(2,1)S(1)}, bf16[8,4224]{1,0:T(8,128)(2,1)S(1)}, u32[]{:S(2)}, u32[]{:S(2)}) collective-permute-start(bf16[8,4224]{1,0:T(8,128)(2,1)S(1)} %shard_map.122.refs_0_), channel_id=1, source_target_pairs={{0,8},{1,9},{2,10},{3,11},{4,12},{5,13},{6,14},{7,15},{8,0},{9,1},... | collective-permute-start | bytes 202760 | tf_op jit(solution)/shard_map/ppermute | solution.py:37
  10.1 0.7 %copy-start = (s32[8]{0:T(128)S(1)}, s32[8]{0:T(128)}, u32[]{:S(2)}) copy-start(s32[8]{0:T(128)} %length_ref.1) | copy-start | bytes 100
  14.9 4.8 %collective-permute-start.4 = (bf16[32,4224]{1,0:T(8,128)(2,1)S(1)}, bf16[32,4224]{1,0:T(8,128)(2,1)S(1)}, u32[]{:S(2)}, u32[]{:S(2)}) collective-permute-start(bf16[32,4224]{1,0:T(8,128)(2,1)S(1)} %shard_map.124.refs_0_), channel_id=1, source_target_pairs={{0,1},{1,0},{2,3},{3,2},{4,5},{5,4},{6,7},{7,6},{8,9},{9,8},{10,11... | collective-permute-start | bytes 811016 | tf_op jit(solution)/shard_map/ppermute | solution.py:37
  15.0 10.5 %collective-permute-start.9 = (bf16[32,4224]{1,0:T(8,128)(2,1)S(1)}, bf16[32,4224]{1,0:T(8,128)(2,1)S(1)}, u32[]{:S(2)}, u32[]{:S(2)}) collective-permute-start(bf16[32,4224]{1,0:T(8,128)(2,1)S(1)} %shard_map.124.refs_0_), channel_id=1, source_target_pairs={{0,4},{1,5},{2,6},{3,7},{4,0},{5,1},{6,2},{7,3},{8,12},{9,13},{10,... | collective-permute-start | bytes 811016 | tf_op jit(solution)/shard_map/ppermute | solution.py:37
  15.6 9.9 %collective-permute-start.5 = (bf16[32,4224]{1,0:T(8,128)(2,1)S(1)}, bf16[32,4224]{1,0:T(8,128)(2,1)S(1)}, u32[]{:S(2)}, u32[]{:S(2)}) collective-permute-start(bf16[32,4224]{1,0:T(8,128)(2,1)S(1)} %shard_map.124.refs_0_), channel_id=1, source_target_pairs={{0,2},{1,3},{2,0},{3,1},{4,6},{5,7},{6,4},{7,5},{8,10},{9,11},{10,... | collective-permute-start | bytes 811016 | tf_op jit(solution)/shard_map/ppermute | solution.py:37
  16.2 7.4 %collective-permute-start.8 = (bf16[8,4224]{1,0:T(8,128)(2,1)S(1)}, bf16[8,4224]{1,0:T(8,128)(2,1)S(1)}, u32[]{:S(2)}, u32[]{:S(2)}) collective-permute-start(bf16[8,4224]{1,0:T(8,128)(2,1)S(1)} %collective-permute-done.1.refs_0_), channel_id=1, source_target_pairs={{0,24},{1,25},{2,26},{3,27},{4,28},{5,29},{6,30},{7,31},{8,16},{9,... | collective-permute-start | bytes 202760 | tf_op jit(solution)/shard_map/ppermute | solution.py:37
  19.7 5.7 %collective-permute-start.7 = (bf16[8,4224]{1,0:T(8,128)(2,1)S(1)}, bf16[8,4224]{1,0:T(8,128)(2,1)S(1)}, u32[]{:S(2)}, u32[]{:S(2)}) collective-permute-start(bf16[8,4224]{1,0:T(8,128)(2,1)S(1)} %collective-permute-done.1.refs_0_), channel_id=1, source_target_pairs={{0,16},{1,17},{2,18},{3,19},{4,20},{5,21},{6,22},{7,23},{8,24},{9,... | collective-permute-start | bytes 202760 | tf_op jit(solution)/shard_map/ppermute | solution.py:37
  19.7 5.7 %collective-permute-start.6 = (bf16[8,4224]{1,0:T(8,128)(2,1)S(1)}, bf16[8,4224]{1,0:T(8,128)(2,1)S(1)}, u32[]{:S(2)}, u32[]{:S(2)}) collective-permute-start(bf16[8,4224]{1,0:T(8,128)(2,1)S(1)} %collective-permute-done.1.refs_0_), channel_id=1, source_target_pairs={{0,8},{1,9},{2,10},{3,11},{4,12},{5,13},{6,14},{7,15},{8,0},{9,1},... | collective-permute-start | bytes 202760 | tf_op jit(solution)/shard_map/ppermute | solution.py:37
  25.5 1.6 %collective-permute-start.10 = (bf16[32,4224]{1,0:T(8,128)(2,1)S(1)}, bf16[32,4224]{1,0:T(8,128)(2,1)S(1)}, u32[]{:S(2)}, u32[]{:S(2)}) collective-permute-start(bf16[32,4224]{1,0:T(8,128)(2,1)S(1)} %collective-permute-done.5.refs_0_), channel_id=1, source_target_pairs={{0,1},{1,0},{2,3},{3,2},{4,5},{5,4},{6,7},{7,6},{8,9},{9,8},{10,11... | collective-permute-start | bytes 811016 | tf_op jit(solution)/shard_map/ppermute | solution.py:37
  25.6 1.9 %collective-permute-start.11 = (bf16[32,4224]{1,0:T(8,128)(2,1)S(1)}, bf16[32,4224]{1,0:T(8,128)(2,1)S(1)}, u32[]{:S(2)}, u32[]{:S(2)}) collective-permute-start(bf16[32,4224]{1,0:T(8,128)(2,1)S(1)} %collective-permute-done.9.refs_1_), channel_id=1, source_target_pairs={{0,1},{1,0},{2,3},{3,2},{4,5},{5,4},{6,7},{7,6},{8,9},{9,8},{10,11... | collective-permute-start | bytes 811016 | tf_op jit(solution)/shard_map/ppermute | solution.py:37
  26.1 3.6 %collective-permute-start.19 = (bf16[32,4224]{1,0:T(8,128)(2,1)S(1)}, bf16[32,4224]{1,0:T(8,128)(2,1)S(1)}, u32[]{:S(2)}, u32[]{:S(2)}) collective-permute-start(bf16[32,4224]{1,0:T(8,128)(2,1)S(1)} %shard_map.126.refs_0_), channel_id=1, source_target_pairs={{0,1},{1,0},{2,3},{3,2},{4,5},{5,4},{6,7},{7,6},{8,9},{9,8},{10,11... | collective-permute-start | bytes 811016 | tf_op jit(solution)/shard_map/ppermute | solution.py:37
  29.4 2.6 %collective-permute-start.13 = (bf16[64,4480]{1,0:T(8,128)(2,1)S(1)}, bf16[64,4480]{1,0:T(8,128)(2,1)S(1)}, u32[]{:S(2)}, u32[]{:S(2)}) collective-permute-start(bf16[64,4480]{1,0:T(8,128)(2,1)S(1)} %get-tuple-element.53), channel_id=1, source_target_pairs={{0,1},{1,0},{2,3},{3,2},{4,5},{5,4},{6,7},{7,6},{8,9},{9,8},{10,11... | collective-permute-start | bytes 1720328 | tf_op jit(solution)/shard_map/ppermute | solution.py:37
  31.4 4.0 %collective-permute-start.20 = (bf16[32,4480]{1,0:T(8,128)(2,1)S(1)}, bf16[32,4480]{1,0:T(8,128)(2,1)S(1)}, u32[]{:S(2)}, u32[]{:S(2)}) collective-permute-start(bf16[32,4480]{1,0:T(8,128)(2,1)S(1)} %get-tuple-element.61), channel_id=1, source_target_pairs={{0,1},{1,0},{2,3},{3,2},{4,5},{5,4},{6,7},{7,6},{8,9},{9,8},{10,11... | collective-permute-start | bytes 860168 | tf_op jit(solution)/shard_map/ppermute | solution.py:37
  31.8 6.7 %collective-permute-start.12 = (bf16[32,4480]{1,0:T(8,128)(2,1)S(1)}, bf16[32,4480]{1,0:T(8,128)(2,1)S(1)}, u32[]{:S(2)}, u32[]{:S(2)}) collective-permute-start(bf16[32,4480]{1,0:T(8,128)(2,1)S(1)} %get-tuple-element.52), channel_id=1, source_target_pairs={{0,1},{1,0},{2,3},{3,2},{4,5},{5,4},{6,7},{7,6},{8,9},{9,8},{10,11... | collective-permute-start | bytes 860168 | tf_op jit(solution)/shard_map/ppermute | solution.py:37
  32.3 9.2 %collective-permute-start.14 = (bf16[32,4480]{1,0:T(8,128)(2,1)S(1)}, bf16[32,4480]{1,0:T(8,128)(2,1)S(1)}, u32[]{:S(2)}, u32[]{:S(2)}) collective-permute-start(bf16[32,4480]{1,0:T(8,128)(2,1)S(1)} %get-tuple-element.54), channel_id=1, source_target_pairs={{0,2},{1,3},{2,0},{3,1},{4,6},{5,7},{6,4},{7,5},{8,10},{9,11},{10,... | collective-permute-start | bytes 860168 | tf_op jit(solution)/shard_map/ppermute | solution.py:37
  33.9 8.8 %collective-permute-start.15 = (bf16[32,4480]{1,0:T(8,128)(2,1)S(1)}, bf16[32,4480]{1,0:T(8,128)(2,1)S(1)}, u32[]{:S(2)}, u32[]{:S(2)}) collective-permute-start(bf16[32,4480]{1,0:T(8,128)(2,1)S(1)} %get-tuple-element.55), channel_id=1, source_target_pairs={{0,4},{1,5},{2,6},{3,7},{4,0},{5,1},{6,2},{7,3},{8,12},{9,13},{10,... | collective-permute-start | bytes 860168 | tf_op jit(solution)/shard_map/ppermute | solution.py:37
  35.6 7.4 %collective-permute-start.23 = (bf16[8,4480]{1,0:T(8,128)(2,1)S(1)}, bf16[8,4480]{1,0:T(8,128)(2,1)S(1)}, u32[]{:S(2)}, u32[]{:S(2)}) collective-permute-start(bf16[8,4480]{1,0:T(8,128)(2,1)S(1)} %get-tuple-element.68), channel_id=1, source_target_pairs={{0,8},{1,9},{2,10},{3,11},{4,12},{5,13},{6,14},{7,15},{8,0},{9,1},... | collective-permute-start | bytes 215048 | tf_op jit(solution)/shard_map/ppermute | solution.py:37
  36.8 6.4 %collective-permute-start.22 = (bf16[8,4480]{1,0:T(8,128)(2,1)S(1)}, bf16[8,4480]{1,0:T(8,128)(2,1)S(1)}, u32[]{:S(2)}, u32[]{:S(2)}) collective-permute-start(bf16[8,4480]{1,0:T(8,128)(2,1)S(1)} %get-tuple-element.66), channel_id=1, source_target_pairs={{0,24},{1,25},{2,26},{3,27},{4,28},{5,29},{6,30},{7,31},{8,16},{9,... | collective-permute-start | bytes 215048 | tf_op jit(solution)/shard_map/ppermute | solution.py:37
  38.6 7.5 %collective-permute-start.21 = (bf16[8,4480]{1,0:T(8,128)(2,1)S(1)}, bf16[8,4480]{1,0:T(8,128)(2,1)S(1)}, u32[]{:S(2)}, u32[]{:S(2)}) collective-permute-start(bf16[8,4480]{1,0:T(8,128)(2,1)S(1)} %get-tuple-element.64), channel_id=1, source_target_pairs={{0,16},{1,17},{2,18},{3,19},{4,20},{5,21},{6,22},{7,23},{8,24},{9,... | collective-permute-start | bytes 215048 | tf_op jit(solution)/shard_map/ppermute | solution.py:37
  46.2 5.3 %collective-permute-start.24 = (bf16[8,4480]{1,0:T(8,128)(2,1)S(1)}, bf16[8,4480]{1,0:T(8,128)(2,1)S(1)}, u32[]{:S(2)}, u32[]{:S(2)}) collective-permute-start(bf16[8,4480]{1,0:T(8,128)(2,1)S(1)} %shard_map.133), channel_id=1, source_target_pairs={{0,6},{1,7},{2,4},{3,5},{4,2},{5,3},{6,0},{7,1},{8,14},{9,15},{10,... | collective-permute-start | bytes 215048 | tf_op jit(solution)/shard_map/ppermute | solution.py:37
  46.8 7.6 %collective-permute-start.16 = (bf16[8,4480]{1,0:T(8,128)(2,1)S(1)}, bf16[8,4480]{1,0:T(8,128)(2,1)S(1)}, u32[]{:S(2)}, u32[]{:S(2)}) collective-permute-start(bf16[8,4480]{1,0:T(8,128)(2,1)S(1)} %get-tuple-element.57), channel_id=1, source_target_pairs={{0,16},{1,17},{2,18},{3,19},{4,20},{5,21},{6,22},{7,23},{8,24},{9,... | collective-permute-start | bytes 215048 | tf_op jit(solution)/shard_map/ppermute | solution.py:37
  47.0 7.4 %collective-permute-start.17 = (bf16[8,4480]{1,0:T(8,128)(2,1)S(1)}, bf16[8,4480]{1,0:T(8,128)(2,1)S(1)}, u32[]{:S(2)}, u32[]{:S(2)}) collective-permute-start(bf16[8,4480]{1,0:T(8,128)(2,1)S(1)} %get-tuple-element.58), channel_id=1, source_target_pairs={{0,24},{1,25},{2,26},{3,27},{4,28},{5,29},{6,30},{7,31},{8,16},{9,... | collective-permute-start | bytes 215048 | tf_op jit(solution)/shard_map/ppermute | solution.py:37
  48.9 5.7 %collective-permute-start.18 = (bf16[8,4480]{1,0:T(8,128)(2,1)S(1)}, bf16[8,4480]{1,0:T(8,128)(2,1)S(1)}, u32[]{:S(2)}, u32[]{:S(2)}) collective-permute-start(bf16[8,4480]{1,0:T(8,128)(2,1)S(1)} %get-tuple-element.59), channel_id=1, source_target_pairs={{0,8},{1,9},{2,10},{3,11},{4,12},{5,13},{6,14},{7,15},{8,0},{9,1},... | collective-permute-start | bytes 215048 | tf_op jit(solution)/shard_map/ppermute | solution.py:37

commit v5 on v4

--- a/solution.py
+++ b/solution.py
@@ -102,13 +102,30 @@
     return [high, middle, value - high - middle]
 
 
+def keep_kernel(count, *refs):
+    copies = fetch(refs[:count], refs[count : 2 * count], refs[2 * count])
+    for copy in copies:
+        copy.wait()
+
+
+def keep(*arrays):
+    return call(
+        functools.partial(keep_kernel, len(arrays)),
+        [pltpu.VMEM(a.shape, a.dtype) for a in arrays],
+        in_hbm(*arrays),
+        in_specs=[HBM] * len(arrays),
+        scratch=[fetched(len(arrays))],
+        flops=4 * 10**9,
+    )
+
+
 def attention_kernel(
-    own, offsets, length_ref, *refs
+    own, offsets, length_hbm, query_hbm, key_hbm, value_hbm, near_ref, far_ref, *scratch
 ):
-    query_hbm, key_hbm, value_hbm, gate_hbm, up_hbm, near_ref, far_ref, gate_out, up_out = refs[:9]
-    query_ref, key_ref, value_ref, dest_ref, sems = refs[9:]
-    sources = [query_hbm, key_hbm, value_hbm, gate_hbm, up_hbm]
-    copies = fetch(sources, [query_ref, key_ref, value_ref, gate_out, up_out], sems)
+    length_ref, query_ref, key_ref, value_ref, dest_ref, sems = scratch
+    sources = [length_hbm, query_hbm, key_hbm, value_hbm]
+    copies = fetch(sources, [length_ref, query_ref, key_ref, value_ref], sems)
+    copies[0].wait()
     me = lax.axis_index("ffn")
     rows, seg_len, _ = key_ref.shape
     per_group = HEADS // KV_HEADS
@@ -123,7 +140,7 @@
     per_dest = max(1, own // HEAD_DIM)
     extra = near_ref.shape[1]
     lane = lax.broadcasted_iota(jnp.int32, (rows, extra), 1)
-    for copy in copies[:3]:
+    for copy in copies[1:]:
         copy.wait()
     for group in range(KV_HEADS):
         cols = slice(group * HEAD_DIM, (group + 1) * HEAD_DIM)
@@ -168,11 +185,9 @@
         for place in range(0, len(offsets), 2):
             pair = [dest_ref[me ^ (offset ^ core)] for offset in offsets[place : place + 2]]
             out_ref[place * rows : (place + 2) * rows] = jnp.concatenate(pair, axis=0).astype(jnp.bfloat16)
-    for copy in copies[3:]:
-        copy.wait()
-
-
-def attend(query, k_cache, v_cache, cache_len, levels, weights):
+
+
+def attend(query, k_cache, v_cache, cache_len, levels):
     devices = lax.axis_size("ffn")
     rows, seg_len, _ = k_cache.shape
     own = query.shape[1] // devices
@@ -182,33 +197,27 @@
     out = jax.ShapeDtypeStruct((len(offsets) * rows, extra), jnp.bfloat16)
     return call(
         functools.partial(attention_kernel, own, offsets),
-        [out, out] + [pltpu.VMEM(w.shape, w.dtype) for w in weights],
-        [cache_len, *in_hbm(stacked, k_cache, v_cache, *weights)],
-        in_specs=[SMEM] + [HBM] * 5,
+        [out, out],
+        in_hbm(cache_len, stacked, k_cache, v_cache),
+        in_specs=[HBM] * 4,
         scratch=[
+            pltpu.SMEM(cache_len.shape, cache_len.dtype),
             pltpu.VMEM(stacked.shape, stacked.dtype),
             pltpu.VMEM(k_cache.shape, k_cache.dtype),
             pltpu.VMEM(v_cache.shape, v_cache.dtype),
             pltpu.VMEM((devices, rows, extra), jnp.float32),
-            fetched(5),
+            fetched(4),
         ],
         flops=4 * 10**9,
-        nbytes=2 * sum(w.size for w in weights),
-    )
-
-
-def expert_kernel(experts, chunks, load, *refs):
+    )
+
+
+def expert_kernel(experts, chunks, *refs):
     count = len(chunks)
     same_refs, other_refs, refs = refs[:count], refs[count : 2 * count], refs[2 * count :]
-    near_ref, far_ref, gate_ref, up_ref, down_ref, own_out, far_out = refs[:7]
+    near_ref, far_ref, gate_ref, up_ref, down_ref, own_out, far_out = refs
     width = gate_ref.shape[0]
     rows = same_refs[0].shape[0]
-    step = 1024
-    cuts = [pl.ds(first, step) for first in range(0, width, step)]
-    copies = [None] * len(cuts)
-    if load:
-        down_hbm, down_ref, sems = down_ref, refs[7], refs[8]
-        copies = fetch([down_hbm.at[:, at] for at in cuts], [down_ref.at[:, at] for at in cuts], sems)
     coded = jnp.concatenate([r[:, width:] for r in same_refs + other_refs], axis=0).astype(jnp.float32)
     lane = lax.broadcasted_iota(jnp.int32, coded.shape, 1)
     mine = (lane < 2 * experts) & (lane % experts == lax.axis_index("ffn") // 2)
@@ -221,32 +230,25 @@
     gate_part = jnp.dot(stacked, gate_ref[...], preferred_element_type=jnp.float32)
     up_part = jnp.dot(stacked, up_ref[...], preferred_element_type=jnp.float32)
     hidden = (gate_part / (1.0 + jnp.exp(-gate_part)) * up_part).astype(jnp.bfloat16)
-    for copy, at in zip(copies, cuts):
-        if load:
-            copy.wait()
+    step = 1024
+    for first in range(0, width, step):
+        at = slice(first, first + step)
         part = jnp.dot(hidden, down_ref[:, at], preferred_element_type=jnp.float32)
         part = (part * share).astype(jnp.bfloat16)
         own_out[:, at] = part[: count * rows]
         far_out[:, at] = part[count * rows :]
 
 
-def apply_expert(same, chunks, sums, weights, load=False):
+def apply_expert(same, other, chunks, sums, weights):
     rows = same[0].shape[0]
     width, hidden = weights[0].shape
     devices = lax.axis_size("ffn")
-    outs = [jax.ShapeDtypeStruct((len(same) * rows, width + sums[0].shape[1]), jnp.bfloat16)] * 2
-    args = [*same, *[exchange(s, 1) for s in same], *sums, *weights]
-    in_specs, scratch = [VMEM] * len(args), []
-    if load:
-        args[-1:], in_specs[-1] = in_hbm(args[-1]), HBM
-        outs.append(pltpu.VMEM(weights[2].shape, weights[2].dtype))
-        scratch.append(fetched(width // 1024))
+    shape = jax.ShapeDtypeStruct((len(same) * rows, width + sums[0].shape[1]), jnp.bfloat16)
+    args = [*same, *other, *sums, *weights]
     return call(
-        functools.partial(expert_kernel, devices // 2, chunks, load),
-        outs,
+        functools.partial(expert_kernel, devices // 2, chunks),
+        [shape, shape],
         args,
-        in_specs=in_specs,
-        scratch=scratch,
         flops=4 * 10**9,
         nbytes=2 * 3 * width * hidden,
         mib=8 + sum(2 * a.size for a in args) // 2**20,
@@ -287,13 +289,13 @@
             out_ref[:, width:] = mean.astype(jnp.bfloat16)
 
 
-def summed(parts, sizes, width, own, last=False):
+def summed(parts, sizes, width, own, last=False, flops=1):
     rows, whole = parts[0].shape
     if last:
         shapes = [jax.ShapeDtypeStruct((rows, n), jnp.bfloat16) for n in (width, own)]
     else:
         shapes = [jax.ShapeDtypeStruct((n, whole), jnp.bfloat16) for n in sizes]
-    return call(functools.partial(sum_kernel, len(parts), width, own, last), shapes, parts)
+    return call(functools.partial(sum_kernel, len(parts), width, own, last), shapes, parts, flops=flops)
 
 
 def stack_kernel(*refs):
@@ -343,34 +345,29 @@
         scratch=[pltpu.VMEM(a.shape, a.dtype) for a in (tokens, norm_gain[None], routes, gate_scores)]
         + [fetched(4)],
     )
-    *sums, w_gate, w_up = attend(query, k_cache, v_cache, cache_len, levels, (w_gate, w_up))
     (stride, radix), *outer = levels
     corner = 3 * stride
-    weights = (w_gate, w_up, w_down)
     rows = rows_dev * (devices // (2 * radix))
     cut = [rows // outer[0][1]] * outer[0][1]
     across = [exchange(block, corner)] if radix == 4 else []
-    base = gather(block, outer, sums[0], *across)
+    w_gate, w_up = keep(w_gate, w_up)
+    weights = (w_gate, w_up, w_down)
+    base = gather(block, outer, w_gate, *across)
     sides = [1, 2] if radix == 4 else [1]
     chunks = [exchange(base, stride * k) for k in sides]
-
-    near, far, w_down = apply_expert([base], [0], sums, weights, load=True)
-    weights = (w_gate, w_up, w_down)
-    ready = [near]
-    if across:
-        last_chunk = gather(across[0], outer, near)
-        ready.append(last_chunk)
-    chunks = [after(chunk, *ready) for chunk in chunks]
-    own_near, own_far = near, far
-    near, far = apply_expert(chunks, sides, sums, weights)
-    own_far = after(own_far, near)
-    if across:
-        corner_near, corner_far = apply_expert([last_chunk], [3], sums, weights)
-    (total,) = summed([own_near, exchange(own_far, 1)], [rows], width, own)
-    pieces = summed([near, exchange(far, 1)], [rows] * len(sides), width, own)
+    sums = attend(after(query, base), k_cache, v_cache, cache_len, levels)
+    last_chunk = [gather(a, outer, sums[0]) for a in across]
+    chunks = [after(chunk, sums[0]) for chunk in chunks]
+    others = [exchange(c, 1) for c in (*chunks, base, *last_chunk)]
+    others = lax.optimization_barrier(others)
+    count = len(sides)
+    near, far = apply_expert(chunks, others[:count], sides, sums, weights)
+    pieces = summed([near, exchange(far, 1)], [rows] * count, width, own)
+    base = after(base, near)
+    near, far = apply_expert([base, *last_chunk], others[count:], [0, 3][: radix - 2], sums, weights)
+    total, *corner_pieces = summed([near, exchange(far, 1)], [rows] + cut * len(across), width, own)
     parts = [total] + [exchange(piece, stride * k) for piece, k in zip(pieces, sides)]
     if across:
-        corner_pieces = summed([corner_near, exchange(corner_far, 1)], cut, width, own)
         corner_parts = scatter(corner_pieces, outer, width, own)
     pieces = summed(parts, cut, width, own)
     last = scatter(pieces, outer, width, own)
@@ -378,6 +375,9 @@
         corner_parts = [after(part, pieces[0]) for part in corner_parts]
         (corner_sum,) = summed(corner_parts, [rows_dev], width, own)
         last.append(exchange(corner_sum, corner))
+    if across:
+        (most,) = summed(last[:-1], [rows_dev], width, own, flops=10**9)
+        last = [most, last[-1]]
     return tuple(summed(last, [], width, own, last=True))
 
 

time: 55.5 us -> 53.3 us (0.960)
  waiting for transfers between devices: 14.1 us -> 12.8 us
  local copies, waits for them, and re-layouts: 0.65 us -> 0.01 us
    ppermute x25 -> x24, waiting for transfers between devices: 14.1 us -> 12.8 us  [exchange(): return lax.ppermute(value, 'ffn', [(i, i ^ distance) for i in range(size)])]
    unnamed x2, local copies, waits for them, and re-layouts: 0.65 us -> 0.01 us
    ppermute x25 -> x24, starting transfers between devices: 26.1 us -> 26.2 us  [exchange(): return lax.ppermute(value, 'ffn', [(i, i ^ distance) for i in range(size)])]
  transfers between devices with their start and end apart: 25 -> 24, of which waited for: 10 -> 12; matrix products, arithmetic and copies ran while one was open for 0% -> 0% of each run, Pallas kernels for 21% -> 18%
where the time goes in v5:
time: 53.3 us; the launch traced here: 53.1 us
  starting transfers between devices  26.2 us (49%)
  Pallas kernels  13.3 us (25%)
  waiting for transfers between devices  12.8 us (24%)
  between operations  0.78 us (1%)
    ppermute x24, starting transfers between devices, exchange(): return lax.ppermute(value, 'ffn', [(i, i ^ distance) for i in range(size)])  26.2 us
    pallas_call x13, Pallas kernels, call(): pl.pallas_call(body, out_shape=out_shape, in_specs=in_specs or [VMEM] * l...  13.3 us
    ppermute x24, waiting for transfers between devices, exchange(): return lax.ppermute(value, 'ffn', [(i, i ^ distance) for i in range(size)])  12.8 us
  transfers between devices with their start and end apart: 24, of which 12 were waited for; matrix products, arithmetic and copies ran while one was open for 0% of the time, Pallas kernels for 18%

profile of v5, /device:TPU:0, one launch (start us, length us, event | category | flops | bytes accessed | tf_op | source)
XLA Modules:
  0.0 53.1 jit_solution(7008675814493912090)
XLA Ops:
  0.6 1.1 %shard_map.122.refs_0_ = bf16[8,4224]{1,0:T(8,128)(2,1)S(1)} custom-call(bf16[8,4096]{1,0:T(8,128)(2,1)} %tokens_hbm.1, f32[1,4096]{1,0:T(1,128)} %bitcast.6, s32[8,8]{1,0:T(8,128)} %routes_hbm.1, f32[8,8]{1,0:T(8,128)} %scores_hbm.1), custom_call_target="tpu_custom_call" | custom-call | flops 1 | bytes 1 | tf_op jit(solution)/shard_map/pallas_call | solution.py:45
  1.7 4.0 %collective-permute-start.1 = (bf16[8,4224]{1,0:T(8,128)(2,1)S(1)}, bf16[8,4224]{1,0:T(8,128)(2,1)S(1)}, u32[]{:S(2)}, u32[]{:S(2)}) collective-permute-start(bf16[8,4224]{1,0:T(8,128)(2,1)S(1)} %shard_map.122.refs_0_), channel_id=1, source_target_pairs={{0,6},{1,7},{2,4},{3,5},{4,2},{5,3},{6,0},{7,1},{8,14},{9,15},{10,... | collective-permute-start | bytes 202760 | tf_op jit(solution)/shard_map/ppermute | solution.py:37
  5.7 2.6 %collective-permute-start.2 = (bf16[8,4224]{1,0:T(8,128)(2,1)S(1)}, bf16[8,4224]{1,0:T(8,128)(2,1)S(1)}, u32[]{:S(2)}, u32[]{:S(2)}) collective-permute-start(bf16[8,4224]{1,0:T(8,128)(2,1)S(1)} %shard_map.122.refs_0_), channel_id=1, source_target_pairs={{0,16},{1,17},{2,18},{3,19},{4,20},{5,21},{6,22},{7,23},{8,24},{9,... | collective-permute-start | bytes 202760 | tf_op jit(solution)/shard_map/ppermute | solution.py:37
  8.3 1.3 %collective-permute-start.3 = (bf16[8,4224]{1,0:T(8,128)(2,1)S(1)}, bf16[8,4224]{1,0:T(8,128)(2,1)S(1)}, u32[]{:S(2)}, u32[]{:S(2)}) collective-permute-start(bf16[8,4224]{1,0:T(8,128)(2,1)S(1)} %shard_map.122.refs_0_), channel_id=1, source_target_pairs={{0,24},{1,25},{2,26},{3,27},{4,28},{5,29},{6,30},{7,31},{8,16},{9,... | collective-permute-start | bytes 202760 | tf_op jit(solution)/shard_map/ppermute | solution.py:37
  9.6 0.2 collective-permute-start
  9.8 2.9 %shard_map.123 = (bf16[4096,384]{1,0:T(8,128)(2,1)S(1)}, bf16[4096,384]{1,0:T(8,128)(2,1)S(1)}) custom-call(bf16[4096,384]{1,0:T(8,128)(2,1)} %refs_0_.1, bf16[4096,384]{1,0:T(8,128)(2,1)} %refs_1_.1), custom_call_target="tpu_custom_call" | custom-call | flops 4000000000 | bytes 1 | tf_op jit(solution)/shard_map/pallas_call | solution.py:45
  12.7 0.0 collective-permute-done.1.refs_0_
  12.7 0.0 collective-permute-done.2.refs_2_
  12.7 1.8 %collective-permute-done.3.refs_3_ = bf16[8,4224]{1,0:T(8,128)(2,1)S(1)} collective-permute-done((bf16[8,4224]{1,0:T(8,128)(2,1)S(1)}, bf16[8,4224]{1,0:T(8,128)(2,1)S(1)}, u32[]{:S(2)}, u32[]{:S(2)}) %collective-permute-start.3) | collective-permute-done | bytes 67616 | tf_op jit(solution)/shard_map/ppermute | solution.py:37
  14.5 0.1 collective-permute-done.refs_1_
  14.6 0.6 %collective-permute-start.5 = (bf16[32,4224]{1,0:T(8,128)(2,1)S(1)}, bf16[32,4224]{1,0:T(8,128)(2,1)S(1)}, u32[]{:S(2)}, u32[]{:S(2)}) collective-permute-start(bf16[32,4224]{1,0:T(8,128)(2,1)S(1)} %shard_map.124.refs_0_), channel_id=1, source_target_pairs={{0,4},{1,5},{2,6},{3,7},{4,0},{5,1},{6,2},{7,3},{8,12},{9,13},{10,... | collective-permute-start | bytes 811016 | tf_op jit(solution)/shard_map/ppermute | solution.py:37
  15.2 0.5 %collective-permute-start.4 = (bf16[32,4224]{1,0:T(8,128)(2,1)S(1)}, bf16[32,4224]{1,0:T(8,128)(2,1)S(1)}, u32[]{:S(2)}, u32[]{:S(2)}) collective-permute-start(bf16[32,4224]{1,0:T(8,128)(2,1)S(1)} %shard_map.124.refs_0_), channel_id=1, source_target_pairs={{0,2},{1,3},{2,0},{3,1},{4,6},{5,7},{6,4},{7,5},{8,10},{9,11},{10,... | collective-permute-start | bytes 811016 | tf_op jit(solution)/shard_map/ppermute | solution.py:37
  15.7 0.7 %collective-permute-start.9 = (bf16[8,4224]{1,0:T(8,128)(2,1)S(1)}, bf16[8,4224]{1,0:T(8,128)(2,1)S(1)}, u32[]{:S(2)}, u32[]{:S(2)}) collective-permute-start(bf16[8,4224]{1,0:T(8,128)(2,1)S(1)} %collective-permute-done.1.refs_0_), channel_id=1, source_target_pairs={{0,8},{1,9},{2,10},{3,11},{4,12},{5,13},{6,14},{7,15},{8,0},{9,1},... | collective-permute-start | bytes 202760 | tf_op jit(solution)/shard_map/ppermute | solution.py:37
  16.5 2.5 %collective-permute-start.10 = (bf16[8,4224]{1,0:T(8,128)(2,1)S(1)}, bf16[8,4224]{1,0:T(8,128)(2,1)S(1)}, u32[]{:S(2)}, u32[]{:S(2)}) collective-permute-start(bf16[8,4224]{1,0:T(8,128)(2,1)S(1)} %collective-permute-done.1.refs_0_), channel_id=1, source_target_pairs={{0,16},{1,17},{2,18},{3,19},{4,20},{5,21},{6,22},{7,23},{8,24},{9,... | collective-permute-start | bytes 202760 | tf_op jit(solution)/shard_map/ppermute | solution.py:37
  19.0 1.1 %collective-permute-start.11 = (bf16[8,4224]{1,0:T(8,128)(2,1)S(1)}, bf16[8,4224]{1,0:T(8,128)(2,1)S(1)}, u32[]{:S(2)}, u32[]{:S(2)}) collective-permute-start(bf16[8,4224]{1,0:T(8,128)(2,1)S(1)} %collective-permute-done.1.refs_0_), channel_id=1, source_target_pairs={{0,24},{1,25},{2,26},{3,27},{4,28},{5,29},{6,30},{7,31},{8,16},{9,... | collective-permute-start | bytes 202760 | tf_op jit(solution)/shard_map/ppermute | solution.py:37
  20.1 0.0 copy-start
  20.1 3.6 %shard_map.125 = (bf16[128,384]{1,0:T(8,128)(2,1)S(1)}, bf16[128,384]{1,0:T(8,128)(2,1)S(1)}) custom-call(s32[8]{0:T(128)} %length_hbm.1, bf16[512,128]{1,0:T(8,128)(2,1)} %bitcast.7, bf16[8,128,512]{2,1,0:T(8,128)(2,1)} %key_hbm.1, bf16[8,128,512]{2,1,0:T(8,128)(2,1)} %value_hbm.1), custom_call_target="tpu_custom_call" | custom-call | flops 4000000000 | bytes 1 | tf_op jit(solution)/shard_map/pallas_call | solution.py:45
  23.8 0.0 collective-permute-done.9.refs_1_
  23.8 0.1 collective-permute-start.8
  23.9 0.0 collective-permute-done.10.refs_2_
  23.9 1.3 %collective-permute-done.11.refs_3_ = bf16[8,4224]{1,0:T(8,128)(2,1)S(1)} collective-permute-done((bf16[8,4224]{1,0:T(8,128)(2,1)S(1)}, bf16[8,4224]{1,0:T(8,128)(2,1)S(1)}, u32[]{:S(2)}, u32[]{:S(2)}) %collective-permute-start.11) | collective-permute-done | bytes 67616 | tf_op jit(solution)/shard_map/ppermute | solution.py:37
  25.2 0.1 collective-permute-start.12
  25.3 0.0 collective-permute-done.5.refs_1_
  25.3 0.5 collective-permute-start.7
  25.8 0.0 collective-permute-done.4.refs_0_
  25.8 0.1 collective-permute-start.6
  25.9 0.0 collective-permute-done.8.refs_2_
  25.9 0.9 %collective-permute-done.12.refs_3_ = bf16[32,4224]{1,0:T(8,128)(2,1)S(1)} collective-permute-done((bf16[32,4224]{1,0:T(8,128)(2,1)S(1)}, bf16[32,4224]{1,0:T(8,128)(2,1)S(1)}, u32[]{:S(2)}, u32[]{:S(2)}) %collective-permute-start.12) | collective-permute-done | bytes 270368 | tf_op jit(solution)/shard_map/ppermute | solution.py:37
  26.8 0.4 collective-permute-done.7.refs_3_
  27.2 0.4 collective-permute-done.6.refs_2_
  27.6 0.0 copy-done
  27.6 1.9 %shard_map.127 = (bf16[64,4480]{1,0:T(8,128)(2,1)S(1)}, bf16[64,4480]{1,0:T(8,128)(2,1)S(1)}) custom-call(bf16[32,4224]{1,0:T(8,128)(2,1)S(1)} %collective-permute-done.4.refs_0_, bf16[32,4224]{1,0:T(8,128)(2,1)S(1)} %collective-permute-done.5.refs_1_, bf16[32,4224]{1,0:T(8,128)(2,1)S(1)} %collective-permute-done.6.refs_2_, ...), custom_call_target="tpu_custom_call" | custom-call | flops 4000000000 | bytes 9437184 | tf_op jit(solution)/shard_map/pallas_call | solution.py:45
  29.6 0.2 collective-permute-start.14
  29.8 1.9 %shard_map.128 = (bf16[64,4480]{1,0:T(8,128)(2,1)S(1)}, bf16[64,4480]{1,0:T(8,128)(2,1)S(1)}) custom-call(bf16[32,4224]{1,0:T(8,128)(2,1)S(1)} %shard_map.124.refs_0_, bf16[32,4224]{1,0:T(8,128)(2,1)S(1)} %shard_map.126.refs_1_, bf16[32,4224]{1,0:T(8,128)(2,1)S(1)} %collective-permute-done.8.refs_2_, bf16[32,4224]{1,0:T(8,128)(2,1)S(1)} %collective-permute-done.12.refs_3_, ...), custom_call_target="tpu_custom_call" | custom-call | flops 4000000000 | bytes 9437184 | tf_op jit(solution)/shard_map/pallas_call | solution.py:45
  31.7 0.4 collective-permute-start.13
  32.1 0.0 collective-permute-done.14.refs_1_
  32.1 0.3 shard_map.130
  32.5 1.6 %collective-permute-start.15 = (bf16[32,4480]{1,0:T(8,128)(2,1)S(1)}, bf16[32,4480]{1,0:T(8,128)(2,1)S(1)}, u32[]{:S(2)}, u32[]{:S(2)}) collective-permute-start(bf16[32,4480]{1,0:T(8,128)(2,1)S(1)} %get-tuple-element.62), channel_id=1, source_target_pairs={{0,2},{1,3},{2,0},{3,1},{4,6},{5,7},{6,4},{7,5},{8,10},{9,11},{10,... | collective-permute-start | bytes 860168 | tf_op jit(solution)/shard_map/ppermute | solution.py:37
  34.1 1.5 %collective-permute-start.16 = (bf16[32,4480]{1,0:T(8,128)(2,1)S(1)}, bf16[32,4480]{1,0:T(8,128)(2,1)S(1)}, u32[]{:S(2)}, u32[]{:S(2)}) collective-permute-start(bf16[32,4480]{1,0:T(8,128)(2,1)S(1)} %get-tuple-element.63), channel_id=1, source_target_pairs={{0,4},{1,5},{2,6},{3,7},{4,0},{5,1},{6,2},{7,3},{8,12},{9,13},{10,... | collective-permute-start | bytes 860168 | tf_op jit(solution)/shard_map/ppermute | solution.py:37
  35.6 0.0 collective-permute-done.13.refs_1_
  35.6 0.3 shard_map.129
  35.9 0.7 %collective-permute-start.22 = (bf16[8,4480]{1,0:T(8,128)(2,1)S(1)}, bf16[8,4480]{1,0:T(8,128)(2,1)S(1)}, u32[]{:S(2)}, u32[]{:S(2)}) collective-permute-start(bf16[8,4480]{1,0:T(8,128)(2,1)S(1)} %get-tuple-element.74), channel_id=1, source_target_pairs={{0,8},{1,9},{2,10},{3,11},{4,12},{5,13},{6,14},{7,15},{8,0},{9,1},... | collective-permute-start | bytes 215048 | tf_op jit(solution)/shard_map/ppermute | solution.py:37
  36.6 2.5 %collective-permute-start.21 = (bf16[8,4480]{1,0:T(8,128)(2,1)S(1)}, bf16[8,4480]{1,0:T(8,128)(2,1)S(1)}, u32[]{:S(2)}, u32[]{:S(2)}) collective-permute-start(bf16[8,4480]{1,0:T(8,128)(2,1)S(1)} %get-tuple-element.72), channel_id=1, source_target_pairs={{0,24},{1,25},{2,26},{3,27},{4,28},{5,29},{6,30},{7,31},{8,16},{9,... | collective-permute-start | bytes 215048 | tf_op jit(solution)/shard_map/ppermute | solution.py:37
  39.1 0.4 collective-permute-start.20
  39.4 2.0 %collective-permute-done.15.refs_1_ = bf16[32,4480]{1,0:T(8,128)(2,1)S(1)} collective-permute-done((bf16[32,4480]{1,0:T(8,128)(2,1)S(1)}, bf16[32,4480]{1,0:T(8,128)(2,1)S(1)}, u32[]{:S(2)}, u32[]{:S(2)}) %collective-permute-start.15) | collective-permute-done | bytes 286752 | tf_op jit(solution)/shard_map/ppermute | solution.py:37
  41.4 1.2 %collective-permute-done.16.refs_2_ = bf16[32,4480]{1,0:T(8,128)(2,1)S(1)} collective-permute-done((bf16[32,4480]{1,0:T(8,128)(2,1)S(1)}, bf16[32,4480]{1,0:T(8,128)(2,1)S(1)}, u32[]{:S(2)}, u32[]{:S(2)}) %collective-permute-start.16) | collective-permute-done | bytes 286752 | tf_op jit(solution)/shard_map/ppermute | solution.py:37
  42.6 0.2 shard_map.131
  42.9 1.7 %collective-permute-start.17 = (bf16[8,4480]{1,0:T(8,128)(2,1)S(1)}, bf16[8,4480]{1,0:T(8,128)(2,1)S(1)}, u32[]{:S(2)}, u32[]{:S(2)}) collective-permute-start(bf16[8,4480]{1,0:T(8,128)(2,1)S(1)} %get-tuple-element.65), channel_id=1, source_target_pairs={{0,16},{1,17},{2,18},{3,19},{4,20},{5,21},{6,22},{7,23},{8,24},{9,... | collective-permute-start | bytes 215048 | tf_op jit(solution)/shard_map/ppermute | solution.py:37
  44.6 1.3 %collective-permute-start.18 = (bf16[8,4480]{1,0:T(8,128)(2,1)S(1)}, bf16[8,4480]{1,0:T(8,128)(2,1)S(1)}, u32[]{:S(2)}, u32[]{:S(2)}) collective-permute-start(bf16[8,4480]{1,0:T(8,128)(2,1)S(1)} %get-tuple-element.66), channel_id=1, source_target_pairs={{0,24},{1,25},{2,26},{3,27},{4,28},{5,29},{6,30},{7,31},{8,16},{9,... | collective-permute-start | bytes 215048 | tf_op jit(solution)/shard_map/ppermute | solution.py:37
  45.9 0.0 collective-permute-done.22.refs_3_
  45.9 0.5 collective-permute-start.19
  46.4 0.0 collective-permute-done.21.refs_2_
  46.4 0.5 collective-permute-done.20.refs_1_
  47.0 0.1 shard_map.133
  47.1 1.0 %collective-permute-start.23 = (bf16[8,4480]{1,0:T(8,128)(2,1)S(1)}, bf16[8,4480]{1,0:T(8,128)(2,1)S(1)}, u32[]{:S(2)}, u32[]{:S(2)}) collective-permute-start(bf16[8,4480]{1,0:T(8,128)(2,1)S(1)} %shard_map.133), channel_id=1, source_target_pairs={{0,6},{1,7},{2,4},{3,5},{4,2},{5,3},{6,0},{7,1},{8,14},{9,15},{10,... | collective-permute-start | bytes 215048 | tf_op jit(solution)/shard_map/ppermute | solution.py:37
  48.1 3.1 %collective-permute-done.17.refs_1_ = bf16[8,4480]{1,0:T(8,128)(2,1)S(1)} collective-permute-done((bf16[8,4480]{1,0:T(8,128)(2,1)S(1)}, bf16[8,4480]{1,0:T(8,128)(2,1)S(1)}, u32[]{:S(2)}, u32[]{:S(2)}) %collective-permute-start.17) | collective-permute-done | bytes 71712 | tf_op jit(solution)/shard_map/ppermute | solution.py:37
  51.2 0.0 collective-permute-done.18.refs_2_
  51.2 0.3 collective-permute-done.19.refs_3_
  51.6 0.1 shard_map.132.refs_0_
  51.7 0.7 %collective-permute-done.23.refs_1_ = bf16[8,4480]{1,0:T(8,128)(2,1)S(1)} collective-permute-done((bf16[8,4480]{1,0:T(8,128)(2,1)S(1)}, bf16[8,4480]{1,0:T(8,128)(2,1)S(1)}, u32[]{:S(2)}, u32[]{:S(2)}) %collective-permute-start.23) | collective-permute-done | bytes 71712 | tf_op jit(solution)/shard_map/ppermute | solution.py:37
  52.4 0.7 %shard_map.134 = (bf16[8,4096]{1,0:T(8,128)(2,1)}, bf16[8,256]{1,0:T(8,128)(2,1)}) custom-call(bf16[8,4480]{1,0:T(8,128)(2,1)S(1)} %shard_map.132.refs_0_, bf16[8,4480]{1,0:T(8,128)(2,1)S(1)} %collective-permute-done.23.refs_1_), custom_call_target="tpu_custom_call" | custom-call | flops 1 | bytes 1 | tf_op jit(solution)/shard_map/pallas_call | solution.py:45
  (2 shorter events, 0.0 us)
Async XLA Ops:
  1.7 11.0 %collective-permute-start.1 = (bf16[8,4224]{1,0:T(8,128)(2,1)S(1)}, bf16[8,4224]{1,0:T(8,128)(2,1)S(1)}, u32[]{:S(2)}, u32[]{:S(2)}) collective-permute-start(bf16[8,4224]{1,0:T(8,128)(2,1)S(1)} %shard_map.122.refs_0_), channel_id=1, source_target_pairs={{0,6},{1,7},{2,4},{3,5},{4,2},{5,3},{6,0},{7,1},{8,14},{9,15},{10,... | collective-permute-start | bytes 202760 | tf_op jit(solution)/shard_map/ppermute | solution.py:37
  5.7 7.1 %collective-permute-start.2 = (bf16[8,4224]{1,0:T(8,128)(2,1)S(1)}, bf16[8,4224]{1,0:T(8,128)(2,1)S(1)}, u32[]{:S(2)}, u32[]{:S(2)}) collective-permute-start(bf16[8,4224]{1,0:T(8,128)(2,1)S(1)} %shard_map.122.refs_0_), channel_id=1, source_target_pairs={{0,16},{1,17},{2,18},{3,19},{4,20},{5,21},{6,22},{7,23},{8,24},{9,... | collective-permute-start | bytes 202760 | tf_op jit(solution)/shard_map/ppermute | solution.py:37
  8.3 6.2 %collective-permute-start.3 = (bf16[8,4224]{1,0:T(8,128)(2,1)S(1)}, bf16[8,4224]{1,0:T(8,128)(2,1)S(1)}, u32[]{:S(2)}, u32[]{:S(2)}) collective-permute-start(bf16[8,4224]{1,0:T(8,128)(2,1)S(1)} %shard_map.122.refs_0_), channel_id=1, source_target_pairs={{0,24},{1,25},{2,26},{3,27},{4,28},{5,29},{6,30},{7,31},{8,16},{9,... | collective-permute-start | bytes 202760 | tf_op jit(solution)/shard_map/ppermute | solution.py:37
  9.6 5.0 %collective-permute-start = (bf16[8,4224]{1,0:T(8,128)(2,1)S(1)}, bf16[8,4224]{1,0:T(8,128)(2,1)S(1)}, u32[]{:S(2)}, u32[]{:S(2)}) collective-permute-start(bf16[8,4224]{1,0:T(8,128)(2,1)S(1)} %shard_map.122.refs_0_), channel_id=1, source_target_pairs={{0,8},{1,9},{2,10},{3,11},{4,12},{5,13},{6,14},{7,15},{8,0},{9,1},... | collective-permute-start | bytes 202760 | tf_op jit(solution)/shard_map/ppermute | solution.py:37
  14.6 10.7 %collective-permute-start.5 = (bf16[32,4224]{1,0:T(8,128)(2,1)S(1)}, bf16[32,4224]{1,0:T(8,128)(2,1)S(1)}, u32[]{:S(2)}, u32[]{:S(2)}) collective-permute-start(bf16[32,4224]{1,0:T(8,128)(2,1)S(1)} %shard_map.124.refs_0_), channel_id=1, source_target_pairs={{0,4},{1,5},{2,6},{3,7},{4,0},{5,1},{6,2},{7,3},{8,12},{9,13},{10,... | collective-permute-start | bytes 811016 | tf_op jit(solution)/shard_map/ppermute | solution.py:37
  15.2 10.6 %collective-permute-start.4 = (bf16[32,4224]{1,0:T(8,128)(2,1)S(1)}, bf16[32,4224]{1,0:T(8,128)(2,1)S(1)}, u32[]{:S(2)}, u32[]{:S(2)}) collective-permute-start(bf16[32,4224]{1,0:T(8,128)(2,1)S(1)} %shard_map.124.refs_0_), channel_id=1, source_target_pairs={{0,2},{1,3},{2,0},{3,1},{4,6},{5,7},{6,4},{7,5},{8,10},{9,11},{10,... | collective-permute-start | bytes 811016 | tf_op jit(solution)/shard_map/ppermute | solution.py:37
  15.7 8.0 %collective-permute-start.9 = (bf16[8,4224]{1,0:T(8,128)(2,1)S(1)}, bf16[8,4224]{1,0:T(8,128)(2,1)S(1)}, u32[]{:S(2)}, u32[]{:S(2)}) collective-permute-start(bf16[8,4224]{1,0:T(8,128)(2,1)S(1)} %collective-permute-done.1.refs_0_), channel_id=1, source_target_pairs={{0,8},{1,9},{2,10},{3,11},{4,12},{5,13},{6,14},{7,15},{8,0},{9,1},... | collective-permute-start | bytes 202760 | tf_op jit(solution)/shard_map/ppermute | solution.py:37
  16.5 7.4 %collective-permute-start.10 = (bf16[8,4224]{1,0:T(8,128)(2,1)S(1)}, bf16[8,4224]{1,0:T(8,128)(2,1)S(1)}, u32[]{:S(2)}, u32[]{:S(2)}) collective-permute-start(bf16[8,4224]{1,0:T(8,128)(2,1)S(1)} %collective-permute-done.1.refs_0_), channel_id=1, source_target_pairs={{0,16},{1,17},{2,18},{3,19},{4,20},{5,21},{6,22},{7,23},{8,24},{9,... | collective-permute-start | bytes 202760 | tf_op jit(solution)/shard_map/ppermute | solution.py:37
  19.0 6.2 %collective-permute-start.11 = (bf16[8,4224]{1,0:T(8,128)(2,1)S(1)}, bf16[8,4224]{1,0:T(8,128)(2,1)S(1)}, u32[]{:S(2)}, u32[]{:S(2)}) collective-permute-start(bf16[8,4224]{1,0:T(8,128)(2,1)S(1)} %collective-permute-done.1.refs_0_), channel_id=1, source_target_pairs={{0,24},{1,25},{2,26},{3,27},{4,28},{5,29},{6,30},{7,31},{8,16},{9,... | collective-permute-start | bytes 202760 | tf_op jit(solution)/shard_map/ppermute | solution.py:37
  20.1 7.5 %copy-start = (bf16[384,4096]{1,0:T(8,128)(2,1)S(1)}, bf16[384,4096]{1,0:T(8,128)(2,1)}, u32[]{:S(2)}) copy-start(bf16[384,4096]{1,0:T(8,128)(2,1)} %refs_8_.3) | copy-start | bytes 9437188
  23.8 2.1 %collective-permute-start.8 = (bf16[32,4224]{1,0:T(8,128)(2,1)S(1)}, bf16[32,4224]{1,0:T(8,128)(2,1)S(1)}, u32[]{:S(2)}, u32[]{:S(2)}) collective-permute-start(bf16[32,4224]{1,0:T(8,128)(2,1)S(1)} %shard_map.124.refs_0_), channel_id=1, source_target_pairs={{0,1},{1,0},{2,3},{3,2},{4,5},{5,4},{6,7},{7,6},{8,9},{9,8},{10,11... | collective-permute-start | bytes 811016 | tf_op jit(solution)/shard_map/ppermute | solution.py:37
  25.2 1.6 %collective-permute-start.12 = (bf16[32,4224]{1,0:T(8,128)(2,1)S(1)}, bf16[32,4224]{1,0:T(8,128)(2,1)S(1)}, u32[]{:S(2)}, u32[]{:S(2)}) collective-permute-start(bf16[32,4224]{1,0:T(8,128)(2,1)S(1)} %shard_map.126.refs_1_), channel_id=1, source_target_pairs={{0,1},{1,0},{2,3},{3,2},{4,5},{5,4},{6,7},{7,6},{8,9},{9,8},{10,11... | collective-permute-start | bytes 811016 | tf_op jit(solution)/shard_map/ppermute | solution.py:37
  25.3 1.9 %collective-permute-start.7 = (bf16[32,4224]{1,0:T(8,128)(2,1)S(1)}, bf16[32,4224]{1,0:T(8,128)(2,1)S(1)}, u32[]{:S(2)}, u32[]{:S(2)}) collective-permute-start(bf16[32,4224]{1,0:T(8,128)(2,1)S(1)} %collective-permute-done.5.refs_1_), channel_id=1, source_target_pairs={{0,1},{1,0},{2,3},{3,2},{4,5},{5,4},{6,7},{7,6},{8,9},{9,8},{10,11... | collective-permute-start | bytes 811016 | tf_op jit(solution)/shard_map/ppermute | solution.py:37
  25.8 1.8 %collective-permute-start.6 = (bf16[32,4224]{1,0:T(8,128)(2,1)S(1)}, bf16[32,4224]{1,0:T(8,128)(2,1)S(1)}, u32[]{:S(2)}, u32[]{:S(2)}) collective-permute-start(bf16[32,4224]{1,0:T(8,128)(2,1)S(1)} %collective-permute-done.4.refs_0_), channel_id=1, source_target_pairs={{0,1},{1,0},{2,3},{3,2},{4,5},{5,4},{6,7},{7,6},{8,9},{9,8},{10,11... | collective-permute-start | bytes 811016 | tf_op jit(solution)/shard_map/ppermute | solution.py:37
  29.6 2.6 %collective-permute-start.14 = (bf16[64,4480]{1,0:T(8,128)(2,1)S(1)}, bf16[64,4480]{1,0:T(8,128)(2,1)S(1)}, u32[]{:S(2)}, u32[]{:S(2)}) collective-permute-start(bf16[64,4480]{1,0:T(8,128)(2,1)S(1)} %get-tuple-element.61), channel_id=1, source_target_pairs={{0,1},{1,0},{2,3},{3,2},{4,5},{5,4},{6,7},{7,6},{8,9},{9,8},{10,11... | collective-permute-start | bytes 1720328 | tf_op jit(solution)/shard_map/ppermute | solution.py:37
  31.7 3.9 %collective-permute-start.13 = (bf16[64,4480]{1,0:T(8,128)(2,1)S(1)}, bf16[64,4480]{1,0:T(8,128)(2,1)S(1)}, u32[]{:S(2)}, u32[]{:S(2)}) collective-permute-start(bf16[64,4480]{1,0:T(8,128)(2,1)S(1)} %get-tuple-element.59), channel_id=1, source_target_pairs={{0,1},{1,0},{2,3},{3,2},{4,5},{5,4},{6,7},{7,6},{8,9},{9,8},{10,11... | collective-permute-start | bytes 1720328 | tf_op jit(solution)/shard_map/ppermute | solution.py:37
  32.5 8.9 %collective-permute-start.15 = (bf16[32,4480]{1,0:T(8,128)(2,1)S(1)}, bf16[32,4480]{1,0:T(8,128)(2,1)S(1)}, u32[]{:S(2)}, u32[]{:S(2)}) collective-permute-start(bf16[32,4480]{1,0:T(8,128)(2,1)S(1)} %get-tuple-element.62), channel_id=1, source_target_pairs={{0,2},{1,3},{2,0},{3,1},{4,6},{5,7},{6,4},{7,5},{8,10},{9,11},{10,... | collective-permute-start | bytes 860168 | tf_op jit(solution)/shard_map/ppermute | solution.py:37
  34.1 8.6 %collective-permute-start.16 = (bf16[32,4480]{1,0:T(8,128)(2,1)S(1)}, bf16[32,4480]{1,0:T(8,128)(2,1)S(1)}, u32[]{:S(2)}, u32[]{:S(2)}) collective-permute-start(bf16[32,4480]{1,0:T(8,128)(2,1)S(1)} %get-tuple-element.63), channel_id=1, source_target_pairs={{0,4},{1,5},{2,6},{3,7},{4,0},{5,1},{6,2},{7,3},{8,12},{9,13},{10,... | collective-permute-start | bytes 860168 | tf_op jit(solution)/shard_map/ppermute | solution.py:37
  35.9 10.1 %collective-permute-start.22 = (bf16[8,4480]{1,0:T(8,128)(2,1)S(1)}, bf16[8,4480]{1,0:T(8,128)(2,1)S(1)}, u32[]{:S(2)}, u32[]{:S(2)}) collective-permute-start(bf16[8,4480]{1,0:T(8,128)(2,1)S(1)} %get-tuple-element.74), channel_id=1, source_target_pairs={{0,8},{1,9},{2,10},{3,11},{4,12},{5,13},{6,14},{7,15},{8,0},{9,1},... | collective-permute-start | bytes 215048 | tf_op jit(solution)/shard_map/ppermute | solution.py:37
  36.6 9.8 %collective-permute-start.21 = (bf16[8,4480]{1,0:T(8,128)(2,1)S(1)}, bf16[8,4480]{1,0:T(8,128)(2,1)S(1)}, u32[]{:S(2)}, u32[]{:S(2)}) collective-permute-start(bf16[8,4480]{1,0:T(8,128)(2,1)S(1)} %get-tuple-element.72), channel_id=1, source_target_pairs={{0,24},{1,25},{2,26},{3,27},{4,28},{5,29},{6,30},{7,31},{8,16},{9,... | collective-permute-start | bytes 215048 | tf_op jit(solution)/shard_map/ppermute | solution.py:37
  39.1 7.9 %collective-permute-start.20 = (bf16[8,4480]{1,0:T(8,128)(2,1)S(1)}, bf16[8,4480]{1,0:T(8,128)(2,1)S(1)}, u32[]{:S(2)}, u32[]{:S(2)}) collective-permute-start(bf16[8,4480]{1,0:T(8,128)(2,1)S(1)} %get-tuple-element.70), channel_id=1, source_target_pairs={{0,16},{1,17},{2,18},{3,19},{4,20},{5,21},{6,22},{7,23},{8,24},{9,... | collective-permute-start | bytes 215048 | tf_op jit(solution)/shard_map/ppermute | solution.py:37
  42.9 8.3 %collective-permute-start.17 = (bf16[8,4480]{1,0:T(8,128)(2,1)S(1)}, bf16[8,4480]{1,0:T(8,128)(2,1)S(1)}, u32[]{:S(2)}, u32[]{:S(2)}) collective-permute-start(bf16[8,4480]{1,0:T(8,128)(2,1)S(1)} %get-tuple-element.65), channel_id=1, source_target_pairs={{0,16},{1,17},{2,18},{3,19},{4,20},{5,21},{6,22},{7,23},{8,24},{9,... | collective-permute-start | bytes 215048 | tf_op jit(solution)/shard_map/ppermute | solution.py:37
  44.6 6.6 %collective-permute-start.18 = (bf16[8,4480]{1,0:T(8,128)(2,1)S(1)}, bf16[8,4480]{1,0:T(8,128)(2,1)S(1)}, u32[]{:S(2)}, u32[]{:S(2)}) collective-permute-start(bf16[8,4480]{1,0:T(8,128)(2,1)S(1)} %get-tuple-element.66), channel_id=1, source_target_pairs={{0,24},{1,25},{2,26},{3,27},{4,28},{5,29},{6,30},{7,31},{8,16},{9,... | collective-permute-start | bytes 215048 | tf_op jit(solution)/shard_map/ppermute | solution.py:37
  45.9 5.6 %collective-permute-start.19 = (bf16[8,4480]{1,0:T(8,128)(2,1)S(1)}, bf16[8,4480]{1,0:T(8,128)(2,1)S(1)}, u32[]{:S(2)}, u32[]{:S(2)}) collective-permute-start(bf16[8,4480]{1,0:T(8,128)(2,1)S(1)} %get-tuple-element.67), channel_id=1, source_target_pairs={{0,8},{1,9},{2,10},{3,11},{4,12},{5,13},{6,14},{7,15},{8,0},{9,1},... | collective-permute-start | bytes 215048 | tf_op jit(solution)/shard_map/ppermute | solution.py:37
  47.1 5.3 %collective-permute-start.23 = (bf16[8,4480]{1,0:T(8,128)(2,1)S(1)}, bf16[8,4480]{1,0:T(8,128)(2,1)S(1)}, u32[]{:S(2)}, u32[]{:S(2)}) collective-permute-start(bf16[8,4480]{1,0:T(8,128)(2,1)S(1)} %shard_map.133), channel_id=1, source_target_pairs={{0,6},{1,7},{2,4},{3,5},{4,2},{5,3},{6,0},{7,1},{8,14},{9,15},{10,... | collective-permute-start | bytes 215048 | tf_op jit(solution)/shard_map/ppermute | solution.py:37

commit v6 on v5

--- a/solution.py
+++ b/solution.py
@@ -298,14 +298,10 @@
     return call(functools.partial(sum_kernel, len(parts), width, own, last), shapes, parts, flops=flops)
 
 
-def stack_kernel(*refs):
-    stacked = jnp.concatenate([ref[...].astype(jnp.float32) for ref in refs[:-1]], axis=0)
+def stack_kernel(places, *refs):
+    blocks = dict(zip(places, refs))
+    stacked = jnp.concatenate([blocks[k][...].astype(jnp.float32) for k in range(len(places))], axis=0)
     refs[-1][...] = stacked.astype(jnp.bfloat16)
-
-
-def stack(parts):
-    rows, width = parts[0].shape
-    return call(stack_kernel, jax.ShapeDtypeStruct((len(parts) * rows, width), jnp.bfloat16), parts)
 
 
 def start_order(radix):
@@ -314,8 +310,16 @@
 
 def gather(block, levels, *ready):
     for stride, radix in reversed(levels):
-        arrived = {k: exchange(block, stride * k) for k in start_order(radix)}
-        block = stack([block] + [after(arrived[k], *ready) for k in range(1, radix)])
+        order = start_order(radix)
+        arrived = [exchange(block, stride * k) for k in order]
+        if ready:
+            arrived = lax.optimization_barrier((*arrived, *ready))[: len(order)]
+        rows, width = block.shape
+        block = call(
+            functools.partial(stack_kernel, [0] + order),
+            jax.ShapeDtypeStruct((radix * rows, width), jnp.bfloat16),
+            [block, *arrived],
+        )
     return block
 
 
@@ -352,14 +356,13 @@
     across = [exchange(block, corner)] if radix == 4 else []
     w_gate, w_up = keep(w_gate, w_up)
     weights = (w_gate, w_up, w_down)
-    base = gather(block, outer, w_gate, *across)
+    base = gather(block, outer, w_gate)
     sides = [1, 2] if radix == 4 else [1]
     chunks = [exchange(base, stride * k) for k in sides]
     sums = attend(after(query, base), k_cache, v_cache, cache_len, levels)
     last_chunk = [gather(a, outer, sums[0]) for a in across]
-    chunks = [after(chunk, sums[0]) for chunk in chunks]
+    chunks = lax.optimization_barrier((*chunks, sums[0], *last_chunk))[: len(chunks)]
     others = [exchange(c, 1) for c in (*chunks, base, *last_chunk)]
-    others = lax.optimization_barrier(others)
     count = len(sides)
     near, far = apply_expert(chunks, others[:count], sides, sums, weights)
     pieces = summed([near, exchange(far, 1)], [rows] * count, width, own)
@@ -372,7 +375,7 @@
     pieces = summed(parts, cut, width, own)
     last = scatter(pieces, outer, width, own)
     if across:
-        corner_parts = [after(part, pieces[0]) for part in corner_parts]
+        corner_parts = lax.optimization_barrier((*corner_parts, pieces[0]))[:-1]
         (corner_sum,) = summed(corner_parts, [rows_dev], width, own)
         last.append(exchange(corner_sum, corner))
     if across:

time: 53.3 us -> 50.4 us (0.946)
  waiting for transfers between devices: 12.8 us -> 9.56 us
    ppermute x24, waiting for transfers between devices: 12.8 us -> 9.56 us  [exchange(): return lax.ppermute(value, 'ffn', [(i, i ^ distance) for i in range(size)])]
  transfers between devices with their start and end apart: 24 -> 24, of which waited for: 12 -> 9; matrix products, arithmetic and copies ran while one was open for 0% -> 0% of each run, Pallas kernels for 18% -> 23%
where the time goes in v6:
time: 50.4 us; the launch traced here: 50.2 us
  starting transfers between devices  26.6 us (53%)
  Pallas kernels  13.3 us (26%)
  waiting for transfers between devices  9.56 us (19%)
  between operations  0.78 us (2%)
    ppermute x24, starting transfers between devices, exchange(): return lax.ppermute(value, 'ffn', [(i, i ^ distance) for i in range(size)])  26.6 us
    pallas_call x13, Pallas kernels, call(): pl.pallas_call(body, out_shape=out_shape, in_specs=in_specs or [VMEM] * l...  13.3 us
    ppermute x24, waiting for transfers between devices, exchange(): return lax.ppermute(value, 'ffn', [(i, i ^ distance) for i in range(size)])  9.56 us
  transfers between devices with their start and end apart: 24, of which 9 were waited for; matrix products, arithmetic and copies ran while one was open for 0% of the time, Pallas kernels for 23%

profile of v6, /device:TPU:0, one launch (start us, length us, event | category | flops | bytes accessed | tf_op | source)
XLA Modules:
  0.0 50.2 jit_solution(4548936437973746865)
XLA Ops:
  0.6 1.1 %shard_map.122.refs_0_ = bf16[8,4224]{1,0:T(8,128)(2,1)S(1)} custom-call(bf16[8,4096]{1,0:T(8,128)(2,1)} %tokens_hbm.1, f32[1,4096]{1,0:T(1,128)} %bitcast.6, s32[8,8]{1,0:T(8,128)} %routes_hbm.1, f32[8,8]{1,0:T(8,128)} %scores_hbm.1), custom_call_target="tpu_custom_call" | custom-call | flops 1 | bytes 1 | tf_op jit(solution)/shard_map/pallas_call | solution.py:45
  1.7 4.1 %collective-permute-start = (bf16[8,4224]{1,0:T(8,128)(2,1)S(1)}, bf16[8,4224]{1,0:T(8,128)(2,1)S(1)}, u32[]{:S(2)}, u32[]{:S(2)}) collective-permute-start(bf16[8,4224]{1,0:T(8,128)(2,1)S(1)} %shard_map.122.refs_0_), channel_id=1, source_target_pairs={{0,16},{1,17},{2,18},{3,19},{4,20},{5,21},{6,22},{7,23},{8,24},{9,... | collective-permute-start | bytes 202760 | tf_op jit(solution)/shard_map/ppermute | solution.py:37
  5.8 1.3 %collective-permute-start.1 = (bf16[8,4224]{1,0:T(8,128)(2,1)S(1)}, bf16[8,4224]{1,0:T(8,128)(2,1)S(1)}, u32[]{:S(2)}, u32[]{:S(2)}) collective-permute-start(bf16[8,4224]{1,0:T(8,128)(2,1)S(1)} %shard_map.122.refs_0_), channel_id=1, source_target_pairs={{0,24},{1,25},{2,26},{3,27},{4,28},{5,29},{6,30},{7,31},{8,16},{9,... | collective-permute-start | bytes 202760 | tf_op jit(solution)/shard_map/ppermute | solution.py:37
  7.2 0.2 collective-permute-start.2
  7.4 2.4 %collective-permute-start.5 = (bf16[8,4224]{1,0:T(8,128)(2,1)S(1)}, bf16[8,4224]{1,0:T(8,128)(2,1)S(1)}, u32[]{:S(2)}, u32[]{:S(2)}) collective-permute-start(bf16[8,4224]{1,0:T(8,128)(2,1)S(1)} %shard_map.122.refs_0_), channel_id=1, source_target_pairs={{0,6},{1,7},{2,4},{3,5},{4,2},{5,3},{6,0},{7,1},{8,14},{9,15},{10,... | collective-permute-start | bytes 202760 | tf_op jit(solution)/shard_map/ppermute | solution.py:37
  9.8 2.9 %shard_map.123 = (bf16[4096,384]{1,0:T(8,128)(2,1)S(1)}, bf16[4096,384]{1,0:T(8,128)(2,1)S(1)}) custom-call(bf16[4096,384]{1,0:T(8,128)(2,1)} %refs_0_.1, bf16[4096,384]{1,0:T(8,128)(2,1)} %refs_1_.1), custom_call_target="tpu_custom_call" | custom-call | flops 4000000000 | bytes 1 | tf_op jit(solution)/shard_map/pallas_call | solution.py:45
  12.7 0.0 collective-permute-done.refs_1_
  12.7 0.0 collective-permute-done.1.refs_2_
  12.7 0.0 collective-permute-done.2.refs_3_
  12.8 1.1 %collective-permute-start.3 = (bf16[32,4224]{1,0:T(8,128)(2,1)S(1)}, bf16[32,4224]{1,0:T(8,128)(2,1)S(1)}, u32[]{:S(2)}, u32[]{:S(2)}) collective-permute-start(bf16[32,4224]{1,0:T(8,128)(2,1)S(1)} %shard_map.124.refs_0_), channel_id=1, source_target_pairs={{0,2},{1,3},{2,0},{3,1},{4,6},{5,7},{6,4},{7,5},{8,10},{9,11},{10,... | collective-permute-start | bytes 811016 | tf_op jit(solution)/shard_map/ppermute | solution.py:37
  13.8 1.5 %collective-permute-start.4 = (bf16[32,4224]{1,0:T(8,128)(2,1)S(1)}, bf16[32,4224]{1,0:T(8,128)(2,1)S(1)}, u32[]{:S(2)}, u32[]{:S(2)}) collective-permute-start(bf16[32,4224]{1,0:T(8,128)(2,1)S(1)} %shard_map.124.refs_0_), channel_id=1, source_target_pairs={{0,4},{1,5},{2,6},{3,7},{4,0},{5,1},{6,2},{7,3},{8,12},{9,13},{10,... | collective-permute-start | bytes 811016 | tf_op jit(solution)/shard_map/ppermute | solution.py:37
  15.4 0.0 collective-permute-done.5.refs_0_
  15.4 2.7 %collective-permute-start.6 = (bf16[8,4224]{1,0:T(8,128)(2,1)S(1)}, bf16[8,4224]{1,0:T(8,128)(2,1)S(1)}, u32[]{:S(2)}, u32[]{:S(2)}) collective-permute-start(bf16[8,4224]{1,0:T(8,128)(2,1)S(1)} %collective-permute-done.5.refs_0_), channel_id=1, source_target_pairs={{0,16},{1,17},{2,18},{3,19},{4,20},{5,21},{6,22},{7,23},{8,24},{9,... | collective-permute-start | bytes 202760 | tf_op jit(solution)/shard_map/ppermute | solution.py:37
  18.1 0.6 %collective-permute-start.7 = (bf16[8,4224]{1,0:T(8,128)(2,1)S(1)}, bf16[8,4224]{1,0:T(8,128)(2,1)S(1)}, u32[]{:S(2)}, u32[]{:S(2)}) collective-permute-start(bf16[8,4224]{1,0:T(8,128)(2,1)S(1)} %collective-permute-done.5.refs_0_), channel_id=1, source_target_pairs={{0,24},{1,25},{2,26},{3,27},{4,28},{5,29},{6,30},{7,31},{8,16},{9,... | collective-permute-start | bytes 202760 | tf_op jit(solution)/shard_map/ppermute | solution.py:37
  18.7 0.3 collective-permute-start.8
  18.9 0.0 copy-start
  18.9 3.6 %shard_map.125 = (bf16[128,384]{1,0:T(8,128)(2,1)S(1)}, bf16[128,384]{1,0:T(8,128)(2,1)S(1)}) custom-call(s32[8]{0:T(128)} %length_hbm.1, bf16[512,128]{1,0:T(8,128)(2,1)} %bitcast.7, bf16[8,128,512]{2,1,0:T(8,128)(2,1)} %key_hbm.1, bf16[8,128,512]{2,1,0:T(8,128)(2,1)} %value_hbm.1), custom_call_target="tpu_custom_call" | custom-call | flops 4000000000 | bytes 1 | tf_op jit(solution)/shard_map/pallas_call | solution.py:45
  22.6 0.0 collective-permute-done.6.refs_1_
  22.6 1.6 %collective-permute-done.7.refs_2_ = bf16[8,4224]{1,0:T(8,128)(2,1)S(1)} collective-permute-done((bf16[8,4224]{1,0:T(8,128)(2,1)S(1)}, bf16[8,4224]{1,0:T(8,128)(2,1)S(1)}, u32[]{:S(2)}, u32[]{:S(2)}) %collective-permute-start.7) | collective-permute-done | bytes 67616 | tf_op jit(solution)/shard_map/ppermute | solution.py:37
  24.2 0.0 collective-permute-done.8.refs_3_
  24.2 0.0 collective-permute-done.3.refs_0_
  24.2 0.0 collective-permute-done.4.refs_1_
  24.2 0.1 collective-permute-start.10
  24.3 0.5 collective-permute-start.9
  24.8 0.1 collective-permute-start.11
  24.9 0.4 collective-permute-start.12
  25.3 0.5 %collective-permute-done.10.refs_3_ = bf16[32,4224]{1,0:T(8,128)(2,1)S(1)} collective-permute-done((bf16[32,4224]{1,0:T(8,128)(2,1)S(1)}, bf16[32,4224]{1,0:T(8,128)(2,1)S(1)}, u32[]{:S(2)}, u32[]{:S(2)}) %collective-permute-start.10) | collective-permute-done | bytes 270368 | tf_op jit(solution)/shard_map/ppermute | solution.py:37
  25.8 0.4 collective-permute-done.9.refs_2_
  26.2 0.0 copy-done
  26.2 1.9 %shard_map.127 = (bf16[64,4480]{1,0:T(8,128)(2,1)S(1)}, bf16[64,4480]{1,0:T(8,128)(2,1)S(1)}) custom-call(bf16[32,4224]{1,0:T(8,128)(2,1)S(1)} %collective-permute-done.3.refs_0_, bf16[32,4224]{1,0:T(8,128)(2,1)S(1)} %collective-permute-done.4.refs_1_, bf16[32,4224]{1,0:T(8,128)(2,1)S(1)} %collective-permute-done.9.refs_2_, ...), custom_call_target="tpu_custom_call" | custom-call | flops 4000000000 | bytes 9437184 | tf_op jit(solution)/shard_map/pallas_call | solution.py:45
  28.2 0.2 collective-permute-start.14
  28.4 0.0 collective-permute-done.11.refs_2_
  28.4 0.0 collective-permute-done.12.refs_3_
  28.4 1.9 %shard_map.128 = (bf16[64,4480]{1,0:T(8,128)(2,1)S(1)}, bf16[64,4480]{1,0:T(8,128)(2,1)S(1)}) custom-call(bf16[32,4224]{1,0:T(8,128)(2,1)S(1)} %shard_map.124.refs_0_, bf16[32,4224]{1,0:T(8,128)(2,1)S(1)} %shard_map.126.refs_1_, bf16[32,4224]{1,0:T(8,128)(2,1)S(1)} %collective-permute-done.11.refs_2_, bf16[32,4224]{1,0:T(8,128)(2,1)S(1)} %collective-permute-done.12.refs_3_, ...), custom_call_target="tpu_custom_call" | custom-call | flops 4000000000 | bytes 9437184 | tf_op jit(solution)/shard_map/pallas_call | solution.py:45
  30.3 0.4 collective-permute-start.13
  30.7 0.0 collective-permute-done.14.refs_1_
  30.7 0.3 shard_map.130
  31.1 0.6 %collective-permute-start.15 = (bf16[32,4480]{1,0:T(8,128)(2,1)S(1)}, bf16[32,4480]{1,0:T(8,128)(2,1)S(1)}, u32[]{:S(2)}, u32[]{:S(2)}) collective-permute-start(bf16[32,4480]{1,0:T(8,128)(2,1)S(1)} %get-tuple-element.54), channel_id=1, source_target_pairs={{0,2},{1,3},{2,0},{3,1},{4,6},{5,7},{6,4},{7,5},{8,10},{9,11},{10,... | collective-permute-start | bytes 860168 | tf_op jit(solution)/shard_map/ppermute | solution.py:37
  31.7 1.4 %collective-permute-start.16 = (bf16[32,4480]{1,0:T(8,128)(2,1)S(1)}, bf16[32,4480]{1,0:T(8,128)(2,1)S(1)}, u32[]{:S(2)}, u32[]{:S(2)}) collective-permute-start(bf16[32,4480]{1,0:T(8,128)(2,1)S(1)} %get-tuple-element.55), channel_id=1, source_target_pairs={{0,4},{1,5},{2,6},{3,7},{4,0},{5,1},{6,2},{7,3},{8,12},{9,13},{10,... | collective-permute-start | bytes 860168 | tf_op jit(solution)/shard_map/ppermute | solution.py:37
  33.0 0.0 collective-permute-done.13.refs_1_
  33.0 0.3 shard_map.129
  33.4 1.8 %collective-permute-start.20 = (bf16[8,4480]{1,0:T(8,128)(2,1)S(1)}, bf16[8,4480]{1,0:T(8,128)(2,1)S(1)}, u32[]{:S(2)}, u32[]{:S(2)}) collective-permute-start(bf16[8,4480]{1,0:T(8,128)(2,1)S(1)} %get-tuple-element.61), channel_id=1, source_target_pairs={{0,16},{1,17},{2,18},{3,19},{4,20},{5,21},{6,22},{7,23},{8,24},{9,... | collective-permute-start | bytes 215048 | tf_op jit(solution)/shard_map/ppermute | solution.py:37
  35.1 1.3 %collective-permute-start.21 = (bf16[8,4480]{1,0:T(8,128)(2,1)S(1)}, bf16[8,4480]{1,0:T(8,128)(2,1)S(1)}, u32[]{:S(2)}, u32[]{:S(2)}) collective-permute-start(bf16[8,4480]{1,0:T(8,128)(2,1)S(1)} %get-tuple-element.62), channel_id=1, source_target_pairs={{0,24},{1,25},{2,26},{3,27},{4,28},{5,29},{6,30},{7,31},{8,16},{9,... | collective-permute-start | bytes 215048 | tf_op jit(solution)/shard_map/ppermute | solution.py:37
  36.5 0.4 collective-permute-start.22
  36.9 3.1 %collective-permute-done.15.refs_1_ = bf16[32,4480]{1,0:T(8,128)(2,1)S(1)} collective-permute-done((bf16[32,4480]{1,0:T(8,128)(2,1)S(1)}, bf16[32,4480]{1,0:T(8,128)(2,1)S(1)}, u32[]{:S(2)}, u32[]{:S(2)}) %collective-permute-start.15) | collective-permute-done | bytes 286752 | tf_op jit(solution)/shard_map/ppermute | solution.py:37
  40.0 0.3 collective-permute-done.16.refs_2_
  40.3 0.2 shard_map.131
  40.5 2.0 %collective-permute-start.17 = (bf16[8,4480]{1,0:T(8,128)(2,1)S(1)}, bf16[8,4480]{1,0:T(8,128)(2,1)S(1)}, u32[]{:S(2)}, u32[]{:S(2)}) collective-permute-start(bf16[8,4480]{1,0:T(8,128)(2,1)S(1)} %get-tuple-element.57), channel_id=1, source_target_pairs={{0,16},{1,17},{2,18},{3,19},{4,20},{5,21},{6,22},{7,23},{8,24},{9,... | collective-permute-start | bytes 215048 | tf_op jit(solution)/shard_map/ppermute | solution.py:37
  42.6 0.9 %collective-permute-start.18 = (bf16[8,4480]{1,0:T(8,128)(2,1)S(1)}, bf16[8,4480]{1,0:T(8,128)(2,1)S(1)}, u32[]{:S(2)}, u32[]{:S(2)}) collective-permute-start(bf16[8,4480]{1,0:T(8,128)(2,1)S(1)} %get-tuple-element.58), channel_id=1, source_target_pairs={{0,24},{1,25},{2,26},{3,27},{4,28},{5,29},{6,30},{7,31},{8,16},{9,... | collective-permute-start | bytes 215048 | tf_op jit(solution)/shard_map/ppermute | solution.py:37
  43.5 0.0 collective-permute-done.20.refs_1_
  43.5 0.6 %collective-permute-start.19 = (bf16[8,4480]{1,0:T(8,128)(2,1)S(1)}, bf16[8,4480]{1,0:T(8,128)(2,1)S(1)}, u32[]{:S(2)}, u32[]{:S(2)}) collective-permute-start(bf16[8,4480]{1,0:T(8,128)(2,1)S(1)} %get-tuple-element.59), channel_id=1, source_target_pairs={{0,8},{1,9},{2,10},{3,11},{4,12},{5,13},{6,14},{7,15},{8,0},{9,1},... | collective-permute-start | bytes 215048 | tf_op jit(solution)/shard_map/ppermute | solution.py:37
  44.1 0.0 collective-permute-done.21.refs_2_
  44.1 0.0 collective-permute-done.22.refs_3_
  44.1 0.1 shard_map.133
  44.2 1.5 %collective-permute-start.23 = (bf16[8,4480]{1,0:T(8,128)(2,1)S(1)}, bf16[8,4480]{1,0:T(8,128)(2,1)S(1)}, u32[]{:S(2)}, u32[]{:S(2)}) collective-permute-start(bf16[8,4480]{1,0:T(8,128)(2,1)S(1)} %shard_map.133), channel_id=1, source_target_pairs={{0,6},{1,7},{2,4},{3,5},{4,2},{5,3},{6,0},{7,1},{8,14},{9,15},{10,... | collective-permute-start | bytes 215048 | tf_op jit(solution)/shard_map/ppermute | solution.py:37
  45.7 2.0 %collective-permute-done.17.refs_1_ = bf16[8,4480]{1,0:T(8,128)(2,1)S(1)} collective-permute-done((bf16[8,4480]{1,0:T(8,128)(2,1)S(1)}, bf16[8,4480]{1,0:T(8,128)(2,1)S(1)}, u32[]{:S(2)}, u32[]{:S(2)}) %collective-permute-start.17) | collective-permute-done | bytes 71712 | tf_op jit(solution)/shard_map/ppermute | solution.py:37
  47.7 1.1 %collective-permute-done.18.refs_2_ = bf16[8,4480]{1,0:T(8,128)(2,1)S(1)} collective-permute-done((bf16[8,4480]{1,0:T(8,128)(2,1)S(1)}, bf16[8,4480]{1,0:T(8,128)(2,1)S(1)}, u32[]{:S(2)}, u32[]{:S(2)}) %collective-permute-start.18) | collective-permute-done | bytes 71712 | tf_op jit(solution)/shard_map/ppermute | solution.py:37
  48.9 0.3 collective-permute-done.19.refs_3_
  49.1 0.1 shard_map.132.refs_0_
  49.3 0.2 collective-permute-done.23.refs_1_
  49.5 0.7 %shard_map.134 = (bf16[8,4096]{1,0:T(8,128)(2,1)}, bf16[8,256]{1,0:T(8,128)(2,1)}) custom-call(bf16[8,4480]{1,0:T(8,128)(2,1)S(1)} %shard_map.132.refs_0_, bf16[8,4480]{1,0:T(8,128)(2,1)S(1)} %collective-permute-done.23.refs_1_), custom_call_target="tpu_custom_call" | custom-call | flops 1 | bytes 1 | tf_op jit(solution)/shard_map/pallas_call | solution.py:45
  (2 shorter events, 0.0 us)
Async XLA Ops:
  1.7 11.0 %collective-permute-start = (bf16[8,4224]{1,0:T(8,128)(2,1)S(1)}, bf16[8,4224]{1,0:T(8,128)(2,1)S(1)}, u32[]{:S(2)}, u32[]{:S(2)}) collective-permute-start(bf16[8,4224]{1,0:T(8,128)(2,1)S(1)} %shard_map.122.refs_0_), channel_id=1, source_target_pairs={{0,16},{1,17},{2,18},{3,19},{4,20},{5,21},{6,22},{7,23},{8,24},{9,... | collective-permute-start | bytes 202760 | tf_op jit(solution)/shard_map/ppermute | solution.py:37
  5.8 6.9 %collective-permute-start.1 = (bf16[8,4224]{1,0:T(8,128)(2,1)S(1)}, bf16[8,4224]{1,0:T(8,128)(2,1)S(1)}, u32[]{:S(2)}, u32[]{:S(2)}) collective-permute-start(bf16[8,4224]{1,0:T(8,128)(2,1)S(1)} %shard_map.122.refs_0_), channel_id=1, source_target_pairs={{0,24},{1,25},{2,26},{3,27},{4,28},{5,29},{6,30},{7,31},{8,16},{9,... | collective-permute-start | bytes 202760 | tf_op jit(solution)/shard_map/ppermute | solution.py:37
  7.2 5.6 %collective-permute-start.2 = (bf16[8,4224]{1,0:T(8,128)(2,1)S(1)}, bf16[8,4224]{1,0:T(8,128)(2,1)S(1)}, u32[]{:S(2)}, u32[]{:S(2)}) collective-permute-start(bf16[8,4224]{1,0:T(8,128)(2,1)S(1)} %shard_map.122.refs_0_), channel_id=1, source_target_pairs={{0,8},{1,9},{2,10},{3,11},{4,12},{5,13},{6,14},{7,15},{8,0},{9,1},... | collective-permute-start | bytes 202760 | tf_op jit(solution)/shard_map/ppermute | solution.py:37
  7.4 8.0 %collective-permute-start.5 = (bf16[8,4224]{1,0:T(8,128)(2,1)S(1)}, bf16[8,4224]{1,0:T(8,128)(2,1)S(1)}, u32[]{:S(2)}, u32[]{:S(2)}) collective-permute-start(bf16[8,4224]{1,0:T(8,128)(2,1)S(1)} %shard_map.122.refs_0_), channel_id=1, source_target_pairs={{0,6},{1,7},{2,4},{3,5},{4,2},{5,3},{6,0},{7,1},{8,14},{9,15},{10,... | collective-permute-start | bytes 202760 | tf_op jit(solution)/shard_map/ppermute | solution.py:37
  12.8 11.4 %collective-permute-start.3 = (bf16[32,4224]{1,0:T(8,128)(2,1)S(1)}, bf16[32,4224]{1,0:T(8,128)(2,1)S(1)}, u32[]{:S(2)}, u32[]{:S(2)}) collective-permute-start(bf16[32,4224]{1,0:T(8,128)(2,1)S(1)} %shard_map.124.refs_0_), channel_id=1, source_target_pairs={{0,2},{1,3},{2,0},{3,1},{4,6},{5,7},{6,4},{7,5},{8,10},{9,11},{10,... | collective-permute-start | bytes 811016 | tf_op jit(solution)/shard_map/ppermute | solution.py:37
  13.8 10.4 %collective-permute-start.4 = (bf16[32,4224]{1,0:T(8,128)(2,1)S(1)}, bf16[32,4224]{1,0:T(8,128)(2,1)S(1)}, u32[]{:S(2)}, u32[]{:S(2)}) collective-permute-start(bf16[32,4224]{1,0:T(8,128)(2,1)S(1)} %shard_map.124.refs_0_), channel_id=1, source_target_pairs={{0,4},{1,5},{2,6},{3,7},{4,0},{5,1},{6,2},{7,3},{8,12},{9,13},{10,... | collective-permute-start | bytes 811016 | tf_op jit(solution)/shard_map/ppermute | solution.py:37
  15.4 7.2 %collective-permute-start.6 = (bf16[8,4224]{1,0:T(8,128)(2,1)S(1)}, bf16[8,4224]{1,0:T(8,128)(2,1)S(1)}, u32[]{:S(2)}, u32[]{:S(2)}) collective-permute-start(bf16[8,4224]{1,0:T(8,128)(2,1)S(1)} %collective-permute-done.5.refs_0_), channel_id=1, source_target_pairs={{0,16},{1,17},{2,18},{3,19},{4,20},{5,21},{6,22},{7,23},{8,24},{9,... | collective-permute-start | bytes 202760 | tf_op jit(solution)/shard_map/ppermute | solution.py:37
  18.1 6.1 %collective-permute-start.7 = (bf16[8,4224]{1,0:T(8,128)(2,1)S(1)}, bf16[8,4224]{1,0:T(8,128)(2,1)S(1)}, u32[]{:S(2)}, u32[]{:S(2)}) collective-permute-start(bf16[8,4224]{1,0:T(8,128)(2,1)S(1)} %collective-permute-done.5.refs_0_), channel_id=1, source_target_pairs={{0,24},{1,25},{2,26},{3,27},{4,28},{5,29},{6,30},{7,31},{8,16},{9,... | collective-permute-start | bytes 202760 | tf_op jit(solution)/shard_map/ppermute | solution.py:37
  18.7 5.5 %collective-permute-start.8 = (bf16[8,4224]{1,0:T(8,128)(2,1)S(1)}, bf16[8,4224]{1,0:T(8,128)(2,1)S(1)}, u32[]{:S(2)}, u32[]{:S(2)}) collective-permute-start(bf16[8,4224]{1,0:T(8,128)(2,1)S(1)} %collective-permute-done.5.refs_0_), channel_id=1, source_target_pairs={{0,8},{1,9},{2,10},{3,11},{4,12},{5,13},{6,14},{7,15},{8,0},{9,1},... | collective-permute-start | bytes 202760 | tf_op jit(solution)/shard_map/ppermute | solution.py:37
  18.9 7.3 %copy-start = (bf16[384,4096]{1,0:T(8,128)(2,1)S(1)}, bf16[384,4096]{1,0:T(8,128)(2,1)}, u32[]{:S(2)}) copy-start(bf16[384,4096]{1,0:T(8,128)(2,1)} %refs_8_.3) | copy-start | bytes 9437188
  24.2 1.6 %collective-permute-start.10 = (bf16[32,4224]{1,0:T(8,128)(2,1)S(1)}, bf16[32,4224]{1,0:T(8,128)(2,1)S(1)}, u32[]{:S(2)}, u32[]{:S(2)}) collective-permute-start(bf16[32,4224]{1,0:T(8,128)(2,1)S(1)} %collective-permute-done.4.refs_1_), channel_id=1, source_target_pairs={{0,1},{1,0},{2,3},{3,2},{4,5},{5,4},{6,7},{7,6},{8,9},{9,8},{10,11... | collective-permute-start | bytes 811016 | tf_op jit(solution)/shard_map/ppermute | solution.py:37
  24.3 1.9 %collective-permute-start.9 = (bf16[32,4224]{1,0:T(8,128)(2,1)S(1)}, bf16[32,4224]{1,0:T(8,128)(2,1)S(1)}, u32[]{:S(2)}, u32[]{:S(2)}) collective-permute-start(bf16[32,4224]{1,0:T(8,128)(2,1)S(1)} %collective-permute-done.3.refs_0_), channel_id=1, source_target_pairs={{0,1},{1,0},{2,3},{3,2},{4,5},{5,4},{6,7},{7,6},{8,9},{9,8},{10,11... | collective-permute-start | bytes 811016 | tf_op jit(solution)/shard_map/ppermute | solution.py:37
  24.8 3.6 %collective-permute-start.11 = (bf16[32,4224]{1,0:T(8,128)(2,1)S(1)}, bf16[32,4224]{1,0:T(8,128)(2,1)S(1)}, u32[]{:S(2)}, u32[]{:S(2)}) collective-permute-start(bf16[32,4224]{1,0:T(8,128)(2,1)S(1)} %shard_map.124.refs_0_), channel_id=1, source_target_pairs={{0,1},{1,0},{2,3},{3,2},{4,5},{5,4},{6,7},{7,6},{8,9},{9,8},{10,11... | collective-permute-start | bytes 811016 | tf_op jit(solution)/shard_map/ppermute | solution.py:37
  24.9 3.5 %collective-permute-start.12 = (bf16[32,4224]{1,0:T(8,128)(2,1)S(1)}, bf16[32,4224]{1,0:T(8,128)(2,1)S(1)}, u32[]{:S(2)}, u32[]{:S(2)}) collective-permute-start(bf16[32,4224]{1,0:T(8,128)(2,1)S(1)} %shard_map.126.refs_1_), channel_id=1, source_target_pairs={{0,1},{1,0},{2,3},{3,2},{4,5},{5,4},{6,7},{7,6},{8,9},{9,8},{10,11... | collective-permute-start | bytes 811016 | tf_op jit(solution)/shard_map/ppermute | solution.py:37
  28.2 2.6 %collective-permute-start.14 = (bf16[64,4480]{1,0:T(8,128)(2,1)S(1)}, bf16[64,4480]{1,0:T(8,128)(2,1)S(1)}, u32[]{:S(2)}, u32[]{:S(2)}) collective-permute-start(bf16[64,4480]{1,0:T(8,128)(2,1)S(1)} %get-tuple-element.53), channel_id=1, source_target_pairs={{0,1},{1,0},{2,3},{3,2},{4,5},{5,4},{6,7},{7,6},{8,9},{9,8},{10,11... | collective-permute-start | bytes 1720328 | tf_op jit(solution)/shard_map/ppermute | solution.py:37
  30.3 2.8 %collective-permute-start.13 = (bf16[64,4480]{1,0:T(8,128)(2,1)S(1)}, bf16[64,4480]{1,0:T(8,128)(2,1)S(1)}, u32[]{:S(2)}, u32[]{:S(2)}) collective-permute-start(bf16[64,4480]{1,0:T(8,128)(2,1)S(1)} %get-tuple-element.51), channel_id=1, source_target_pairs={{0,1},{1,0},{2,3},{3,2},{4,5},{5,4},{6,7},{7,6},{8,9},{9,8},{10,11... | collective-permute-start | bytes 1720328 | tf_op jit(solution)/shard_map/ppermute | solution.py:37
  31.1 8.9 %collective-permute-start.15 = (bf16[32,4480]{1,0:T(8,128)(2,1)S(1)}, bf16[32,4480]{1,0:T(8,128)(2,1)S(1)}, u32[]{:S(2)}, u32[]{:S(2)}) collective-permute-start(bf16[32,4480]{1,0:T(8,128)(2,1)S(1)} %get-tuple-element.54), channel_id=1, source_target_pairs={{0,2},{1,3},{2,0},{3,1},{4,6},{5,7},{6,4},{7,5},{8,10},{9,11},{10,... | collective-permute-start | bytes 860168 | tf_op jit(solution)/shard_map/ppermute | solution.py:37
  31.7 8.6 %collective-permute-start.16 = (bf16[32,4480]{1,0:T(8,128)(2,1)S(1)}, bf16[32,4480]{1,0:T(8,128)(2,1)S(1)}, u32[]{:S(2)}, u32[]{:S(2)}) collective-permute-start(bf16[32,4480]{1,0:T(8,128)(2,1)S(1)} %get-tuple-element.55), channel_id=1, source_target_pairs={{0,4},{1,5},{2,6},{3,7},{4,0},{5,1},{6,2},{7,3},{8,12},{9,13},{10,... | collective-permute-start | bytes 860168 | tf_op jit(solution)/shard_map/ppermute | solution.py:37
  33.4 10.1 %collective-permute-start.20 = (bf16[8,4480]{1,0:T(8,128)(2,1)S(1)}, bf16[8,4480]{1,0:T(8,128)(2,1)S(1)}, u32[]{:S(2)}, u32[]{:S(2)}) collective-permute-start(bf16[8,4480]{1,0:T(8,128)(2,1)S(1)} %get-tuple-element.61), channel_id=1, source_target_pairs={{0,16},{1,17},{2,18},{3,19},{4,20},{5,21},{6,22},{7,23},{8,24},{9,... | collective-permute-start | bytes 215048 | tf_op jit(solution)/shard_map/ppermute | solution.py:37
  35.1 9.0 %collective-permute-start.21 = (bf16[8,4480]{1,0:T(8,128)(2,1)S(1)}, bf16[8,4480]{1,0:T(8,128)(2,1)S(1)}, u32[]{:S(2)}, u32[]{:S(2)}) collective-permute-start(bf16[8,4480]{1,0:T(8,128)(2,1)S(1)} %get-tuple-element.62), channel_id=1, source_target_pairs={{0,24},{1,25},{2,26},{3,27},{4,28},{5,29},{6,30},{7,31},{8,16},{9,... | collective-permute-start | bytes 215048 | tf_op jit(solution)/shard_map/ppermute | solution.py:37
  36.5 7.6 %collective-permute-start.22 = (bf16[8,4480]{1,0:T(8,128)(2,1)S(1)}, bf16[8,4480]{1,0:T(8,128)(2,1)S(1)}, u32[]{:S(2)}, u32[]{:S(2)}) collective-permute-start(bf16[8,4480]{1,0:T(8,128)(2,1)S(1)} %get-tuple-element.63), channel_id=1, source_target_pairs={{0,8},{1,9},{2,10},{3,11},{4,12},{5,13},{6,14},{7,15},{8,0},{9,1},... | collective-permute-start | bytes 215048 | tf_op jit(solution)/shard_map/ppermute | solution.py:37
  40.5 7.2 %collective-permute-start.17 = (bf16[8,4480]{1,0:T(8,128)(2,1)S(1)}, bf16[8,4480]{1,0:T(8,128)(2,1)S(1)}, u32[]{:S(2)}, u32[]{:S(2)}) collective-permute-start(bf16[8,4480]{1,0:T(8,128)(2,1)S(1)} %get-tuple-element.57), channel_id=1, source_target_pairs={{0,16},{1,17},{2,18},{3,19},{4,20},{5,21},{6,22},{7,23},{8,24},{9,... | collective-permute-start | bytes 215048 | tf_op jit(solution)/shard_map/ppermute | solution.py:37
  42.6 6.3 %collective-permute-start.18 = (bf16[8,4480]{1,0:T(8,128)(2,1)S(1)}, bf16[8,4480]{1,0:T(8,128)(2,1)S(1)}, u32[]{:S(2)}, u32[]{:S(2)}) collective-permute-start(bf16[8,4480]{1,0:T(8,128)(2,1)S(1)} %get-tuple-element.58), channel_id=1, source_target_pairs={{0,24},{1,25},{2,26},{3,27},{4,28},{5,29},{6,30},{7,31},{8,16},{9,... | collective-permute-start | bytes 215048 | tf_op jit(solution)/shard_map/ppermute | solution.py:37
  43.5 5.7 %collective-permute-start.19 = (bf16[8,4480]{1,0:T(8,128)(2,1)S(1)}, bf16[8,4480]{1,0:T(8,128)(2,1)S(1)}, u32[]{:S(2)}, u32[]{:S(2)}) collective-permute-start(bf16[8,4480]{1,0:T(8,128)(2,1)S(1)} %get-tuple-element.59), channel_id=1, source_target_pairs={{0,8},{1,9},{2,10},{3,11},{4,12},{5,13},{6,14},{7,15},{8,0},{9,1},... | collective-permute-start | bytes 215048 | tf_op jit(solution)/shard_map/ppermute | solution.py:37
  44.2 5.3 %collective-permute-start.23 = (bf16[8,4480]{1,0:T(8,128)(2,1)S(1)}, bf16[8,4480]{1,0:T(8,128)(2,1)S(1)}, u32[]{:S(2)}, u32[]{:S(2)}) collective-permute-start(bf16[8,4480]{1,0:T(8,128)(2,1)S(1)} %shard_map.133), channel_id=1, source_target_pairs={{0,6},{1,7},{2,4},{3,5},{4,2},{5,3},{6,0},{7,1},{8,14},{9,15},{10,... | collective-permute-start | bytes 215048 | tf_op jit(solution)/shard_map/ppermute | solution.py:37

commit v7 on v6

--- a/solution.py
+++ b/solution.py
@@ -119,75 +119,73 @@
     )
 
 
-def attention_kernel(
-    own, offsets, length_hbm, query_hbm, key_hbm, value_hbm, near_ref, far_ref, *scratch
-):
-    length_ref, query_ref, key_ref, value_ref, dest_ref, sems = scratch
-    sources = [length_hbm, query_hbm, key_hbm, value_hbm]
-    copies = fetch(sources, [length_ref, query_ref, key_ref, value_ref], sems)
-    copies[0].wait()
+def attention_kernel(own, offsets, *refs):
+    length_hbm, query_hbm, key_hbm, value_hbm, weight_hbm, near_ref, far_ref, weight_out = refs[:8]
+    length_ref, query_ref, key_ref, value_ref, wide_ref, mean_ref, logs_ref, dest_ref, sems = refs[8:]
+    sources = [length_hbm, query_hbm, key_hbm, value_hbm, weight_hbm]
+    copies = fetch(sources, [length_ref, query_ref, key_ref, value_ref, weight_out], sems)
     me = lax.axis_index("ffn")
     rows, seg_len, _ = key_ref.shape
     per_group = HEADS // KV_HEADS
-    shape = (per_group * rows, rows * seg_len)
-    row_of = lax.broadcasted_iota(jnp.int32, shape, 0) % rows
-    key_at = lax.broadcasted_iota(jnp.int32, shape, 1)
-    limit = jnp.full((1, rows * seg_len), 0, jnp.int32)
-    lane_row = lax.broadcasted_iota(jnp.int32, limit.shape, 1) // seg_len
-    for row in range(rows):
-        limit = jnp.where(lane_row == row, length_ref[row] + row * seg_len - me * seg_len, limit)
-    usable = (row_of == key_at // seg_len) & (key_at < limit)
+    place = lax.broadcasted_iota(jnp.int32, (KV_HEADS * per_group, seg_len), 1) + me * seg_len
     per_dest = max(1, own // HEAD_DIM)
     extra = near_ref.shape[1]
     lane = lax.broadcasted_iota(jnp.int32, (rows, extra), 1)
-    for copy in copies[1:]:
-        copy.wait()
-    for group in range(KV_HEADS):
-        cols = slice(group * HEAD_DIM, (group + 1) * HEAD_DIM)
-        keys = key_ref[:, :, cols].reshape(rows * seg_len, HEAD_DIM)
-        values = value_ref[:, :, cols].reshape(rows * seg_len, HEAD_DIM)
-        scores = lax.dot_general(
-            query_ref[group * per_group * rows : (group + 1) * per_group * rows],
-            keys,
-            (((1,), (1,)), ((), ())),
-            preferred_element_type=jnp.float32,
-        ) * HEAD_DIM ** (-0.5)
-        peak = jnp.max(jnp.where(usable, scores, -1e30), axis=-1, keepdims=True)
-        weights = jnp.where(usable, jnp.exp(scores - peak), 0.0).astype(jnp.bfloat16)
-        total = jnp.sum(weights.astype(jnp.float32), axis=-1, keepdims=True)
-        acc = jnp.dot(weights, values, preferred_element_type=jnp.float32)
-        some = total > 0.0
-        safe = jnp.where(some, total, 1.0)
-        mean = acc / safe
-        logs = jnp.where(some, peak + jnp.log(safe), -1e30)
-        if own >= HEAD_DIM:
-            for first in range(0, per_group, per_dest):
-                dest = (group * per_group + first) // per_dest
-                stats = jnp.zeros(lane.shape, jnp.float32)
-                for slot in range(per_dest):
-                    at = slice((first + slot) * rows, (first + slot + 1) * rows)
-                    dest_ref[dest, :, slot * HEAD_DIM : (slot + 1) * HEAD_DIM] = mean[at]
-                    for place, part in enumerate(coded_log(logs[at])):
-                        stats = jnp.where(lane == own + 3 * slot + place, part, stats)
-                dest_ref[dest, :, own:] = stats[:, own:]
-        else:
-            for head in range(per_group):
-                at = slice(head * rows, (head + 1) * rows)
-                for half in range(HEAD_DIM // own):
-                    dest = (group * per_group + head) * (HEAD_DIM // own) + half
-                    block = jnp.zeros(lane.shape, jnp.float32)
-                    moved = mean[at] if half == 0 else pltpu.roll(mean[at], HEAD_DIM - half * own, 1)
-                    block = jnp.where(lane < own, moved, block)
-                    for place, part in enumerate(coded_log(logs[at])):
-                        block = jnp.where(lane == own + place, part, block)
-                    dest_ref[dest] = block
+    copies[0].wait()
+    copies[1].wait()
+    wide_ref[...] = query_ref[...].astype(jnp.float32)
+    copies[2].wait()
+    copies[3].wait()
+    pairs = [(row, group) for row in range(rows) for group in range(KV_HEADS)]
+    heads = [pl.ds(group * per_group * rows + row, per_group, rows) for row, group in pairs]
+    cols = [slice(group * HEAD_DIM, (group + 1) * HEAD_DIM) for _, group in pairs]
+    queries = [wide_ref[at, :].astype(jnp.bfloat16) for at in heads]
+    scores = [
+        lax.dot_general(q, key_ref[row, :, c], (((1,), (1,)), ((), ())), preferred_element_type=jnp.float32)
+        for q, c, (row, _) in zip(queries, cols, pairs)
+    ]
+    scores = jnp.stack(scores).reshape(rows, KV_HEADS * per_group, seg_len) * HEAD_DIM ** (-0.5)
+    usable = jnp.stack([place < length_ref[row] for row in range(rows)])
+    peak = jnp.max(jnp.where(usable, scores, -1e30), axis=-1, keepdims=True)
+    weights = jnp.where(usable, jnp.exp(scores - peak), 0.0).astype(jnp.bfloat16)
+    total = jnp.sum(weights.astype(jnp.float32), axis=-1, keepdims=True)
+    some = total > 0.0
+    safe = jnp.where(some, total, 1.0)
+    logs = jnp.where(some, peak + jnp.log(safe), -1e30)
+    parts = [slice(group * per_group, (group + 1) * per_group) for _, group in pairs]
+    accs = [
+        jnp.dot(weights[row, part], value_ref[row, :, c], preferred_element_type=jnp.float32)
+        for part, c, (row, _) in zip(parts, cols, pairs)
+    ]
+    for acc, part, at, (row, _) in zip(accs, parts, heads, pairs):
+        mean_ref[at, :] = acc / safe[row, part]
+        logs_ref[at, :] = jnp.broadcast_to(logs[row, part], acc.shape)
+    if own >= HEAD_DIM:
+        for dest in range(HEADS // per_dest):
+            stats = jnp.zeros((rows, extra - own), jnp.float32)
+            for slot in range(per_dest):
+                at = slice((dest * per_dest + slot) * rows, (dest * per_dest + slot + 1) * rows)
+                dest_ref[dest, :, slot * HEAD_DIM : (slot + 1) * HEAD_DIM] = mean_ref[at, :]
+                for number, part in enumerate(coded_log(logs_ref[at, :1])):
+                    stats = jnp.where(lane[:, own:] == own + 3 * slot + number, part, stats)
+            dest_ref[dest, :, own:] = stats
+    else:
+        for head in range(HEADS):
+            mean, logs = mean_ref[head * rows : (head + 1) * rows, :], logs_ref[head * rows : (head + 1) * rows, :1]
+            for half in range(HEAD_DIM // own):
+                moved = mean if half == 0 else pltpu.roll(mean, HEAD_DIM - half * own, 1)
+                block = jnp.where(lane < own, moved, 0.0)
+                for number, part in enumerate(coded_log(logs)):
+                    block = jnp.where(lane == own + number, part, block)
+                dest_ref[head * (HEAD_DIM // own) + half] = block
     for out_ref, core in ((near_ref, 0), (far_ref, 1)):
-        for place in range(0, len(offsets), 2):
-            pair = [dest_ref[me ^ (offset ^ core)] for offset in offsets[place : place + 2]]
-            out_ref[place * rows : (place + 2) * rows] = jnp.concatenate(pair, axis=0).astype(jnp.bfloat16)
-
-
-def attend(query, k_cache, v_cache, cache_len, levels):
+        for first in range(0, len(offsets), 2):
+            pair = [dest_ref[me ^ (offset ^ core)] for offset in offsets[first : first + 2]]
+            out_ref[first * rows : (first + 2) * rows] = jnp.concatenate(pair, axis=0).astype(jnp.bfloat16)
+    copies[4].wait()
+
+
+def attend(query, k_cache, v_cache, cache_len, levels, weight):
     devices = lax.axis_size("ffn")
     rows, seg_len, _ = k_cache.shape
     own = query.shape[1] // devices
@@ -197,16 +195,17 @@
     out = jax.ShapeDtypeStruct((len(offsets) * rows, extra), jnp.bfloat16)
     return call(
         functools.partial(attention_kernel, own, offsets),
-        [out, out],
-        in_hbm(cache_len, stacked, k_cache, v_cache),
-        in_specs=[HBM] * 4,
+        [out, out, pltpu.VMEM(weight.shape, weight.dtype)],
+        in_hbm(cache_len, stacked, k_cache, v_cache, weight),
+        in_specs=[HBM] * 5,
         scratch=[
             pltpu.SMEM(cache_len.shape, cache_len.dtype),
             pltpu.VMEM(stacked.shape, stacked.dtype),
             pltpu.VMEM(k_cache.shape, k_cache.dtype),
             pltpu.VMEM(v_cache.shape, v_cache.dtype),
+            *[pltpu.VMEM(stacked.shape, jnp.float32)] * 3,
             pltpu.VMEM((devices, rows, extra), jnp.float32),
-            fetched(4),
+            fetched(5),
         ],
         flops=4 * 10**9,
     )
@@ -308,7 +307,7 @@
     return [2, 3, 1] if radix == 4 else [1]
 
 
-def gather(block, levels, *ready):
+def gather(block, levels, *ready, flops=1):
     for stride, radix in reversed(levels):
         order = start_order(radix)
         arrived = [exchange(block, stride * k) for k in order]
@@ -319,6 +318,7 @@
             functools.partial(stack_kernel, [0] + order),
             jax.ShapeDtypeStruct((radix * rows, width), jnp.bfloat16),
             [block, *arrived],
+            flops=flops,
         )
     return block
 
@@ -354,16 +354,17 @@
     rows = rows_dev * (devices // (2 * radix))
     cut = [rows // outer[0][1]] * outer[0][1]
     across = [exchange(block, corner)] if radix == 4 else []
-    w_gate, w_up = keep(w_gate, w_up)
-    weights = (w_gate, w_up, w_down)
+    (w_gate,) = keep(w_gate)
     base = gather(block, outer, w_gate)
     sides = [1, 2] if radix == 4 else [1]
     chunks = [exchange(base, stride * k) for k in sides]
-    sums = attend(after(query, base), k_cache, v_cache, cache_len, levels)
-    last_chunk = [gather(a, outer, sums[0]) for a in across]
-    chunks = lax.optimization_barrier((*chunks, sums[0], *last_chunk))[: len(chunks)]
+    *sums, w_up = attend(after(query, base), k_cache, v_cache, cache_len, levels, w_up)
+    weights = (w_gate, w_up, w_down)
+    last_chunk = [gather(a, outer, sums[0], flops=25 * 10**8) for a in across]
+    count = len(sides)
+    chunks = lax.optimization_barrier((*chunks, sums[0]))[:count]
     others = [exchange(c, 1) for c in (*chunks, base, *last_chunk)]
-    count = len(sides)
+    chunks = lax.optimization_barrier((*chunks, *last_chunk))[:count]
     near, far = apply_expert(chunks, others[:count], sides, sums, weights)
     pieces = summed([near, exchange(far, 1)], [rows] * count, width, own)
     base = after(base, near)

time: 50.4 us -> 48.9 us (0.970)
  Pallas kernels: 13.3 us -> 11.5 us
  waiting for transfers between devices: 9.56 us -> 10.6 us
  starting transfers between devices: 26.6 us -> 25.9 us
    pallas_call x13, Pallas kernels: 13.3 us -> 11.5 us  [call(): pl.pallas_call(body, out_shape=out_shape, in_specs=in_specs or [VMEM] * l...]
    ppermute x24, waiting for transfers between devices: 9.56 us -> 10.6 us  [exchange(): return lax.ppermute(value, 'ffn', [(i, i ^ distance) for i in range(size)])]
    ppermute x24, starting transfers between devices: 26.6 us -> 25.9 us  [exchange(): return lax.ppermute(value, 'ffn', [(i, i ^ distance) for i in range(size)])]
  transfers between devices with their start and end apart: 24 -> 24, of which waited for: 9 -> 9; matrix products, arithmetic and copies ran while one was open for 0% -> 0% of each run, Pallas kernels for 23% -> 20%
where the time goes in v7:
time: 48.9 us; the launch traced here: 48.7 us
  starting transfers between devices  25.9 us (53%)
  Pallas kernels  11.5 us (24%)
  waiting for transfers between devices  10.6 us (22%)
  between operations  0.8 us (2%)
    ppermute x24, starting transfers between devices, exchange(): return lax.ppermute(value, 'ffn', [(i, i ^ distance) for i in range(size)])  25.9 us
    pallas_call x13, Pallas kernels, call(): pl.pallas_call(body, out_shape=out_shape, in_specs=in_specs or [VMEM] * l...  11.5 us
    ppermute x24, waiting for transfers between devices, exchange(): return lax.ppermute(value, 'ffn', [(i, i ^ distance) for i in range(size)])  10.6 us
  transfers between devices with their start and end apart: 24, of which 9 were waited for; matrix products, arithmetic and copies ran while one was open for 0% of the time, Pallas kernels for 20%

profile of v7, /device:TPU:0, one launch (start us, length us, event | category | flops | bytes accessed | tf_op | source)
XLA Modules:
  0.0 48.7 jit_solution(2055797873335032843)
XLA Ops:
  0.6 1.1 %shard_map.122.refs_0_ = bf16[8,4224]{1,0:T(8,128)(2,1)S(1)} custom-call(bf16[8,4096]{1,0:T(8,128)(2,1)} %tokens_hbm.1, f32[1,4096]{1,0:T(1,128)} %bitcast.6, s32[8,8]{1,0:T(8,128)} %routes_hbm.1, f32[8,8]{1,0:T(8,128)} %scores_hbm.1), custom_call_target="tpu_custom_call" | custom-call | flops 1 | bytes 1 | tf_op jit(solution)/shard_map/pallas_call | solution.py:45
  1.7 4.1 %collective-permute-start = (bf16[8,4224]{1,0:T(8,128)(2,1)S(1)}, bf16[8,4224]{1,0:T(8,128)(2,1)S(1)}, u32[]{:S(2)}, u32[]{:S(2)}) collective-permute-start(bf16[8,4224]{1,0:T(8,128)(2,1)S(1)} %shard_map.122.refs_0_), channel_id=1, source_target_pairs={{0,16},{1,17},{2,18},{3,19},{4,20},{5,21},{6,22},{7,23},{8,24},{9,... | collective-permute-start | bytes 202760 | tf_op jit(solution)/shard_map/ppermute | solution.py:37
  5.8 1.3 %collective-permute-start.1 = (bf16[8,4224]{1,0:T(8,128)(2,1)S(1)}, bf16[8,4224]{1,0:T(8,128)(2,1)S(1)}, u32[]{:S(2)}, u32[]{:S(2)}) collective-permute-start(bf16[8,4224]{1,0:T(8,128)(2,1)S(1)} %shard_map.122.refs_0_), channel_id=1, source_target_pairs={{0,24},{1,25},{2,26},{3,27},{4,28},{5,29},{6,30},{7,31},{8,16},{9,... | collective-permute-start | bytes 202760 | tf_op jit(solution)/shard_map/ppermute | solution.py:37
  7.2 0.2 collective-permute-start.2
  7.4 2.4 %collective-permute-start.5 = (bf16[8,4224]{1,0:T(8,128)(2,1)S(1)}, bf16[8,4224]{1,0:T(8,128)(2,1)S(1)}, u32[]{:S(2)}, u32[]{:S(2)}) collective-permute-start(bf16[8,4224]{1,0:T(8,128)(2,1)S(1)} %shard_map.122.refs_0_), channel_id=1, source_target_pairs={{0,6},{1,7},{2,4},{3,5},{4,2},{5,3},{6,0},{7,1},{8,14},{9,15},{10,... | collective-permute-start | bytes 202760 | tf_op jit(solution)/shard_map/ppermute | solution.py:37
  9.8 1.9 %shard_map.123.refs_6_ = bf16[4096,384]{1,0:T(8,128)(2,1)S(1)} custom-call(bf16[4096,384]{1,0:T(8,128)(2,1)} %refs_0_.2), custom_call_target="tpu_custom_call" | custom-call | flops 4000000000 | bytes 1 | tf_op jit(solution)/shard_map/pallas_call | solution.py:45
  11.7 0.0 collective-permute-done.refs_1_
  11.8 0.3 collective-permute-done.1.refs_2_
  12.1 0.1 collective-permute-done.2.refs_3_
  12.2 1.6 %collective-permute-start.3 = (bf16[32,4224]{1,0:T(8,128)(2,1)S(1)}, bf16[32,4224]{1,0:T(8,128)(2,1)S(1)}, u32[]{:S(2)}, u32[]{:S(2)}) collective-permute-start(bf16[32,4224]{1,0:T(8,128)(2,1)S(1)} %shard_map.124.refs_0_), channel_id=1, source_target_pairs={{0,2},{1,3},{2,0},{3,1},{4,6},{5,7},{6,4},{7,5},{8,10},{9,11},{10,... | collective-permute-start | bytes 811016 | tf_op jit(solution)/shard_map/ppermute | solution.py:37
  13.8 1.5 %collective-permute-start.4 = (bf16[32,4224]{1,0:T(8,128)(2,1)S(1)}, bf16[32,4224]{1,0:T(8,128)(2,1)S(1)}, u32[]{:S(2)}, u32[]{:S(2)}) collective-permute-start(bf16[32,4224]{1,0:T(8,128)(2,1)S(1)} %shard_map.124.refs_0_), channel_id=1, source_target_pairs={{0,4},{1,5},{2,6},{3,7},{4,0},{5,1},{6,2},{7,3},{8,12},{9,13},{10,... | collective-permute-start | bytes 811016 | tf_op jit(solution)/shard_map/ppermute | solution.py:37
  15.4 0.0 collective-permute-done.5.refs_0_
  15.4 2.7 %collective-permute-start.6 = (bf16[8,4224]{1,0:T(8,128)(2,1)S(1)}, bf16[8,4224]{1,0:T(8,128)(2,1)S(1)}, u32[]{:S(2)}, u32[]{:S(2)}) collective-permute-start(bf16[8,4224]{1,0:T(8,128)(2,1)S(1)} %collective-permute-done.5.refs_0_), channel_id=1, source_target_pairs={{0,16},{1,17},{2,18},{3,19},{4,20},{5,21},{6,22},{7,23},{8,24},{9,... | collective-permute-start | bytes 202760 | tf_op jit(solution)/shard_map/ppermute | solution.py:37
  18.1 0.6 %collective-permute-start.7 = (bf16[8,4224]{1,0:T(8,128)(2,1)S(1)}, bf16[8,4224]{1,0:T(8,128)(2,1)S(1)}, u32[]{:S(2)}, u32[]{:S(2)}) collective-permute-start(bf16[8,4224]{1,0:T(8,128)(2,1)S(1)} %collective-permute-done.5.refs_0_), channel_id=1, source_target_pairs={{0,24},{1,25},{2,26},{3,27},{4,28},{5,29},{6,30},{7,31},{8,16},{9,... | collective-permute-start | bytes 202760 | tf_op jit(solution)/shard_map/ppermute | solution.py:37
  18.7 0.3 collective-permute-start.8
  18.9 2.7 %shard_map.125 = (bf16[128,384]{1,0:T(8,128)(2,1)S(1)}, bf16[128,384]{1,0:T(8,128)(2,1)S(1)}, bf16[4096,384]{1,0:T(8,128)(2,1)S(1)}) custom-call(s32[8]{0:T(128)} %refs_0_.3, bf16[512,128]{1,0:T(8,128)(2,1)} %bitcast.7, bf16[8,128,512]{2,1,0:T(8,128)(2,1)} %refs_2_.1, bf16[8,128,512]{2,1,0:T(8,128)(2,1)} %refs_3_.1, bf16[4096,384]{1,0:T(8,128)(2,1)} %refs_4_.1), custom_call_target="tpu_custom_call" | custom-call | flops 4000000000 | bytes 1 | tf_op jit(solution)/shard_map/pallas_call | solution.py:45
  21.7 0.0 collective-permute-done.3.refs_0_
  21.7 0.0 collective-permute-done.4.refs_1_
  21.7 0.0 copy-start
  21.7 0.1 collective-permute-start.10
  21.8 0.5 %collective-permute-start.9 = (bf16[32,4224]{1,0:T(8,128)(2,1)S(1)}, bf16[32,4224]{1,0:T(8,128)(2,1)S(1)}, u32[]{:S(2)}, u32[]{:S(2)}) collective-permute-start(bf16[32,4224]{1,0:T(8,128)(2,1)S(1)} %collective-permute-done.3.refs_0_), channel_id=1, source_target_pairs={{0,1},{1,0},{2,3},{3,2},{4,5},{5,4},{6,7},{7,6},{8,9},{9,8},{10,11... | collective-permute-start | bytes 811016 | tf_op jit(solution)/shard_map/ppermute | solution.py:37
  22.3 0.2 collective-permute-done.6.refs_1_
  22.5 0.0 collective-permute-start.11
  22.5 1.7 %collective-permute-done.7.refs_2_ = bf16[8,4224]{1,0:T(8,128)(2,1)S(1)} collective-permute-done((bf16[8,4224]{1,0:T(8,128)(2,1)S(1)}, bf16[8,4224]{1,0:T(8,128)(2,1)S(1)}, u32[]{:S(2)}, u32[]{:S(2)}) %collective-permute-start.7) | collective-permute-done | bytes 67616 | tf_op jit(solution)/shard_map/ppermute | solution.py:37
  24.2 0.0 collective-permute-done.8.refs_3_
  24.2 0.1 collective-permute-start.12
  24.3 0.0 collective-permute-done.10.refs_3_
  24.3 0.0 collective-permute-done.9.refs_2_
  24.3 0.0 copy-done
  24.3 1.9 %shard_map.127 = (bf16[64,4480]{1,0:T(8,128)(2,1)S(1)}, bf16[64,4480]{1,0:T(8,128)(2,1)S(1)}) custom-call(bf16[32,4224]{1,0:T(8,128)(2,1)S(1)} %collective-permute-done.3.refs_0_, bf16[32,4224]{1,0:T(8,128)(2,1)S(1)} %collective-permute-done.4.refs_1_, bf16[32,4224]{1,0:T(8,128)(2,1)S(1)} %collective-permute-done.9.refs_2_, ...), custom_call_target="tpu_custom_call" | custom-call | flops 4000000000 | bytes 9437184 | tf_op jit(solution)/shard_map/pallas_call | solution.py:45
  26.3 0.5 %collective-permute-start.14 = (bf16[64,4480]{1,0:T(8,128)(2,1)S(1)}, bf16[64,4480]{1,0:T(8,128)(2,1)S(1)}, u32[]{:S(2)}, u32[]{:S(2)}) collective-permute-start(bf16[64,4480]{1,0:T(8,128)(2,1)S(1)} %get-tuple-element.55), channel_id=1, source_target_pairs={{0,1},{1,0},{2,3},{3,2},{4,5},{5,4},{6,7},{7,6},{8,9},{9,8},{10,11... | collective-permute-start | bytes 1720328 | tf_op jit(solution)/shard_map/ppermute | solution.py:37
  26.8 0.0 collective-permute-done.11.refs_2_
  26.8 0.0 collective-permute-done.12.refs_3_
  26.8 2.0 %shard_map.128 = (bf16[64,4480]{1,0:T(8,128)(2,1)S(1)}, bf16[64,4480]{1,0:T(8,128)(2,1)S(1)}) custom-call(bf16[32,4224]{1,0:T(8,128)(2,1)S(1)} %shard_map.124.refs_0_, bf16[32,4224]{1,0:T(8,128)(2,1)S(1)} %shard_map.126.refs_1_, bf16[32,4224]{1,0:T(8,128)(2,1)S(1)} %collective-permute-done.11.refs_2_, bf16[32,4224]{1,0:T(8,128)(2,1)S(1)} %collective-permute-done.12.refs_3_, ...), custom_call_target="tpu_custom_call" | custom-call | flops 4000000000 | bytes 9437184 | tf_op jit(solution)/shard_map/pallas_call | solution.py:45
  28.8 0.1 collective-permute-start.13
  28.9 0.0 collective-permute-done.14.refs_1_
  28.9 0.3 shard_map.130
  29.2 0.6 %collective-permute-start.15 = (bf16[32,4480]{1,0:T(8,128)(2,1)S(1)}, bf16[32,4480]{1,0:T(8,128)(2,1)S(1)}, u32[]{:S(2)}, u32[]{:S(2)}) collective-permute-start(bf16[32,4480]{1,0:T(8,128)(2,1)S(1)} %get-tuple-element.56), channel_id=1, source_target_pairs={{0,2},{1,3},{2,0},{3,1},{4,6},{5,7},{6,4},{7,5},{8,10},{9,11},{10,... | collective-permute-start | bytes 860168 | tf_op jit(solution)/shard_map/ppermute | solution.py:37
  29.8 0.5 %collective-permute-start.16 = (bf16[32,4480]{1,0:T(8,128)(2,1)S(1)}, bf16[32,4480]{1,0:T(8,128)(2,1)S(1)}, u32[]{:S(2)}, u32[]{:S(2)}) collective-permute-start(bf16[32,4480]{1,0:T(8,128)(2,1)S(1)} %get-tuple-element.57), channel_id=1, source_target_pairs={{0,4},{1,5},{2,6},{3,7},{4,0},{5,1},{6,2},{7,3},{8,12},{9,13},{10,... | collective-permute-start | bytes 860168 | tf_op jit(solution)/shard_map/ppermute | solution.py:37
  30.3 0.5 %collective-permute-done.13.refs_1_ = bf16[64,4480]{1,0:T(8,128)(2,1)S(1)} collective-permute-done((bf16[64,4480]{1,0:T(8,128)(2,1)S(1)}, bf16[64,4480]{1,0:T(8,128)(2,1)S(1)}, u32[]{:S(2)}, u32[]{:S(2)}) %collective-permute-start.13) | collective-permute-done | bytes 573472 | tf_op jit(solution)/shard_map/ppermute | solution.py:37
  30.8 0.3 shard_map.129
  31.1 2.7 %collective-permute-start.20 = (bf16[8,4480]{1,0:T(8,128)(2,1)S(1)}, bf16[8,4480]{1,0:T(8,128)(2,1)S(1)}, u32[]{:S(2)}, u32[]{:S(2)}) collective-permute-start(bf16[8,4480]{1,0:T(8,128)(2,1)S(1)} %get-tuple-element.63), channel_id=1, source_target_pairs={{0,16},{1,17},{2,18},{3,19},{4,20},{5,21},{6,22},{7,23},{8,24},{9,... | collective-permute-start | bytes 215048 | tf_op jit(solution)/shard_map/ppermute | solution.py:37
  33.8 0.8 %collective-permute-start.21 = (bf16[8,4480]{1,0:T(8,128)(2,1)S(1)}, bf16[8,4480]{1,0:T(8,128)(2,1)S(1)}, u32[]{:S(2)}, u32[]{:S(2)}) collective-permute-start(bf16[8,4480]{1,0:T(8,128)(2,1)S(1)} %get-tuple-element.64), channel_id=1, source_target_pairs={{0,24},{1,25},{2,26},{3,27},{4,28},{5,29},{6,30},{7,31},{8,16},{9,... | collective-permute-start | bytes 215048 | tf_op jit(solution)/shard_map/ppermute | solution.py:37
  34.6 0.1 collective-permute-start.22
  34.7 3.8 %collective-permute-done.15.refs_1_ = bf16[32,4480]{1,0:T(8,128)(2,1)S(1)} collective-permute-done((bf16[32,4480]{1,0:T(8,128)(2,1)S(1)}, bf16[32,4480]{1,0:T(8,128)(2,1)S(1)}, u32[]{:S(2)}, u32[]{:S(2)}) %collective-permute-start.15) | collective-permute-done | bytes 286752 | tf_op jit(solution)/shard_map/ppermute | solution.py:37
  38.5 0.3 collective-permute-done.16.refs_2_
  38.8 0.2 shard_map.131
  39.0 2.7 %collective-permute-start.17 = (bf16[8,4480]{1,0:T(8,128)(2,1)S(1)}, bf16[8,4480]{1,0:T(8,128)(2,1)S(1)}, u32[]{:S(2)}, u32[]{:S(2)}) collective-permute-start(bf16[8,4480]{1,0:T(8,128)(2,1)S(1)} %get-tuple-element.59), channel_id=1, source_target_pairs={{0,16},{1,17},{2,18},{3,19},{4,20},{5,21},{6,22},{7,23},{8,24},{9,... | collective-permute-start | bytes 215048 | tf_op jit(solution)/shard_map/ppermute | solution.py:37
  41.6 0.6 %collective-permute-start.18 = (bf16[8,4480]{1,0:T(8,128)(2,1)S(1)}, bf16[8,4480]{1,0:T(8,128)(2,1)S(1)}, u32[]{:S(2)}, u32[]{:S(2)}) collective-permute-start(bf16[8,4480]{1,0:T(8,128)(2,1)S(1)} %get-tuple-element.60), channel_id=1, source_target_pairs={{0,24},{1,25},{2,26},{3,27},{4,28},{5,29},{6,30},{7,31},{8,16},{9,... | collective-permute-start | bytes 215048 | tf_op jit(solution)/shard_map/ppermute | solution.py:37
  42.2 0.0 collective-permute-done.20.refs_1_
  42.2 0.3 collective-permute-start.19
  42.5 0.0 collective-permute-done.21.refs_2_
  42.5 0.0 collective-permute-done.22.refs_3_
  42.5 0.1 shard_map.133
  42.7 1.5 %collective-permute-start.23 = (bf16[8,4480]{1,0:T(8,128)(2,1)S(1)}, bf16[8,4480]{1,0:T(8,128)(2,1)S(1)}, u32[]{:S(2)}, u32[]{:S(2)}) collective-permute-start(bf16[8,4480]{1,0:T(8,128)(2,1)S(1)} %shard_map.133), channel_id=1, source_target_pairs={{0,6},{1,7},{2,4},{3,5},{4,2},{5,3},{6,0},{7,1},{8,14},{9,15},{10,... | collective-permute-start | bytes 215048 | tf_op jit(solution)/shard_map/ppermute | solution.py:37
  44.2 2.4 %collective-permute-done.17.refs_1_ = bf16[8,4480]{1,0:T(8,128)(2,1)S(1)} collective-permute-done((bf16[8,4480]{1,0:T(8,128)(2,1)S(1)}, bf16[8,4480]{1,0:T(8,128)(2,1)S(1)}, u32[]{:S(2)}, u32[]{:S(2)}) %collective-permute-start.17) | collective-permute-done | bytes 71712 | tf_op jit(solution)/shard_map/ppermute | solution.py:37
  46.6 1.3 %collective-permute-done.18.refs_2_ = bf16[8,4480]{1,0:T(8,128)(2,1)S(1)} collective-permute-done((bf16[8,4480]{1,0:T(8,128)(2,1)S(1)}, bf16[8,4480]{1,0:T(8,128)(2,1)S(1)}, u32[]{:S(2)}, u32[]{:S(2)}) %collective-permute-start.18) | collective-permute-done | bytes 71712 | tf_op jit(solution)/shard_map/ppermute | solution.py:37
  47.9 0.0 collective-permute-done.19.refs_3_
  47.9 0.1 shard_map.132.refs_0_
  48.0 0.0 collective-permute-done.23.refs_1_
  48.0 0.7 %shard_map.134 = (bf16[8,4096]{1,0:T(8,128)(2,1)}, bf16[8,256]{1,0:T(8,128)(2,1)}) custom-call(bf16[8,4480]{1,0:T(8,128)(2,1)S(1)} %shard_map.132.refs_0_, bf16[8,4480]{1,0:T(8,128)(2,1)S(1)} %collective-permute-done.23.refs_1_), custom_call_target="tpu_custom_call" | custom-call | flops 1 | bytes 1 | tf_op jit(solution)/shard_map/pallas_call | solution.py:45
  (2 shorter events, 0.0 us)
Async XLA Ops:
  1.7 10.0 %collective-permute-start = (bf16[8,4224]{1,0:T(8,128)(2,1)S(1)}, bf16[8,4224]{1,0:T(8,128)(2,1)S(1)}, u32[]{:S(2)}, u32[]{:S(2)}) collective-permute-start(bf16[8,4224]{1,0:T(8,128)(2,1)S(1)} %shard_map.122.refs_0_), channel_id=1, source_target_pairs={{0,16},{1,17},{2,18},{3,19},{4,20},{5,21},{6,22},{7,23},{8,24},{9,... | collective-permute-start | bytes 202760 | tf_op jit(solution)/shard_map/ppermute | solution.py:37
  5.8 6.3 %collective-permute-start.1 = (bf16[8,4224]{1,0:T(8,128)(2,1)S(1)}, bf16[8,4224]{1,0:T(8,128)(2,1)S(1)}, u32[]{:S(2)}, u32[]{:S(2)}) collective-permute-start(bf16[8,4224]{1,0:T(8,128)(2,1)S(1)} %shard_map.122.refs_0_), channel_id=1, source_target_pairs={{0,24},{1,25},{2,26},{3,27},{4,28},{5,29},{6,30},{7,31},{8,16},{9,... | collective-permute-start | bytes 202760 | tf_op jit(solution)/shard_map/ppermute | solution.py:37
  7.2 5.0 %collective-permute-start.2 = (bf16[8,4224]{1,0:T(8,128)(2,1)S(1)}, bf16[8,4224]{1,0:T(8,128)(2,1)S(1)}, u32[]{:S(2)}, u32[]{:S(2)}) collective-permute-start(bf16[8,4224]{1,0:T(8,128)(2,1)S(1)} %shard_map.122.refs_0_), channel_id=1, source_target_pairs={{0,8},{1,9},{2,10},{3,11},{4,12},{5,13},{6,14},{7,15},{8,0},{9,1},... | collective-permute-start | bytes 202760 | tf_op jit(solution)/shard_map/ppermute | solution.py:37
  7.4 8.0 %collective-permute-start.5 = (bf16[8,4224]{1,0:T(8,128)(2,1)S(1)}, bf16[8,4224]{1,0:T(8,128)(2,1)S(1)}, u32[]{:S(2)}, u32[]{:S(2)}) collective-permute-start(bf16[8,4224]{1,0:T(8,128)(2,1)S(1)} %shard_map.122.refs_0_), channel_id=1, source_target_pairs={{0,6},{1,7},{2,4},{3,5},{4,2},{5,3},{6,0},{7,1},{8,14},{9,15},{10,... | collective-permute-start | bytes 202760 | tf_op jit(solution)/shard_map/ppermute | solution.py:37
  12.2 9.5 %collective-permute-start.3 = (bf16[32,4224]{1,0:T(8,128)(2,1)S(1)}, bf16[32,4224]{1,0:T(8,128)(2,1)S(1)}, u32[]{:S(2)}, u32[]{:S(2)}) collective-permute-start(bf16[32,4224]{1,0:T(8,128)(2,1)S(1)} %shard_map.124.refs_0_), channel_id=1, source_target_pairs={{0,2},{1,3},{2,0},{3,1},{4,6},{5,7},{6,4},{7,5},{8,10},{9,11},{10,... | collective-permute-start | bytes 811016 | tf_op jit(solution)/shard_map/ppermute | solution.py:37
  13.8 7.9 %collective-permute-start.4 = (bf16[32,4224]{1,0:T(8,128)(2,1)S(1)}, bf16[32,4224]{1,0:T(8,128)(2,1)S(1)}, u32[]{:S(2)}, u32[]{:S(2)}) collective-permute-start(bf16[32,4224]{1,0:T(8,128)(2,1)S(1)} %shard_map.124.refs_0_), channel_id=1, source_target_pairs={{0,4},{1,5},{2,6},{3,7},{4,0},{5,1},{6,2},{7,3},{8,12},{9,13},{10,... | collective-permute-start | bytes 811016 | tf_op jit(solution)/shard_map/ppermute | solution.py:37
  15.4 7.1 %collective-permute-start.6 = (bf16[8,4224]{1,0:T(8,128)(2,1)S(1)}, bf16[8,4224]{1,0:T(8,128)(2,1)S(1)}, u32[]{:S(2)}, u32[]{:S(2)}) collective-permute-start(bf16[8,4224]{1,0:T(8,128)(2,1)S(1)} %collective-permute-done.5.refs_0_), channel_id=1, source_target_pairs={{0,16},{1,17},{2,18},{3,19},{4,20},{5,21},{6,22},{7,23},{8,24},{9,... | collective-permute-start | bytes 202760 | tf_op jit(solution)/shard_map/ppermute | solution.py:37
  18.1 6.1 %collective-permute-start.7 = (bf16[8,4224]{1,0:T(8,128)(2,1)S(1)}, bf16[8,4224]{1,0:T(8,128)(2,1)S(1)}, u32[]{:S(2)}, u32[]{:S(2)}) collective-permute-start(bf16[8,4224]{1,0:T(8,128)(2,1)S(1)} %collective-permute-done.5.refs_0_), channel_id=1, source_target_pairs={{0,24},{1,25},{2,26},{3,27},{4,28},{5,29},{6,30},{7,31},{8,16},{9,... | collective-permute-start | bytes 202760 | tf_op jit(solution)/shard_map/ppermute | solution.py:37
  18.7 5.5 %collective-permute-start.8 = (bf16[8,4224]{1,0:T(8,128)(2,1)S(1)}, bf16[8,4224]{1,0:T(8,128)(2,1)S(1)}, u32[]{:S(2)}, u32[]{:S(2)}) collective-permute-start(bf16[8,4224]{1,0:T(8,128)(2,1)S(1)} %collective-permute-done.5.refs_0_), channel_id=1, source_target_pairs={{0,8},{1,9},{2,10},{3,11},{4,12},{5,13},{6,14},{7,15},{8,0},{9,1},... | collective-permute-start | bytes 202760 | tf_op jit(solution)/shard_map/ppermute | solution.py:37
  21.7 2.6 %copy-start = (bf16[384,4096]{1,0:T(8,128)(2,1)S(1)}, bf16[384,4096]{1,0:T(8,128)(2,1)}, u32[]{:S(2)}) copy-start(bf16[384,4096]{1,0:T(8,128)(2,1)} %refs_8_.3) | copy-start | bytes 9437188
  21.7 2.6 %collective-permute-start.10 = (bf16[32,4224]{1,0:T(8,128)(2,1)S(1)}, bf16[32,4224]{1,0:T(8,128)(2,1)S(1)}, u32[]{:S(2)}, u32[]{:S(2)}) collective-permute-start(bf16[32,4224]{1,0:T(8,128)(2,1)S(1)} %collective-permute-done.4.refs_1_), channel_id=1, source_target_pairs={{0,1},{1,0},{2,3},{3,2},{4,5},{5,4},{6,7},{7,6},{8,9},{9,8},{10,11... | collective-permute-start | bytes 811016 | tf_op jit(solution)/shard_map/ppermute | solution.py:37
  21.8 2.5 %collective-permute-start.9 = (bf16[32,4224]{1,0:T(8,128)(2,1)S(1)}, bf16[32,4224]{1,0:T(8,128)(2,1)S(1)}, u32[]{:S(2)}, u32[]{:S(2)}) collective-permute-start(bf16[32,4224]{1,0:T(8,128)(2,1)S(1)} %collective-permute-done.3.refs_0_), channel_id=1, source_target_pairs={{0,1},{1,0},{2,3},{3,2},{4,5},{5,4},{6,7},{7,6},{8,9},{9,8},{10,11... | collective-permute-start | bytes 811016 | tf_op jit(solution)/shard_map/ppermute | solution.py:37
  22.5 4.3 %collective-permute-start.11 = (bf16[32,4224]{1,0:T(8,128)(2,1)S(1)}, bf16[32,4224]{1,0:T(8,128)(2,1)S(1)}, u32[]{:S(2)}, u32[]{:S(2)}) collective-permute-start(bf16[32,4224]{1,0:T(8,128)(2,1)S(1)} %shard_map.124.refs_0_), channel_id=1, source_target_pairs={{0,1},{1,0},{2,3},{3,2},{4,5},{5,4},{6,7},{7,6},{8,9},{9,8},{10,11... | collective-permute-start | bytes 811016 | tf_op jit(solution)/shard_map/ppermute | solution.py:37
  24.2 2.6 %collective-permute-start.12 = (bf16[32,4224]{1,0:T(8,128)(2,1)S(1)}, bf16[32,4224]{1,0:T(8,128)(2,1)S(1)}, u32[]{:S(2)}, u32[]{:S(2)}) collective-permute-start(bf16[32,4224]{1,0:T(8,128)(2,1)S(1)} %shard_map.126.refs_1_), channel_id=1, source_target_pairs={{0,1},{1,0},{2,3},{3,2},{4,5},{5,4},{6,7},{7,6},{8,9},{9,8},{10,11... | collective-permute-start | bytes 811016 | tf_op jit(solution)/shard_map/ppermute | solution.py:37
  26.3 2.6 %collective-permute-start.14 = (bf16[64,4480]{1,0:T(8,128)(2,1)S(1)}, bf16[64,4480]{1,0:T(8,128)(2,1)S(1)}, u32[]{:S(2)}, u32[]{:S(2)}) collective-permute-start(bf16[64,4480]{1,0:T(8,128)(2,1)S(1)} %get-tuple-element.55), channel_id=1, source_target_pairs={{0,1},{1,0},{2,3},{3,2},{4,5},{5,4},{6,7},{7,6},{8,9},{9,8},{10,11... | collective-permute-start | bytes 1720328 | tf_op jit(solution)/shard_map/ppermute | solution.py:37
  28.8 2.0 %collective-permute-start.13 = (bf16[64,4480]{1,0:T(8,128)(2,1)S(1)}, bf16[64,4480]{1,0:T(8,128)(2,1)S(1)}, u32[]{:S(2)}, u32[]{:S(2)}) collective-permute-start(bf16[64,4480]{1,0:T(8,128)(2,1)S(1)} %get-tuple-element.53), channel_id=1, source_target_pairs={{0,1},{1,0},{2,3},{3,2},{4,5},{5,4},{6,7},{7,6},{8,9},{9,8},{10,11... | collective-permute-start | bytes 1720328 | tf_op jit(solution)/shard_map/ppermute | solution.py:37
  29.2 9.3 %collective-permute-start.15 = (bf16[32,4480]{1,0:T(8,128)(2,1)S(1)}, bf16[32,4480]{1,0:T(8,128)(2,1)S(1)}, u32[]{:S(2)}, u32[]{:S(2)}) collective-permute-start(bf16[32,4480]{1,0:T(8,128)(2,1)S(1)} %get-tuple-element.56), channel_id=1, source_target_pairs={{0,2},{1,3},{2,0},{3,1},{4,6},{5,7},{6,4},{7,5},{8,10},{9,11},{10,... | collective-permute-start | bytes 860168 | tf_op jit(solution)/shard_map/ppermute | solution.py:37
  29.8 8.9 %collective-permute-start.16 = (bf16[32,4480]{1,0:T(8,128)(2,1)S(1)}, bf16[32,4480]{1,0:T(8,128)(2,1)S(1)}, u32[]{:S(2)}, u32[]{:S(2)}) collective-permute-start(bf16[32,4480]{1,0:T(8,128)(2,1)S(1)} %get-tuple-element.57), channel_id=1, source_target_pairs={{0,4},{1,5},{2,6},{3,7},{4,0},{5,1},{6,2},{7,3},{8,12},{9,13},{10,... | collective-permute-start | bytes 860168 | tf_op jit(solution)/shard_map/ppermute | solution.py:37
  31.1 11.1 %collective-permute-start.20 = (bf16[8,4480]{1,0:T(8,128)(2,1)S(1)}, bf16[8,4480]{1,0:T(8,128)(2,1)S(1)}, u32[]{:S(2)}, u32[]{:S(2)}) collective-permute-start(bf16[8,4480]{1,0:T(8,128)(2,1)S(1)} %get-tuple-element.63), channel_id=1, source_target_pairs={{0,16},{1,17},{2,18},{3,19},{4,20},{5,21},{6,22},{7,23},{8,24},{9,... | collective-permute-start | bytes 215048 | tf_op jit(solution)/shard_map/ppermute | solution.py:37
  33.8 8.7 %collective-permute-start.21 = (bf16[8,4480]{1,0:T(8,128)(2,1)S(1)}, bf16[8,4480]{1,0:T(8,128)(2,1)S(1)}, u32[]{:S(2)}, u32[]{:S(2)}) collective-permute-start(bf16[8,4480]{1,0:T(8,128)(2,1)S(1)} %get-tuple-element.64), channel_id=1, source_target_pairs={{0,24},{1,25},{2,26},{3,27},{4,28},{5,29},{6,30},{7,31},{8,16},{9,... | collective-permute-start | bytes 215048 | tf_op jit(solution)/shard_map/ppermute | solution.py:37
  34.6 7.9 %collective-permute-start.22 = (bf16[8,4480]{1,0:T(8,128)(2,1)S(1)}, bf16[8,4480]{1,0:T(8,128)(2,1)S(1)}, u32[]{:S(2)}, u32[]{:S(2)}) collective-permute-start(bf16[8,4480]{1,0:T(8,128)(2,1)S(1)} %get-tuple-element.65), channel_id=1, source_target_pairs={{0,8},{1,9},{2,10},{3,11},{4,12},{5,13},{6,14},{7,15},{8,0},{9,1},... | collective-permute-start | bytes 215048 | tf_op jit(solution)/shard_map/ppermute | solution.py:37
  39.0 7.6 %collective-permute-start.17 = (bf16[8,4480]{1,0:T(8,128)(2,1)S(1)}, bf16[8,4480]{1,0:T(8,128)(2,1)S(1)}, u32[]{:S(2)}, u32[]{:S(2)}) collective-permute-start(bf16[8,4480]{1,0:T(8,128)(2,1)S(1)} %get-tuple-element.59), channel_id=1, source_target_pairs={{0,16},{1,17},{2,18},{3,19},{4,20},{5,21},{6,22},{7,23},{8,24},{9,... | collective-permute-start | bytes 215048 | tf_op jit(solution)/shard_map/ppermute | solution.py:37
  41.6 6.2 %collective-permute-start.18 = (bf16[8,4480]{1,0:T(8,128)(2,1)S(1)}, bf16[8,4480]{1,0:T(8,128)(2,1)S(1)}, u32[]{:S(2)}, u32[]{:S(2)}) collective-permute-start(bf16[8,4480]{1,0:T(8,128)(2,1)S(1)} %get-tuple-element.60), channel_id=1, source_target_pairs={{0,24},{1,25},{2,26},{3,27},{4,28},{5,29},{6,30},{7,31},{8,16},{9,... | collective-permute-start | bytes 215048 | tf_op jit(solution)/shard_map/ppermute | solution.py:37
  42.2 5.7 %collective-permute-start.19 = (bf16[8,4480]{1,0:T(8,128)(2,1)S(1)}, bf16[8,4480]{1,0:T(8,128)(2,1)S(1)}, u32[]{:S(2)}, u32[]{:S(2)}) collective-permute-start(bf16[8,4480]{1,0:T(8,128)(2,1)S(1)} %get-tuple-element.61), channel_id=1, source_target_pairs={{0,8},{1,9},{2,10},{3,11},{4,12},{5,13},{6,14},{7,15},{8,0},{9,1},... | collective-permute-start | bytes 215048 | tf_op jit(solution)/shard_map/ppermute | solution.py:37
  42.7 5.3 %collective-permute-start.23 = (bf16[8,4480]{1,0:T(8,128)(2,1)S(1)}, bf16[8,4480]{1,0:T(8,128)(2,1)S(1)}, u32[]{:S(2)}, u32[]{:S(2)}) collective-permute-start(bf16[8,4480]{1,0:T(8,128)(2,1)S(1)} %shard_map.133), channel_id=1, source_target_pairs={{0,6},{1,7},{2,4},{3,5},{4,2},{5,3},{6,0},{7,1},{8,14},{9,15},{10,... | collective-permute-start | bytes 215048 | tf_op jit(solution)/shard_map/ppermute | solution.py:37

commit v8 on v7

--- a/solution.py
+++ b/solution.py
@@ -120,10 +120,9 @@
 
 
 def attention_kernel(own, offsets, *refs):
-    length_hbm, query_hbm, key_hbm, value_hbm, weight_hbm, near_ref, far_ref, weight_out = refs[:8]
-    length_ref, query_ref, key_ref, value_ref, wide_ref, mean_ref, logs_ref, dest_ref, sems = refs[8:]
-    sources = [length_hbm, query_hbm, key_hbm, value_hbm, weight_hbm]
-    copies = fetch(sources, [length_ref, query_ref, key_ref, value_ref, weight_out], sems)
+    length_hbm, weight_hbm, query_ref, key_ref, value_ref, near_ref, far_ref, weight_out = refs[:8]
+    length_ref, wide_ref, mean_ref, logs_ref, dest_ref, sems = refs[8:]
+    copies = fetch([length_hbm, weight_hbm], [length_ref, weight_out], sems)
     me = lax.axis_index("ffn")
     rows, seg_len, _ = key_ref.shape
     per_group = HEADS // KV_HEADS
@@ -131,11 +130,7 @@
     per_dest = max(1, own // HEAD_DIM)
     extra = near_ref.shape[1]
     lane = lax.broadcasted_iota(jnp.int32, (rows, extra), 1)
-    copies[0].wait()
-    copies[1].wait()
     wide_ref[...] = query_ref[...].astype(jnp.float32)
-    copies[2].wait()
-    copies[3].wait()
     pairs = [(row, group) for row in range(rows) for group in range(KV_HEADS)]
     heads = [pl.ds(group * per_group * rows + row, per_group, rows) for row, group in pairs]
     cols = [slice(group * HEAD_DIM, (group + 1) * HEAD_DIM) for _, group in pairs]
@@ -145,6 +140,7 @@
         for q, c, (row, _) in zip(queries, cols, pairs)
     ]
     scores = jnp.stack(scores).reshape(rows, KV_HEADS * per_group, seg_len) * HEAD_DIM ** (-0.5)
+    copies[0].wait()
     usable = jnp.stack([place < length_ref[row] for row in range(rows)])
     peak = jnp.max(jnp.where(usable, scores, -1e30), axis=-1, keepdims=True)
     weights = jnp.where(usable, jnp.exp(scores - peak), 0.0).astype(jnp.bfloat16)
@@ -182,30 +178,26 @@
         for first in range(0, len(offsets), 2):
             pair = [dest_ref[me ^ (offset ^ core)] for offset in offsets[first : first + 2]]
             out_ref[first * rows : (first + 2) * rows] = jnp.concatenate(pair, axis=0).astype(jnp.bfloat16)
-    copies[4].wait()
-
-
-def attend(query, k_cache, v_cache, cache_len, levels, weight):
+    copies[1].wait()
+
+
+def attend(stacked, k_cache, v_cache, cache_len, levels, weight):
     devices = lax.axis_size("ffn")
-    rows, seg_len, _ = k_cache.shape
-    own = query.shape[1] // devices
+    rows, _, _ = k_cache.shape
+    own = HEADS * HEAD_DIM // devices
     extra = -(-(own + 3 * max(1, own // HEAD_DIM)) // LANES) * LANES
-    stacked = query.reshape(rows, HEADS, HEAD_DIM).transpose(1, 0, 2).reshape(HEADS * rows, HEAD_DIM)
     offsets = offsets_of(levels)
     out = jax.ShapeDtypeStruct((len(offsets) * rows, extra), jnp.bfloat16)
     return call(
         functools.partial(attention_kernel, own, offsets),
         [out, out, pltpu.VMEM(weight.shape, weight.dtype)],
-        in_hbm(cache_len, stacked, k_cache, v_cache, weight),
-        in_specs=[HBM] * 5,
+        [*in_hbm(cache_len, weight), stacked, k_cache, v_cache],
+        in_specs=[HBM] * 2 + [VMEM] * 3,
         scratch=[
             pltpu.SMEM(cache_len.shape, cache_len.dtype),
-            pltpu.VMEM(stacked.shape, stacked.dtype),
-            pltpu.VMEM(k_cache.shape, k_cache.dtype),
-            pltpu.VMEM(v_cache.shape, v_cache.dtype),
             *[pltpu.VMEM(stacked.shape, jnp.float32)] * 3,
             pltpu.VMEM((devices, rows, extra), jnp.float32),
-            fetched(5),
+            fetched(2),
         ],
         flops=4 * 10**9,
     )
@@ -273,19 +265,24 @@
 
 def sum_kernel(count, width, own, last, *refs):
     refs, outs = refs[:count], refs[count:]
-    first = 0
-    for out_ref in outs[:1] if last else outs:
-        rows = out_ref.shape[0]
-        at = slice(first, first + rows)
-        first += rows
+    rows = refs[0].shape[0]
+    step = min(rows, 16)
+    for first in range(0, rows, step):
+        at = slice(first, first + step)
         total = sum(ref[at, :width].astype(jnp.float32) for ref in refs)
         mean = merged(own, [ref[at, width:].astype(jnp.float32) for ref in refs])
         if last:
-            outs[0][...] = total.astype(jnp.bfloat16)
-            outs[1][...] = mean[:, :own].astype(jnp.bfloat16)
-        else:
-            out_ref[:, :width] = total.astype(jnp.bfloat16)
-            out_ref[:, width:] = mean.astype(jnp.bfloat16)
+            outs[0][at] = total.astype(jnp.bfloat16)
+            outs[1][at] = mean[:, :own].astype(jnp.bfloat16)
+            continue
+        start = 0
+        for out_ref in outs:
+            low, high = max(first, start), min(first + step, start + out_ref.shape[0])
+            if low < high:
+                here, part = slice(low - start, high - start), slice(low - first, high - first)
+                out_ref[here, :width] = total[part].astype(jnp.bfloat16)
+                out_ref[here, width:] = mean[part].astype(jnp.bfloat16)
+            start += out_ref.shape[0]
 
 
 def summed(parts, sizes, width, own, last=False, flops=1):
@@ -354,11 +351,12 @@
     rows = rows_dev * (devices // (2 * radix))
     cut = [rows // outer[0][1]] * outer[0][1]
     across = [exchange(block, corner)] if radix == 4 else []
-    (w_gate,) = keep(w_gate)
+    stacked = query.reshape(-1, HEADS, HEAD_DIM).transpose(1, 0, 2).reshape(-1, HEAD_DIM)
+    w_gate, stacked, k_cache, v_cache = keep(w_gate, stacked, k_cache, v_cache)
     base = gather(block, outer, w_gate)
     sides = [1, 2] if radix == 4 else [1]
     chunks = [exchange(base, stride * k) for k in sides]
-    *sums, w_up = attend(after(query, base), k_cache, v_cache, cache_len, levels, w_up)
+    *sums, w_up = attend(after(stacked, base), k_cache, v_cache, cache_len, levels, w_up)
     weights = (w_gate, w_up, w_down)
     last_chunk = [gather(a, outer, sums[0], flops=25 * 10**8) for a in across]
     count = len(sides)

time: 48.9 us -> 48.8 us (level)
  waiting for transfers between devices: 10.6 us -> 9.65 us
  starting transfers between devices: 25.9 us -> 26.4 us
    ppermute x24, waiting for transfers between devices: 10.6 us -> 9.65 us  [exchange(): return lax.ppermute(value, 'ffn', [(i, i ^ distance) for i in range(size)])]
    ppermute x24, starting transfers between devices: 25.9 us -> 26.4 us  [exchange(): return lax.ppermute(value, 'ffn', [(i, i ^ distance) for i in range(size)])]
  transfers between devices with their start and end apart: 24 -> 24, of which waited for: 9 -> 7; matrix products, arithmetic and copies ran while one was open for 0% -> 0% of each run, Pallas kernels for 20% -> 21%
where the time goes in v8:
time: 48.8 us; the launch traced here: 48.6 us
  starting transfers between devices  26.4 us (54%)
  Pallas kernels  11.8 us (24%)
  waiting for transfers between devices  9.65 us (20%)
  between operations  0.82 us (2%)
    ppermute x24, starting transfers between devices, exchange(): return lax.ppermute(value, 'ffn', [(i, i ^ distance) for i in range(size)])  26.4 us
    pallas_call x13, Pallas kernels, call(): pl.pallas_call(body, out_shape=out_shape, in_specs=in_specs or [VMEM] * l...  11.8 us
    ppermute x24, waiting for transfers between devices, exchange(): return lax.ppermute(value, 'ffn', [(i, i ^ distance) for i in range(size)])  9.65 us
  transfers between devices with their start and end apart: 24, of which 7 were waited for; matrix products, arithmetic and copies ran while one was open for 0% of the time, Pallas kernels for 21%

profile of v8, /device:TPU:0, one launch (start us, length us, event | category | flops | bytes accessed | tf_op | source)
XLA Modules:
  0.0 48.6 jit_solution(10208332776938560288)
XLA Ops:
  0.6 1.1 %shard_map.122.refs_0_ = bf16[8,4224]{1,0:T(8,128)(2,1)S(1)} custom-call(bf16[8,4096]{1,0:T(8,128)(2,1)} %tokens_hbm.1, f32[1,4096]{1,0:T(1,128)} %bitcast.6, s32[8,8]{1,0:T(8,128)} %routes_hbm.1, f32[8,8]{1,0:T(8,128)} %scores_hbm.1), custom_call_target="tpu_custom_call" | custom-call | flops 1 | bytes 1 | tf_op jit(solution)/shard_map/pallas_call | solution.py:45
  1.7 4.1 %collective-permute-start = (bf16[8,4224]{1,0:T(8,128)(2,1)S(1)}, bf16[8,4224]{1,0:T(8,128)(2,1)S(1)}, u32[]{:S(2)}, u32[]{:S(2)}) collective-permute-start(bf16[8,4224]{1,0:T(8,128)(2,1)S(1)} %shard_map.122.refs_0_), channel_id=1, source_target_pairs={{0,16},{1,17},{2,18},{3,19},{4,20},{5,21},{6,22},{7,23},{8,24},{9,... | collective-permute-start | bytes 202760 | tf_op jit(solution)/shard_map/ppermute | solution.py:37
  5.8 1.3 %collective-permute-start.1 = (bf16[8,4224]{1,0:T(8,128)(2,1)S(1)}, bf16[8,4224]{1,0:T(8,128)(2,1)S(1)}, u32[]{:S(2)}, u32[]{:S(2)}) collective-permute-start(bf16[8,4224]{1,0:T(8,128)(2,1)S(1)} %shard_map.122.refs_0_), channel_id=1, source_target_pairs={{0,24},{1,25},{2,26},{3,27},{4,28},{5,29},{6,30},{7,31},{8,16},{9,... | collective-permute-start | bytes 202760 | tf_op jit(solution)/shard_map/ppermute | solution.py:37
  7.2 0.2 collective-permute-start.2
  7.4 2.4 %collective-permute-start.5 = (bf16[8,4224]{1,0:T(8,128)(2,1)S(1)}, bf16[8,4224]{1,0:T(8,128)(2,1)S(1)}, u32[]{:S(2)}, u32[]{:S(2)}) collective-permute-start(bf16[8,4224]{1,0:T(8,128)(2,1)S(1)} %shard_map.122.refs_0_), channel_id=1, source_target_pairs={{0,6},{1,7},{2,4},{3,5},{4,2},{5,3},{6,0},{7,1},{8,14},{9,15},{10,... | collective-permute-start | bytes 202760 | tf_op jit(solution)/shard_map/ppermute | solution.py:37
  9.8 2.6 %shard_map.123 = (bf16[4096,384]{1,0:T(8,128)(2,1)S(1)}, bf16[512,128]{1,0:T(8,128)(2,1)S(1)}, bf16[8,128,512]{2,1,0:T(8,128)(2,1)S(1)}, bf16[8,128,512]{2,1,0:T(8,128)(2,1)S(1)}) custom-call(bf16[4096,384]{1,0:T(8,128)(2,1)} %refs_0_.2, bf16[512,128]{1,0:T(8,128)(2,1)} %bitcast.7, bf16[8,128,512]{2,1,0:T(8,128)(2,1)} %refs_2_.1, bf16[8,128,512]{2,1,0:T(8,128)(2,1)} %refs_3_.1), custom_call_target="tpu_custom_call" | custom-call | flops 4000000000 | bytes 1 | tf_op jit(solution)/shard_map/pallas_call | solution.py:45
  12.4 0.0 collective-permute-done.refs_1_
  12.4 0.0 collective-permute-done.1.refs_2_
  12.4 0.0 collective-permute-done.2.refs_3_
  12.5 1.4 %collective-permute-start.3 = (bf16[32,4224]{1,0:T(8,128)(2,1)S(1)}, bf16[32,4224]{1,0:T(8,128)(2,1)S(1)}, u32[]{:S(2)}, u32[]{:S(2)}) collective-permute-start(bf16[32,4224]{1,0:T(8,128)(2,1)S(1)} %shard_map.124.refs_0_), channel_id=1, source_target_pairs={{0,2},{1,3},{2,0},{3,1},{4,6},{5,7},{6,4},{7,5},{8,10},{9,11},{10,... | collective-permute-start | bytes 811016 | tf_op jit(solution)/shard_map/ppermute | solution.py:37
  13.8 1.5 %collective-permute-start.4 = (bf16[32,4224]{1,0:T(8,128)(2,1)S(1)}, bf16[32,4224]{1,0:T(8,128)(2,1)S(1)}, u32[]{:S(2)}, u32[]{:S(2)}) collective-permute-start(bf16[32,4224]{1,0:T(8,128)(2,1)S(1)} %shard_map.124.refs_0_), channel_id=1, source_target_pairs={{0,4},{1,5},{2,6},{3,7},{4,0},{5,1},{6,2},{7,3},{8,12},{9,13},{10,... | collective-permute-start | bytes 811016 | tf_op jit(solution)/shard_map/ppermute | solution.py:37
  15.4 0.0 collective-permute-done.5.refs_0_
  15.4 2.7 %collective-permute-start.6 = (bf16[8,4224]{1,0:T(8,128)(2,1)S(1)}, bf16[8,4224]{1,0:T(8,128)(2,1)S(1)}, u32[]{:S(2)}, u32[]{:S(2)}) collective-permute-start(bf16[8,4224]{1,0:T(8,128)(2,1)S(1)} %collective-permute-done.5.refs_0_), channel_id=1, source_target_pairs={{0,16},{1,17},{2,18},{3,19},{4,20},{5,21},{6,22},{7,23},{8,24},{9,... | collective-permute-start | bytes 202760 | tf_op jit(solution)/shard_map/ppermute | solution.py:37
  18.1 0.6 %collective-permute-start.7 = (bf16[8,4224]{1,0:T(8,128)(2,1)S(1)}, bf16[8,4224]{1,0:T(8,128)(2,1)S(1)}, u32[]{:S(2)}, u32[]{:S(2)}) collective-permute-start(bf16[8,4224]{1,0:T(8,128)(2,1)S(1)} %collective-permute-done.5.refs_0_), channel_id=1, source_target_pairs={{0,24},{1,25},{2,26},{3,27},{4,28},{5,29},{6,30},{7,31},{8,16},{9,... | collective-permute-start | bytes 202760 | tf_op jit(solution)/shard_map/ppermute | solution.py:37
  18.7 0.3 collective-permute-start.8
  18.9 2.4 %shard_map.125 = (bf16[128,384]{1,0:T(8,128)(2,1)S(1)}, bf16[128,384]{1,0:T(8,128)(2,1)S(1)}, bf16[4096,384]{1,0:T(8,128)(2,1)S(1)}) custom-call(s32[8]{0:T(128)} %refs_0_.3, bf16[4096,384]{1,0:T(8,128)(2,1)} %refs_1_.1, bf16[512,128]{1,0:T(8,128)(2,1)S(1)} %get-tuple-element.45.refs_2_, bf16[8,128,512]{2,1,0:T(8,128)(2,1)S(1)} %get-tuple-element.46.refs_3_, ...), custom_call_target="tpu_custom_call" | custom-call | flops 4000000000 | bytes 1 | tf_op jit(solution)/shard_map/pallas_call | solution.py:45
  21.4 0.0 collective-permute-done.3.refs_0_
  21.4 0.0 collective-permute-done.4.refs_1_
  21.4 0.0 copy-start
  21.4 0.1 collective-permute-start.10
  21.5 0.5 %collective-permute-start.9 = (bf16[32,4224]{1,0:T(8,128)(2,1)S(1)}, bf16[32,4224]{1,0:T(8,128)(2,1)S(1)}, u32[]{:S(2)}, u32[]{:S(2)}) collective-permute-start(bf16[32,4224]{1,0:T(8,128)(2,1)S(1)} %collective-permute-done.3.refs_0_), channel_id=1, source_target_pairs={{0,1},{1,0},{2,3},{3,2},{4,5},{5,4},{6,7},{7,6},{8,9},{9,8},{10,11... | collective-permute-start | bytes 811016 | tf_op jit(solution)/shard_map/ppermute | solution.py:37
  22.0 0.5 collective-permute-done.6.refs_1_
  22.5 0.0 collective-permute-start.11
  22.5 1.7 %collective-permute-done.7.refs_2_ = bf16[8,4224]{1,0:T(8,128)(2,1)S(1)} collective-permute-done((bf16[8,4224]{1,0:T(8,128)(2,1)S(1)}, bf16[8,4224]{1,0:T(8,128)(2,1)S(1)}, u32[]{:S(2)}, u32[]{:S(2)}) %collective-permute-start.7) | collective-permute-done | bytes 67616 | tf_op jit(solution)/shard_map/ppermute | solution.py:37
  24.2 0.0 collective-permute-done.8.refs_3_
  24.2 0.1 collective-permute-start.12
  24.3 0.0 collective-permute-done.10.refs_3_
  24.3 0.0 collective-permute-done.9.refs_2_
  24.3 0.0 copy-done
  24.3 1.9 %shard_map.127 = (bf16[64,4480]{1,0:T(8,128)(2,1)S(1)}, bf16[64,4480]{1,0:T(8,128)(2,1)S(1)}) custom-call(bf16[32,4224]{1,0:T(8,128)(2,1)S(1)} %collective-permute-done.3.refs_0_, bf16[32,4224]{1,0:T(8,128)(2,1)S(1)} %collective-permute-done.4.refs_1_, bf16[32,4224]{1,0:T(8,128)(2,1)S(1)} %collective-permute-done.9.refs_2_, ...), custom_call_target="tpu_custom_call" | custom-call | flops 4000000000 | bytes 9437184 | tf_op jit(solution)/shard_map/pallas_call | solution.py:45
  26.3 0.5 %collective-permute-start.14 = (bf16[64,4480]{1,0:T(8,128)(2,1)S(1)}, bf16[64,4480]{1,0:T(8,128)(2,1)S(1)}, u32[]{:S(2)}, u32[]{:S(2)}) collective-permute-start(bf16[64,4480]{1,0:T(8,128)(2,1)S(1)} %get-tuple-element.63), channel_id=1, source_target_pairs={{0,1},{1,0},{2,3},{3,2},{4,5},{5,4},{6,7},{7,6},{8,9},{9,8},{10,11... | collective-permute-start | bytes 1720328 | tf_op jit(solution)/shard_map/ppermute | solution.py:37
  26.8 0.0 collective-permute-done.11.refs_2_
  26.8 0.0 collective-permute-done.12.refs_3_
  26.8 2.0 %shard_map.128 = (bf16[64,4480]{1,0:T(8,128)(2,1)S(1)}, bf16[64,4480]{1,0:T(8,128)(2,1)S(1)}) custom-call(bf16[32,4224]{1,0:T(8,128)(2,1)S(1)} %shard_map.124.refs_0_, bf16[32,4224]{1,0:T(8,128)(2,1)S(1)} %shard_map.126.refs_1_, bf16[32,4224]{1,0:T(8,128)(2,1)S(1)} %collective-permute-done.11.refs_2_, bf16[32,4224]{1,0:T(8,128)(2,1)S(1)} %collective-permute-done.12.refs_3_, ...), custom_call_target="tpu_custom_call" | custom-call | flops 4000000000 | bytes 9437184 | tf_op jit(solution)/shard_map/pallas_call | solution.py:45
  28.8 0.1 collective-permute-start.13
  28.9 0.0 collective-permute-done.14.refs_1_
  28.9 0.3 shard_map.130
  29.2 0.6 %collective-permute-start.15 = (bf16[32,4480]{1,0:T(8,128)(2,1)S(1)}, bf16[32,4480]{1,0:T(8,128)(2,1)S(1)}, u32[]{:S(2)}, u32[]{:S(2)}) collective-permute-start(bf16[32,4480]{1,0:T(8,128)(2,1)S(1)} %get-tuple-element.64), channel_id=1, source_target_pairs={{0,2},{1,3},{2,0},{3,1},{4,6},{5,7},{6,4},{7,5},{8,10},{9,11},{10,... | collective-permute-start | bytes 860168 | tf_op jit(solution)/shard_map/ppermute | solution.py:37
  29.8 1.0 %collective-permute-start.16 = (bf16[32,4480]{1,0:T(8,128)(2,1)S(1)}, bf16[32,4480]{1,0:T(8,128)(2,1)S(1)}, u32[]{:S(2)}, u32[]{:S(2)}) collective-permute-start(bf16[32,4480]{1,0:T(8,128)(2,1)S(1)} %get-tuple-element.65), channel_id=1, source_target_pairs={{0,4},{1,5},{2,6},{3,7},{4,0},{5,1},{6,2},{7,3},{8,12},{9,13},{10,... | collective-permute-start | bytes 860168 | tf_op jit(solution)/shard_map/ppermute | solution.py:37
  30.8 0.0 collective-permute-done.13.refs_1_
  30.8 0.3 shard_map.129
  31.1 2.6 %collective-permute-start.20 = (bf16[8,4480]{1,0:T(8,128)(2,1)S(1)}, bf16[8,4480]{1,0:T(8,128)(2,1)S(1)}, u32[]{:S(2)}, u32[]{:S(2)}) collective-permute-start(bf16[8,4480]{1,0:T(8,128)(2,1)S(1)} %get-tuple-element.71), channel_id=1, source_target_pairs={{0,16},{1,17},{2,18},{3,19},{4,20},{5,21},{6,22},{7,23},{8,24},{9,... | collective-permute-start | bytes 215048 | tf_op jit(solution)/shard_map/ppermute | solution.py:37
  33.7 1.2 %collective-permute-start.21 = (bf16[8,4480]{1,0:T(8,128)(2,1)S(1)}, bf16[8,4480]{1,0:T(8,128)(2,1)S(1)}, u32[]{:S(2)}, u32[]{:S(2)}) collective-permute-start(bf16[8,4480]{1,0:T(8,128)(2,1)S(1)} %get-tuple-element.72), channel_id=1, source_target_pairs={{0,24},{1,25},{2,26},{3,27},{4,28},{5,29},{6,30},{7,31},{8,16},{9,... | collective-permute-start | bytes 215048 | tf_op jit(solution)/shard_map/ppermute | solution.py:37
  34.9 0.0 collective-permute-start.22
  34.9 3.6 %collective-permute-done.15.refs_1_ = bf16[32,4480]{1,0:T(8,128)(2,1)S(1)} collective-permute-done((bf16[32,4480]{1,0:T(8,128)(2,1)S(1)}, bf16[32,4480]{1,0:T(8,128)(2,1)S(1)}, u32[]{:S(2)}, u32[]{:S(2)}) %collective-permute-start.15) | collective-permute-done | bytes 286752 | tf_op jit(solution)/shard_map/ppermute | solution.py:37
  38.4 0.3 collective-permute-done.16.refs_2_
  38.7 0.2 shard_map.131
  38.9 2.4 %collective-permute-start.17 = (bf16[8,4480]{1,0:T(8,128)(2,1)S(1)}, bf16[8,4480]{1,0:T(8,128)(2,1)S(1)}, u32[]{:S(2)}, u32[]{:S(2)}) collective-permute-start(bf16[8,4480]{1,0:T(8,128)(2,1)S(1)} %get-tuple-element.67), channel_id=1, source_target_pairs={{0,16},{1,17},{2,18},{3,19},{4,20},{5,21},{6,22},{7,23},{8,24},{9,... | collective-permute-start | bytes 215048 | tf_op jit(solution)/shard_map/ppermute | solution.py:37
  41.3 0.6 %collective-permute-start.18 = (bf16[8,4480]{1,0:T(8,128)(2,1)S(1)}, bf16[8,4480]{1,0:T(8,128)(2,1)S(1)}, u32[]{:S(2)}, u32[]{:S(2)}) collective-permute-start(bf16[8,4480]{1,0:T(8,128)(2,1)S(1)} %get-tuple-element.68), channel_id=1, source_target_pairs={{0,24},{1,25},{2,26},{3,27},{4,28},{5,29},{6,30},{7,31},{8,16},{9,... | collective-permute-start | bytes 215048 | tf_op jit(solution)/shard_map/ppermute | solution.py:37
  41.9 0.0 collective-permute-done.20.refs_1_
  41.9 0.6 %collective-permute-start.19 = (bf16[8,4480]{1,0:T(8,128)(2,1)S(1)}, bf16[8,4480]{1,0:T(8,128)(2,1)S(1)}, u32[]{:S(2)}, u32[]{:S(2)}) collective-permute-start(bf16[8,4480]{1,0:T(8,128)(2,1)S(1)} %get-tuple-element.69), channel_id=1, source_target_pairs={{0,8},{1,9},{2,10},{3,11},{4,12},{5,13},{6,14},{7,15},{8,0},{9,1},... | collective-permute-start | bytes 215048 | tf_op jit(solution)/shard_map/ppermute | solution.py:37
  42.5 0.0 collective-permute-done.21.refs_2_
  42.5 0.0 collective-permute-done.22.refs_3_
  42.5 0.1 shard_map.133
  42.6 1.5 %collective-permute-start.23 = (bf16[8,4480]{1,0:T(8,128)(2,1)S(1)}, bf16[8,4480]{1,0:T(8,128)(2,1)S(1)}, u32[]{:S(2)}, u32[]{:S(2)}) collective-permute-start(bf16[8,4480]{1,0:T(8,128)(2,1)S(1)} %shard_map.133), channel_id=1, source_target_pairs={{0,6},{1,7},{2,4},{3,5},{4,2},{5,3},{6,0},{7,1},{8,14},{9,15},{10,... | collective-permute-start | bytes 215048 | tf_op jit(solution)/shard_map/ppermute | solution.py:37
  44.1 2.1 %collective-permute-done.17.refs_1_ = bf16[8,4480]{1,0:T(8,128)(2,1)S(1)} collective-permute-done((bf16[8,4480]{1,0:T(8,128)(2,1)S(1)}, bf16[8,4480]{1,0:T(8,128)(2,1)S(1)}, u32[]{:S(2)}, u32[]{:S(2)}) %collective-permute-start.17) | collective-permute-done | bytes 71712 | tf_op jit(solution)/shard_map/ppermute | solution.py:37
  46.2 1.3 %collective-permute-done.18.refs_2_ = bf16[8,4480]{1,0:T(8,128)(2,1)S(1)} collective-permute-done((bf16[8,4480]{1,0:T(8,128)(2,1)S(1)}, bf16[8,4480]{1,0:T(8,128)(2,1)S(1)}, u32[]{:S(2)}, u32[]{:S(2)}) %collective-permute-start.18) | collective-permute-done | bytes 71712 | tf_op jit(solution)/shard_map/ppermute | solution.py:37
  47.6 0.0 collective-permute-done.19.refs_3_
  47.6 0.1 shard_map.132.refs_0_
  47.7 0.2 collective-permute-done.23.refs_1_
  47.9 0.7 %shard_map.134 = (bf16[8,4096]{1,0:T(8,128)(2,1)}, bf16[8,256]{1,0:T(8,128)(2,1)}) custom-call(bf16[8,4480]{1,0:T(8,128)(2,1)S(1)} %shard_map.132.refs_0_, bf16[8,4480]{1,0:T(8,128)(2,1)S(1)} %collective-permute-done.23.refs_1_), custom_call_target="tpu_custom_call" | custom-call | flops 1 | bytes 1 | tf_op jit(solution)/shard_map/pallas_call | solution.py:45
  (2 shorter events, 0.0 us)
Async XLA Ops:
  1.7 10.7 %collective-permute-start = (bf16[8,4224]{1,0:T(8,128)(2,1)S(1)}, bf16[8,4224]{1,0:T(8,128)(2,1)S(1)}, u32[]{:S(2)}, u32[]{:S(2)}) collective-permute-start(bf16[8,4224]{1,0:T(8,128)(2,1)S(1)} %shard_map.122.refs_0_), channel_id=1, source_target_pairs={{0,16},{1,17},{2,18},{3,19},{4,20},{5,21},{6,22},{7,23},{8,24},{9,... | collective-permute-start | bytes 202760 | tf_op jit(solution)/shard_map/ppermute | solution.py:37
  5.8 6.6 %collective-permute-start.1 = (bf16[8,4224]{1,0:T(8,128)(2,1)S(1)}, bf16[8,4224]{1,0:T(8,128)(2,1)S(1)}, u32[]{:S(2)}, u32[]{:S(2)}) collective-permute-start(bf16[8,4224]{1,0:T(8,128)(2,1)S(1)} %shard_map.122.refs_0_), channel_id=1, source_target_pairs={{0,24},{1,25},{2,26},{3,27},{4,28},{5,29},{6,30},{7,31},{8,16},{9,... | collective-permute-start | bytes 202760 | tf_op jit(solution)/shard_map/ppermute | solution.py:37
  7.2 5.3 %collective-permute-start.2 = (bf16[8,4224]{1,0:T(8,128)(2,1)S(1)}, bf16[8,4224]{1,0:T(8,128)(2,1)S(1)}, u32[]{:S(2)}, u32[]{:S(2)}) collective-permute-start(bf16[8,4224]{1,0:T(8,128)(2,1)S(1)} %shard_map.122.refs_0_), channel_id=1, source_target_pairs={{0,8},{1,9},{2,10},{3,11},{4,12},{5,13},{6,14},{7,15},{8,0},{9,1},... | collective-permute-start | bytes 202760 | tf_op jit(solution)/shard_map/ppermute | solution.py:37
  7.4 8.0 %collective-permute-start.5 = (bf16[8,4224]{1,0:T(8,128)(2,1)S(1)}, bf16[8,4224]{1,0:T(8,128)(2,1)S(1)}, u32[]{:S(2)}, u32[]{:S(2)}) collective-permute-start(bf16[8,4224]{1,0:T(8,128)(2,1)S(1)} %shard_map.122.refs_0_), channel_id=1, source_target_pairs={{0,6},{1,7},{2,4},{3,5},{4,2},{5,3},{6,0},{7,1},{8,14},{9,15},{10,... | collective-permute-start | bytes 202760 | tf_op jit(solution)/shard_map/ppermute | solution.py:37
  12.5 8.9 %collective-permute-start.3 = (bf16[32,4224]{1,0:T(8,128)(2,1)S(1)}, bf16[32,4224]{1,0:T(8,128)(2,1)S(1)}, u32[]{:S(2)}, u32[]{:S(2)}) collective-permute-start(bf16[32,4224]{1,0:T(8,128)(2,1)S(1)} %shard_map.124.refs_0_), channel_id=1, source_target_pairs={{0,2},{1,3},{2,0},{3,1},{4,6},{5,7},{6,4},{7,5},{8,10},{9,11},{10,... | collective-permute-start | bytes 811016 | tf_op jit(solution)/shard_map/ppermute | solution.py:37
  13.8 7.6 %collective-permute-start.4 = (bf16[32,4224]{1,0:T(8,128)(2,1)S(1)}, bf16[32,4224]{1,0:T(8,128)(2,1)S(1)}, u32[]{:S(2)}, u32[]{:S(2)}) collective-permute-start(bf16[32,4224]{1,0:T(8,128)(2,1)S(1)} %shard_map.124.refs_0_), channel_id=1, source_target_pairs={{0,4},{1,5},{2,6},{3,7},{4,0},{5,1},{6,2},{7,3},{8,12},{9,13},{10,... | collective-permute-start | bytes 811016 | tf_op jit(solution)/shard_map/ppermute | solution.py:37
  15.4 7.1 %collective-permute-start.6 = (bf16[8,4224]{1,0:T(8,128)(2,1)S(1)}, bf16[8,4224]{1,0:T(8,128)(2,1)S(1)}, u32[]{:S(2)}, u32[]{:S(2)}) collective-permute-start(bf16[8,4224]{1,0:T(8,128)(2,1)S(1)} %collective-permute-done.5.refs_0_), channel_id=1, source_target_pairs={{0,16},{1,17},{2,18},{3,19},{4,20},{5,21},{6,22},{7,23},{8,24},{9,... | collective-permute-start | bytes 202760 | tf_op jit(solution)/shard_map/ppermute | solution.py:37
  18.1 6.1 %collective-permute-start.7 = (bf16[8,4224]{1,0:T(8,128)(2,1)S(1)}, bf16[8,4224]{1,0:T(8,128)(2,1)S(1)}, u32[]{:S(2)}, u32[]{:S(2)}) collective-permute-start(bf16[8,4224]{1,0:T(8,128)(2,1)S(1)} %collective-permute-done.5.refs_0_), channel_id=1, source_target_pairs={{0,24},{1,25},{2,26},{3,27},{4,28},{5,29},{6,30},{7,31},{8,16},{9,... | collective-permute-start | bytes 202760 | tf_op jit(solution)/shard_map/ppermute | solution.py:37
  18.7 5.5 %collective-permute-start.8 = (bf16[8,4224]{1,0:T(8,128)(2,1)S(1)}, bf16[8,4224]{1,0:T(8,128)(2,1)S(1)}, u32[]{:S(2)}, u32[]{:S(2)}) collective-permute-start(bf16[8,4224]{1,0:T(8,128)(2,1)S(1)} %collective-permute-done.5.refs_0_), channel_id=1, source_target_pairs={{0,8},{1,9},{2,10},{3,11},{4,12},{5,13},{6,14},{7,15},{8,0},{9,1},... | collective-permute-start | bytes 202760 | tf_op jit(solution)/shard_map/ppermute | solution.py:37
  21.4 2.9 %copy-start = (bf16[384,4096]{1,0:T(8,128)(2,1)S(1)}, bf16[384,4096]{1,0:T(8,128)(2,1)}, u32[]{:S(2)}) copy-start(bf16[384,4096]{1,0:T(8,128)(2,1)} %refs_8_.3) | copy-start | bytes 9437188
  21.4 2.9 %collective-permute-start.10 = (bf16[32,4224]{1,0:T(8,128)(2,1)S(1)}, bf16[32,4224]{1,0:T(8,128)(2,1)S(1)}, u32[]{:S(2)}, u32[]{:S(2)}) collective-permute-start(bf16[32,4224]{1,0:T(8,128)(2,1)S(1)} %collective-permute-done.4.refs_1_), channel_id=1, source_target_pairs={{0,1},{1,0},{2,3},{3,2},{4,5},{5,4},{6,7},{7,6},{8,9},{9,8},{10,11... | collective-permute-start | bytes 811016 | tf_op jit(solution)/shard_map/ppermute | solution.py:37
  21.5 2.8 %collective-permute-start.9 = (bf16[32,4224]{1,0:T(8,128)(2,1)S(1)}, bf16[32,4224]{1,0:T(8,128)(2,1)S(1)}, u32[]{:S(2)}, u32[]{:S(2)}) collective-permute-start(bf16[32,4224]{1,0:T(8,128)(2,1)S(1)} %collective-permute-done.3.refs_0_), channel_id=1, source_target_pairs={{0,1},{1,0},{2,3},{3,2},{4,5},{5,4},{6,7},{7,6},{8,9},{9,8},{10,11... | collective-permute-start | bytes 811016 | tf_op jit(solution)/shard_map/ppermute | solution.py:37
  22.5 4.3 %collective-permute-start.11 = (bf16[32,4224]{1,0:T(8,128)(2,1)S(1)}, bf16[32,4224]{1,0:T(8,128)(2,1)S(1)}, u32[]{:S(2)}, u32[]{:S(2)}) collective-permute-start(bf16[32,4224]{1,0:T(8,128)(2,1)S(1)} %shard_map.124.refs_0_), channel_id=1, source_target_pairs={{0,1},{1,0},{2,3},{3,2},{4,5},{5,4},{6,7},{7,6},{8,9},{9,8},{10,11... | collective-permute-start | bytes 811016 | tf_op jit(solution)/shard_map/ppermute | solution.py:37
  24.2 2.6 %collective-permute-start.12 = (bf16[32,4224]{1,0:T(8,128)(2,1)S(1)}, bf16[32,4224]{1,0:T(8,128)(2,1)S(1)}, u32[]{:S(2)}, u32[]{:S(2)}) collective-permute-start(bf16[32,4224]{1,0:T(8,128)(2,1)S(1)} %shard_map.126.refs_1_), channel_id=1, source_target_pairs={{0,1},{1,0},{2,3},{3,2},{4,5},{5,4},{6,7},{7,6},{8,9},{9,8},{10,11... | collective-permute-start | bytes 811016 | tf_op jit(solution)/shard_map/ppermute | solution.py:37
  26.3 2.6 %collective-permute-start.14 = (bf16[64,4480]{1,0:T(8,128)(2,1)S(1)}, bf16[64,4480]{1,0:T(8,128)(2,1)S(1)}, u32[]{:S(2)}, u32[]{:S(2)}) collective-permute-start(bf16[64,4480]{1,0:T(8,128)(2,1)S(1)} %get-tuple-element.63), channel_id=1, source_target_pairs={{0,1},{1,0},{2,3},{3,2},{4,5},{5,4},{6,7},{7,6},{8,9},{9,8},{10,11... | collective-permute-start | bytes 1720328 | tf_op jit(solution)/shard_map/ppermute | solution.py:37
  28.8 2.1 %collective-permute-start.13 = (bf16[64,4480]{1,0:T(8,128)(2,1)S(1)}, bf16[64,4480]{1,0:T(8,128)(2,1)S(1)}, u32[]{:S(2)}, u32[]{:S(2)}) collective-permute-start(bf16[64,4480]{1,0:T(8,128)(2,1)S(1)} %get-tuple-element.61), channel_id=1, source_target_pairs={{0,1},{1,0},{2,3},{3,2},{4,5},{5,4},{6,7},{7,6},{8,9},{9,8},{10,11... | collective-permute-start | bytes 1720328 | tf_op jit(solution)/shard_map/ppermute | solution.py:37
  29.2 9.3 %collective-permute-start.15 = (bf16[32,4480]{1,0:T(8,128)(2,1)S(1)}, bf16[32,4480]{1,0:T(8,128)(2,1)S(1)}, u32[]{:S(2)}, u32[]{:S(2)}) collective-permute-start(bf16[32,4480]{1,0:T(8,128)(2,1)S(1)} %get-tuple-element.64), channel_id=1, source_target_pairs={{0,2},{1,3},{2,0},{3,1},{4,6},{5,7},{6,4},{7,5},{8,10},{9,11},{10,... | collective-permute-start | bytes 860168 | tf_op jit(solution)/shard_map/ppermute | solution.py:37
  29.8 8.9 %collective-permute-start.16 = (bf16[32,4480]{1,0:T(8,128)(2,1)S(1)}, bf16[32,4480]{1,0:T(8,128)(2,1)S(1)}, u32[]{:S(2)}, u32[]{:S(2)}) collective-permute-start(bf16[32,4480]{1,0:T(8,128)(2,1)S(1)} %get-tuple-element.65), channel_id=1, source_target_pairs={{0,4},{1,5},{2,6},{3,7},{4,0},{5,1},{6,2},{7,3},{8,12},{9,13},{10,... | collective-permute-start | bytes 860168 | tf_op jit(solution)/shard_map/ppermute | solution.py:37
  31.1 10.8 %collective-permute-start.20 = (bf16[8,4480]{1,0:T(8,128)(2,1)S(1)}, bf16[8,4480]{1,0:T(8,128)(2,1)S(1)}, u32[]{:S(2)}, u32[]{:S(2)}) collective-permute-start(bf16[8,4480]{1,0:T(8,128)(2,1)S(1)} %get-tuple-element.71), channel_id=1, source_target_pairs={{0,16},{1,17},{2,18},{3,19},{4,20},{5,21},{6,22},{7,23},{8,24},{9,... | collective-permute-start | bytes 215048 | tf_op jit(solution)/shard_map/ppermute | solution.py:37
  33.7 8.8 %collective-permute-start.21 = (bf16[8,4480]{1,0:T(8,128)(2,1)S(1)}, bf16[8,4480]{1,0:T(8,128)(2,1)S(1)}, u32[]{:S(2)}, u32[]{:S(2)}) collective-permute-start(bf16[8,4480]{1,0:T(8,128)(2,1)S(1)} %get-tuple-element.72), channel_id=1, source_target_pairs={{0,24},{1,25},{2,26},{3,27},{4,28},{5,29},{6,30},{7,31},{8,16},{9,... | collective-permute-start | bytes 215048 | tf_op jit(solution)/shard_map/ppermute | solution.py:37
  34.9 7.6 %collective-permute-start.22 = (bf16[8,4480]{1,0:T(8,128)(2,1)S(1)}, bf16[8,4480]{1,0:T(8,128)(2,1)S(1)}, u32[]{:S(2)}, u32[]{:S(2)}) collective-permute-start(bf16[8,4480]{1,0:T(8,128)(2,1)S(1)} %get-tuple-element.73), channel_id=1, source_target_pairs={{0,8},{1,9},{2,10},{3,11},{4,12},{5,13},{6,14},{7,15},{8,0},{9,1},... | collective-permute-start | bytes 215048 | tf_op jit(solution)/shard_map/ppermute | solution.py:37
  38.9 7.3 %collective-permute-start.17 = (bf16[8,4480]{1,0:T(8,128)(2,1)S(1)}, bf16[8,4480]{1,0:T(8,128)(2,1)S(1)}, u32[]{:S(2)}, u32[]{:S(2)}) collective-permute-start(bf16[8,4480]{1,0:T(8,128)(2,1)S(1)} %get-tuple-element.67), channel_id=1, source_target_pairs={{0,16},{1,17},{2,18},{3,19},{4,20},{5,21},{6,22},{7,23},{8,24},{9,... | collective-permute-start | bytes 215048 | tf_op jit(solution)/shard_map/ppermute | solution.py:37
  41.3 6.3 %collective-permute-start.18 = (bf16[8,4480]{1,0:T(8,128)(2,1)S(1)}, bf16[8,4480]{1,0:T(8,128)(2,1)S(1)}, u32[]{:S(2)}, u32[]{:S(2)}) collective-permute-start(bf16[8,4480]{1,0:T(8,128)(2,1)S(1)} %get-tuple-element.68), channel_id=1, source_target_pairs={{0,24},{1,25},{2,26},{3,27},{4,28},{5,29},{6,30},{7,31},{8,16},{9,... | collective-permute-start | bytes 215048 | tf_op jit(solution)/shard_map/ppermute | solution.py:37
  41.9 5.7 %collective-permute-start.19 = (bf16[8,4480]{1,0:T(8,128)(2,1)S(1)}, bf16[8,4480]{1,0:T(8,128)(2,1)S(1)}, u32[]{:S(2)}, u32[]{:S(2)}) collective-permute-start(bf16[8,4480]{1,0:T(8,128)(2,1)S(1)} %get-tuple-element.69), channel_id=1, source_target_pairs={{0,8},{1,9},{2,10},{3,11},{4,12},{5,13},{6,14},{7,15},{8,0},{9,1},... | collective-permute-start | bytes 215048 | tf_op jit(solution)/shard_map/ppermute | solution.py:37
  42.6 5.3 %collective-permute-start.23 = (bf16[8,4480]{1,0:T(8,128)(2,1)S(1)}, bf16[8,4480]{1,0:T(8,128)(2,1)S(1)}, u32[]{:S(2)}, u32[]{:S(2)}) collective-permute-start(bf16[8,4480]{1,0:T(8,128)(2,1)S(1)} %shard_map.133), channel_id=1, source_target_pairs={{0,6},{1,7},{2,4},{3,5},{4,2},{5,3},{6,0},{7,1},{8,14},{9,15},{10,... | collective-permute-start | bytes 215048 | tf_op jit(solution)/shard_map/ppermute | solution.py:37

commit v9 on v8

--- a/solution.py
+++ b/solution.py
@@ -11,6 +11,7 @@
 KV_HEADS = 4
 HEAD_DIM = 128
 LANES = 128
+STRIPS = 4
 VMEM = pl.BlockSpec(memory_space=pltpu.VMEM)
 SMEM = pl.BlockSpec(memory_space=pltpu.SMEM)
 HBM = pl.BlockSpec(memory_space=pltpu.HBM)
@@ -66,6 +67,11 @@
     for copy in copies:
         copy.start()
     return copies
+
+
+def strips(ref, count):
+    rows = ref.shape[0] // count
+    return [ref.at[pl.ds(first * rows, rows)] for first in range(count)]
 
 
 def payload_kernel(
@@ -102,19 +108,23 @@
     return [high, middle, value - high - middle]
 
 
-def keep_kernel(count, *refs):
-    copies = fetch(refs[:count], refs[count : 2 * count], refs[2 * count])
+def keep_kernel(cuts, *refs):
+    count = len(cuts)
+    sources = sum([strips(ref, cut) for ref, cut in zip(refs, cuts)], [])
+    targets = sum([strips(ref, cut) for ref, cut in zip(refs[count:], cuts)], [])
+    copies = fetch(sources, targets, refs[2 * count])
     for copy in copies:
         copy.wait()
 
 
 def keep(*arrays):
+    cuts = [STRIPS if a.size >= 2**20 else 1 for a in arrays]
     return call(
-        functools.partial(keep_kernel, len(arrays)),
+        functools.partial(keep_kernel, cuts),
         [pltpu.VMEM(a.shape, a.dtype) for a in arrays],
         in_hbm(*arrays),
         in_specs=[HBM] * len(arrays),
-        scratch=[fetched(len(arrays))],
+        scratch=[fetched(sum(cuts))],
         flops=4 * 10**9,
     )
 
@@ -122,7 +132,8 @@
 def attention_kernel(own, offsets, *refs):
     length_hbm, weight_hbm, query_ref, key_ref, value_ref, near_ref, far_ref, weight_out = refs[:8]
     length_ref, wide_ref, mean_ref, logs_ref, dest_ref, sems = refs[8:]
-    copies = fetch([length_hbm, weight_hbm], [length_ref, weight_out], sems)
+    sources = [length_hbm, *strips(weight_hbm, STRIPS)]
+    copies = fetch(sources, [length_ref, *strips(weight_out, STRIPS)], sems)
     me = lax.axis_index("ffn")
     rows, seg_len, _ = key_ref.shape
     per_group = HEADS // KV_HEADS
@@ -178,7 +189,8 @@
         for first in range(0, len(offsets), 2):
             pair = [dest_ref[me ^ (offset ^ core)] for offset in offsets[first : first + 2]]
             out_ref[first * rows : (first + 2) * rows] = jnp.concatenate(pair, axis=0).astype(jnp.bfloat16)
-    copies[1].wait()
+    for copy in copies[1:]:
+        copy.wait()
 
 
 def attend(stacked, k_cache, v_cache, cache_len, levels, weight):
@@ -197,7 +209,7 @@
             pltpu.SMEM(cache_len.shape, cache_len.dtype),
             *[pltpu.VMEM(stacked.shape, jnp.float32)] * 3,
             pltpu.VMEM((devices, rows, extra), jnp.float32),
-            fetched(2),
+            fetched(1 + STRIPS),
         ],
         flops=4 * 10**9,
     )
@@ -366,7 +378,7 @@
     near, far = apply_expert(chunks, others[:count], sides, sums, weights)
     pieces = summed([near, exchange(far, 1)], [rows] * count, width, own)
     base = after(base, near)
-    near, far = apply_expert([base, *last_chunk], others[count:], [0, 3][: radix - 2], sums, weights)
+    near, far = apply_expert([base, *last_chunk], others[count:], [0] + [3] * len(across), sums, weights)
     total, *corner_pieces = summed([near, exchange(far, 1)], [rows] + cut * len(across), width, own)
     parts = [total] + [exchange(piece, stride * k) for piece, k in zip(pieces, sides)]
     if across:

time: 48.8 us -> 48.8 us (level)
  no operation moved by 1% of the time
where the time goes in v9:
time: 48.8 us; the launch traced here: 48.6 us
  starting transfers between devices  26.4 us (54%)
  Pallas kernels  11.8 us (24%)
  waiting for transfers between devices  9.65 us (20%)
  between operations  0.82 us (2%)
    ppermute x24, starting transfers between devices, exchange(): return lax.ppermute(value, 'ffn', [(i, i ^ distance) for i in range(size)])  26.4 us
    pallas_call x13, Pallas kernels, call(): pl.pallas_call(body, out_shape=out_shape, in_specs=in_specs or [VMEM] * l...  11.8 us
    ppermute x24, waiting for transfers between devices, exchange(): return lax.ppermute(value, 'ffn', [(i, i ^ distance) for i in range(size)])  9.65 us
  transfers between devices with their start and end apart: 24, of which 7 were waited for; matrix products, arithmetic and copies ran while one was open for 0% of the time, Pallas kernels for 21%

profile of v9, /device:TPU:0, one launch (start us, length us, event | category | flops | bytes accessed | tf_op | source)
XLA Modules:
  0.0 48.6 jit_solution(10338919498786043107)
XLA Ops:
  0.6 1.1 %shard_map.122.refs_0_ = bf16[8,4224]{1,0:T(8,128)(2,1)S(1)} custom-call(bf16[8,4096]{1,0:T(8,128)(2,1)} %tokens_hbm.1, f32[1,4096]{1,0:T(1,128)} %bitcast.6, s32[8,8]{1,0:T(8,128)} %routes_hbm.1, f32[8,8]{1,0:T(8,128)} %scores_hbm.1), custom_call_target="tpu_custom_call" | custom-call | flops 1 | bytes 1 | tf_op jit(solution)/shard_map/pallas_call | solution.py:46
  1.7 4.1 %collective-permute-start = (bf16[8,4224]{1,0:T(8,128)(2,1)S(1)}, bf16[8,4224]{1,0:T(8,128)(2,1)S(1)}, u32[]{:S(2)}, u32[]{:S(2)}) collective-permute-start(bf16[8,4224]{1,0:T(8,128)(2,1)S(1)} %shard_map.122.refs_0_), channel_id=1, source_target_pairs={{0,16},{1,17},{2,18},{3,19},{4,20},{5,21},{6,22},{7,23},{8,24},{9,... | collective-permute-start | bytes 202760 | tf_op jit(solution)/shard_map/ppermute | solution.py:38
  5.8 1.3 %collective-permute-start.1 = (bf16[8,4224]{1,0:T(8,128)(2,1)S(1)}, bf16[8,4224]{1,0:T(8,128)(2,1)S(1)}, u32[]{:S(2)}, u32[]{:S(2)}) collective-permute-start(bf16[8,4224]{1,0:T(8,128)(2,1)S(1)} %shard_map.122.refs_0_), channel_id=1, source_target_pairs={{0,24},{1,25},{2,26},{3,27},{4,28},{5,29},{6,30},{7,31},{8,16},{9,... | collective-permute-start | bytes 202760 | tf_op jit(solution)/shard_map/ppermute | solution.py:38
  7.2 0.2 collective-permute-start.2
  7.4 2.4 %collective-permute-start.5 = (bf16[8,4224]{1,0:T(8,128)(2,1)S(1)}, bf16[8,4224]{1,0:T(8,128)(2,1)S(1)}, u32[]{:S(2)}, u32[]{:S(2)}) collective-permute-start(bf16[8,4224]{1,0:T(8,128)(2,1)S(1)} %shard_map.122.refs_0_), channel_id=1, source_target_pairs={{0,6},{1,7},{2,4},{3,5},{4,2},{5,3},{6,0},{7,1},{8,14},{9,15},{10,... | collective-permute-start | bytes 202760 | tf_op jit(solution)/shard_map/ppermute | solution.py:38
  9.8 2.6 %shard_map.123 = (bf16[4096,384]{1,0:T(8,128)(2,1)S(1)}, bf16[512,128]{1,0:T(8,128)(2,1)S(1)}, bf16[8,128,512]{2,1,0:T(8,128)(2,1)S(1)}, bf16[8,128,512]{2,1,0:T(8,128)(2,1)S(1)}) custom-call(bf16[4096,384]{1,0:T(8,128)(2,1)} %refs_0_.2, bf16[512,128]{1,0:T(8,128)(2,1)} %bitcast.7, bf16[8,128,512]{2,1,0:T(8,128)(2,1)} %refs_2_.1, bf16[8,128,512]{2,1,0:T(8,128)(2,1)} %refs_3_.1), custom_call_target="tpu_custom_call" | custom-call | flops 4000000000 | bytes 1 | tf_op jit(solution)/shard_map/pallas_call | solution.py:46
  12.4 0.0 collective-permute-done.refs_1_
  12.4 0.0 collective-permute-done.1.refs_2_
  12.5 0.0 collective-permute-done.2.refs_3_
  12.5 1.3 %collective-permute-start.3 = (bf16[32,4224]{1,0:T(8,128)(2,1)S(1)}, bf16[32,4224]{1,0:T(8,128)(2,1)S(1)}, u32[]{:S(2)}, u32[]{:S(2)}) collective-permute-start(bf16[32,4224]{1,0:T(8,128)(2,1)S(1)} %shard_map.124.refs_0_), channel_id=1, source_target_pairs={{0,2},{1,3},{2,0},{3,1},{4,6},{5,7},{6,4},{7,5},{8,10},{9,11},{10,... | collective-permute-start | bytes 811016 | tf_op jit(solution)/shard_map/ppermute | solution.py:38
  13.8 1.5 %collective-permute-start.4 = (bf16[32,4224]{1,0:T(8,128)(2,1)S(1)}, bf16[32,4224]{1,0:T(8,128)(2,1)S(1)}, u32[]{:S(2)}, u32[]{:S(2)}) collective-permute-start(bf16[32,4224]{1,0:T(8,128)(2,1)S(1)} %shard_map.124.refs_0_), channel_id=1, source_target_pairs={{0,4},{1,5},{2,6},{3,7},{4,0},{5,1},{6,2},{7,3},{8,12},{9,13},{10,... | collective-permute-start | bytes 811016 | tf_op jit(solution)/shard_map/ppermute | solution.py:38
  15.4 0.0 collective-permute-done.5.refs_0_
  15.4 2.7 %collective-permute-start.6 = (bf16[8,4224]{1,0:T(8,128)(2,1)S(1)}, bf16[8,4224]{1,0:T(8,128)(2,1)S(1)}, u32[]{:S(2)}, u32[]{:S(2)}) collective-permute-start(bf16[8,4224]{1,0:T(8,128)(2,1)S(1)} %collective-permute-done.5.refs_0_), channel_id=1, source_target_pairs={{0,16},{1,17},{2,18},{3,19},{4,20},{5,21},{6,22},{7,23},{8,24},{9,... | collective-permute-start | bytes 202760 | tf_op jit(solution)/shard_map/ppermute | solution.py:38
  18.1 0.6 %collective-permute-start.7 = (bf16[8,4224]{1,0:T(8,128)(2,1)S(1)}, bf16[8,4224]{1,0:T(8,128)(2,1)S(1)}, u32[]{:S(2)}, u32[]{:S(2)}) collective-permute-start(bf16[8,4224]{1,0:T(8,128)(2,1)S(1)} %collective-permute-done.5.refs_0_), channel_id=1, source_target_pairs={{0,24},{1,25},{2,26},{3,27},{4,28},{5,29},{6,30},{7,31},{8,16},{9,... | collective-permute-start | bytes 202760 | tf_op jit(solution)/shard_map/ppermute | solution.py:38
  18.7 0.3 collective-permute-start.8
  18.9 2.4 %shard_map.125 = (bf16[128,384]{1,0:T(8,128)(2,1)S(1)}, bf16[128,384]{1,0:T(8,128)(2,1)S(1)}, bf16[4096,384]{1,0:T(8,128)(2,1)S(1)}) custom-call(s32[8]{0:T(128)} %refs_0_.3, bf16[4096,384]{1,0:T(8,128)(2,1)} %refs_1_.1, bf16[512,128]{1,0:T(8,128)(2,1)S(1)} %get-tuple-element.45.refs_2_, bf16[8,128,512]{2,1,0:T(8,128)(2,1)S(1)} %get-tuple-element.46.refs_3_, ...), custom_call_target="tpu_custom_call" | custom-call | flops 4000000000 | bytes 1 | tf_op jit(solution)/shard_map/pallas_call | solution.py:46
  21.4 0.0 collective-permute-done.3.refs_0_
  21.4 0.0 collective-permute-done.4.refs_1_
  21.4 0.0 copy-start
  21.4 0.1 collective-permute-start.10
  21.5 0.5 %collective-permute-start.9 = (bf16[32,4224]{1,0:T(8,128)(2,1)S(1)}, bf16[32,4224]{1,0:T(8,128)(2,1)S(1)}, u32[]{:S(2)}, u32[]{:S(2)}) collective-permute-start(bf16[32,4224]{1,0:T(8,128)(2,1)S(1)} %collective-permute-done.3.refs_0_), channel_id=1, source_target_pairs={{0,1},{1,0},{2,3},{3,2},{4,5},{5,4},{6,7},{7,6},{8,9},{9,8},{10,11... | collective-permute-start | bytes 811016 | tf_op jit(solution)/shard_map/ppermute | solution.py:38
  22.0 0.5 %collective-permute-done.6.refs_1_ = bf16[8,4224]{1,0:T(8,128)(2,1)S(1)} collective-permute-done((bf16[8,4224]{1,0:T(8,128)(2,1)S(1)}, bf16[8,4224]{1,0:T(8,128)(2,1)S(1)}, u32[]{:S(2)}, u32[]{:S(2)}) %collective-permute-start.6) | collective-permute-done | bytes 67616 | tf_op jit(solution)/shard_map/ppermute | solution.py:38
  22.5 0.0 collective-permute-start.11
  22.5 1.7 %collective-permute-done.7.refs_2_ = bf16[8,4224]{1,0:T(8,128)(2,1)S(1)} collective-permute-done((bf16[8,4224]{1,0:T(8,128)(2,1)S(1)}, bf16[8,4224]{1,0:T(8,128)(2,1)S(1)}, u32[]{:S(2)}, u32[]{:S(2)}) %collective-permute-start.7) | collective-permute-done | bytes 67616 | tf_op jit(solution)/shard_map/ppermute | solution.py:38
  24.2 0.0 collective-permute-done.8.refs_3_
  24.2 0.1 collective-permute-start.12
  24.3 0.0 collective-permute-done.10.refs_3_
  24.3 0.0 collective-permute-done.9.refs_2_
  24.3 0.0 copy-done
  24.3 1.9 %shard_map.127 = (bf16[64,4480]{1,0:T(8,128)(2,1)S(1)}, bf16[64,4480]{1,0:T(8,128)(2,1)S(1)}) custom-call(bf16[32,4224]{1,0:T(8,128)(2,1)S(1)} %collective-permute-done.3.refs_0_, bf16[32,4224]{1,0:T(8,128)(2,1)S(1)} %collective-permute-done.4.refs_1_, bf16[32,4224]{1,0:T(8,128)(2,1)S(1)} %collective-permute-done.9.refs_2_, ...), custom_call_target="tpu_custom_call" | custom-call | flops 4000000000 | bytes 9437184 | tf_op jit(solution)/shard_map/pallas_call | solution.py:46
  26.3 0.5 %collective-permute-start.14 = (bf16[64,4480]{1,0:T(8,128)(2,1)S(1)}, bf16[64,4480]{1,0:T(8,128)(2,1)S(1)}, u32[]{:S(2)}, u32[]{:S(2)}) collective-permute-start(bf16[64,4480]{1,0:T(8,128)(2,1)S(1)} %get-tuple-element.63), channel_id=1, source_target_pairs={{0,1},{1,0},{2,3},{3,2},{4,5},{5,4},{6,7},{7,6},{8,9},{9,8},{10,11... | collective-permute-start | bytes 1720328 | tf_op jit(solution)/shard_map/ppermute | solution.py:38
  26.8 0.0 collective-permute-done.11.refs_2_
  26.8 0.0 collective-permute-done.12.refs_3_
  26.8 2.0 %shard_map.128 = (bf16[64,4480]{1,0:T(8,128)(2,1)S(1)}, bf16[64,4480]{1,0:T(8,128)(2,1)S(1)}) custom-call(bf16[32,4224]{1,0:T(8,128)(2,1)S(1)} %shard_map.124.refs_0_, bf16[32,4224]{1,0:T(8,128)(2,1)S(1)} %shard_map.126.refs_1_, bf16[32,4224]{1,0:T(8,128)(2,1)S(1)} %collective-permute-done.11.refs_2_, bf16[32,4224]{1,0:T(8,128)(2,1)S(1)} %collective-permute-done.12.refs_3_, ...), custom_call_target="tpu_custom_call" | custom-call | flops 4000000000 | bytes 9437184 | tf_op jit(solution)/shard_map/pallas_call | solution.py:46
  28.8 0.1 collective-permute-start.13
  28.9 0.0 collective-permute-done.14.refs_1_
  28.9 0.3 shard_map.130
  29.2 0.6 %collective-permute-start.15 = (bf16[32,4480]{1,0:T(8,128)(2,1)S(1)}, bf16[32,4480]{1,0:T(8,128)(2,1)S(1)}, u32[]{:S(2)}, u32[]{:S(2)}) collective-permute-start(bf16[32,4480]{1,0:T(8,128)(2,1)S(1)} %get-tuple-element.64), channel_id=1, source_target_pairs={{0,2},{1,3},{2,0},{3,1},{4,6},{5,7},{6,4},{7,5},{8,10},{9,11},{10,... | collective-permute-start | bytes 860168 | tf_op jit(solution)/shard_map/ppermute | solution.py:38
  29.8 1.1 %collective-permute-start.16 = (bf16[32,4480]{1,0:T(8,128)(2,1)S(1)}, bf16[32,4480]{1,0:T(8,128)(2,1)S(1)}, u32[]{:S(2)}, u32[]{:S(2)}) collective-permute-start(bf16[32,4480]{1,0:T(8,128)(2,1)S(1)} %get-tuple-element.65), channel_id=1, source_target_pairs={{0,4},{1,5},{2,6},{3,7},{4,0},{5,1},{6,2},{7,3},{8,12},{9,13},{10,... | collective-permute-start | bytes 860168 | tf_op jit(solution)/shard_map/ppermute | solution.py:38
  30.8 0.0 collective-permute-done.13.refs_1_
  30.8 0.3 shard_map.129
  31.1 2.5 %collective-permute-start.20 = (bf16[8,4480]{1,0:T(8,128)(2,1)S(1)}, bf16[8,4480]{1,0:T(8,128)(2,1)S(1)}, u32[]{:S(2)}, u32[]{:S(2)}) collective-permute-start(bf16[8,4480]{1,0:T(8,128)(2,1)S(1)} %get-tuple-element.71), channel_id=1, source_target_pairs={{0,16},{1,17},{2,18},{3,19},{4,20},{5,21},{6,22},{7,23},{8,24},{9,... | collective-permute-start | bytes 215048 | tf_op jit(solution)/shard_map/ppermute | solution.py:38
  33.7 1.2 %collective-permute-start.21 = (bf16[8,4480]{1,0:T(8,128)(2,1)S(1)}, bf16[8,4480]{1,0:T(8,128)(2,1)S(1)}, u32[]{:S(2)}, u32[]{:S(2)}) collective-permute-start(bf16[8,4480]{1,0:T(8,128)(2,1)S(1)} %get-tuple-element.72), channel_id=1, source_target_pairs={{0,24},{1,25},{2,26},{3,27},{4,28},{5,29},{6,30},{7,31},{8,16},{9,... | collective-permute-start | bytes 215048 | tf_op jit(solution)/shard_map/ppermute | solution.py:38
  34.9 0.0 collective-permute-start.22
  34.9 3.5 %collective-permute-done.15.refs_1_ = bf16[32,4480]{1,0:T(8,128)(2,1)S(1)} collective-permute-done((bf16[32,4480]{1,0:T(8,128)(2,1)S(1)}, bf16[32,4480]{1,0:T(8,128)(2,1)S(1)}, u32[]{:S(2)}, u32[]{:S(2)}) %collective-permute-start.15) | collective-permute-done | bytes 286752 | tf_op jit(solution)/shard_map/ppermute | solution.py:38
  38.4 0.3 collective-permute-done.16.refs_2_
  38.7 0.2 shard_map.131
  38.9 2.4 %collective-permute-start.17 = (bf16[8,4480]{1,0:T(8,128)(2,1)S(1)}, bf16[8,4480]{1,0:T(8,128)(2,1)S(1)}, u32[]{:S(2)}, u32[]{:S(2)}) collective-permute-start(bf16[8,4480]{1,0:T(8,128)(2,1)S(1)} %get-tuple-element.67), channel_id=1, source_target_pairs={{0,16},{1,17},{2,18},{3,19},{4,20},{5,21},{6,22},{7,23},{8,24},{9,... | collective-permute-start | bytes 215048 | tf_op jit(solution)/shard_map/ppermute | solution.py:38
  41.3 0.6 %collective-permute-start.18 = (bf16[8,4480]{1,0:T(8,128)(2,1)S(1)}, bf16[8,4480]{1,0:T(8,128)(2,1)S(1)}, u32[]{:S(2)}, u32[]{:S(2)}) collective-permute-start(bf16[8,4480]{1,0:T(8,128)(2,1)S(1)} %get-tuple-element.68), channel_id=1, source_target_pairs={{0,24},{1,25},{2,26},{3,27},{4,28},{5,29},{6,30},{7,31},{8,16},{9,... | collective-permute-start | bytes 215048 | tf_op jit(solution)/shard_map/ppermute | solution.py:38
  41.9 0.0 collective-permute-done.20.refs_1_
  41.9 0.6 %collective-permute-start.19 = (bf16[8,4480]{1,0:T(8,128)(2,1)S(1)}, bf16[8,4480]{1,0:T(8,128)(2,1)S(1)}, u32[]{:S(2)}, u32[]{:S(2)}) collective-permute-start(bf16[8,4480]{1,0:T(8,128)(2,1)S(1)} %get-tuple-element.69), channel_id=1, source_target_pairs={{0,8},{1,9},{2,10},{3,11},{4,12},{5,13},{6,14},{7,15},{8,0},{9,1},... | collective-permute-start | bytes 215048 | tf_op jit(solution)/shard_map/ppermute | solution.py:38
  42.5 0.0 collective-permute-done.21.refs_2_
  42.5 0.0 collective-permute-done.22.refs_3_
  42.5 0.1 shard_map.133
  42.6 1.5 %collective-permute-start.23 = (bf16[8,4480]{1,0:T(8,128)(2,1)S(1)}, bf16[8,4480]{1,0:T(8,128)(2,1)S(1)}, u32[]{:S(2)}, u32[]{:S(2)}) collective-permute-start(bf16[8,4480]{1,0:T(8,128)(2,1)S(1)} %shard_map.133), channel_id=1, source_target_pairs={{0,6},{1,7},{2,4},{3,5},{4,2},{5,3},{6,0},{7,1},{8,14},{9,15},{10,... | collective-permute-start | bytes 215048 | tf_op jit(solution)/shard_map/ppermute | solution.py:38
  44.1 2.1 %collective-permute-done.17.refs_1_ = bf16[8,4480]{1,0:T(8,128)(2,1)S(1)} collective-permute-done((bf16[8,4480]{1,0:T(8,128)(2,1)S(1)}, bf16[8,4480]{1,0:T(8,128)(2,1)S(1)}, u32[]{:S(2)}, u32[]{:S(2)}) %collective-permute-start.17) | collective-permute-done | bytes 71712 | tf_op jit(solution)/shard_map/ppermute | solution.py:38
  46.2 1.4 %collective-permute-done.18.refs_2_ = bf16[8,4480]{1,0:T(8,128)(2,1)S(1)} collective-permute-done((bf16[8,4480]{1,0:T(8,128)(2,1)S(1)}, bf16[8,4480]{1,0:T(8,128)(2,1)S(1)}, u32[]{:S(2)}, u32[]{:S(2)}) %collective-permute-start.18) | collective-permute-done | bytes 71712 | tf_op jit(solution)/shard_map/ppermute | solution.py:38
  47.6 0.0 collective-permute-done.19.refs_3_
  47.6 0.1 shard_map.132.refs_0_
  47.7 0.2 collective-permute-done.23.refs_1_
  47.9 0.7 %shard_map.134 = (bf16[8,4096]{1,0:T(8,128)(2,1)}, bf16[8,256]{1,0:T(8,128)(2,1)}) custom-call(bf16[8,4480]{1,0:T(8,128)(2,1)S(1)} %shard_map.132.refs_0_, bf16[8,4480]{1,0:T(8,128)(2,1)S(1)} %collective-permute-done.23.refs_1_), custom_call_target="tpu_custom_call" | custom-call | flops 1 | bytes 1 | tf_op jit(solution)/shard_map/pallas_call | solution.py:46
  (2 shorter events, 0.0 us)
Async XLA Ops:
  1.7 10.7 %collective-permute-start = (bf16[8,4224]{1,0:T(8,128)(2,1)S(1)}, bf16[8,4224]{1,0:T(8,128)(2,1)S(1)}, u32[]{:S(2)}, u32[]{:S(2)}) collective-permute-start(bf16[8,4224]{1,0:T(8,128)(2,1)S(1)} %shard_map.122.refs_0_), channel_id=1, source_target_pairs={{0,16},{1,17},{2,18},{3,19},{4,20},{5,21},{6,22},{7,23},{8,24},{9,... | collective-permute-start | bytes 202760 | tf_op jit(solution)/shard_map/ppermute | solution.py:38
  5.8 6.6 %collective-permute-start.1 = (bf16[8,4224]{1,0:T(8,128)(2,1)S(1)}, bf16[8,4224]{1,0:T(8,128)(2,1)S(1)}, u32[]{:S(2)}, u32[]{:S(2)}) collective-permute-start(bf16[8,4224]{1,0:T(8,128)(2,1)S(1)} %shard_map.122.refs_0_), channel_id=1, source_target_pairs={{0,24},{1,25},{2,26},{3,27},{4,28},{5,29},{6,30},{7,31},{8,16},{9,... | collective-permute-start | bytes 202760 | tf_op jit(solution)/shard_map/ppermute | solution.py:38
  7.2 5.3 %collective-permute-start.2 = (bf16[8,4224]{1,0:T(8,128)(2,1)S(1)}, bf16[8,4224]{1,0:T(8,128)(2,1)S(1)}, u32[]{:S(2)}, u32[]{:S(2)}) collective-permute-start(bf16[8,4224]{1,0:T(8,128)(2,1)S(1)} %shard_map.122.refs_0_), channel_id=1, source_target_pairs={{0,8},{1,9},{2,10},{3,11},{4,12},{5,13},{6,14},{7,15},{8,0},{9,1},... | collective-permute-start | bytes 202760 | tf_op jit(solution)/shard_map/ppermute | solution.py:38
  7.4 8.0 %collective-permute-start.5 = (bf16[8,4224]{1,0:T(8,128)(2,1)S(1)}, bf16[8,4224]{1,0:T(8,128)(2,1)S(1)}, u32[]{:S(2)}, u32[]{:S(2)}) collective-permute-start(bf16[8,4224]{1,0:T(8,128)(2,1)S(1)} %shard_map.122.refs_0_), channel_id=1, source_target_pairs={{0,6},{1,7},{2,4},{3,5},{4,2},{5,3},{6,0},{7,1},{8,14},{9,15},{10,... | collective-permute-start | bytes 202760 | tf_op jit(solution)/shard_map/ppermute | solution.py:38
  12.5 8.9 %collective-permute-start.3 = (bf16[32,4224]{1,0:T(8,128)(2,1)S(1)}, bf16[32,4224]{1,0:T(8,128)(2,1)S(1)}, u32[]{:S(2)}, u32[]{:S(2)}) collective-permute-start(bf16[32,4224]{1,0:T(8,128)(2,1)S(1)} %shard_map.124.refs_0_), channel_id=1, source_target_pairs={{0,2},{1,3},{2,0},{3,1},{4,6},{5,7},{6,4},{7,5},{8,10},{9,11},{10,... | collective-permute-start | bytes 811016 | tf_op jit(solution)/shard_map/ppermute | solution.py:38
  13.8 7.5 %collective-permute-start.4 = (bf16[32,4224]{1,0:T(8,128)(2,1)S(1)}, bf16[32,4224]{1,0:T(8,128)(2,1)S(1)}, u32[]{:S(2)}, u32[]{:S(2)}) collective-permute-start(bf16[32,4224]{1,0:T(8,128)(2,1)S(1)} %shard_map.124.refs_0_), channel_id=1, source_target_pairs={{0,4},{1,5},{2,6},{3,7},{4,0},{5,1},{6,2},{7,3},{8,12},{9,13},{10,... | collective-permute-start | bytes 811016 | tf_op jit(solution)/shard_map/ppermute | solution.py:38
  15.4 7.1 %collective-permute-start.6 = (bf16[8,4224]{1,0:T(8,128)(2,1)S(1)}, bf16[8,4224]{1,0:T(8,128)(2,1)S(1)}, u32[]{:S(2)}, u32[]{:S(2)}) collective-permute-start(bf16[8,4224]{1,0:T(8,128)(2,1)S(1)} %collective-permute-done.5.refs_0_), channel_id=1, source_target_pairs={{0,16},{1,17},{2,18},{3,19},{4,20},{5,21},{6,22},{7,23},{8,24},{9,... | collective-permute-start | bytes 202760 | tf_op jit(solution)/shard_map/ppermute | solution.py:38
  18.1 6.1 %collective-permute-start.7 = (bf16[8,4224]{1,0:T(8,128)(2,1)S(1)}, bf16[8,4224]{1,0:T(8,128)(2,1)S(1)}, u32[]{:S(2)}, u32[]{:S(2)}) collective-permute-start(bf16[8,4224]{1,0:T(8,128)(2,1)S(1)} %collective-permute-done.5.refs_0_), channel_id=1, source_target_pairs={{0,24},{1,25},{2,26},{3,27},{4,28},{5,29},{6,30},{7,31},{8,16},{9,... | collective-permute-start | bytes 202760 | tf_op jit(solution)/shard_map/ppermute | solution.py:38
  18.7 5.5 %collective-permute-start.8 = (bf16[8,4224]{1,0:T(8,128)(2,1)S(1)}, bf16[8,4224]{1,0:T(8,128)(2,1)S(1)}, u32[]{:S(2)}, u32[]{:S(2)}) collective-permute-start(bf16[8,4224]{1,0:T(8,128)(2,1)S(1)} %collective-permute-done.5.refs_0_), channel_id=1, source_target_pairs={{0,8},{1,9},{2,10},{3,11},{4,12},{5,13},{6,14},{7,15},{8,0},{9,1},... | collective-permute-start | bytes 202760 | tf_op jit(solution)/shard_map/ppermute | solution.py:38
  21.4 2.9 %copy-start = (bf16[384,4096]{1,0:T(8,128)(2,1)S(1)}, bf16[384,4096]{1,0:T(8,128)(2,1)}, u32[]{:S(2)}) copy-start(bf16[384,4096]{1,0:T(8,128)(2,1)} %refs_8_.3) | copy-start | bytes 9437188
  21.4 2.9 %collective-permute-start.10 = (bf16[32,4224]{1,0:T(8,128)(2,1)S(1)}, bf16[32,4224]{1,0:T(8,128)(2,1)S(1)}, u32[]{:S(2)}, u32[]{:S(2)}) collective-permute-start(bf16[32,4224]{1,0:T(8,128)(2,1)S(1)} %collective-permute-done.4.refs_1_), channel_id=1, source_target_pairs={{0,1},{1,0},{2,3},{3,2},{4,5},{5,4},{6,7},{7,6},{8,9},{9,8},{10,11... | collective-permute-start | bytes 811016 | tf_op jit(solution)/shard_map/ppermute | solution.py:38
  21.5 2.8 %collective-permute-start.9 = (bf16[32,4224]{1,0:T(8,128)(2,1)S(1)}, bf16[32,4224]{1,0:T(8,128)(2,1)S(1)}, u32[]{:S(2)}, u32[]{:S(2)}) collective-permute-start(bf16[32,4224]{1,0:T(8,128)(2,1)S(1)} %collective-permute-done.3.refs_0_), channel_id=1, source_target_pairs={{0,1},{1,0},{2,3},{3,2},{4,5},{5,4},{6,7},{7,6},{8,9},{9,8},{10,11... | collective-permute-start | bytes 811016 | tf_op jit(solution)/shard_map/ppermute | solution.py:38
  22.5 4.3 %collective-permute-start.11 = (bf16[32,4224]{1,0:T(8,128)(2,1)S(1)}, bf16[32,4224]{1,0:T(8,128)(2,1)S(1)}, u32[]{:S(2)}, u32[]{:S(2)}) collective-permute-start(bf16[32,4224]{1,0:T(8,128)(2,1)S(1)} %shard_map.124.refs_0_), channel_id=1, source_target_pairs={{0,1},{1,0},{2,3},{3,2},{4,5},{5,4},{6,7},{7,6},{8,9},{9,8},{10,11... | collective-permute-start | bytes 811016 | tf_op jit(solution)/shard_map/ppermute | solution.py:38
  24.2 2.6 %collective-permute-start.12 = (bf16[32,4224]{1,0:T(8,128)(2,1)S(1)}, bf16[32,4224]{1,0:T(8,128)(2,1)S(1)}, u32[]{:S(2)}, u32[]{:S(2)}) collective-permute-start(bf16[32,4224]{1,0:T(8,128)(2,1)S(1)} %shard_map.126.refs_1_), channel_id=1, source_target_pairs={{0,1},{1,0},{2,3},{3,2},{4,5},{5,4},{6,7},{7,6},{8,9},{9,8},{10,11... | collective-permute-start | bytes 811016 | tf_op jit(solution)/shard_map/ppermute | solution.py:38
  26.3 2.6 %collective-permute-start.14 = (bf16[64,4480]{1,0:T(8,128)(2,1)S(1)}, bf16[64,4480]{1,0:T(8,128)(2,1)S(1)}, u32[]{:S(2)}, u32[]{:S(2)}) collective-permute-start(bf16[64,4480]{1,0:T(8,128)(2,1)S(1)} %get-tuple-element.63), channel_id=1, source_target_pairs={{0,1},{1,0},{2,3},{3,2},{4,5},{5,4},{6,7},{7,6},{8,9},{9,8},{10,11... | collective-permute-start | bytes 1720328 | tf_op jit(solution)/shard_map/ppermute | solution.py:38
  28.8 2.1 %collective-permute-start.13 = (bf16[64,4480]{1,0:T(8,128)(2,1)S(1)}, bf16[64,4480]{1,0:T(8,128)(2,1)S(1)}, u32[]{:S(2)}, u32[]{:S(2)}) collective-permute-start(bf16[64,4480]{1,0:T(8,128)(2,1)S(1)} %get-tuple-element.61), channel_id=1, source_target_pairs={{0,1},{1,0},{2,3},{3,2},{4,5},{5,4},{6,7},{7,6},{8,9},{9,8},{10,11... | collective-permute-start | bytes 1720328 | tf_op jit(solution)/shard_map/ppermute | solution.py:38
  29.2 9.3 %collective-permute-start.15 = (bf16[32,4480]{1,0:T(8,128)(2,1)S(1)}, bf16[32,4480]{1,0:T(8,128)(2,1)S(1)}, u32[]{:S(2)}, u32[]{:S(2)}) collective-permute-start(bf16[32,4480]{1,0:T(8,128)(2,1)S(1)} %get-tuple-element.64), channel_id=1, source_target_pairs={{0,2},{1,3},{2,0},{3,1},{4,6},{5,7},{6,4},{7,5},{8,10},{9,11},{10,... | collective-permute-start | bytes 860168 | tf_op jit(solution)/shard_map/ppermute | solution.py:38
  29.8 8.9 %collective-permute-start.16 = (bf16[32,4480]{1,0:T(8,128)(2,1)S(1)}, bf16[32,4480]{1,0:T(8,128)(2,1)S(1)}, u32[]{:S(2)}, u32[]{:S(2)}) collective-permute-start(bf16[32,4480]{1,0:T(8,128)(2,1)S(1)} %get-tuple-element.65), channel_id=1, source_target_pairs={{0,4},{1,5},{2,6},{3,7},{4,0},{5,1},{6,2},{7,3},{8,12},{9,13},{10,... | collective-permute-start | bytes 860168 | tf_op jit(solution)/shard_map/ppermute | solution.py:38
  31.1 10.8 %collective-permute-start.20 = (bf16[8,4480]{1,0:T(8,128)(2,1)S(1)}, bf16[8,4480]{1,0:T(8,128)(2,1)S(1)}, u32[]{:S(2)}, u32[]{:S(2)}) collective-permute-start(bf16[8,4480]{1,0:T(8,128)(2,1)S(1)} %get-tuple-element.71), channel_id=1, source_target_pairs={{0,16},{1,17},{2,18},{3,19},{4,20},{5,21},{6,22},{7,23},{8,24},{9,... | collective-permute-start | bytes 215048 | tf_op jit(solution)/shard_map/ppermute | solution.py:38
  33.7 8.8 %collective-permute-start.21 = (bf16[8,4480]{1,0:T(8,128)(2,1)S(1)}, bf16[8,4480]{1,0:T(8,128)(2,1)S(1)}, u32[]{:S(2)}, u32[]{:S(2)}) collective-permute-start(bf16[8,4480]{1,0:T(8,128)(2,1)S(1)} %get-tuple-element.72), channel_id=1, source_target_pairs={{0,24},{1,25},{2,26},{3,27},{4,28},{5,29},{6,30},{7,31},{8,16},{9,... | collective-permute-start | bytes 215048 | tf_op jit(solution)/shard_map/ppermute | solution.py:38
  34.9 7.6 %collective-permute-start.22 = (bf16[8,4480]{1,0:T(8,128)(2,1)S(1)}, bf16[8,4480]{1,0:T(8,128)(2,1)S(1)}, u32[]{:S(2)}, u32[]{:S(2)}) collective-permute-start(bf16[8,4480]{1,0:T(8,128)(2,1)S(1)} %get-tuple-element.73), channel_id=1, source_target_pairs={{0,8},{1,9},{2,10},{3,11},{4,12},{5,13},{6,14},{7,15},{8,0},{9,1},... | collective-permute-start | bytes 215048 | tf_op jit(solution)/shard_map/ppermute | solution.py:38
  38.9 7.3 %collective-permute-start.17 = (bf16[8,4480]{1,0:T(8,128)(2,1)S(1)}, bf16[8,4480]{1,0:T(8,128)(2,1)S(1)}, u32[]{:S(2)}, u32[]{:S(2)}) collective-permute-start(bf16[8,4480]{1,0:T(8,128)(2,1)S(1)} %get-tuple-element.67), channel_id=1, source_target_pairs={{0,16},{1,17},{2,18},{3,19},{4,20},{5,21},{6,22},{7,23},{8,24},{9,... | collective-permute-start | bytes 215048 | tf_op jit(solution)/shard_map/ppermute | solution.py:38
  41.3 6.3 %collective-permute-start.18 = (bf16[8,4480]{1,0:T(8,128)(2,1)S(1)}, bf16[8,4480]{1,0:T(8,128)(2,1)S(1)}, u32[]{:S(2)}, u32[]{:S(2)}) collective-permute-start(bf16[8,4480]{1,0:T(8,128)(2,1)S(1)} %get-tuple-element.68), channel_id=1, source_target_pairs={{0,24},{1,25},{2,26},{3,27},{4,28},{5,29},{6,30},{7,31},{8,16},{9,... | collective-permute-start | bytes 215048 | tf_op jit(solution)/shard_map/ppermute | solution.py:38
  41.9 5.7 %collective-permute-start.19 = (bf16[8,4480]{1,0:T(8,128)(2,1)S(1)}, bf16[8,4480]{1,0:T(8,128)(2,1)S(1)}, u32[]{:S(2)}, u32[]{:S(2)}) collective-permute-start(bf16[8,4480]{1,0:T(8,128)(2,1)S(1)} %get-tuple-element.69), channel_id=1, source_target_pairs={{0,8},{1,9},{2,10},{3,11},{4,12},{5,13},{6,14},{7,15},{8,0},{9,1},... | collective-permute-start | bytes 215048 | tf_op jit(solution)/shard_map/ppermute | solution.py:38
  42.6 5.3 %collective-permute-start.23 = (bf16[8,4480]{1,0:T(8,128)(2,1)S(1)}, bf16[8,4480]{1,0:T(8,128)(2,1)S(1)}, u32[]{:S(2)}, u32[]{:S(2)}) collective-permute-start(bf16[8,4480]{1,0:T(8,128)(2,1)S(1)} %shard_map.133), channel_id=1, source_target_pairs={{0,6},{1,7},{2,4},{3,5},{4,2},{5,3},{6,0},{7,1},{8,14},{9,15},{10,... | collective-permute-start | bytes 215048 | tf_op jit(solution)/shard_map/ppermute | solution.py:38

commit v10 on v9

--- a/solution.py
+++ b/solution.py
@@ -312,13 +312,13 @@
     refs[-1][...] = stacked.astype(jnp.bfloat16)
 
 
-def start_order(radix):
-    return [2, 3, 1] if radix == 4 else [1]
-
-
-def gather(block, levels, *ready, flops=1):
+def start_order(radix, order):
+    return order if radix == 4 else [1]
+
+
+def gather(block, levels, *ready, flops=1, order=[2, 3, 1]):
     for stride, radix in reversed(levels):
-        order = start_order(radix)
+        order = start_order(radix, order)
         arrived = [exchange(block, stride * k) for k in order]
         if ready:
             arrived = lax.optimization_barrier((*arrived, *ready))[: len(order)]
@@ -332,13 +332,13 @@
     return block
 
 
-def scatter(pieces, levels, width, own):
+def scatter(pieces, levels, width, own, order=[2, 3, 1]):
     stride, radix = levels[0]
-    parts = [pieces[0]] + [exchange(pieces[k], stride * k) for k in start_order(radix)]
+    parts = [pieces[0]] + [exchange(pieces[k], stride * k) for k in start_order(radix, order)]
     if len(levels) == 1:
         return parts
     rows = parts[0].shape[0] // levels[1][1]
-    return scatter(summed(parts, [rows] * levels[1][1], width, own), levels[1:], width, own)
+    return scatter(summed(parts, [rows] * levels[1][1], width, own), levels[1:], width, own, order)
 
 
 def per_device(
@@ -365,12 +365,12 @@
     across = [exchange(block, corner)] if radix == 4 else []
     stacked = query.reshape(-1, HEADS, HEAD_DIM).transpose(1, 0, 2).reshape(-1, HEAD_DIM)
     w_gate, stacked, k_cache, v_cache = keep(w_gate, stacked, k_cache, v_cache)
-    base = gather(block, outer, w_gate)
-    sides = [1, 2] if radix == 4 else [1]
+    base = gather(block, outer, w_gate, order=[2, 1, 3])
+    sides = [2, 1] if radix == 4 else [1]
     chunks = [exchange(base, stride * k) for k in sides]
     *sums, w_up = attend(after(stacked, base), k_cache, v_cache, cache_len, levels, w_up)
     weights = (w_gate, w_up, w_down)
-    last_chunk = [gather(a, outer, sums[0], flops=25 * 10**8) for a in across]
+    last_chunk = [gather(a, outer, sums[0], flops=25 * 10**8, order=[2, 3, 1]) for a in across]
     count = len(sides)
     chunks = lax.optimization_barrier((*chunks, sums[0]))[:count]
     others = [exchange(c, 1) for c in (*chunks, base, *last_chunk)]
@@ -382,9 +382,9 @@
     total, *corner_pieces = summed([near, exchange(far, 1)], [rows] + cut * len(across), width, own)
     parts = [total] + [exchange(piece, stride * k) for piece, k in zip(pieces, sides)]
     if across:
-        corner_parts = scatter(corner_pieces, outer, width, own)
+        corner_parts = scatter(corner_pieces, outer, width, own, [2, 3, 1])
     pieces = summed(parts, cut, width, own)
-    last = scatter(pieces, outer, width, own)
+    last = scatter(pieces, outer, width, own, [2, 3, 1])
     if across:
         corner_parts = lax.optimization_barrier((*corner_parts, pieces[0]))[:-1]
         (corner_sum,) = summed(corner_parts, [rows_dev], width, own)

time: 48.8 us -> 48.7 us (level)
  transfers between devices with their start and end apart: 24 -> 24, of which waited for: 7 -> 9; matrix products, arithmetic and copies ran while one was open for 0% -> 0% of each run, Pallas kernels for 21% -> 21%
where the time goes in v10:
time: 48.7 us; the launch traced here: 48.6 us
  starting transfers between devices  26.2 us (54%)
  Pallas kernels  11.8 us (24%)
  waiting for transfers between devices  9.76 us (20%)
  between operations  0.79 us (2%)
    ppermute x24, starting transfers between devices, exchange(): return lax.ppermute(value, 'ffn', [(i, i ^ distance) for i in range(size)])  26.2 us
    pallas_call x13, Pallas kernels, call(): pl.pallas_call(body, out_shape=out_shape, in_specs=in_specs or [VMEM] * l...  11.8 us
    ppermute x24, waiting for transfers between devices, exchange(): return lax.ppermute(value, 'ffn', [(i, i ^ distance) for i in range(size)])  9.76 us
  transfers between devices with their start and end apart: 24, of which 9 were waited for; matrix products, arithmetic and copies ran while one was open for 0% of the time, Pallas kernels for 21%

profile of v10, /device:TPU:0, one launch (start us, length us, event | category | flops | bytes accessed | tf_op | source)
XLA Modules:
  0.0 48.6 jit_solution(11390415931343445257)
XLA Ops:
  0.6 1.1 %shard_map.122.refs_0_ = bf16[8,4224]{1,0:T(8,128)(2,1)S(1)} custom-call(bf16[8,4096]{1,0:T(8,128)(2,1)} %tokens_hbm.1, f32[1,4096]{1,0:T(1,128)} %bitcast.6, s32[8,8]{1,0:T(8,128)} %routes_hbm.1, f32[8,8]{1,0:T(8,128)} %scores_hbm.1), custom_call_target="tpu_custom_call" | custom-call | flops 1 | bytes 1 | tf_op jit(solution)/shard_map/pallas_call | solution.py:46
  1.7 4.1 %collective-permute-start = (bf16[8,4224]{1,0:T(8,128)(2,1)S(1)}, bf16[8,4224]{1,0:T(8,128)(2,1)S(1)}, u32[]{:S(2)}, u32[]{:S(2)}) collective-permute-start(bf16[8,4224]{1,0:T(8,128)(2,1)S(1)} %shard_map.122.refs_0_), channel_id=1, source_target_pairs={{0,16},{1,17},{2,18},{3,19},{4,20},{5,21},{6,22},{7,23},{8,24},{9,... | collective-permute-start | bytes 202760 | tf_op jit(solution)/shard_map/ppermute | solution.py:38
  5.8 1.6 %collective-permute-start.1 = (bf16[8,4224]{1,0:T(8,128)(2,1)S(1)}, bf16[8,4224]{1,0:T(8,128)(2,1)S(1)}, u32[]{:S(2)}, u32[]{:S(2)}) collective-permute-start(bf16[8,4224]{1,0:T(8,128)(2,1)S(1)} %shard_map.122.refs_0_), channel_id=1, source_target_pairs={{0,8},{1,9},{2,10},{3,11},{4,12},{5,13},{6,14},{7,15},{8,0},{9,1},... | collective-permute-start | bytes 202760 | tf_op jit(solution)/shard_map/ppermute | solution.py:38
  7.4 0.0 collective-permute-start.2
  7.4 2.7 %collective-permute-start.5 = (bf16[8,4224]{1,0:T(8,128)(2,1)S(1)}, bf16[8,4224]{1,0:T(8,128)(2,1)S(1)}, u32[]{:S(2)}, u32[]{:S(2)}) collective-permute-start(bf16[8,4224]{1,0:T(8,128)(2,1)S(1)} %shard_map.122.refs_0_), channel_id=1, source_target_pairs={{0,6},{1,7},{2,4},{3,5},{4,2},{5,3},{6,0},{7,1},{8,14},{9,15},{10,... | collective-permute-start | bytes 202760 | tf_op jit(solution)/shard_map/ppermute | solution.py:38
  10.1 2.6 %shard_map.123 = (bf16[4096,384]{1,0:T(8,128)(2,1)S(1)}, bf16[512,128]{1,0:T(8,128)(2,1)S(1)}, bf16[8,128,512]{2,1,0:T(8,128)(2,1)S(1)}, bf16[8,128,512]{2,1,0:T(8,128)(2,1)S(1)}) custom-call(bf16[4096,384]{1,0:T(8,128)(2,1)} %refs_0_.2, bf16[512,128]{1,0:T(8,128)(2,1)} %bitcast.7, bf16[8,128,512]{2,1,0:T(8,128)(2,1)} %refs_2_.1, bf16[8,128,512]{2,1,0:T(8,128)(2,1)} %refs_3_.1), custom_call_target="tpu_custom_call" | custom-call | flops 4000000000 | bytes 1 | tf_op jit(solution)/shard_map/pallas_call | solution.py:46
  12.7 0.0 collective-permute-done.refs_1_
  12.7 0.0 collective-permute-done.1.refs_2_
  12.7 0.8 %collective-permute-done.2.refs_3_ = bf16[8,4224]{1,0:T(8,128)(2,1)S(1)} collective-permute-done((bf16[8,4224]{1,0:T(8,128)(2,1)S(1)}, bf16[8,4224]{1,0:T(8,128)(2,1)S(1)}, u32[]{:S(2)}, u32[]{:S(2)}) %collective-permute-start.2) | collective-permute-done | bytes 67616 | tf_op jit(solution)/shard_map/ppermute | solution.py:38
  13.5 1.6 %collective-permute-start.3 = (bf16[32,4224]{1,0:T(8,128)(2,1)S(1)}, bf16[32,4224]{1,0:T(8,128)(2,1)S(1)}, u32[]{:S(2)}, u32[]{:S(2)}) collective-permute-start(bf16[32,4224]{1,0:T(8,128)(2,1)S(1)} %shard_map.124.refs_0_), channel_id=1, source_target_pairs={{0,4},{1,5},{2,6},{3,7},{4,0},{5,1},{6,2},{7,3},{8,12},{9,13},{10,... | collective-permute-start | bytes 811016 | tf_op jit(solution)/shard_map/ppermute | solution.py:38
  15.1 1.5 %collective-permute-start.4 = (bf16[32,4224]{1,0:T(8,128)(2,1)S(1)}, bf16[32,4224]{1,0:T(8,128)(2,1)S(1)}, u32[]{:S(2)}, u32[]{:S(2)}) collective-permute-start(bf16[32,4224]{1,0:T(8,128)(2,1)S(1)} %shard_map.124.refs_0_), channel_id=1, source_target_pairs={{0,2},{1,3},{2,0},{3,1},{4,6},{5,7},{6,4},{7,5},{8,10},{9,11},{10,... | collective-permute-start | bytes 811016 | tf_op jit(solution)/shard_map/ppermute | solution.py:38
  16.6 0.0 collective-permute-done.5.refs_0_
  16.6 1.5 %collective-permute-start.6 = (bf16[8,4224]{1,0:T(8,128)(2,1)S(1)}, bf16[8,4224]{1,0:T(8,128)(2,1)S(1)}, u32[]{:S(2)}, u32[]{:S(2)}) collective-permute-start(bf16[8,4224]{1,0:T(8,128)(2,1)S(1)} %collective-permute-done.5.refs_0_), channel_id=1, source_target_pairs={{0,16},{1,17},{2,18},{3,19},{4,20},{5,21},{6,22},{7,23},{8,24},{9,... | collective-permute-start | bytes 202760 | tf_op jit(solution)/shard_map/ppermute | solution.py:38
  18.0 0.4 collective-permute-start.7
  18.5 1.6 %collective-permute-start.8 = (bf16[8,4224]{1,0:T(8,128)(2,1)S(1)}, bf16[8,4224]{1,0:T(8,128)(2,1)S(1)}, u32[]{:S(2)}, u32[]{:S(2)}) collective-permute-start(bf16[8,4224]{1,0:T(8,128)(2,1)S(1)} %collective-permute-done.5.refs_0_), channel_id=1, source_target_pairs={{0,8},{1,9},{2,10},{3,11},{4,12},{5,13},{6,14},{7,15},{8,0},{9,1},... | collective-permute-start | bytes 202760 | tf_op jit(solution)/shard_map/ppermute | solution.py:38
  20.1 2.4 %shard_map.125 = (bf16[128,384]{1,0:T(8,128)(2,1)S(1)}, bf16[128,384]{1,0:T(8,128)(2,1)S(1)}, bf16[4096,384]{1,0:T(8,128)(2,1)S(1)}) custom-call(s32[8]{0:T(128)} %refs_0_.3, bf16[4096,384]{1,0:T(8,128)(2,1)} %refs_1_.1, bf16[512,128]{1,0:T(8,128)(2,1)S(1)} %get-tuple-element.45.refs_2_, bf16[8,128,512]{2,1,0:T(8,128)(2,1)S(1)} %get-tuple-element.46.refs_3_, ...), custom_call_target="tpu_custom_call" | custom-call | flops 4000000000 | bytes 1 | tf_op jit(solution)/shard_map/pallas_call | solution.py:46
  22.5 0.0 collective-permute-done.3.refs_0_
  22.5 0.0 collective-permute-done.4.refs_1_
  22.5 0.0 copy-start
  22.5 0.1 collective-permute-start.10
  22.6 0.5 %collective-permute-start.9 = (bf16[32,4224]{1,0:T(8,128)(2,1)S(1)}, bf16[32,4224]{1,0:T(8,128)(2,1)S(1)}, u32[]{:S(2)}, u32[]{:S(2)}) collective-permute-start(bf16[32,4224]{1,0:T(8,128)(2,1)S(1)} %collective-permute-done.3.refs_0_), channel_id=1, source_target_pairs={{0,1},{1,0},{2,3},{3,2},{4,5},{5,4},{6,7},{7,6},{8,9},{9,8},{10,11... | collective-permute-start | bytes 811016 | tf_op jit(solution)/shard_map/ppermute | solution.py:38
  23.1 0.0 collective-permute-done.6.refs_1_
  23.1 0.1 collective-permute-start.11
  23.2 0.9 %collective-permute-done.7.refs_2_ = bf16[8,4224]{1,0:T(8,128)(2,1)S(1)} collective-permute-done((bf16[8,4224]{1,0:T(8,128)(2,1)S(1)}, bf16[8,4224]{1,0:T(8,128)(2,1)S(1)}, u32[]{:S(2)}, u32[]{:S(2)}) %collective-permute-start.7) | collective-permute-done | bytes 67616 | tf_op jit(solution)/shard_map/ppermute | solution.py:38
  24.1 0.0 collective-permute-done.8.refs_3_
  24.1 0.1 collective-permute-start.12
  24.2 0.0 collective-permute-done.10.refs_3_
  24.2 0.3 collective-permute-done.9.refs_2_
  24.5 0.0 copy-done
  24.5 1.9 %shard_map.127 = (bf16[64,4480]{1,0:T(8,128)(2,1)S(1)}, bf16[64,4480]{1,0:T(8,128)(2,1)S(1)}) custom-call(bf16[32,4224]{1,0:T(8,128)(2,1)S(1)} %collective-permute-done.3.refs_0_, bf16[32,4224]{1,0:T(8,128)(2,1)S(1)} %collective-permute-done.4.refs_1_, bf16[32,4224]{1,0:T(8,128)(2,1)S(1)} %collective-permute-done.9.refs_2_, ...), custom_call_target="tpu_custom_call" | custom-call | flops 4000000000 | bytes 9437184 | tf_op jit(solution)/shard_map/pallas_call | solution.py:46
  26.5 0.3 collective-permute-start.14
  26.7 0.0 collective-permute-done.11.refs_2_
  26.7 0.0 collective-permute-done.12.refs_3_
  26.7 2.0 %shard_map.128 = (bf16[64,4480]{1,0:T(8,128)(2,1)S(1)}, bf16[64,4480]{1,0:T(8,128)(2,1)S(1)}) custom-call(bf16[32,4224]{1,0:T(8,128)(2,1)S(1)} %shard_map.124.refs_0_, bf16[32,4224]{1,0:T(8,128)(2,1)S(1)} %shard_map.126.refs_1_, bf16[32,4224]{1,0:T(8,128)(2,1)S(1)} %collective-permute-done.11.refs_2_, bf16[32,4224]{1,0:T(8,128)(2,1)S(1)} %collective-permute-done.12.refs_3_, ...), custom_call_target="tpu_custom_call" | custom-call | flops 4000000000 | bytes 9437184 | tf_op jit(solution)/shard_map/pallas_call | solution.py:46
  28.7 0.4 collective-permute-start.13
  29.1 0.0 collective-permute-done.14.refs_1_
  29.1 0.3 shard_map.130
  29.4 0.6 %collective-permute-start.15 = (bf16[32,4480]{1,0:T(8,128)(2,1)S(1)}, bf16[32,4480]{1,0:T(8,128)(2,1)S(1)}, u32[]{:S(2)}, u32[]{:S(2)}) collective-permute-start(bf16[32,4480]{1,0:T(8,128)(2,1)S(1)} %get-tuple-element.64), channel_id=1, source_target_pairs={{0,4},{1,5},{2,6},{3,7},{4,0},{5,1},{6,2},{7,3},{8,12},{9,13},{10,... | collective-permute-start | bytes 860168 | tf_op jit(solution)/shard_map/ppermute | solution.py:38
  30.0 0.7 %collective-permute-start.16 = (bf16[32,4480]{1,0:T(8,128)(2,1)S(1)}, bf16[32,4480]{1,0:T(8,128)(2,1)S(1)}, u32[]{:S(2)}, u32[]{:S(2)}) collective-permute-start(bf16[32,4480]{1,0:T(8,128)(2,1)S(1)} %get-tuple-element.65), channel_id=1, source_target_pairs={{0,2},{1,3},{2,0},{3,1},{4,6},{5,7},{6,4},{7,5},{8,10},{9,11},{10,... | collective-permute-start | bytes 860168 | tf_op jit(solution)/shard_map/ppermute | solution.py:38
  30.7 0.1 collective-permute-done.13.refs_1_
  30.8 0.3 shard_map.129
  31.0 2.5 %collective-permute-start.20 = (bf16[8,4480]{1,0:T(8,128)(2,1)S(1)}, bf16[8,4480]{1,0:T(8,128)(2,1)S(1)}, u32[]{:S(2)}, u32[]{:S(2)}) collective-permute-start(bf16[8,4480]{1,0:T(8,128)(2,1)S(1)} %get-tuple-element.71), channel_id=1, source_target_pairs={{0,16},{1,17},{2,18},{3,19},{4,20},{5,21},{6,22},{7,23},{8,24},{9,... | collective-permute-start | bytes 215048 | tf_op jit(solution)/shard_map/ppermute | solution.py:38
  33.5 1.0 %collective-permute-start.21 = (bf16[8,4480]{1,0:T(8,128)(2,1)S(1)}, bf16[8,4480]{1,0:T(8,128)(2,1)S(1)}, u32[]{:S(2)}, u32[]{:S(2)}) collective-permute-start(bf16[8,4480]{1,0:T(8,128)(2,1)S(1)} %get-tuple-element.72), channel_id=1, source_target_pairs={{0,24},{1,25},{2,26},{3,27},{4,28},{5,29},{6,30},{7,31},{8,16},{9,... | collective-permute-start | bytes 215048 | tf_op jit(solution)/shard_map/ppermute | solution.py:38
  34.6 0.0 collective-permute-start.22
  34.6 3.8 %collective-permute-done.15.refs_1_ = bf16[32,4480]{1,0:T(8,128)(2,1)S(1)} collective-permute-done((bf16[32,4480]{1,0:T(8,128)(2,1)S(1)}, bf16[32,4480]{1,0:T(8,128)(2,1)S(1)}, u32[]{:S(2)}, u32[]{:S(2)}) %collective-permute-start.15) | collective-permute-done | bytes 286752 | tf_op jit(solution)/shard_map/ppermute | solution.py:38
  38.4 0.2 collective-permute-done.16.refs_2_
  38.6 0.2 shard_map.131
  38.8 2.4 %collective-permute-start.17 = (bf16[8,4480]{1,0:T(8,128)(2,1)S(1)}, bf16[8,4480]{1,0:T(8,128)(2,1)S(1)}, u32[]{:S(2)}, u32[]{:S(2)}) collective-permute-start(bf16[8,4480]{1,0:T(8,128)(2,1)S(1)} %get-tuple-element.67), channel_id=1, source_target_pairs={{0,16},{1,17},{2,18},{3,19},{4,20},{5,21},{6,22},{7,23},{8,24},{9,... | collective-permute-start | bytes 215048 | tf_op jit(solution)/shard_map/ppermute | solution.py:38
  41.2 0.4 collective-permute-start.18
  41.6 0.0 collective-permute-done.20.refs_1_
  41.6 0.8 %collective-permute-start.19 = (bf16[8,4480]{1,0:T(8,128)(2,1)S(1)}, bf16[8,4480]{1,0:T(8,128)(2,1)S(1)}, u32[]{:S(2)}, u32[]{:S(2)}) collective-permute-start(bf16[8,4480]{1,0:T(8,128)(2,1)S(1)} %get-tuple-element.69), channel_id=1, source_target_pairs={{0,8},{1,9},{2,10},{3,11},{4,12},{5,13},{6,14},{7,15},{8,0},{9,1},... | collective-permute-start | bytes 215048 | tf_op jit(solution)/shard_map/ppermute | solution.py:38
  42.4 0.0 collective-permute-done.21.refs_2_
  42.4 0.0 collective-permute-done.22.refs_3_
  42.4 0.1 shard_map.133
  42.6 1.6 %collective-permute-start.23 = (bf16[8,4480]{1,0:T(8,128)(2,1)S(1)}, bf16[8,4480]{1,0:T(8,128)(2,1)S(1)}, u32[]{:S(2)}, u32[]{:S(2)}) collective-permute-start(bf16[8,4480]{1,0:T(8,128)(2,1)S(1)} %shard_map.133), channel_id=1, source_target_pairs={{0,6},{1,7},{2,4},{3,5},{4,2},{5,3},{6,0},{7,1},{8,14},{9,15},{10,... | collective-permute-start | bytes 215048 | tf_op jit(solution)/shard_map/ppermute | solution.py:38
  44.1 1.9 %collective-permute-done.17.refs_1_ = bf16[8,4480]{1,0:T(8,128)(2,1)S(1)} collective-permute-done((bf16[8,4480]{1,0:T(8,128)(2,1)S(1)}, bf16[8,4480]{1,0:T(8,128)(2,1)S(1)}, u32[]{:S(2)}, u32[]{:S(2)}) %collective-permute-start.17) | collective-permute-done | bytes 71712 | tf_op jit(solution)/shard_map/ppermute | solution.py:38
  46.0 1.4 %collective-permute-done.18.refs_2_ = bf16[8,4480]{1,0:T(8,128)(2,1)S(1)} collective-permute-done((bf16[8,4480]{1,0:T(8,128)(2,1)S(1)}, bf16[8,4480]{1,0:T(8,128)(2,1)S(1)}, u32[]{:S(2)}, u32[]{:S(2)}) %collective-permute-start.18) | collective-permute-done | bytes 71712 | tf_op jit(solution)/shard_map/ppermute | solution.py:38
  47.4 0.0 collective-permute-done.19.refs_3_
  47.4 0.1 shard_map.132.refs_0_
  47.6 0.3 collective-permute-done.23.refs_1_
  47.9 0.7 %shard_map.134 = (bf16[8,4096]{1,0:T(8,128)(2,1)}, bf16[8,256]{1,0:T(8,128)(2,1)}) custom-call(bf16[8,4480]{1,0:T(8,128)(2,1)S(1)} %shard_map.132.refs_0_, bf16[8,4480]{1,0:T(8,128)(2,1)S(1)} %collective-permute-done.23.refs_1_), custom_call_target="tpu_custom_call" | custom-call | flops 1 | bytes 1 | tf_op jit(solution)/shard_map/pallas_call | solution.py:46
  (2 shorter events, 0.0 us)
Async XLA Ops:
  1.7 10.9 %collective-permute-start = (bf16[8,4224]{1,0:T(8,128)(2,1)S(1)}, bf16[8,4224]{1,0:T(8,128)(2,1)S(1)}, u32[]{:S(2)}, u32[]{:S(2)}) collective-permute-start(bf16[8,4224]{1,0:T(8,128)(2,1)S(1)} %shard_map.122.refs_0_), channel_id=1, source_target_pairs={{0,16},{1,17},{2,18},{3,19},{4,20},{5,21},{6,22},{7,23},{8,24},{9,... | collective-permute-start | bytes 202760 | tf_op jit(solution)/shard_map/ppermute | solution.py:38
  5.8 6.9 %collective-permute-start.1 = (bf16[8,4224]{1,0:T(8,128)(2,1)S(1)}, bf16[8,4224]{1,0:T(8,128)(2,1)S(1)}, u32[]{:S(2)}, u32[]{:S(2)}) collective-permute-start(bf16[8,4224]{1,0:T(8,128)(2,1)S(1)} %shard_map.122.refs_0_), channel_id=1, source_target_pairs={{0,8},{1,9},{2,10},{3,11},{4,12},{5,13},{6,14},{7,15},{8,0},{9,1},... | collective-permute-start | bytes 202760 | tf_op jit(solution)/shard_map/ppermute | solution.py:38
  7.4 6.1 %collective-permute-start.2 = (bf16[8,4224]{1,0:T(8,128)(2,1)S(1)}, bf16[8,4224]{1,0:T(8,128)(2,1)S(1)}, u32[]{:S(2)}, u32[]{:S(2)}) collective-permute-start(bf16[8,4224]{1,0:T(8,128)(2,1)S(1)} %shard_map.122.refs_0_), channel_id=1, source_target_pairs={{0,24},{1,25},{2,26},{3,27},{4,28},{5,29},{6,30},{7,31},{8,16},{9,... | collective-permute-start | bytes 202760 | tf_op jit(solution)/shard_map/ppermute | solution.py:38
  7.4 9.2 %collective-permute-start.5 = (bf16[8,4224]{1,0:T(8,128)(2,1)S(1)}, bf16[8,4224]{1,0:T(8,128)(2,1)S(1)}, u32[]{:S(2)}, u32[]{:S(2)}) collective-permute-start(bf16[8,4224]{1,0:T(8,128)(2,1)S(1)} %shard_map.122.refs_0_), channel_id=1, source_target_pairs={{0,6},{1,7},{2,4},{3,5},{4,2},{5,3},{6,0},{7,1},{8,14},{9,15},{10,... | collective-permute-start | bytes 202760 | tf_op jit(solution)/shard_map/ppermute | solution.py:38
  13.5 9.0 %collective-permute-start.3 = (bf16[32,4224]{1,0:T(8,128)(2,1)S(1)}, bf16[32,4224]{1,0:T(8,128)(2,1)S(1)}, u32[]{:S(2)}, u32[]{:S(2)}) collective-permute-start(bf16[32,4224]{1,0:T(8,128)(2,1)S(1)} %shard_map.124.refs_0_), channel_id=1, source_target_pairs={{0,4},{1,5},{2,6},{3,7},{4,0},{5,1},{6,2},{7,3},{8,12},{9,13},{10,... | collective-permute-start | bytes 811016 | tf_op jit(solution)/shard_map/ppermute | solution.py:38
  15.1 7.4 %collective-permute-start.4 = (bf16[32,4224]{1,0:T(8,128)(2,1)S(1)}, bf16[32,4224]{1,0:T(8,128)(2,1)S(1)}, u32[]{:S(2)}, u32[]{:S(2)}) collective-permute-start(bf16[32,4224]{1,0:T(8,128)(2,1)S(1)} %shard_map.124.refs_0_), channel_id=1, source_target_pairs={{0,2},{1,3},{2,0},{3,1},{4,6},{5,7},{6,4},{7,5},{8,10},{9,11},{10,... | collective-permute-start | bytes 811016 | tf_op jit(solution)/shard_map/ppermute | solution.py:38
  16.6 6.5 %collective-permute-start.6 = (bf16[8,4224]{1,0:T(8,128)(2,1)S(1)}, bf16[8,4224]{1,0:T(8,128)(2,1)S(1)}, u32[]{:S(2)}, u32[]{:S(2)}) collective-permute-start(bf16[8,4224]{1,0:T(8,128)(2,1)S(1)} %collective-permute-done.5.refs_0_), channel_id=1, source_target_pairs={{0,16},{1,17},{2,18},{3,19},{4,20},{5,21},{6,22},{7,23},{8,24},{9,... | collective-permute-start | bytes 202760 | tf_op jit(solution)/shard_map/ppermute | solution.py:38
  18.0 6.1 %collective-permute-start.7 = (bf16[8,4224]{1,0:T(8,128)(2,1)S(1)}, bf16[8,4224]{1,0:T(8,128)(2,1)S(1)}, u32[]{:S(2)}, u32[]{:S(2)}) collective-permute-start(bf16[8,4224]{1,0:T(8,128)(2,1)S(1)} %collective-permute-done.5.refs_0_), channel_id=1, source_target_pairs={{0,24},{1,25},{2,26},{3,27},{4,28},{5,29},{6,30},{7,31},{8,16},{9,... | collective-permute-start | bytes 202760 | tf_op jit(solution)/shard_map/ppermute | solution.py:38
  18.5 5.6 %collective-permute-start.8 = (bf16[8,4224]{1,0:T(8,128)(2,1)S(1)}, bf16[8,4224]{1,0:T(8,128)(2,1)S(1)}, u32[]{:S(2)}, u32[]{:S(2)}) collective-permute-start(bf16[8,4224]{1,0:T(8,128)(2,1)S(1)} %collective-permute-done.5.refs_0_), channel_id=1, source_target_pairs={{0,8},{1,9},{2,10},{3,11},{4,12},{5,13},{6,14},{7,15},{8,0},{9,1},... | collective-permute-start | bytes 202760 | tf_op jit(solution)/shard_map/ppermute | solution.py:38
  22.5 2.0 %copy-start = (bf16[384,4096]{1,0:T(8,128)(2,1)S(1)}, bf16[384,4096]{1,0:T(8,128)(2,1)}, u32[]{:S(2)}) copy-start(bf16[384,4096]{1,0:T(8,128)(2,1)} %refs_8_.3) | copy-start | bytes 9437188
  22.5 1.7 %collective-permute-start.10 = (bf16[32,4224]{1,0:T(8,128)(2,1)S(1)}, bf16[32,4224]{1,0:T(8,128)(2,1)S(1)}, u32[]{:S(2)}, u32[]{:S(2)}) collective-permute-start(bf16[32,4224]{1,0:T(8,128)(2,1)S(1)} %collective-permute-done.4.refs_1_), channel_id=1, source_target_pairs={{0,1},{1,0},{2,3},{3,2},{4,5},{5,4},{6,7},{7,6},{8,9},{9,8},{10,11... | collective-permute-start | bytes 811016 | tf_op jit(solution)/shard_map/ppermute | solution.py:38
  22.6 1.9 %collective-permute-start.9 = (bf16[32,4224]{1,0:T(8,128)(2,1)S(1)}, bf16[32,4224]{1,0:T(8,128)(2,1)S(1)}, u32[]{:S(2)}, u32[]{:S(2)}) collective-permute-start(bf16[32,4224]{1,0:T(8,128)(2,1)S(1)} %collective-permute-done.3.refs_0_), channel_id=1, source_target_pairs={{0,1},{1,0},{2,3},{3,2},{4,5},{5,4},{6,7},{7,6},{8,9},{9,8},{10,11... | collective-permute-start | bytes 811016 | tf_op jit(solution)/shard_map/ppermute | solution.py:38
  23.1 3.6 %collective-permute-start.11 = (bf16[32,4224]{1,0:T(8,128)(2,1)S(1)}, bf16[32,4224]{1,0:T(8,128)(2,1)S(1)}, u32[]{:S(2)}, u32[]{:S(2)}) collective-permute-start(bf16[32,4224]{1,0:T(8,128)(2,1)S(1)} %shard_map.124.refs_0_), channel_id=1, source_target_pairs={{0,1},{1,0},{2,3},{3,2},{4,5},{5,4},{6,7},{7,6},{8,9},{9,8},{10,11... | collective-permute-start | bytes 811016 | tf_op jit(solution)/shard_map/ppermute | solution.py:38
  24.1 2.6 %collective-permute-start.12 = (bf16[32,4224]{1,0:T(8,128)(2,1)S(1)}, bf16[32,4224]{1,0:T(8,128)(2,1)S(1)}, u32[]{:S(2)}, u32[]{:S(2)}) collective-permute-start(bf16[32,4224]{1,0:T(8,128)(2,1)S(1)} %shard_map.126.refs_1_), channel_id=1, source_target_pairs={{0,1},{1,0},{2,3},{3,2},{4,5},{5,4},{6,7},{7,6},{8,9},{9,8},{10,11... | collective-permute-start | bytes 811016 | tf_op jit(solution)/shard_map/ppermute | solution.py:38
  26.5 2.6 %collective-permute-start.14 = (bf16[64,4480]{1,0:T(8,128)(2,1)S(1)}, bf16[64,4480]{1,0:T(8,128)(2,1)S(1)}, u32[]{:S(2)}, u32[]{:S(2)}) collective-permute-start(bf16[64,4480]{1,0:T(8,128)(2,1)S(1)} %get-tuple-element.63), channel_id=1, source_target_pairs={{0,1},{1,0},{2,3},{3,2},{4,5},{5,4},{6,7},{7,6},{8,9},{9,8},{10,11... | collective-permute-start | bytes 1720328 | tf_op jit(solution)/shard_map/ppermute | solution.py:38
  28.7 2.0 %collective-permute-start.13 = (bf16[64,4480]{1,0:T(8,128)(2,1)S(1)}, bf16[64,4480]{1,0:T(8,128)(2,1)S(1)}, u32[]{:S(2)}, u32[]{:S(2)}) collective-permute-start(bf16[64,4480]{1,0:T(8,128)(2,1)S(1)} %get-tuple-element.61), channel_id=1, source_target_pairs={{0,1},{1,0},{2,3},{3,2},{4,5},{5,4},{6,7},{7,6},{8,9},{9,8},{10,11... | collective-permute-start | bytes 1720328 | tf_op jit(solution)/shard_map/ppermute | solution.py:38
  29.4 9.0 %collective-permute-start.15 = (bf16[32,4480]{1,0:T(8,128)(2,1)S(1)}, bf16[32,4480]{1,0:T(8,128)(2,1)S(1)}, u32[]{:S(2)}, u32[]{:S(2)}) collective-permute-start(bf16[32,4480]{1,0:T(8,128)(2,1)S(1)} %get-tuple-element.64), channel_id=1, source_target_pairs={{0,4},{1,5},{2,6},{3,7},{4,0},{5,1},{6,2},{7,3},{8,12},{9,13},{10,... | collective-permute-start | bytes 860168 | tf_op jit(solution)/shard_map/ppermute | solution.py:38
  30.0 8.7 %collective-permute-start.16 = (bf16[32,4480]{1,0:T(8,128)(2,1)S(1)}, bf16[32,4480]{1,0:T(8,128)(2,1)S(1)}, u32[]{:S(2)}, u32[]{:S(2)}) collective-permute-start(bf16[32,4480]{1,0:T(8,128)(2,1)S(1)} %get-tuple-element.65), channel_id=1, source_target_pairs={{0,2},{1,3},{2,0},{3,1},{4,6},{5,7},{6,4},{7,5},{8,10},{9,11},{10,... | collective-permute-start | bytes 860168 | tf_op jit(solution)/shard_map/ppermute | solution.py:38
  31.0 10.6 %collective-permute-start.20 = (bf16[8,4480]{1,0:T(8,128)(2,1)S(1)}, bf16[8,4480]{1,0:T(8,128)(2,1)S(1)}, u32[]{:S(2)}, u32[]{:S(2)}) collective-permute-start(bf16[8,4480]{1,0:T(8,128)(2,1)S(1)} %get-tuple-element.71), channel_id=1, source_target_pairs={{0,16},{1,17},{2,18},{3,19},{4,20},{5,21},{6,22},{7,23},{8,24},{9,... | collective-permute-start | bytes 215048 | tf_op jit(solution)/shard_map/ppermute | solution.py:38
  33.5 8.9 %collective-permute-start.21 = (bf16[8,4480]{1,0:T(8,128)(2,1)S(1)}, bf16[8,4480]{1,0:T(8,128)(2,1)S(1)}, u32[]{:S(2)}, u32[]{:S(2)}) collective-permute-start(bf16[8,4480]{1,0:T(8,128)(2,1)S(1)} %get-tuple-element.72), channel_id=1, source_target_pairs={{0,24},{1,25},{2,26},{3,27},{4,28},{5,29},{6,30},{7,31},{8,16},{9,... | collective-permute-start | bytes 215048 | tf_op jit(solution)/shard_map/ppermute | solution.py:38
  34.6 7.8 %collective-permute-start.22 = (bf16[8,4480]{1,0:T(8,128)(2,1)S(1)}, bf16[8,4480]{1,0:T(8,128)(2,1)S(1)}, u32[]{:S(2)}, u32[]{:S(2)}) collective-permute-start(bf16[8,4480]{1,0:T(8,128)(2,1)S(1)} %get-tuple-element.73), channel_id=1, source_target_pairs={{0,8},{1,9},{2,10},{3,11},{4,12},{5,13},{6,14},{7,15},{8,0},{9,1},... | collective-permute-start | bytes 215048 | tf_op jit(solution)/shard_map/ppermute | solution.py:38
  38.8 7.2 %collective-permute-start.17 = (bf16[8,4480]{1,0:T(8,128)(2,1)S(1)}, bf16[8,4480]{1,0:T(8,128)(2,1)S(1)}, u32[]{:S(2)}, u32[]{:S(2)}) collective-permute-start(bf16[8,4480]{1,0:T(8,128)(2,1)S(1)} %get-tuple-element.67), channel_id=1, source_target_pairs={{0,16},{1,17},{2,18},{3,19},{4,20},{5,21},{6,22},{7,23},{8,24},{9,... | collective-permute-start | bytes 215048 | tf_op jit(solution)/shard_map/ppermute | solution.py:38
  41.2 6.2 %collective-permute-start.18 = (bf16[8,4480]{1,0:T(8,128)(2,1)S(1)}, bf16[8,4480]{1,0:T(8,128)(2,1)S(1)}, u32[]{:S(2)}, u32[]{:S(2)}) collective-permute-start(bf16[8,4480]{1,0:T(8,128)(2,1)S(1)} %get-tuple-element.68), channel_id=1, source_target_pairs={{0,24},{1,25},{2,26},{3,27},{4,28},{5,29},{6,30},{7,31},{8,16},{9,... | collective-permute-start | bytes 215048 | tf_op jit(solution)/shard_map/ppermute | solution.py:38
  41.6 5.8 %collective-permute-start.19 = (bf16[8,4480]{1,0:T(8,128)(2,1)S(1)}, bf16[8,4480]{1,0:T(8,128)(2,1)S(1)}, u32[]{:S(2)}, u32[]{:S(2)}) collective-permute-start(bf16[8,4480]{1,0:T(8,128)(2,1)S(1)} %get-tuple-element.69), channel_id=1, source_target_pairs={{0,8},{1,9},{2,10},{3,11},{4,12},{5,13},{6,14},{7,15},{8,0},{9,1},... | collective-permute-start | bytes 215048 | tf_op jit(solution)/shard_map/ppermute | solution.py:38
  42.6 5.3 %collective-permute-start.23 = (bf16[8,4480]{1,0:T(8,128)(2,1)S(1)}, bf16[8,4480]{1,0:T(8,128)(2,1)S(1)}, u32[]{:S(2)}, u32[]{:S(2)}) collective-permute-start(bf16[8,4480]{1,0:T(8,128)(2,1)S(1)} %shard_map.133), channel_id=1, source_target_pairs={{0,6},{1,7},{2,4},{3,5},{4,2},{5,3},{6,0},{7,1},{8,14},{9,15},{10,... | collective-permute-start | bytes 215048 | tf_op jit(solution)/shard_map/ppermute | solution.py:38

commit v11 on v10

--- a/solution.py
+++ b/solution.py
@@ -380,7 +380,7 @@
     base = after(base, near)
     near, far = apply_expert([base, *last_chunk], others[count:], [0] + [3] * len(across), sums, weights)
     total, *corner_pieces = summed([near, exchange(far, 1)], [rows] + cut * len(across), width, own)
-    parts = [total] + [exchange(piece, stride * k) for piece, k in zip(pieces, sides)]
+    parts = [total] + [exchange(piece, stride * k) for piece, k in list(zip(pieces, sides))[::-1]]
     if across:
         corner_parts = scatter(corner_pieces, outer, width, own, [2, 3, 1])
     pieces = summed(parts, cut, width, own)

time: 48.7 us -> 48.8 us (level)
  transfers between devices with their start and end apart: 24 -> 24, of which waited for: 9 -> 8; matrix products, arithmetic and copies ran while one was open for 0% -> 0% of each run, Pallas kernels for 21% -> 21%
where the time goes in v11:
time: 48.8 us; the launch traced here: 48.6 us
  starting transfers between devices  26.1 us (53%)
  Pallas kernels  11.8 us (24%)
  waiting for transfers between devices  9.85 us (20%)
  between operations  0.79 us (2%)
    ppermute x24, starting transfers between devices, exchange(): return lax.ppermute(value, 'ffn', [(i, i ^ distance) for i in range(size)])  26.1 us
    pallas_call x13, Pallas kernels, call(): pl.pallas_call(body, out_shape=out_shape, in_specs=in_specs or [VMEM] * l...  11.8 us
    ppermute x24, waiting for transfers between devices, exchange(): return lax.ppermute(value, 'ffn', [(i, i ^ distance) for i in range(size)])  9.85 us
  transfers between devices with their start and end apart: 24, of which 8 were waited for; matrix products, arithmetic and copies ran while one was open for 0% of the time, Pallas kernels for 21%

profile of v11, /device:TPU:0, one launch (start us, length us, event | category | flops | bytes accessed | tf_op | source)
XLA Modules:
  0.0 48.6 jit_solution(16523193905309159395)
XLA Ops:
  0.6 1.1 %shard_map.122.refs_0_ = bf16[8,4224]{1,0:T(8,128)(2,1)S(1)} custom-call(bf16[8,4096]{1,0:T(8,128)(2,1)} %tokens_hbm.1, f32[1,4096]{1,0:T(1,128)} %bitcast.6, s32[8,8]{1,0:T(8,128)} %routes_hbm.1, f32[8,8]{1,0:T(8,128)} %scores_hbm.1), custom_call_target="tpu_custom_call" | custom-call | flops 1 | bytes 1 | tf_op jit(solution)/shard_map/pallas_call | solution.py:46
  1.7 4.1 %collective-permute-start = (bf16[8,4224]{1,0:T(8,128)(2,1)S(1)}, bf16[8,4224]{1,0:T(8,128)(2,1)S(1)}, u32[]{:S(2)}, u32[]{:S(2)}) collective-permute-start(bf16[8,4224]{1,0:T(8,128)(2,1)S(1)} %shard_map.122.refs_0_), channel_id=1, source_target_pairs={{0,16},{1,17},{2,18},{3,19},{4,20},{5,21},{6,22},{7,23},{8,24},{9,... | collective-permute-start | bytes 202760 | tf_op jit(solution)/shard_map/ppermute | solution.py:38
  5.8 1.6 %collective-permute-start.1 = (bf16[8,4224]{1,0:T(8,128)(2,1)S(1)}, bf16[8,4224]{1,0:T(8,128)(2,1)S(1)}, u32[]{:S(2)}, u32[]{:S(2)}) collective-permute-start(bf16[8,4224]{1,0:T(8,128)(2,1)S(1)} %shard_map.122.refs_0_), channel_id=1, source_target_pairs={{0,8},{1,9},{2,10},{3,11},{4,12},{5,13},{6,14},{7,15},{8,0},{9,1},... | collective-permute-start | bytes 202760 | tf_op jit(solution)/shard_map/ppermute | solution.py:38
  7.4 0.0 collective-permute-start.2
  7.4 2.7 %collective-permute-start.5 = (bf16[8,4224]{1,0:T(8,128)(2,1)S(1)}, bf16[8,4224]{1,0:T(8,128)(2,1)S(1)}, u32[]{:S(2)}, u32[]{:S(2)}) collective-permute-start(bf16[8,4224]{1,0:T(8,128)(2,1)S(1)} %shard_map.122.refs_0_), channel_id=1, source_target_pairs={{0,6},{1,7},{2,4},{3,5},{4,2},{5,3},{6,0},{7,1},{8,14},{9,15},{10,... | collective-permute-start | bytes 202760 | tf_op jit(solution)/shard_map/ppermute | solution.py:38
  10.1 2.6 %shard_map.123 = (bf16[4096,384]{1,0:T(8,128)(2,1)S(1)}, bf16[512,128]{1,0:T(8,128)(2,1)S(1)}, bf16[8,128,512]{2,1,0:T(8,128)(2,1)S(1)}, bf16[8,128,512]{2,1,0:T(8,128)(2,1)S(1)}) custom-call(bf16[4096,384]{1,0:T(8,128)(2,1)} %refs_0_.2, bf16[512,128]{1,0:T(8,128)(2,1)} %bitcast.7, bf16[8,128,512]{2,1,0:T(8,128)(2,1)} %refs_2_.1, bf16[8,128,512]{2,1,0:T(8,128)(2,1)} %refs_3_.1), custom_call_target="tpu_custom_call" | custom-call | flops 4000000000 | bytes 1 | tf_op jit(solution)/shard_map/pallas_call | solution.py:46
  12.7 0.0 collective-permute-done.refs_1_
  12.7 0.0 collective-permute-done.1.refs_2_
  12.7 0.8 %collective-permute-done.2.refs_3_ = bf16[8,4224]{1,0:T(8,128)(2,1)S(1)} collective-permute-done((bf16[8,4224]{1,0:T(8,128)(2,1)S(1)}, bf16[8,4224]{1,0:T(8,128)(2,1)S(1)}, u32[]{:S(2)}, u32[]{:S(2)}) %collective-permute-start.2) | collective-permute-done | bytes 67616 | tf_op jit(solution)/shard_map/ppermute | solution.py:38
  13.5 1.6 %collective-permute-start.3 = (bf16[32,4224]{1,0:T(8,128)(2,1)S(1)}, bf16[32,4224]{1,0:T(8,128)(2,1)S(1)}, u32[]{:S(2)}, u32[]{:S(2)}) collective-permute-start(bf16[32,4224]{1,0:T(8,128)(2,1)S(1)} %shard_map.124.refs_0_), channel_id=1, source_target_pairs={{0,4},{1,5},{2,6},{3,7},{4,0},{5,1},{6,2},{7,3},{8,12},{9,13},{10,... | collective-permute-start | bytes 811016 | tf_op jit(solution)/shard_map/ppermute | solution.py:38
  15.1 1.5 %collective-permute-start.4 = (bf16[32,4224]{1,0:T(8,128)(2,1)S(1)}, bf16[32,4224]{1,0:T(8,128)(2,1)S(1)}, u32[]{:S(2)}, u32[]{:S(2)}) collective-permute-start(bf16[32,4224]{1,0:T(8,128)(2,1)S(1)} %shard_map.124.refs_0_), channel_id=1, source_target_pairs={{0,2},{1,3},{2,0},{3,1},{4,6},{5,7},{6,4},{7,5},{8,10},{9,11},{10,... | collective-permute-start | bytes 811016 | tf_op jit(solution)/shard_map/ppermute | solution.py:38
  16.6 0.0 collective-permute-done.5.refs_0_
  16.6 1.5 %collective-permute-start.6 = (bf16[8,4224]{1,0:T(8,128)(2,1)S(1)}, bf16[8,4224]{1,0:T(8,128)(2,1)S(1)}, u32[]{:S(2)}, u32[]{:S(2)}) collective-permute-start(bf16[8,4224]{1,0:T(8,128)(2,1)S(1)} %collective-permute-done.5.refs_0_), channel_id=1, source_target_pairs={{0,16},{1,17},{2,18},{3,19},{4,20},{5,21},{6,22},{7,23},{8,24},{9,... | collective-permute-start | bytes 202760 | tf_op jit(solution)/shard_map/ppermute | solution.py:38
  18.0 0.4 collective-permute-start.7
  18.5 1.6 %collective-permute-start.8 = (bf16[8,4224]{1,0:T(8,128)(2,1)S(1)}, bf16[8,4224]{1,0:T(8,128)(2,1)S(1)}, u32[]{:S(2)}, u32[]{:S(2)}) collective-permute-start(bf16[8,4224]{1,0:T(8,128)(2,1)S(1)} %collective-permute-done.5.refs_0_), channel_id=1, source_target_pairs={{0,8},{1,9},{2,10},{3,11},{4,12},{5,13},{6,14},{7,15},{8,0},{9,1},... | collective-permute-start | bytes 202760 | tf_op jit(solution)/shard_map/ppermute | solution.py:38
  20.1 2.4 %shard_map.125 = (bf16[128,384]{1,0:T(8,128)(2,1)S(1)}, bf16[128,384]{1,0:T(8,128)(2,1)S(1)}, bf16[4096,384]{1,0:T(8,128)(2,1)S(1)}) custom-call(s32[8]{0:T(128)} %refs_0_.3, bf16[4096,384]{1,0:T(8,128)(2,1)} %refs_1_.1, bf16[512,128]{1,0:T(8,128)(2,1)S(1)} %get-tuple-element.45.refs_2_, bf16[8,128,512]{2,1,0:T(8,128)(2,1)S(1)} %get-tuple-element.46.refs_3_, ...), custom_call_target="tpu_custom_call" | custom-call | flops 4000000000 | bytes 1 | tf_op jit(solution)/shard_map/pallas_call | solution.py:46
  22.5 0.0 collective-permute-done.3.refs_0_
  22.5 0.0 collective-permute-done.4.refs_1_
  22.5 0.0 copy-start
  22.5 0.1 collective-permute-start.10
  22.6 0.5 %collective-permute-start.9 = (bf16[32,4224]{1,0:T(8,128)(2,1)S(1)}, bf16[32,4224]{1,0:T(8,128)(2,1)S(1)}, u32[]{:S(2)}, u32[]{:S(2)}) collective-permute-start(bf16[32,4224]{1,0:T(8,128)(2,1)S(1)} %collective-permute-done.3.refs_0_), channel_id=1, source_target_pairs={{0,1},{1,0},{2,3},{3,2},{4,5},{5,4},{6,7},{7,6},{8,9},{9,8},{10,11... | collective-permute-start | bytes 811016 | tf_op jit(solution)/shard_map/ppermute | solution.py:38
  23.1 0.0 collective-permute-done.6.refs_1_
  23.1 0.1 collective-permute-start.11
  23.2 0.9 %collective-permute-done.7.refs_2_ = bf16[8,4224]{1,0:T(8,128)(2,1)S(1)} collective-permute-done((bf16[8,4224]{1,0:T(8,128)(2,1)S(1)}, bf16[8,4224]{1,0:T(8,128)(2,1)S(1)}, u32[]{:S(2)}, u32[]{:S(2)}) %collective-permute-start.7) | collective-permute-done | bytes 67616 | tf_op jit(solution)/shard_map/ppermute | solution.py:38
  24.1 0.0 collective-permute-done.8.refs_3_
  24.1 0.1 collective-permute-start.12
  24.2 0.0 collective-permute-done.10.refs_3_
  24.2 0.3 collective-permute-done.9.refs_2_
  24.5 0.0 copy-done
  24.5 1.9 %shard_map.127 = (bf16[64,4480]{1,0:T(8,128)(2,1)S(1)}, bf16[64,4480]{1,0:T(8,128)(2,1)S(1)}) custom-call(bf16[32,4224]{1,0:T(8,128)(2,1)S(1)} %collective-permute-done.3.refs_0_, bf16[32,4224]{1,0:T(8,128)(2,1)S(1)} %collective-permute-done.4.refs_1_, bf16[32,4224]{1,0:T(8,128)(2,1)S(1)} %collective-permute-done.9.refs_2_, ...), custom_call_target="tpu_custom_call" | custom-call | flops 4000000000 | bytes 9437184 | tf_op jit(solution)/shard_map/pallas_call | solution.py:46
  26.5 0.3 collective-permute-start.14
  26.7 0.0 collective-permute-done.11.refs_2_
  26.7 0.0 collective-permute-done.12.refs_3_
  26.7 2.0 %shard_map.128 = (bf16[64,4480]{1,0:T(8,128)(2,1)S(1)}, bf16[64,4480]{1,0:T(8,128)(2,1)S(1)}) custom-call(bf16[32,4224]{1,0:T(8,128)(2,1)S(1)} %shard_map.124.refs_0_, bf16[32,4224]{1,0:T(8,128)(2,1)S(1)} %shard_map.126.refs_1_, bf16[32,4224]{1,0:T(8,128)(2,1)S(1)} %collective-permute-done.11.refs_2_, bf16[32,4224]{1,0:T(8,128)(2,1)S(1)} %collective-permute-done.12.refs_3_, ...), custom_call_target="tpu_custom_call" | custom-call | flops 4000000000 | bytes 9437184 | tf_op jit(solution)/shard_map/pallas_call | solution.py:46
  28.7 0.4 collective-permute-start.13
  29.1 0.0 collective-permute-done.14.refs_1_
  29.1 0.3 shard_map.130
  29.4 0.6 %collective-permute-start.15 = (bf16[32,4480]{1,0:T(8,128)(2,1)S(1)}, bf16[32,4480]{1,0:T(8,128)(2,1)S(1)}, u32[]{:S(2)}, u32[]{:S(2)}) collective-permute-start(bf16[32,4480]{1,0:T(8,128)(2,1)S(1)} %get-tuple-element.64), channel_id=1, source_target_pairs={{0,2},{1,3},{2,0},{3,1},{4,6},{5,7},{6,4},{7,5},{8,10},{9,11},{10,... | collective-permute-start | bytes 860168 | tf_op jit(solution)/shard_map/ppermute | solution.py:38
  30.0 0.7 %collective-permute-start.16 = (bf16[32,4480]{1,0:T(8,128)(2,1)S(1)}, bf16[32,4480]{1,0:T(8,128)(2,1)S(1)}, u32[]{:S(2)}, u32[]{:S(2)}) collective-permute-start(bf16[32,4480]{1,0:T(8,128)(2,1)S(1)} %get-tuple-element.65), channel_id=1, source_target_pairs={{0,4},{1,5},{2,6},{3,7},{4,0},{5,1},{6,2},{7,3},{8,12},{9,13},{10,... | collective-permute-start | bytes 860168 | tf_op jit(solution)/shard_map/ppermute | solution.py:38
  30.7 0.1 collective-permute-done.13.refs_1_
  30.8 0.3 shard_map.129
  31.0 2.5 %collective-permute-start.20 = (bf16[8,4480]{1,0:T(8,128)(2,1)S(1)}, bf16[8,4480]{1,0:T(8,128)(2,1)S(1)}, u32[]{:S(2)}, u32[]{:S(2)}) collective-permute-start(bf16[8,4480]{1,0:T(8,128)(2,1)S(1)} %get-tuple-element.71), channel_id=1, source_target_pairs={{0,16},{1,17},{2,18},{3,19},{4,20},{5,21},{6,22},{7,23},{8,24},{9,... | collective-permute-start | bytes 215048 | tf_op jit(solution)/shard_map/ppermute | solution.py:38
  33.5 1.0 %collective-permute-start.21 = (bf16[8,4480]{1,0:T(8,128)(2,1)S(1)}, bf16[8,4480]{1,0:T(8,128)(2,1)S(1)}, u32[]{:S(2)}, u32[]{:S(2)}) collective-permute-start(bf16[8,4480]{1,0:T(8,128)(2,1)S(1)} %get-tuple-element.72), channel_id=1, source_target_pairs={{0,24},{1,25},{2,26},{3,27},{4,28},{5,29},{6,30},{7,31},{8,16},{9,... | collective-permute-start | bytes 215048 | tf_op jit(solution)/shard_map/ppermute | solution.py:38
  34.6 0.0 collective-permute-start.22
  34.6 3.8 %collective-permute-done.15.refs_1_ = bf16[32,4480]{1,0:T(8,128)(2,1)S(1)} collective-permute-done((bf16[32,4480]{1,0:T(8,128)(2,1)S(1)}, bf16[32,4480]{1,0:T(8,128)(2,1)S(1)}, u32[]{:S(2)}, u32[]{:S(2)}) %collective-permute-start.15) | collective-permute-done | bytes 286752 | tf_op jit(solution)/shard_map/ppermute | solution.py:38
  38.4 0.3 collective-permute-done.16.refs_2_
  38.7 0.2 shard_map.131
  38.9 2.7 %collective-permute-start.17 = (bf16[8,4480]{1,0:T(8,128)(2,1)S(1)}, bf16[8,4480]{1,0:T(8,128)(2,1)S(1)}, u32[]{:S(2)}, u32[]{:S(2)}) collective-permute-start(bf16[8,4480]{1,0:T(8,128)(2,1)S(1)} %get-tuple-element.67), channel_id=1, source_target_pairs={{0,16},{1,17},{2,18},{3,19},{4,20},{5,21},{6,22},{7,23},{8,24},{9,... | collective-permute-start | bytes 215048 | tf_op jit(solution)/shard_map/ppermute | solution.py:38
  41.6 0.3 collective-permute-start.18
  41.9 0.0 collective-permute-done.20.refs_1_
  41.9 0.6 %collective-permute-start.19 = (bf16[8,4480]{1,0:T(8,128)(2,1)S(1)}, bf16[8,4480]{1,0:T(8,128)(2,1)S(1)}, u32[]{:S(2)}, u32[]{:S(2)}) collective-permute-start(bf16[8,4480]{1,0:T(8,128)(2,1)S(1)} %get-tuple-element.69), channel_id=1, source_target_pairs={{0,8},{1,9},{2,10},{3,11},{4,12},{5,13},{6,14},{7,15},{8,0},{9,1},... | collective-permute-start | bytes 215048 | tf_op jit(solution)/shard_map/ppermute | solution.py:38
  42.4 0.0 collective-permute-done.21.refs_2_
  42.4 0.0 collective-permute-done.22.refs_3_
  42.4 0.1 shard_map.133
  42.6 1.5 %collective-permute-start.23 = (bf16[8,4480]{1,0:T(8,128)(2,1)S(1)}, bf16[8,4480]{1,0:T(8,128)(2,1)S(1)}, u32[]{:S(2)}, u32[]{:S(2)}) collective-permute-start(bf16[8,4480]{1,0:T(8,128)(2,1)S(1)} %shard_map.133), channel_id=1, source_target_pairs={{0,6},{1,7},{2,4},{3,5},{4,2},{5,3},{6,0},{7,1},{8,14},{9,15},{10,... | collective-permute-start | bytes 215048 | tf_op jit(solution)/shard_map/ppermute | solution.py:38
  44.1 2.0 %collective-permute-done.17.refs_1_ = bf16[8,4480]{1,0:T(8,128)(2,1)S(1)} collective-permute-done((bf16[8,4480]{1,0:T(8,128)(2,1)S(1)}, bf16[8,4480]{1,0:T(8,128)(2,1)S(1)}, u32[]{:S(2)}, u32[]{:S(2)}) %collective-permute-start.17) | collective-permute-done | bytes 71712 | tf_op jit(solution)/shard_map/ppermute | solution.py:38
  46.1 1.6 %collective-permute-done.18.refs_2_ = bf16[8,4480]{1,0:T(8,128)(2,1)S(1)} collective-permute-done((bf16[8,4480]{1,0:T(8,128)(2,1)S(1)}, bf16[8,4480]{1,0:T(8,128)(2,1)S(1)}, u32[]{:S(2)}, u32[]{:S(2)}) %collective-permute-start.18) | collective-permute-done | bytes 71712 | tf_op jit(solution)/shard_map/ppermute | solution.py:38
  47.7 0.0 collective-permute-done.19.refs_3_
  47.7 0.1 shard_map.132.refs_0_
  47.9 0.0 collective-permute-done.23.refs_1_
  47.9 0.7 %shard_map.134 = (bf16[8,4096]{1,0:T(8,128)(2,1)}, bf16[8,256]{1,0:T(8,128)(2,1)}) custom-call(bf16[8,4480]{1,0:T(8,128)(2,1)S(1)} %shard_map.132.refs_0_, bf16[8,4480]{1,0:T(8,128)(2,1)S(1)} %collective-permute-done.23.refs_1_), custom_call_target="tpu_custom_call" | custom-call | flops 1 | bytes 1 | tf_op jit(solution)/shard_map/pallas_call | solution.py:46
  (2 shorter events, 0.0 us)
Async XLA Ops:
  1.7 10.9 %collective-permute-start = (bf16[8,4224]{1,0:T(8,128)(2,1)S(1)}, bf16[8,4224]{1,0:T(8,128)(2,1)S(1)}, u32[]{:S(2)}, u32[]{:S(2)}) collective-permute-start(bf16[8,4224]{1,0:T(8,128)(2,1)S(1)} %shard_map.122.refs_0_), channel_id=1, source_target_pairs={{0,16},{1,17},{2,18},{3,19},{4,20},{5,21},{6,22},{7,23},{8,24},{9,... | collective-permute-start | bytes 202760 | tf_op jit(solution)/shard_map/ppermute | solution.py:38
  5.8 6.9 %collective-permute-start.1 = (bf16[8,4224]{1,0:T(8,128)(2,1)S(1)}, bf16[8,4224]{1,0:T(8,128)(2,1)S(1)}, u32[]{:S(2)}, u32[]{:S(2)}) collective-permute-start(bf16[8,4224]{1,0:T(8,128)(2,1)S(1)} %shard_map.122.refs_0_), channel_id=1, source_target_pairs={{0,8},{1,9},{2,10},{3,11},{4,12},{5,13},{6,14},{7,15},{8,0},{9,1},... | collective-permute-start | bytes 202760 | tf_op jit(solution)/shard_map/ppermute | solution.py:38
  7.4 6.1 %collective-permute-start.2 = (bf16[8,4224]{1,0:T(8,128)(2,1)S(1)}, bf16[8,4224]{1,0:T(8,128)(2,1)S(1)}, u32[]{:S(2)}, u32[]{:S(2)}) collective-permute-start(bf16[8,4224]{1,0:T(8,128)(2,1)S(1)} %shard_map.122.refs_0_), channel_id=1, source_target_pairs={{0,24},{1,25},{2,26},{3,27},{4,28},{5,29},{6,30},{7,31},{8,16},{9,... | collective-permute-start | bytes 202760 | tf_op jit(solution)/shard_map/ppermute | solution.py:38
  7.4 9.2 %collective-permute-start.5 = (bf16[8,4224]{1,0:T(8,128)(2,1)S(1)}, bf16[8,4224]{1,0:T(8,128)(2,1)S(1)}, u32[]{:S(2)}, u32[]{:S(2)}) collective-permute-start(bf16[8,4224]{1,0:T(8,128)(2,1)S(1)} %shard_map.122.refs_0_), channel_id=1, source_target_pairs={{0,6},{1,7},{2,4},{3,5},{4,2},{5,3},{6,0},{7,1},{8,14},{9,15},{10,... | collective-permute-start | bytes 202760 | tf_op jit(solution)/shard_map/ppermute | solution.py:38
  13.5 9.0 %collective-permute-start.3 = (bf16[32,4224]{1,0:T(8,128)(2,1)S(1)}, bf16[32,4224]{1,0:T(8,128)(2,1)S(1)}, u32[]{:S(2)}, u32[]{:S(2)}) collective-permute-start(bf16[32,4224]{1,0:T(8,128)(2,1)S(1)} %shard_map.124.refs_0_), channel_id=1, source_target_pairs={{0,4},{1,5},{2,6},{3,7},{4,0},{5,1},{6,2},{7,3},{8,12},{9,13},{10,... | collective-permute-start | bytes 811016 | tf_op jit(solution)/shard_map/ppermute | solution.py:38
  15.1 7.4 %collective-permute-start.4 = (bf16[32,4224]{1,0:T(8,128)(2,1)S(1)}, bf16[32,4224]{1,0:T(8,128)(2,1)S(1)}, u32[]{:S(2)}, u32[]{:S(2)}) collective-permute-start(bf16[32,4224]{1,0:T(8,128)(2,1)S(1)} %shard_map.124.refs_0_), channel_id=1, source_target_pairs={{0,2},{1,3},{2,0},{3,1},{4,6},{5,7},{6,4},{7,5},{8,10},{9,11},{10,... | collective-permute-start | bytes 811016 | tf_op jit(solution)/shard_map/ppermute | solution.py:38
  16.6 6.5 %collective-permute-start.6 = (bf16[8,4224]{1,0:T(8,128)(2,1)S(1)}, bf16[8,4224]{1,0:T(8,128)(2,1)S(1)}, u32[]{:S(2)}, u32[]{:S(2)}) collective-permute-start(bf16[8,4224]{1,0:T(8,128)(2,1)S(1)} %collective-permute-done.5.refs_0_), channel_id=1, source_target_pairs={{0,16},{1,17},{2,18},{3,19},{4,20},{5,21},{6,22},{7,23},{8,24},{9,... | collective-permute-start | bytes 202760 | tf_op jit(solution)/shard_map/ppermute | solution.py:38
  18.0 6.1 %collective-permute-start.7 = (bf16[8,4224]{1,0:T(8,128)(2,1)S(1)}, bf16[8,4224]{1,0:T(8,128)(2,1)S(1)}, u32[]{:S(2)}, u32[]{:S(2)}) collective-permute-start(bf16[8,4224]{1,0:T(8,128)(2,1)S(1)} %collective-permute-done.5.refs_0_), channel_id=1, source_target_pairs={{0,24},{1,25},{2,26},{3,27},{4,28},{5,29},{6,30},{7,31},{8,16},{9,... | collective-permute-start | bytes 202760 | tf_op jit(solution)/shard_map/ppermute | solution.py:38
  18.5 5.6 %collective-permute-start.8 = (bf16[8,4224]{1,0:T(8,128)(2,1)S(1)}, bf16[8,4224]{1,0:T(8,128)(2,1)S(1)}, u32[]{:S(2)}, u32[]{:S(2)}) collective-permute-start(bf16[8,4224]{1,0:T(8,128)(2,1)S(1)} %collective-permute-done.5.refs_0_), channel_id=1, source_target_pairs={{0,8},{1,9},{2,10},{3,11},{4,12},{5,13},{6,14},{7,15},{8,0},{9,1},... | collective-permute-start | bytes 202760 | tf_op jit(solution)/shard_map/ppermute | solution.py:38
  22.5 2.0 %copy-start = (bf16[384,4096]{1,0:T(8,128)(2,1)S(1)}, bf16[384,4096]{1,0:T(8,128)(2,1)}, u32[]{:S(2)}) copy-start(bf16[384,4096]{1,0:T(8,128)(2,1)} %refs_8_.3) | copy-start | bytes 9437188
  22.5 1.7 %collective-permute-start.10 = (bf16[32,4224]{1,0:T(8,128)(2,1)S(1)}, bf16[32,4224]{1,0:T(8,128)(2,1)S(1)}, u32[]{:S(2)}, u32[]{:S(2)}) collective-permute-start(bf16[32,4224]{1,0:T(8,128)(2,1)S(1)} %collective-permute-done.4.refs_1_), channel_id=1, source_target_pairs={{0,1},{1,0},{2,3},{3,2},{4,5},{5,4},{6,7},{7,6},{8,9},{9,8},{10,11... | collective-permute-start | bytes 811016 | tf_op jit(solution)/shard_map/ppermute | solution.py:38
  22.6 1.9 %collective-permute-start.9 = (bf16[32,4224]{1,0:T(8,128)(2,1)S(1)}, bf16[32,4224]{1,0:T(8,128)(2,1)S(1)}, u32[]{:S(2)}, u32[]{:S(2)}) collective-permute-start(bf16[32,4224]{1,0:T(8,128)(2,1)S(1)} %collective-permute-done.3.refs_0_), channel_id=1, source_target_pairs={{0,1},{1,0},{2,3},{3,2},{4,5},{5,4},{6,7},{7,6},{8,9},{9,8},{10,11... | collective-permute-start | bytes 811016 | tf_op jit(solution)/shard_map/ppermute | solution.py:38
  23.1 3.6 %collective-permute-start.11 = (bf16[32,4224]{1,0:T(8,128)(2,1)S(1)}, bf16[32,4224]{1,0:T(8,128)(2,1)S(1)}, u32[]{:S(2)}, u32[]{:S(2)}) collective-permute-start(bf16[32,4224]{1,0:T(8,128)(2,1)S(1)} %shard_map.124.refs_0_), channel_id=1, source_target_pairs={{0,1},{1,0},{2,3},{3,2},{4,5},{5,4},{6,7},{7,6},{8,9},{9,8},{10,11... | collective-permute-start | bytes 811016 | tf_op jit(solution)/shard_map/ppermute | solution.py:38
  24.1 2.6 %collective-permute-start.12 = (bf16[32,4224]{1,0:T(8,128)(2,1)S(1)}, bf16[32,4224]{1,0:T(8,128)(2,1)S(1)}, u32[]{:S(2)}, u32[]{:S(2)}) collective-permute-start(bf16[32,4224]{1,0:T(8,128)(2,1)S(1)} %shard_map.126.refs_1_), channel_id=1, source_target_pairs={{0,1},{1,0},{2,3},{3,2},{4,5},{5,4},{6,7},{7,6},{8,9},{9,8},{10,11... | collective-permute-start | bytes 811016 | tf_op jit(solution)/shard_map/ppermute | solution.py:38
  26.5 2.6 %collective-permute-start.14 = (bf16[64,4480]{1,0:T(8,128)(2,1)S(1)}, bf16[64,4480]{1,0:T(8,128)(2,1)S(1)}, u32[]{:S(2)}, u32[]{:S(2)}) collective-permute-start(bf16[64,4480]{1,0:T(8,128)(2,1)S(1)} %get-tuple-element.63), channel_id=1, source_target_pairs={{0,1},{1,0},{2,3},{3,2},{4,5},{5,4},{6,7},{7,6},{8,9},{9,8},{10,11... | collective-permute-start | bytes 1720328 | tf_op jit(solution)/shard_map/ppermute | solution.py:38
  28.7 2.0 %collective-permute-start.13 = (bf16[64,4480]{1,0:T(8,128)(2,1)S(1)}, bf16[64,4480]{1,0:T(8,128)(2,1)S(1)}, u32[]{:S(2)}, u32[]{:S(2)}) collective-permute-start(bf16[64,4480]{1,0:T(8,128)(2,1)S(1)} %get-tuple-element.61), channel_id=1, source_target_pairs={{0,1},{1,0},{2,3},{3,2},{4,5},{5,4},{6,7},{7,6},{8,9},{9,8},{10,11... | collective-permute-start | bytes 1720328 | tf_op jit(solution)/shard_map/ppermute | solution.py:38
  29.4 9.0 %collective-permute-start.15 = (bf16[32,4480]{1,0:T(8,128)(2,1)S(1)}, bf16[32,4480]{1,0:T(8,128)(2,1)S(1)}, u32[]{:S(2)}, u32[]{:S(2)}) collective-permute-start(bf16[32,4480]{1,0:T(8,128)(2,1)S(1)} %get-tuple-element.64), channel_id=1, source_target_pairs={{0,2},{1,3},{2,0},{3,1},{4,6},{5,7},{6,4},{7,5},{8,10},{9,11},{10,... | collective-permute-start | bytes 860168 | tf_op jit(solution)/shard_map/ppermute | solution.py:38
  30.0 8.7 %collective-permute-start.16 = (bf16[32,4480]{1,0:T(8,128)(2,1)S(1)}, bf16[32,4480]{1,0:T(8,128)(2,1)S(1)}, u32[]{:S(2)}, u32[]{:S(2)}) collective-permute-start(bf16[32,4480]{1,0:T(8,128)(2,1)S(1)} %get-tuple-element.65), channel_id=1, source_target_pairs={{0,4},{1,5},{2,6},{3,7},{4,0},{5,1},{6,2},{7,3},{8,12},{9,13},{10,... | collective-permute-start | bytes 860168 | tf_op jit(solution)/shard_map/ppermute | solution.py:38
  31.0 10.8 %collective-permute-start.20 = (bf16[8,4480]{1,0:T(8,128)(2,1)S(1)}, bf16[8,4480]{1,0:T(8,128)(2,1)S(1)}, u32[]{:S(2)}, u32[]{:S(2)}) collective-permute-start(bf16[8,4480]{1,0:T(8,128)(2,1)S(1)} %get-tuple-element.71), channel_id=1, source_target_pairs={{0,16},{1,17},{2,18},{3,19},{4,20},{5,21},{6,22},{7,23},{8,24},{9,... | collective-permute-start | bytes 215048 | tf_op jit(solution)/shard_map/ppermute | solution.py:38
  33.5 8.9 %collective-permute-start.21 = (bf16[8,4480]{1,0:T(8,128)(2,1)S(1)}, bf16[8,4480]{1,0:T(8,128)(2,1)S(1)}, u32[]{:S(2)}, u32[]{:S(2)}) collective-permute-start(bf16[8,4480]{1,0:T(8,128)(2,1)S(1)} %get-tuple-element.72), channel_id=1, source_target_pairs={{0,24},{1,25},{2,26},{3,27},{4,28},{5,29},{6,30},{7,31},{8,16},{9,... | collective-permute-start | bytes 215048 | tf_op jit(solution)/shard_map/ppermute | solution.py:38
  34.6 7.9 %collective-permute-start.22 = (bf16[8,4480]{1,0:T(8,128)(2,1)S(1)}, bf16[8,4480]{1,0:T(8,128)(2,1)S(1)}, u32[]{:S(2)}, u32[]{:S(2)}) collective-permute-start(bf16[8,4480]{1,0:T(8,128)(2,1)S(1)} %get-tuple-element.73), channel_id=1, source_target_pairs={{0,8},{1,9},{2,10},{3,11},{4,12},{5,13},{6,14},{7,15},{8,0},{9,1},... | collective-permute-start | bytes 215048 | tf_op jit(solution)/shard_map/ppermute | solution.py:38
  38.9 7.3 %collective-permute-start.17 = (bf16[8,4480]{1,0:T(8,128)(2,1)S(1)}, bf16[8,4480]{1,0:T(8,128)(2,1)S(1)}, u32[]{:S(2)}, u32[]{:S(2)}) collective-permute-start(bf16[8,4480]{1,0:T(8,128)(2,1)S(1)} %get-tuple-element.67), channel_id=1, source_target_pairs={{0,16},{1,17},{2,18},{3,19},{4,20},{5,21},{6,22},{7,23},{8,24},{9,... | collective-permute-start | bytes 215048 | tf_op jit(solution)/shard_map/ppermute | solution.py:38
  41.6 6.1 %collective-permute-start.18 = (bf16[8,4480]{1,0:T(8,128)(2,1)S(1)}, bf16[8,4480]{1,0:T(8,128)(2,1)S(1)}, u32[]{:S(2)}, u32[]{:S(2)}) collective-permute-start(bf16[8,4480]{1,0:T(8,128)(2,1)S(1)} %get-tuple-element.68), channel_id=1, source_target_pairs={{0,24},{1,25},{2,26},{3,27},{4,28},{5,29},{6,30},{7,31},{8,16},{9,... | collective-permute-start | bytes 215048 | tf_op jit(solution)/shard_map/ppermute | solution.py:38
  41.9 5.8 %collective-permute-start.19 = (bf16[8,4480]{1,0:T(8,128)(2,1)S(1)}, bf16[8,4480]{1,0:T(8,128)(2,1)S(1)}, u32[]{:S(2)}, u32[]{:S(2)}) collective-permute-start(bf16[8,4480]{1,0:T(8,128)(2,1)S(1)} %get-tuple-element.69), channel_id=1, source_target_pairs={{0,8},{1,9},{2,10},{3,11},{4,12},{5,13},{6,14},{7,15},{8,0},{9,1},... | collective-permute-start | bytes 215048 | tf_op jit(solution)/shard_map/ppermute | solution.py:38
  42.6 5.3 %collective-permute-start.23 = (bf16[8,4480]{1,0:T(8,128)(2,1)S(1)}, bf16[8,4480]{1,0:T(8,128)(2,1)S(1)}, u32[]{:S(2)}, u32[]{:S(2)}) collective-permute-start(bf16[8,4480]{1,0:T(8,128)(2,1)S(1)} %shard_map.133), channel_id=1, source_target_pairs={{0,6},{1,7},{2,4},{3,5},{4,2},{5,3},{6,0},{7,1},{8,14},{9,15},{10,... | collective-permute-start | bytes 215048 | tf_op jit(solution)/shard_map/ppermute | solution.py:38
